TPU v7x, 32 devices: a whole 2x2x4 slice. The times are simulated.
32 devices in a mesh: shard: 8 (over z, y), rep: 4 (over x, core).
Axes of the slice: x: 2, y: 2, z: 4, core: 2. Of those that a mesh axis runs over, the one named last changes fastest.
Arguments:
- tokens: bfloat16 [4, 8, 1024, 1024], P('rep', 'shard'), may hold values from -6 to 6
- cotangent: bfloat16 [4, 8, 1024, 1024], P('rep', 'shard'), may hold values from -6 to 6
- routes: int32 [4, 8, 1024, 8], P('rep', 'shard'), may hold values from 0 to 15, all different within a row; in each aligned block of 1024 rows (0 to 1023, 1024 to 2047, ..., all dimensions but the last counted through in order) at most 640 rows name the same one
- branch: int32 [4, 8], P('rep', 'shard'), may hold values from 512 to 4096, as said below
- attn_gain: bfloat16 [1024], P('shard'), may hold values from 0.5 to 1.5
- query_key_value_weight: bfloat16 [1024, 2048], P('shard'), may hold values from -0.1875 to 0.1875
- w_attn_out: bfloat16 [1024, 1024], P('shard'), may hold values from -6 to 6
- ffn_gain: bfloat16 [1024], P('shard'), may hold values from 0.5 to 1.5
- w_router: bfloat16 [1024, 16], P('shard'), may hold values from -0.375 to 0.375
- w_in: bfloat16 [1024, 16384], P('shard'), may hold values from -0.1875 to 0.1875
- w_out: bfloat16 [1024, 8192], P('shard'), may hold values from -0.25 to 0.25
- adam_first: float32 [4, 8, 3541248], P('rep', 'shard'), may hold values from -0.00030517578 to 0.00030517578
- adam_second: float32 [4, 8, 3541248], P('rep', 'shard'), may hold values from 1.7649145e-10 to 7.059658e-09
- outer_mom: float32 [8, 3541248], P('shard'), may hold values from -0.15625 to 0.15625
Outputs:
- block_out: bfloat16 [4, 8, 1024, 1024], P('rep', 'shard')
- grad_tokens: float32 [4, 8, 1024, 1024], P('rep', 'shard')
- weight_grad: float32 [8, 3541248], P('shard')
- grad_norm: float32 [], replicated
- new_adam_first: float32 [4, 8, 3541248], P('rep', 'shard')
- new_adam_second: float32 [4, 8, 3541248], P('rep', 'shard')
- new_outer_mom: float32 [8, 3541248], P('shard')
- weight_update: float32 [8, 3541248], P('shard')
Inputs may be any that keep to these rules, and one draw needn't show every extreme that they name: `routes`: among the tokens of one device, no expert is named by more than 640 of them, and some expert reaches 640. `branch`: in every prompt group one continuation follows the whole prompt.
All inputs are finite; a program needn't handle non-finite values.
Results may differ from a plain program's by a relative error of at most 0.023.
Values may be sent and summed in bfloat16 or wider, within the bound.
A program may use at most 576 MiB of HBM per device.

v0:
```python
import jax
import jax.numpy as jnp
from jax import lax
from jax.sharding import PartitionSpec as P

QUERY_HEADS = 16
KEY_VALUE_HEADS = 8
HEAD_SIZE = 64
F = 512
EXPERTS = 16
TOP = 8
GROUP_SIZE = 8
CONTINUATION_LEN = 512
STEP = 10
CAP = 640


EPSILON = 1e-06
NEGATIVE = -1e30
ROPE_BASE = 10000.0
BETA_ONE = 0.9
BETA_TWO = 0.95
ADAM_EPS = 1e-08
INNER_RATE = 0.01
DECAY_RATE = 0.1
OUTER_RATE = 0.7
OUTER_MOMENTUM = 0.9
CLIP_NORM = 1.0


def partner(x, axis, bit):
    return lax.ppermute(x, axis, [(i, i ^ 1 << bit) for i in range(lax.axis_size(axis))])


def rope_angles(positions, head_dim):
    half_dim = head_dim // 2
    inverse_freq = ROPE_BASE ** (-(jnp.arange(half_dim, dtype=jnp.float32) * 2.0) / head_dim)
    return positions.astype(jnp.float32)[:, None] * inverse_freq[None, :]


def apply_rotary(value_rows, rotary_angles):
    half_dim = value_rows.shape[-1] // 2
    cosine = jnp.cos(rotary_angles)[:, None, :]
    sine = jnp.sin(rotary_angles)[:, None, :]
    front = value_rows[..., :half_dim]
    back_half = value_rows[..., half_dim:]
    return jnp.concatenate(
        [front * cosine - back_half * sine, back_half * cosine + front * sine], axis=-1
    )


def unrotate(grads, rotary_angles):
    half_dim = grads.shape[-1] // 2
    cosine = jnp.cos(rotary_angles)[:, None, :]
    sine = jnp.sin(rotary_angles)[:, None, :]
    front = grads[..., :half_dim]
    back_half = grads[..., half_dim:]
    return jnp.concatenate(
        [front * cosine + back_half * sine, back_half * cosine - front * sine], axis=-1
    )


def dot_last(left, right):
    return lax.dot_general(
        left, right, (((1,), (1,)), ((), ())), preferred_element_type=jnp.float32
    )


def dot_first(left, right):
    return lax.dot_general(
        left, right, (((0,), (0,)), ((), ())), preferred_element_type=jnp.float32
    )


def rms_forward(value_rows, gain):
    scale = lax.rsqrt(jnp.mean(value_rows * value_rows, axis=-1, keepdims=True) + EPSILON)
    return (value_rows * scale * gain, scale)


def rms_backward(value_rows, scale, gain, grad_out):
    model_width = value_rows.shape[-1]
    grad_gain = jnp.sum(grad_out * value_rows * scale, axis=0)
    inner = jnp.sum(grad_out * gain * value_rows, axis=-1, keepdims=True)
    grad_in = scale * gain * grad_out - value_rows * scale * scale * scale * inner / model_width
    return (grad_in, grad_gain)


def dispatch(route_ids):
    flat_ids = route_ids.reshape(-1)
    onehot = (flat_ids[:, None] == jnp.arange(EXPERTS, dtype=jnp.int32)[None, :]).astype(jnp.int32)
    running = jnp.cumsum(onehot, axis=0)
    slots = jnp.sum((running - 1) * onehot, axis=1)
    row_of = flat_ids * CAP + slots
    owners = jnp.arange(flat_ids.shape[0], dtype=jnp.int32) // TOP
    token_of_row = jnp.zeros((EXPERTS * CAP,), jnp.int32).at[row_of].set(owners)
    return (row_of, token_of_row)


def group_gather(own_part, shard_pos, level_list):
    current = own_part
    for level in range(level_list):
        peer_part = partner(current, "shard", level)
        upper = shard_pos // 2**level % 2
        current = jnp.where(
            upper == 1,
            jnp.concatenate([peer_part, current], axis=1),
            jnp.concatenate([current, peer_part], axis=1),
        )
    return current


def group_reduce(grads, shard_pos, level_list):
    current = grads
    for level in reversed(range(level_list)):
        middle = current.shape[1] // 2
        upper = shard_pos // 2**level % 2
        lower_half = current[:, :middle]
        upper_half = current[:, middle:]
        outgoing = jnp.where(upper == 1, lower_half, upper_half)
        kept = jnp.where(upper == 1, upper_half, lower_half)
        current = kept + partner(outgoing.astype(jnp.bfloat16), "shard", level).astype(
            outgoing.dtype
        )
    return current


def source_block(source, index, extent):
    portion = lax.dynamic_slice_in_dim(source, index * extent, extent, 1)
    return (
        portion[0].reshape(extent, KEY_VALUE_HEADS, HEAD_SIZE),
        portion[1].reshape(extent, KEY_VALUE_HEADS, HEAD_SIZE),
    )


def block_scores(query_g, key_part, limit, offset):
    raw = jnp.einsum(
        "qhgd,khd->hgqk", query_g, key_part, preferred_element_type=jnp.float32
    ) * HEAD_SIZE ** (-0.5)
    key_pos = offset + jnp.arange(key_part.shape[0], dtype=jnp.int32)
    allowed = (key_pos[None, :] < limit[:, None])[None, None]
    return (raw, allowed)


def stats_pass(query_g, source, count, extent, limit, carry):

    def stats_advance(index, state):
        peak, total = state
        key_part, value_part = source_block(source, index, extent)
        raw, allowed = block_scores(query_g, key_part, limit, index * extent)
        masked = jnp.where(allowed, raw, NEGATIVE)
        new_peak = jnp.maximum(peak, jnp.max(masked, axis=-1))
        weights = jnp.where(allowed, jnp.exp(masked - new_peak[..., None]), 0.0)
        return (new_peak, total * jnp.exp(peak - new_peak) + jnp.sum(weights, axis=-1))

    return lax.fori_loop(0, count, stats_advance, carry)


def output_pass(query_g, source, count, extent, limit, log_total, carry):

    def output_advance(index, total_out):
        key_part, value_part = source_block(source, index, extent)
        raw, allowed = block_scores(query_g, key_part, limit, index * extent)
        probs = jnp.where(allowed, jnp.exp(raw - log_total[..., None]), 0.0).astype(jnp.bfloat16)
        return total_out + jnp.einsum(
            "hgqk,khd->qhgd", probs, value_part, preferred_element_type=jnp.float32
        )

    return lax.fori_loop(0, count, output_advance, carry)


def grad_pass(query_g, grad_g, delta, source, count, extent, limit, log_total, carry):

    def grad_advance(index, state):
        grad_query, grad_source = state
        key_part, value_part = source_block(source, index, extent)
        raw, allowed = block_scores(query_g, key_part, limit, index * extent)
        probs = jnp.where(allowed, jnp.exp(raw - log_total[..., None]), 0.0)
        grad_probs = jnp.einsum(
            "qhgd,khd->hgqk", grad_g, value_part, preferred_element_type=jnp.float32
        )
        grad_scores = (probs * (grad_probs - delta[..., None])).astype(jnp.bfloat16)
        grad_query = grad_query + jnp.einsum(
            "hgqk,khd->qhgd", grad_scores, key_part, preferred_element_type=jnp.float32
        ) * HEAD_SIZE ** (-0.5)
        grad_key = jnp.einsum(
            "hgqk,qhgd->khd", grad_scores, query_g, preferred_element_type=jnp.float32
        ) * HEAD_SIZE ** (-0.5)
        grad_value = jnp.einsum(
            "hgqk,qhgd->khd", probs.astype(jnp.bfloat16), grad_g, preferred_element_type=jnp.float32
        )
        addition = jnp.stack([grad_key.reshape(extent, -1), grad_value.reshape(extent, -1)])
        previous = lax.dynamic_slice_in_dim(grad_source, index * extent, extent, 1)
        grad_source = lax.dynamic_update_slice_in_dim(
            grad_source, previous + addition, index * extent, 1
        )
        return (grad_query, grad_source)

    return lax.fori_loop(0, count, grad_advance, carry)


def attend(query_g, parts):
    row_block = query_g.shape[0]
    shape = (query_g.shape[1], query_g.shape[2], row_block)
    state = (jnp.full(shape, NEGATIVE, jnp.float32), jnp.zeros(shape, jnp.float32))
    for source, count, extent, limit in parts:
        state = stats_pass(query_g, source, count, extent, limit, state)
    log_total = state[0] + jnp.log(state[1])
    result = jnp.zeros(query_g.shape, jnp.float32)
    for source, count, extent, limit in parts:
        result = output_pass(query_g, source, count, extent, limit, log_total, result)
    return (result, log_total)


def per_device(
    tokens,
    cotangent,
    routes,
    branch,
    attn_gain,
    query_key_value_weight,
    w_attn_out,
    ffn_gain,
    w_router,
    w_in,
    w_out,
    adam_first,
    adam_second,
    outer_mom,
):
    tokens_per_shard = tokens.shape[2]
    model_width = tokens.shape[3]
    prompt_per_shard = tokens_per_shard - CONTINUATION_LEN
    prompt_len = GROUP_SIZE * prompt_per_shard
    key_block = min(512, prompt_len)
    group_count = QUERY_HEADS // KEY_VALUE_HEADS
    query_total_width = QUERY_HEADS * HEAD_SIZE
    key_value_width = KEY_VALUE_HEADS * HEAD_SIZE
    level_list = GROUP_SIZE.bit_length() - 1
    x_in = tokens.reshape(tokens_per_shard, model_width).astype(jnp.float32)
    grad_top = cotangent.reshape(tokens_per_shard, model_width).astype(jnp.float32)
    route_ids = routes.reshape(tokens_per_shard, TOP)
    branch_len = branch.reshape(())
    shard_pos = lax.axis_index("shard") % GROUP_SIZE
    attn_gain_full, qkv_full, attn_out_full = (
        lax.all_gather(attn_gain, "shard", axis=0, tiled=True),
        lax.all_gather(query_key_value_weight, "shard", axis=0, tiled=True),
        lax.all_gather(w_attn_out, "shard", axis=0, tiled=True),
    )
    attn_gain_f = attn_gain_full.astype(jnp.float32)
    normed_attn_f, attn_scale = rms_forward(x_in, attn_gain_f)
    normed_attn = normed_attn_f.astype(jnp.bfloat16)
    projected_rows = jnp.dot(normed_attn, qkv_full, preferred_element_type=jnp.float32)
    positions = jnp.concatenate(
        [
            shard_pos * prompt_per_shard + jnp.arange(prompt_per_shard, dtype=jnp.int32),
            branch_len + jnp.arange(CONTINUATION_LEN, dtype=jnp.int32),
        ]
    )
    rotary_angles = rope_angles(positions, HEAD_SIZE)
    query_matrix = apply_rotary(
        projected_rows[:, :query_total_width].reshape(tokens_per_shard, QUERY_HEADS, HEAD_SIZE),
        rotary_angles,
    ).astype(jnp.bfloat16)
    key_rows = apply_rotary(
        projected_rows[:, query_total_width : query_total_width + key_value_width].reshape(
            tokens_per_shard, KEY_VALUE_HEADS, HEAD_SIZE
        ),
        rotary_angles,
    ).astype(jnp.bfloat16)
    value_rows = projected_rows[:, query_total_width + key_value_width :].astype(jnp.bfloat16)
    keys_flat = key_rows.reshape(tokens_per_shard, key_value_width)
    prompt_own = jnp.stack([keys_flat[:prompt_per_shard], value_rows[:prompt_per_shard]])
    prompt_kv = group_gather(prompt_own, shard_pos, level_list)
    cont_kv = jnp.stack([keys_flat[prompt_per_shard:], value_rows[prompt_per_shard:]])
    prompt_limit = shard_pos * prompt_per_shard + jnp.arange(prompt_per_shard, dtype=jnp.int32) + 1
    branch_limit = jnp.full((CONTINUATION_LEN,), branch_len, jnp.int32)
    cont_limit = jnp.arange(CONTINUATION_LEN, dtype=jnp.int32) + 1
    prompt_count = (shard_pos * prompt_per_shard + prompt_per_shard + key_block - 1) // key_block
    cont_count = (branch_len + key_block - 1) // key_block
    prompt_query_rows = query_matrix[:prompt_per_shard].reshape(
        prompt_per_shard, KEY_VALUE_HEADS, group_count, HEAD_SIZE
    )
    continuation_query = query_matrix[prompt_per_shard:].reshape(
        CONTINUATION_LEN, KEY_VALUE_HEADS, group_count, HEAD_SIZE
    )
    prompt_attn, prompt_lse = attend(
        prompt_query_rows, [(prompt_kv, prompt_count, key_block, prompt_limit)]
    )
    cont_attn, cont_lse = attend(
        continuation_query,
        [
            (prompt_kv, cont_count, key_block, branch_limit),
            (cont_kv, 1, CONTINUATION_LEN, cont_limit),
        ],
    )
    attention_unscaled = jnp.concatenate([prompt_attn, cont_attn]).reshape(
        tokens_per_shard, query_total_width
    )
    attn_low = attention_unscaled.astype(jnp.bfloat16)
    x_mid = x_in + dot_last(attn_low, attn_out_full)
    ffn_gain_full, router_full, w_in_full, w_out_full = (
        lax.all_gather(ffn_gain, "shard", axis=0, tiled=True),
        lax.all_gather(w_router, "shard", axis=0, tiled=True),
        lax.all_gather(w_in, "shard", axis=0, tiled=True),
        lax.all_gather(w_out, "shard", axis=0, tiled=True),
    )
    ffn_gain_f = ffn_gain_full.astype(jnp.float32)
    normed_ffn_f, ffn_scale = rms_forward(x_mid, ffn_gain_f)
    normed_ffn = normed_ffn_f.astype(jnp.bfloat16)
    logits = jnp.dot(normed_ffn, router_full, preferred_element_type=jnp.float32)
    route_hot = (
        route_ids[:, :, None] == jnp.arange(EXPERTS, dtype=jnp.int32)[None, None, :]
    ).astype(jnp.float32)
    picked = jnp.sum(route_hot * logits[:, None, :], axis=-1)
    gates = jax.nn.softmax(picked, axis=-1)
    row_of, token_of_row = dispatch(route_ids)
    gate_of_row = jnp.zeros((EXPERTS * CAP,), jnp.float32).at[row_of].set(gates.reshape(-1))
    expert_in = normed_ffn[token_of_row].reshape(EXPERTS, CAP, model_width)
    w_in_grid = w_in_full.reshape(model_width, EXPERTS, 2 * F)
    w_out_grid = w_out_full.reshape(model_width, EXPERTS, F)
    gate_up = jnp.einsum("ecd,def->ecf", expert_in, w_in_grid, preferred_element_type=jnp.float32)
    gate_part = gate_up[..., :F]
    up_part = gate_up[..., F:]
    sigmoid_gate = jax.nn.sigmoid(gate_part)
    activated = gate_part * sigmoid_gate
    hidden_low = (activated * up_part).astype(jnp.bfloat16)
    expert_out = jnp.einsum(
        "ecf,def->ecd", hidden_low, w_out_grid, preferred_element_type=jnp.float32
    ).reshape(EXPERTS * CAP, model_width)
    routed = expert_out[row_of].reshape(tokens_per_shard, TOP, model_width)
    x_final = x_mid + jnp.sum(gates[:, :, None] * routed, axis=1)
    block_out = x_final.astype(jnp.bfloat16)
    w_in_back, w_out_back = (
        lax.all_gather(w_in, "shard", axis=0, tiled=True),
        lax.all_gather(w_out, "shard", axis=0, tiled=True),
    )
    w_in_grid = w_in_back.reshape(model_width, EXPERTS, 2 * F)
    w_out_grid = w_out_back.reshape(model_width, EXPERTS, F)
    grad_gates = jnp.sum(routed * grad_top[:, None, :], axis=-1)
    grad_expert_out = (
        (gate_of_row[:, None] * grad_top[token_of_row])
        .astype(jnp.bfloat16)
        .reshape(EXPERTS, CAP, model_width)
    )
    grad_hidden = jnp.einsum(
        "ecd,def->ecf", grad_expert_out, w_out_grid, preferred_element_type=jnp.float32
    )
    grad_gate = grad_hidden * up_part * sigmoid_gate * (1.0 + gate_part * (1.0 - sigmoid_gate))
    grad_up = grad_hidden * activated
    grad_gate_up = jnp.concatenate([grad_gate, grad_up], axis=-1).astype(jnp.bfloat16)
    grad_expert_in = jnp.einsum(
        "ecf,def->ecd", grad_gate_up, w_in_grid, preferred_element_type=jnp.float32
    ).reshape(EXPERTS * CAP, model_width)
    grad_from_experts = jax.ops.segment_sum(
        grad_expert_in, token_of_row, num_segments=tokens_per_shard
    )
    grad_picked = gates * (grad_gates - jnp.sum(gates * grad_gates, axis=-1, keepdims=True))
    grad_logits = jnp.sum(route_hot * grad_picked[:, :, None], axis=1).astype(jnp.bfloat16)
    grad_router_w = dot_first(normed_ffn, grad_logits)
    grad_normed_ffn = grad_from_experts + dot_last(grad_logits, router_full)
    grad_mid_norm, grad_ffn_gain = rms_backward(x_mid, ffn_scale, ffn_gain_f, grad_normed_ffn)
    grad_mid = grad_top + grad_mid_norm
    grad_branch = grad_mid.astype(jnp.bfloat16)
    grad_attn_w = dot_first(grad_branch, attn_low)
    grad_attention_narrow = jnp.dot(
        grad_branch, attn_out_full, preferred_element_type=jnp.float32
    ).astype(jnp.bfloat16)
    delta_all = jnp.sum(
        (grad_attention_narrow.astype(jnp.float32) * attention_unscaled).reshape(
            tokens_per_shard, KEY_VALUE_HEADS, group_count, HEAD_SIZE
        ),
        axis=-1,
    ).transpose(1, 2, 0)
    gradient_layout = grad_attention_narrow.reshape(
        tokens_per_shard, KEY_VALUE_HEADS, group_count, HEAD_SIZE
    )
    prompt_grad_src = jnp.zeros((2, prompt_len, key_value_width), jnp.float32)
    grad_prompt_query, prompt_grad_src = grad_pass(
        prompt_query_rows,
        gradient_layout[:prompt_per_shard],
        delta_all[..., :prompt_per_shard],
        prompt_kv,
        prompt_count,
        key_block,
        prompt_limit,
        prompt_lse,
        (jnp.zeros(prompt_query_rows.shape, jnp.float32), prompt_grad_src),
    )
    grad_cont_query, prompt_grad_src = grad_pass(
        continuation_query,
        gradient_layout[prompt_per_shard:],
        delta_all[..., prompt_per_shard:],
        prompt_kv,
        cont_count,
        key_block,
        branch_limit,
        cont_lse,
        (jnp.zeros(continuation_query.shape, jnp.float32), prompt_grad_src),
    )
    grad_cont_query, continuation_grad_source = grad_pass(
        continuation_query,
        gradient_layout[prompt_per_shard:],
        delta_all[..., prompt_per_shard:],
        cont_kv,
        1,
        CONTINUATION_LEN,
        cont_limit,
        cont_lse,
        (grad_cont_query, jnp.zeros((2, CONTINUATION_LEN, key_value_width), jnp.float32)),
    )
    prompt_self_gradient = group_reduce(prompt_grad_src, shard_pos, level_list)
    gradient_key_rows = jnp.concatenate(
        [prompt_self_gradient[0], continuation_grad_source[0]]
    ).reshape(tokens_per_shard, KEY_VALUE_HEADS, HEAD_SIZE)
    grad_values = jnp.concatenate([prompt_self_gradient[1], continuation_grad_source[1]])
    grad_queries = jnp.concatenate([grad_prompt_query, grad_cont_query]).reshape(
        tokens_per_shard, QUERY_HEADS, HEAD_SIZE
    )
    grad_projected = jnp.concatenate(
        [
            unrotate(grad_queries, rotary_angles).reshape(tokens_per_shard, -1),
            unrotate(gradient_key_rows, rotary_angles).reshape(tokens_per_shard, -1),
            grad_values,
        ],
        axis=1,
    ).astype(jnp.bfloat16)
    grad_qkv_w = dot_first(normed_attn, grad_projected)
    grad_normed_attn = dot_last(grad_projected, qkv_full)
    grad_x_norm, grad_attn_gain = rms_backward(x_in, attn_scale, attn_gain_f, grad_normed_attn)
    grad_input = grad_mid + grad_x_norm
    owned = (
        lax.psum_scatter(grad_attn_gain, "shard", scatter_dimension=0, tiled=True),
        lax.psum_scatter(grad_qkv_w, "shard", scatter_dimension=0, tiled=True),
        lax.psum_scatter(grad_attn_w, "shard", scatter_dimension=0, tiled=True),
        lax.psum_scatter(grad_ffn_gain, "shard", scatter_dimension=0, tiled=True),
        lax.psum_scatter(grad_router_w, "shard", scatter_dimension=0, tiled=True),
    )
    other_flat = jnp.concatenate(
        [owned[0], owned[1].reshape(-1), owned[2].reshape(-1), owned[3], owned[4].reshape(-1)]
    )
    own_rows = model_width // lax.axis_size("shard")
    term_in = jnp.einsum(
        "ecd,ecf->def", expert_in, grad_gate_up, preferred_element_type=jnp.float32
    ).reshape(own_rows * lax.axis_size("shard"), -1)
    term_out = jnp.einsum(
        "ecd,ecf->def", grad_expert_out, hidden_low, preferred_element_type=jnp.float32
    ).reshape(own_rows * lax.axis_size("shard"), -1)
    expert_grads = lax.psum_scatter(
        jnp.concatenate([term_in, term_out], axis=1), "shard", scatter_dimension=0, tiled=True
    )
    local_grad = jnp.concatenate(
        [
            other_flat,
            expert_grads[:, : EXPERTS * 2 * F].reshape(-1),
            expert_grads[:, EXPERTS * 2 * F :].reshape(-1),
        ]
    )
    total_grad = lax.psum(local_grad.astype(jnp.bfloat16), "rep").astype(jnp.float32)
    norm_square = lax.psum(jnp.sum(total_grad * total_grad), "shard")
    grad_norm = jnp.sqrt(norm_square)
    clipped = total_grad * (CLIP_NORM / jnp.maximum(grad_norm, CLIP_NORM))
    new_first = BETA_ONE * adam_first.reshape(-1) + (1.0 - BETA_ONE) * clipped
    new_second = BETA_TWO * adam_second.reshape(-1) + (1.0 - BETA_TWO) * clipped * clipped
    weight_flat = jnp.concatenate(
        [
            portion.astype(jnp.float32).reshape(-1)
            for portion in (
                attn_gain,
                query_key_value_weight,
                w_attn_out,
                ffn_gain,
                w_router,
                w_in,
                w_out,
            )
        ]
    )
    step_delta = -INNER_RATE * (
        new_first
        / (1.0 - BETA_ONE**STEP)
        / (jnp.sqrt(new_second / (1.0 - BETA_TWO**STEP)) + ADAM_EPS)
        + DECAY_RATE * weight_flat
    )
    mean_delta = lax.psum(step_delta.astype(jnp.bfloat16), "rep").astype(
        jnp.float32
    ) / lax.axis_size("rep")
    pseudo = -mean_delta
    new_mom = OUTER_MOMENTUM * outer_mom.reshape(-1) + pseudo
    weight_update = -OUTER_RATE * (pseudo + OUTER_MOMENTUM * new_mom)
    return (
        block_out.reshape(tokens.shape),
        grad_input.reshape(tokens.shape),
        total_grad.reshape(outer_mom.shape),
        grad_norm,
        new_first.reshape(adam_first.shape),
        new_second.reshape(adam_second.shape),
        new_mom.reshape(outer_mom.shape),
        weight_update.reshape(outer_mom.shape),
    )


def solution(mesh):
    placed = (
        P("rep", "shard", None, None),
        P("rep", "shard", None, None),
        P("rep", "shard", None, None),
        P("rep", "shard"),
        P("shard"),
        P("shard", None),
        P("shard", None),
        P("shard"),
        P("shard", None),
        P("shard", None),
        P("shard", None),
        P("rep", "shard", None),
        P("rep", "shard", None),
        P("shard", None),
    )
    return jax.shard_map(
        per_device,
        mesh=mesh,
        in_specs=placed,
        out_specs=(
            P("rep", "shard", None, None),
            P("rep", "shard", None, None),
            P("shard", None),
            P(),
            P("rep", "shard", None),
            P("rep", "shard", None),
            P("shard", None),
            P("shard", None),
        ),
        check_vma=False,
    )
```

profile of v0, /device:TPU:0, one launch (start us, length us, event | category | flops | bytes accessed | tf_op | source)
XLA Modules:
  0.0 4982.1 jit_solution(18252569437376783560)
XLA Ops:
  18.7 22.4 all-gather
  42.2 44.1 all-gather.7.cloned.1.call-done
  86.3 8.6 fusion.133
  113.2 34.7 collective-permute-done
  169.2 72.8 %collective-permute-done.1 = bf16[2,1024,512]{2,1,0:T(8,128)(2,1)} collective-permute-done((bf16[2,1024,512]{2,1,0:T(8,128)(2,1)}, bf16[2,1024,512]{2,1,0:T(8,128)(2,1)}, u32[]{:S(2)}, u32[]{:S(2)}) %collective-permute-start.1) | collective-permute-done | bytes 2097184 | tf_op jit(solution)/shard_map/ppermute | solution.py:32
  251.9 220.4 %all-gather.1 = bf16[8,1,128]{2,1,0:T(2,128)(2,1)S(1)} all-gather(bf16[1,1,128]{2,1,0:T(2,128)(2,1)S(1)} %bitcast.638), channel_id=1, replica_groups=mesh['shard'=8,'rep'=4] {'shard'}, dimensions={0}, use_global_device_ids=true | all-gather | bytes 2304 | tf_op jit(solution)/shard_map/all_gather | solution.py:302
  481.2 30.6 scatter_custom_fusion
  511.9 56.6 %gather_fusion.2 = f32[10240,1024]{1,0:T(8,128)} fusion(f32[1024,1024]{1,0:T(8,128)} %copy.262, s32[10240]{0:T(1024)S(1)} %fusion.105), kind=kCustom, calls=%fused_computation.2 | custom fusion | bytes 83927040 | tf_op jit(solution)/shard_map/gather | solution.py:341
  568.5 228.0 %all_gather.27 = bf16[1024,16]{0,1:T(8,128)(2,1)} all-gather(bf16[128,16]{0,1:T(8,128)(2,1)S(1)} %copy-done.87), channel_id=1, replica_groups=mesh['shard'=8,'rep'=4] {'shard'}, dimensions={0}, use_global_device_ids=true | all-gather | bytes 36864 | tf_op jit(solution)/shard_map/all_gather | solution.py:303
  819.1 9.6 maximum_select_fusion
  828.7 11.9 copy.246
  840.7 47.2 while.93
  904.4 8.9 fusion.103
  914.9 46.7 while.94
  967.7 9.7 while.92
  996.1 44.0 gather_fusion
  1043.9 30.8 scatter_custom_fusion.1
  1074.8 40.4 fusion.136
  1115.2 45.3 multiply_convert_fusion.2
  1160.5 25.4 fusion.137
  1185.9 56.7 %gather_fusion.1 = f32[8192,1024]{1,0:T(8,128)} fusion(f32[10240,1024]{1,0:T(8,128)} %bitcast.543, s32[8192]{0:T(1024)S(1)} %copy-done.70), kind=kCustom, calls=%fused_computation.1 | custom fusion | bytes 67141632 | tf_op jit(solution)/shard_map/gather | solution.py:330
  1242.7 18.0 fusion.51
  1263.7 38.3 fusion.61
  1302.0 92.4 %scatter_fusion = f32[1024,1024]{1,0:T(8,128)} fusion(f32[1024,1024]{1,0:T(8,128)} %fusion.140, s32[10240]{0:T(1024)S(1)} %copy-done.65, f32[10240,1024]{1,0:T(8,128)} %bitcast.564), kind=kCustom, calls=%fused_computation.5 | custom fusion | flops 10485760 | bytes 125870080 | tf_op jit(solution)/shard_map/scatter-add | solution.py:354
  1431.9 42.4 while.95
  1437.5 9.6 fusion.264
  1454.1 10.3 fusion.265
  1475.9 189.3 %while.96 = (s32[]{:T(128)}, f32[512,8,2,64]{0,3,2,1:T(8,128)}, f32[2,4096,512]{1,2,0:T(8,128)}, s32[]{:T(128)}, bf16[2,4096,512]{1,2,0:T(8,128)(2,1)}, /*index=...) while((s32[]{:T(128)}, f32[512,8,2,64]{0,3,2,1:T(8,128)}, ...), condition=%wide.region_34.35_spmd.clone, body=%wide.region_33.34_spmd.clone.sunk | while | flops 2728657920 | bytes 163415888 | solution.py:198
  1480.3 9.5 fusion.279
  1518.2 9.5 fusion.279
  1556.0 9.5 fusion.279
  1593.9 9.5 fusion.279
  1631.8 9.5 fusion.279
  1665.2 8.4 select_convert_fusion
  1673.7 291.4 %collective-permute-start.3 = (bf16[2,2048,512]{1,2,0:T(8,128)(2,1)}, bf16[2,2048,512]{1,2,0:T(8,128)(2,1)}, u32[]{:S(2)}, u32[]{:S(2)}) collective-permute-start(bf16[2,2048,512]{1,2,0:T(8,128)(2,1)} %select_convert_fusion), channel_id=1, source_target_pairs={{0,16},{4,20},{8,24},{12,28},{16,0},{20,4},{24,8},{28,12},{1,17},{... | collective-permute-start | bytes 12582920 | tf_op jit(solution)/shard_map/ppermute | solution.py:32
  1974.2 8.8 fusion.54
  1983.0 68.5 %collective-permute-done.3 = bf16[2,2048,512]{1,2,0:T(8,128)(2,1)} collective-permute-done((bf16[2,2048,512]{1,2,0:T(8,128)(2,1)}, bf16[2,2048,512]{1,2,0:T(8,128)(2,1)}, u32[]{:S(2)}, u32[]{:S(2)}) %collective-permute-start.3) | collective-permute-done | bytes 4194336 | tf_op jit(solution)/shard_map/ppermute | solution.py:32
  2072.2 15.6 collective-permute-done.4
  2096.7 87.8 %collective-permute-start.5 = (bf16[2,512,512]{1,2,0:T(8,128)(2,1)}, bf16[2,512,512]{1,2,0:T(8,128)(2,1)}, u32[]{:S(2)}, u32[]{:S(2)}) collective-permute-start(bf16[2,512,512]{1,2,0:T(8,128)(2,1)} %select_convert_fusion.2), channel_id=1, source_target_pairs={{0,4},{4,0},{8,12},{12,8},{16,20},{20,16},{24,28},{28,24},{1,5},{5... | collective-permute-start | bytes 3145736 | tf_op jit(solution)/shard_map/ppermute | solution.py:32
  2202.4 13.9 fusion.87
  2217.0 30.1 fusion.63
  2247.2 31.1 copy.285
  2278.3 40.6 fusion.60
  2318.9 66.2 %copy.284 = f32[1024,16384]{1,0:T(8,128)} copy(f32[1024,16384]{0,1:T(8,128)} %bitcast.58) | data formatting | bytes 134217728 | tf_op jit(solution)/shard_map/reshape | solution.py:444
  2385.0 67.4 %pad_maximum_fusion = f32[1024,24576]{1,0:T(8,128)} fusion(f32[1024,8192]{1,0:T(8,128)} %copy.285, f32[1024,16384]{1,0:T(8,128)} %copy.284), kind=kLoop, calls=%fused_computation.90 | loop fusion | flops 25165824 | bytes 201326592 | tf_op jit(solution)/shard_map/concatenate | solution.py:449
  2465.8 9.1 dynamic-update-slice.1
  2483.1 65.0 %dynamic-update-slice.5 = bf16[3541248]{0:T(1024)(128)(2,1)} dynamic-update-slice(bf16[3541248]{0:T(1024)(128)(2,1)} %dynamic-update-slice.4, bf16[2097152]{0:T(1024)(128)(2,1)} %bitcast.574, s32[]{} %constant.344) | dynamic-update-slice | bytes 8388612
  2549.0 10.0 fusion.77
  2559.0 19.3 all-reduce.3
  2582.5 9.1 dynamic-update-slice.8
  2599.7 1528.9 %reduce-scatter.13.cloned.1.call-done = f32[128,24576]{1,0:T(8,128)} async-done(((f32[1024,24576]{1,0:T(8,128)}), f32[128,24576]{1,0:T(8,128)}) %reduce-scatter.13.cloned.1.call-update) | async-done | bytes 12582928
  4138.5 64.9 %dynamic-update-slice.12 = bf16[3541248]{0:T(1024)(128)(2,1)} dynamic-update-slice(bf16[3541248]{0:T(1024)(128)(2,1)} %dynamic-update-slice.11, bf16[2097152]{0:T(1024)(128)(2,1)} %bitcast.575, s32[]{} %constant.344) | dynamic-update-slice | bytes 8388612
  4203.4 32.4 dynamic-update-slice.13
  4235.8 159.3 %multiply_reduce_fusion.2 = (f32[3541248]{0:T(1024)}, f32[3541248]{0:T(1024)}) fusion(f32[1,1,3541248]{2,1,0:T(1,128)} %param.38, f32[1,1,3541248]{2,1,0:T(1,128)} %param.37), kind=kLoop, calls=%fused_computation.120 | loop fusion | flops 7082496 | bytes 56659968 | tf_op jit(solution)/shard_map/mul | solution.py:463
  4401.7 32.4 dynamic-update-slice.6
  4434.1 20.5 psum.22
  4455.4 26.0 multiply_convert_fusion.4
  4481.4 152.2 %multiply_reduce_fusion.1 = f32[3541248]{0:T(1024)} fusion(f32[1,3541248]{1,0:T(1,128)} %param.39), kind=kLoop, calls=%fused_computation.119 | loop fusion | flops 3541248 | bytes 28329984 | tf_op jit(solution)/shard_map/mul | solution.py:488
  4649.7 54.4 %reshape.676 = f32[1,1,3541248]{2,1,0:T(1,128)} reshape(f32[3541248]{0:T(1024)} %get-tuple-element.858) | data formatting | bytes 28329984 | tf_op jit(solution)/shard_map/reshape | solution.py:495
  4704.2 54.3 %reshape.677 = f32[1,1,3541248]{2,1,0:T(1,128)} reshape(f32[3541248]{0:T(1024)} %get-tuple-element.857) | data formatting | bytes 28329984 | tf_op jit(solution)/shard_map/reshape | solution.py:496
  4758.5 81.7 %reshape.675 = f32[1,3541248]{1,0:T(1,128)} reshape(bf16[3541248]{0:T(1024)(128)(2,1)S(1)} %bitcast.561) | data formatting | bytes 21247488 | tf_op jit(solution)/shard_map/reshape | solution.py:493
  4840.1 12.4 add_multiply_fusion
  4852.5 54.1 %reshape.683 = f32[1,3541248]{1,0:T(1,128)} reshape(f32[3541248]{0:T(1024)} %get-tuple-element.881) | data formatting | bytes 28329984 | tf_op jit(solution)/shard_map/reshape | solution.py:497
  4906.6 67.3 %reshape.684 = f32[1,3541248]{1,0:T(1,128)} reshape(f32[3541248]{0:T(1024)S(1)} %get-tuple-element.880) | data formatting | bytes 28329984 | tf_op jit(solution)/shard_map/reshape | solution.py:498
  (526 shorter events, 579.1 us)
Async XLA Ops:
  7.2 79.1 %all-gather.7.cloned.1.call-start = ((), (), s32[]{:S(2)}) async-start(), calls=%async_computation.4 | async-start | bytes 4718592 | tf_op jit(solution)/shard_map/all_gather | solution.py:246
  7.9 976.2 %all-gather.9.cloned.1.call-start = ((), (), s32[]{:S(2)}) async-start(), calls=%async_computation.5 | async-start | bytes 2359296 | tf_op jit(solution)/shard_map/all_gather | solution.py:247
  8.7 1066.1 %all-gather.11.cloned.1.call-start = ((), (), s32[]{:S(2)}) async-start(), calls=%async_computation.6 | async-start | bytes 37748736 | tf_op jit(solution)/shard_map/all_gather | solution.py:304
  15.1 1100.1 %all-gather.13.cloned.1.call-start = ((), (), s32[]{:S(2)}) async-start(), calls=%async_computation.7 | async-start | bytes 18874368 | tf_op jit(solution)/shard_map/all_gather | solution.py:305
  18.7 76.3 %copy-start.16 = (bf16[1,1,1024,1024]{2,3,1,0:T(8,128)(2,1)}, bf16[1,1,1024,1024]{2,3,1,0:T(8,128)(2,1)S(1)}, u32[]{:S(2)}) copy-start(bf16[1,1,1024,1024]{2,3,1,0:T(8,128)(2,1)S(1)} %copy.241) | copy-start | bytes 6291460
  41.1 53.9 %copy-start.89 = (f32[8,1,128]{2,1,0:T(1,128)}, f32[8,1,128]{2,1,0:T(1,128)S(1)}, u32[]{:S(2)}) copy-start(f32[8,1,128]{2,1,0:T(1,128)S(1)} %convert_element_type.165) | copy-start | bytes 12292
  41.6 53.3 %copy-start.92 = (f32[1024]{0:T(1024)}, f32[1024]{0:T(1024)S(1)}, u32[]{:S(2)}) copy-start(f32[1024]{0:T(1024)S(1)} %add_rsqrt_fusion.1) | copy-start | bytes 12292
  42.2 60.7 %copy-start.40 = (f32[1024,32]{0,1:T(8,128)}, f32[1024,32]{0,1:T(8,128)S(1)}, u32[]{:S(2)}) copy-start(f32[1024,32]{0,1:T(8,128)S(1)} %get-tuple-element.901) | copy-start | bytes 393220
  42.2 766.5 %copy-start.37 = (f32[1024,32]{0,1:T(8,128)}, f32[1024,32]{0,1:T(8,128)S(1)}, u32[]{:S(2)}) copy-start(f32[1024,32]{0,1:T(8,128)S(1)} %get-tuple-element.900) | copy-start | bytes 393220
  99.8 52.6 %copy-start.28 = (bf16[128,8192]{1,0:T(8,128)(2,1)S(1)}, bf16[128,8192]{1,0:T(8,128)(2,1)}, u32[]{:S(2)}) copy-start(bf16[128,8192]{1,0:T(8,128)(2,1)} %param.36) | copy-start | bytes 6291460
  104.8 707.1 %copy-start.23 = (bf16[1024,8,32]{0,2,1:T(8,128)(2,1)}, bf16[1024,8,32]{0,2,1:T(8,128)(2,1)S(1)}, u32[]{:S(2)}) copy-start(bf16[1024,8,32]{0,2,1:T(8,128)(2,1)S(1)} %get-tuple-element.892) | copy-start | bytes 1572868
  104.8 707.1 %copy-start.25 = (bf16[1024,8,32]{0,2,1:T(8,128)(2,1)}, bf16[1024,8,32]{0,2,1:T(8,128)(2,1)S(1)}, u32[]{:S(2)}) copy-start(bf16[1024,8,32]{0,2,1:T(8,128)(2,1)S(1)} %get-tuple-element.893) | copy-start | bytes 1572868
  104.8 50.2 %copy-start.56 = (s32[1,1,1024,8]{2,3,1,0:T(8,128)S(1)}, s32[1,1,1024,8]{2,3,1,0:T(8,128)}, u32[]{:S(2)}) copy-start(s32[1,1,1024,8]{2,3,1,0:T(8,128)} %param.28) | copy-start | bytes 98308
  112.6 35.3 collective-permute-start
  151.4 90.6 %collective-permute-start.1 = (bf16[2,1024,512]{2,1,0:T(8,128)(2,1)}, bf16[2,1024,512]{2,1,0:T(8,128)(2,1)}, u32[]{:S(2)}, u32[]{:S(2)}) collective-permute-start(bf16[2,1024,512]{2,1,0:T(8,128)(2,1)} %maximum_select_fusion.2), channel_id=1, source_target_pairs={{0,8},{4,12},{8,0},{12,4},{16,24},{20,28},{24,16},{28,20},{1,9},{5... | collective-permute-start | bytes 6291464 | tf_op jit(solution)/shard_map/ppermute | solution.py:32
  154.9 2393.2 %reduce-scatter.11.cloned.1.call-start = ((), (), s32[]{:S(2)}) async-start(), calls=%async_computation.10 | async-start | bytes 73728 | tf_op jit(solution)/shard_map/reduce_scatter | solution.py:436
  164.2 309.8 %copy-start.14 = (bf16[1,1,1024,1024]{2,3,1,0:T(8,128)(2,1)}, bf16[1,1,1024,1024]{2,3,1,0:T(8,128)(2,1)S(1)}, u32[]{:S(2)}) copy-start(bf16[1,1,1024,1024]{2,3,1,0:T(8,128)(2,1)S(1)} %copy.261) | copy-start | bytes 6291460
  164.2 87.7 %copy-start.97 = (bf16[128]{0:T(256)(128)(2,1)S(1)}, bf16[128]{0:T(256)(128)(2,1)}, u32[]{:S(2)}) copy-start(bf16[128]{0:T(256)(128)(2,1)} %param.33) | copy-start | bytes 772
  248.2 571.0 %collective-permute-start.2 = (bf16[2,2048,512]{2,1,0:T(8,128)(2,1)}, bf16[2,2048,512]{2,1,0:T(8,128)(2,1)}, u32[]{:S(2)}, u32[]{:S(2)}) collective-permute-start(bf16[2,2048,512]{2,1,0:T(8,128)(2,1)} %maximum_select_fusion.1), channel_id=1, source_target_pairs={{0,16},{4,20},{8,24},{12,28},{16,0},{20,4},{24,8},{28,12},{1,17},{... | collective-permute-start | bytes 12582920 | tf_op jit(solution)/shard_map/ppermute | solution.py:32
  481.2 315.4 %copy-start.71 = (s32[8192,1]{0,1:T(1,128)}, s32[8192,1]{0,1:T(1,128)S(1)}, u32[]{:S(2)}) copy-start(s32[8192,1]{0,1:T(1,128)S(1)} %compare_select_fusion) | copy-start | bytes 98308
  511.9 56.7 %copy-start.64 = (s32[10240]{0:T(1024)}, s32[10240]{0:T(1024)S(1)}, u32[]{:S(2)}) copy-start(s32[10240]{0:T(1024)S(1)} %scatter_custom_fusion) | copy-start | bytes 122884
  511.9 56.6 %copy-start.62 = (s32[10240]{0:T(1024)}, s32[10240]{0:T(1024)S(1)}, u32[]{:S(2)}) copy-start(s32[10240]{0:T(1024)S(1)} %fusion.105) | copy-start | bytes 122884
  511.9 56.6 %copy-start.87 = (bf16[128,16]{0,1:T(8,128)(2,1)S(1)}, bf16[128,16]{0,1:T(8,128)(2,1)}, u32[]{:S(2)}) copy-start(bf16[128,16]{0,1:T(8,128)(2,1)} %param.34) | copy-start | bytes 12292
  797.4 107.0 %copy-start.35 = (pred[512,512]{0,1:T(8,128)(4,1)}, pred[512,512]{0,1:T(8,128)(4,1)S(1)}, u32[]{:S(2)}) copy-start(pred[512,512]{0,1:T(8,128)(4,1)S(1)} %iota_compare_fusion) | copy-start | bytes 786436
  977.3 12.2 copy-start.4
  977.3 12.2 copy-start.83
  996.1 44.0 copy-start.68
  996.1 46.0 copy-start.57
  1043.6 71.6 %copy-start.29 = (f32[1024,8]{1,0:T(8,128)}, f32[1024,8]{1,0:T(8,128)S(1)}, u32[]{:S(2)}) copy-start(f32[1024,8]{1,0:T(8,128)S(1)} %copy.251) | copy-start | bytes 98308
  1074.7 40.5 copy-start.54
  1160.5 25.4 copy-start.70
  1185.9 56.7 %copy-start.30 = (f32[1024,8]{1,0:T(8,128)S(1)}, f32[1024,8]{1,0:T(8,128)}, u32[]{:S(2)}) copy-start(f32[1024,8]{1,0:T(8,128)} %copy-done.29) | copy-start | bytes 98308
  1242.6 18.2 copy-start.49
  1242.6 18.2 copy-start.73
  1242.6 18.2 copy-start.75
  1242.7 18.2 copy-start.58
  1242.7 18.3 copy-start.69
  1263.7 38.3 copy-start.65
  1431.9 44.0 copy-start.3
  1665.2 299.8 %copy-start.11 = (bf16[1024,1024]{0,1:T(8,128)(2,1)S(1)}, bf16[1024,1024]{0,1:T(8,128)(2,1)}, u32[]{:S(2)}) copy-start(bf16[1024,1024]{0,1:T(8,128)(2,1)} %multiply_convert_fusion.7) | copy-start | bytes 6291460
  1665.2 299.8 %copy-start.67 = (bf16[1024,16]{0,1:T(8,128)(2,1)S(1)}, bf16[1024,16]{0,1:T(8,128)(2,1)}, u32[]{:S(2)}) copy-start(bf16[1024,16]{0,1:T(8,128)(2,1)} %copy-done.66) | copy-start | bytes 98308
  1673.7 377.8 %collective-permute-start.3 = (bf16[2,2048,512]{1,2,0:T(8,128)(2,1)}, bf16[2,2048,512]{1,2,0:T(8,128)(2,1)}, u32[]{:S(2)}, u32[]{:S(2)}) collective-permute-start(bf16[2,2048,512]{1,2,0:T(8,128)(2,1)} %select_convert_fusion), channel_id=1, source_target_pairs={{0,16},{4,20},{8,24},{12,28},{16,0},{20,4},{24,8},{28,12},{1,17},{... | collective-permute-start | bytes 12582920 | tf_op jit(solution)/shard_map/ppermute | solution.py:32
  1966.4 613.5 %reduce-scatter.9.cloned.1.call-start = ((), (), s32[]{:S(2)}) async-start(), calls=%async_computation.9 | async-start | bytes 4718592 | tf_op jit(solution)/shard_map/reduce_scatter | solution.py:434
  1974.0 607.1 %reduce-scatter.7.cloned.1.call-start = ((), (), s32[]{:S(2)}) async-start(), calls=%async_computation.8 | async-start | bytes 9437184 | tf_op jit(solution)/shard_map/reduce_scatter | solution.py:433
  1983.0 78.4 %copy-start.8 = (bf16[8,2,512,512]{2,3,1,0:T(8,128)(2,1)}, bf16[8,2,512,512]{2,3,1,0:T(8,128)(2,1)S(1)}, u32[]{:S(2)}) copy-start(bf16[8,2,512,512]{2,3,1,0:T(8,128)(2,1)S(1)} %fusion.54) | copy-start | bytes 25165828
  1983.0 78.4 %copy-start.24 = (bf16[1024,8,32]{0,2,1:T(8,128)(2,1)S(1)}, bf16[1024,8,32]{0,2,1:T(8,128)(2,1)}, u32[]{:S(2)}) copy-start(bf16[1024,8,32]{0,2,1:T(8,128)(2,1)} %copy-done.23) | copy-start | bytes 1572868
  1983.0 78.4 %copy-start.26 = (bf16[1024,8,32]{0,2,1:T(8,128)(2,1)S(1)}, bf16[1024,8,32]{0,2,1:T(8,128)(2,1)}, u32[]{:S(2)}) copy-start(bf16[1024,8,32]{0,2,1:T(8,128)(2,1)} %copy-done.25) | copy-start | bytes 1572868
  2061.4 26.4 collective-permute-start.4
  2069.6 114.9 %slice-start = ((s8[16777216]{0:T(1024)(128)(4,1)}), s8[4194304]{0:T(1024)(128)(4,1)S(1)}, s32[]{:S(2)}) async-start(s8[16777216]{0:T(1024)(128)(4,1)} %bitcast.554), calls=%async_computation.14 | async-start | bytes 8388608
  2069.6 114.9 %slice-start.1 = ((s8[16777216]{0:T(1024)(128)(4,1)}), s8[4194304]{0:T(1024)(128)(4,1)S(1)}, s32[]{:S(2)}) async-start(s8[16777216]{0:T(1024)(128)(4,1)} %bitcast.554), calls=%async_computation.15 | async-start | bytes 8388608
  2069.6 114.9 %slice-start.2 = ((s8[16777216]{0:T(1024)(128)(4,1)}), s8[4194304]{0:T(1024)(128)(4,1)S(1)}, s32[]{:S(2)}) async-start(s8[16777216]{0:T(1024)(128)(4,1)} %bitcast.554), calls=%async_computation.16 | async-start | bytes 8388608
  2072.2 112.3 %slice-start.3 = ((s8[16777216]{0:T(1024)(128)(4,1)}), s8[4194304]{0:T(1024)(128)(4,1)S(1)}, s32[]{:S(2)}) async-start(s8[16777216]{0:T(1024)(128)(4,1)} %bitcast.554), calls=%async_computation.17 | async-start | bytes 8388608
  2096.7 100.9 %collective-permute-start.5 = (bf16[2,512,512]{1,2,0:T(8,128)(2,1)}, bf16[2,512,512]{1,2,0:T(8,128)(2,1)}, u32[]{:S(2)}, u32[]{:S(2)}) collective-permute-start(bf16[2,512,512]{1,2,0:T(8,128)(2,1)} %select_convert_fusion.2), channel_id=1, source_target_pairs={{0,4},{4,0},{8,12},{12,8},{16,20},{20,16},{24,28},{28,24},{1,5},{5... | collective-permute-start | bytes 3145736 | tf_op jit(solution)/shard_map/ppermute | solution.py:32
  2216.3 1912.4 %reduce-scatter.13.cloned.1.call-start = ((), (), s32[]{:S(2)}) async-start(), calls=%async_computation.13 | async-start | bytes 113246208
  2452.5 27.7 copy-start.98
  2452.5 1942.7 %all-reduce.7.cloned.1.call-start = ((), (), s32[]{:S(2)}) async-start(), calls=%async_computation.11 | async-start | bytes 14168064 | tf_op jit(solution)/shard_map/psum | solution.py:458
  2459.2 89.8 %copy-start.18 = (bf16[1,1,1024,1024]{2,3,1,0:T(8,128)(2,1)S(1)}, bf16[1,1,1024,1024]{2,3,1,0:T(8,128)(2,1)}, u32[]{:S(2)}) copy-start(bf16[1,1,1024,1024]{2,3,1,0:T(8,128)(2,1)} %copy-done.16) | copy-start | bytes 6291460
  2459.2 89.8 %copy-start.91 = (f32[8,1,128]{2,1,0:T(1,128)S(1)}, f32[8,1,128]{2,1,0:T(1,128)}, u32[]{:S(2)}) copy-start(f32[8,1,128]{2,1,0:T(1,128)} %copy-done.89) | copy-start | bytes 12292
  2459.2 89.8 %copy-start.94 = (f32[1024]{0:T(1024)S(1)}, f32[1024]{0:T(1024)}, u32[]{:S(2)}) copy-start(f32[1024]{0:T(1024)} %copy-done.92) | copy-start | bytes 12292
  2474.9 74.1 %copy-start.51 = (bf16[1024,8,64]{0,2,1:T(8,128)(2,1)S(1)}, bf16[1024,8,64]{0,2,1:T(8,128)(2,1)}, u32[]{:S(2)}) copy-start(bf16[1024,8,64]{0,2,1:T(8,128)(2,1)} %copy-done.50) | copy-start | bytes 3145732
  4235.8 604.4 %all-reduce.9.cloned.1.call-start = ((), (), s32[]{:S(2)}) async-start(), calls=%async_computation.12 | async-start | bytes 14168064 | tf_op jit(solution)/shard_map/psum | solution.py:484
  4481.4 156.1 %copy-start.19 = (bf16[1,1,1024,1024]{2,3,1,0:T(8,128)(2,1)S(1)}, bf16[1,1,1024,1024]{2,3,1,0:T(8,128)(2,1)}, u32[]{:S(2)}) copy-start(bf16[1,1,1024,1024]{2,3,1,0:T(8,128)(2,1)} %copy-done.16) | copy-start | bytes 6291460
  4649.7 108.7 %slice-start.4 = ((s8[7084032]{0:T(1024)(128)(4,1)}), s8[4194304]{0:T(1024)(128)(4,1)S(1)}, s32[]{:S(2)}) async-start(s8[7084032]{0:T(1024)(128)(4,1)} %bitcast.560), calls=%async_computation.18 | async-start | bytes 8388608
  4704.2 54.3 %slice-start.5 = ((s8[7084032]{0:T(1024)(128)(4,1)}), s8[2889728]{0:T(1024)(128)(4,1)S(1)}, s32[]{:S(2)}) async-start(s8[7084032]{0:T(1024)(128)(4,1)} %bitcast.560), calls=%async_computation.19 | async-start | bytes 5779456
  (74 other events, 429.1 us)
Sparse Core Ops, SparseCore 0:
  10.1 76.1 all-gather.6
  88.4 58.9 all-gather.8
  149.5 689.9 all-gather.10
  841.4 265.5 all-gather.12
  1966.5 336.5 reduce-scatter.10
  2306.5 87.1 reduce-scatter.8
  2398.3 148.7 reduce-scatter.6
  2551.0 1577.6 reduce-scatter.12
  4235.9 131.9 all-reduce.6
  4481.5 129.9 all-reduce.8
where the time goes:
time: 5070 us; the launch traced here: 4980 us
  waiting for transfers between devices  1770 us (35%)
  local copies, waits for them, and re-layouts  1010 us (20%)
  other arithmetic  711 us (14%)
  matrix products  570 us (11%)
  blocking collectives  511 us (10%)
  starting transfers between devices  384 us (8%)
    unnamed x11, waiting for transfers between devices  1530 us
    ppermute x6, starting transfers between devices, partner(): lax.ppermute(x, axis, [(i, i ^ 1 << bit) for i in range(lax.axis_size(axi...  383 us
    unnamed x244, local copies, waits for them, and re-layouts  236 us
    all_gather x1, blocking collectives, per_device(): lax.all_gather(w_router, 'shard', axis=0, tiled=True)  228 us
    all_gather x1, blocking collectives, per_device(): lax.all_gather(ffn_gain, 'shard', axis=0, tiled=True)  220 us
    ppermute x6, waiting for transfers between devices, partner(): lax.ppermute(x, axis, [(i, i ^ 1 << bit) for i in range(lax.axis_size(axi...  199 us
    mul x1, other arithmetic, per_device(): BETA_TWO * adam_second.reshape(-1) + (1.0 - BETA_TWO) * clipped * clipped  159 us
    mul x1, other arithmetic, per_device(): new_mom = OUTER_MOMENTUM * outer_mom.reshape(-1) + pseudo  152 us
  transfers between devices with their start and end apart: 16, of which 7 were waited for; matrix products, arithmetic and copies ran while one was open for 28% of the time, Pallas kernels for 0%

commit v1 on v0

v1 whole, which is shorter than its diff:
```python
import functools

import jax
import jax.numpy as jnp
from jax import lax
from jax.experimental import pallas as pl
from jax.experimental.pallas import tpu as pltpu
from jax.sharding import PartitionSpec as P

QUERY_HEADS = 16
KEY_VALUE_HEADS = 8
HEAD_SIZE = 64
F = 512
EXPERTS = 16
TOP = 8
GROUP_SIZE = 8
CONTINUATION_LEN = 512
STEP = 10

EPSILON = 1e-06
NEGATIVE = -1e30
ROPE_BASE = 10000.0
BETA_ONE = 0.9
BETA_TWO = 0.95
ADAM_EPS = 1e-08
INNER_RATE = 0.01
DECAY_RATE = 0.1
OUTER_RATE = 0.7
OUTER_MOMENTUM = 0.9
CLIP_NORM = 1.0

LOG2E = 1.4426950408889634
LANES = 128
MIB = 1 << 20
BF16 = jnp.bfloat16
F32 = jnp.float32
PER_KEY = QUERY_HEADS // KEY_VALUE_HEADS
Q_WIDTH = QUERY_HEADS * HEAD_SIZE
KV_WIDTH = KEY_VALUE_HEADS * HEAD_SIZE


def dot(left, right, dims):
    return lax.dot_general(left, right, ((dims[:1], dims[1:]), ((), ())), preferred_element_type=F32)


def split_three(value):
    high = value.astype(BF16)
    rest = value - high.astype(F32)
    middle = rest.astype(BF16)
    low = (rest - middle.astype(F32)).astype(BF16)
    return high, middle, low


def augment_query(q_ref, start, width):
    rows = jnp.concatenate([q_ref[g, :, start : start + width] for g in range(PER_KEY)], axis=1)
    scaled = rows.astype(F32) * (HEAD_SIZE**-0.5 * LOG2E)
    high = scaled.astype(BF16)
    low = (scaled - high.astype(F32)).astype(BF16)
    return rows, high, low


def causal(width, columns):
    key_pos = lax.broadcasted_iota(jnp.int32, (width, columns), 0)
    query_pos = lax.broadcasted_iota(jnp.int32, (width, columns), 1) % width
    return key_pos <= query_pos


def attn_forward_kernel(where_ref, q_ref, kv_ref, own_ref, o_ref, lse_ref, peak_ref, sum_ref, acc_ref):
    block = own_ref.shape[-1]
    columns = PER_KEY * block
    shard_pos = where_ref[0]
    branch = where_ref[1]

    def advance(query, key, value, mask):
        scores = dot(jnp.concatenate([key, key], axis=0), query, (0, 0))
        if mask is not None:
            scores = jnp.where(mask, scores, NEGATIVE)
        old = peak_ref[...]
        new = jnp.maximum(old, jnp.max(scores, axis=0, keepdims=True))
        probs = jnp.exp2(scores - new).astype(BF16)
        shrink = jnp.exp2(old - new)
        ones = jnp.ones((16, block), BF16)
        part = dot(jnp.concatenate([value, ones], axis=0), probs, (1, 0))
        peak_ref[...] = new
        sum_ref[...] = sum_ref[...] * shrink + part[HEAD_SIZE : HEAD_SIZE + 1]
        acc_ref[...] = acc_ref[...] * shrink + part[:HEAD_SIZE]

    def begin(start):
        _, high, low = augment_query(q_ref, start, block)
        peak_ref[...] = jnp.full_like(peak_ref, NEGATIVE)
        sum_ref[...] = jnp.zeros_like(sum_ref)
        acc_ref[...] = jnp.zeros_like(acc_ref)
        return jnp.concatenate([high, low], axis=0)

    def finish(start):
        total = sum_ref[...]
        result = acc_ref[...] / total
        lse = peak_ref[...] + jnp.log2(total)
        for g in range(PER_KEY):
            o_ref[g, :, start : start + block] = result[:, g * block : (g + 1) * block]
            lse_ref[0, g : g + 1, start : start + block] = lse[:, g * block : (g + 1) * block]

    def full(query):
        def body(index, carry):
            advance(query, kv_ref[index, 0, 0], kv_ref[index, 1, 0], None)
            return carry

        return body

    query = begin(0)
    lax.fori_loop(0, shard_pos, full(query), 0)
    advance(query, kv_ref[shard_pos, 0, 0], kv_ref[shard_pos, 1, 0], causal(block, columns))
    finish(0)

    query = begin(block)
    whole = branch // block
    lax.fori_loop(0, whole, full(query), 0)

    @pl.when(branch % block != 0)
    def _():
        key_pos = lax.broadcasted_iota(jnp.int32, (block, columns), 0)
        advance(query, kv_ref[whole, 0, 0], kv_ref[whole, 1, 0], key_pos < branch % block)

    advance(query, own_ref[0, 0], own_ref[1, 0], causal(block, columns))
    finish(block)


def attn_forward(where, query, prompt_kv, own_kv):
    tokens = query.shape[-1]
    block = own_kv.shape[-1]
    columns = PER_KEY * block
    parts = prompt_kv.shape[0]
    return pl.pallas_call(
        attn_forward_kernel,
        grid=(query.shape[0] // PER_KEY,),
        in_specs=[
            pl.BlockSpec(memory_space=pltpu.SMEM),
            pl.BlockSpec((PER_KEY, HEAD_SIZE, tokens), lambda h: (h, 0, 0)),
            pl.BlockSpec((parts, 2, 1, HEAD_SIZE, block), lambda h: (0, 0, h, 0, 0)),
            pl.BlockSpec((2, 1, HEAD_SIZE, block), lambda h: (0, h, 0, 0)),
        ],
        out_specs=[
            pl.BlockSpec((PER_KEY, HEAD_SIZE, tokens), lambda h: (h, 0, 0)),
            pl.BlockSpec((1, PER_KEY, tokens), lambda h: (h, 0, 0)),
        ],
        out_shape=[
            jax.ShapeDtypeStruct(query.shape, F32),
            jax.ShapeDtypeStruct((query.shape[0] // PER_KEY, PER_KEY, tokens), F32),
        ],
        scratch_shapes=[
            pltpu.VMEM((1, columns), F32),
            pltpu.VMEM((1, columns), F32),
            pltpu.VMEM((HEAD_SIZE, columns), F32),
        ],
        compiler_params=pltpu.CompilerParams(vmem_limit_bytes=48 * MIB),
        cost_estimate=pl.CostEstimate(
            flops=4 * tokens * parts * block * query.shape[0] * HEAD_SIZE,
            bytes_accessed=16 * MIB,
            transcendentals=query.shape[0] * tokens * parts * block,
        ),
        name="attn_forward",
    )(where, query, prompt_kv, own_kv)


def attn_backward_kernel(
    where_ref, q_ref, kv_ref, own_ref, go_ref, lse_ref, delta_ref, dq_ref, dkv_ref, down_ref, dkv_acc, dq_acc
):
    block = own_ref.shape[-1]
    columns = PER_KEY * block
    shard_pos = where_ref[0]
    branch = where_ref[1]
    ones = jnp.ones((16, block), BF16)
    pad = jnp.zeros((16 - 3, columns), BF16)

    def begin(start):
        rows, high, low = augment_query(q_ref, start, block)

        def lanes(ref):
            return jnp.concatenate([ref[0, g : g + 1, start : start + block] for g in range(PER_KEY)], axis=1)

        lse = split_three(-lanes(lse_ref))
        delta = split_three(-lanes(delta_ref))
        grad = jnp.concatenate([go_ref[g, :, start : start + block] for g in range(PER_KEY)], axis=1)
        query = jnp.concatenate([high, low, *lse, pad], axis=0)
        grad_plus = jnp.concatenate([grad, *delta, pad], axis=0)
        dq_acc[...] = jnp.zeros_like(dq_acc)
        scaled = (rows.astype(F32) * HEAD_SIZE**-0.5).astype(BF16)
        return query, scaled, grad_plus, grad

    def terms(state, key, value, mask):
        query, scaled, grad_plus, grad = state
        scores = dot(jnp.concatenate([key, key, ones], axis=0), query, (0, 0))
        if mask is not None:
            scores = jnp.where(mask, scores, NEGATIVE)
        probs = jnp.exp2(scores)
        grad_probs = dot(jnp.concatenate([value, ones], axis=0), grad_plus, (0, 0))
        grad_scores = (probs * grad_probs).astype(BF16)
        dq_acc[...] += dot(key, grad_scores, (1, 0))
        return dot(scaled, grad_scores, (1, 1)), dot(grad, probs.astype(BF16), (1, 1))

    def add(index, state, mask):
        dk, dv = terms(state, kv_ref[index, 0, 0], kv_ref[index, 1, 0], mask)
        dkv_acc[index, 0] += dk
        dkv_acc[index, 1] += dv

    def finish(start):
        total = dq_acc[...] * HEAD_SIZE**-0.5
        for g in range(PER_KEY):
            dq_ref[g, :, start : start + block] = total[:, g * block : (g + 1) * block]

    def full(state):
        def body(index, carry):
            add(index, state, None)
            return carry

        return body

    dkv_acc[...] = jnp.zeros_like(dkv_acc)
    state = begin(0)
    lax.fori_loop(0, shard_pos, full(state), 0)
    add(shard_pos, state, causal(block, columns))
    finish(0)

    state = begin(block)
    whole = branch // block
    lax.fori_loop(0, whole, full(state), 0)

    @pl.when(branch % block != 0)
    def _():
        key_pos = lax.broadcasted_iota(jnp.int32, (block, columns), 0)
        add(whole, state, key_pos < branch % block)

    dk, dv = terms(state, own_ref[0, 0], own_ref[1, 0], causal(block, columns))
    down_ref[0, 0] = dk
    down_ref[1, 0] = dv
    finish(block)
    dkv_ref[:, :, 0] = dkv_acc[...].astype(BF16)


def attn_backward(where, query, prompt_kv, own_kv, grad_out, lse, delta):
    tokens = query.shape[-1]
    block = own_kv.shape[-1]
    columns = PER_KEY * block
    parts = prompt_kv.shape[0]
    by_head = pl.BlockSpec((PER_KEY, HEAD_SIZE, tokens), lambda h: (h, 0, 0))
    by_parts = pl.BlockSpec((parts, 2, 1, HEAD_SIZE, block), lambda h: (0, 0, h, 0, 0))
    by_own = pl.BlockSpec((2, 1, HEAD_SIZE, block), lambda h: (0, h, 0, 0))
    by_row = pl.BlockSpec((1, PER_KEY, tokens), lambda h: (h, 0, 0))
    return pl.pallas_call(
        attn_backward_kernel,
        grid=(query.shape[0] // PER_KEY,),
        in_specs=[pl.BlockSpec(memory_space=pltpu.SMEM), by_head, by_parts, by_own, by_head, by_row, by_row],
        out_specs=[by_head, by_parts, by_own],
        out_shape=[
            jax.ShapeDtypeStruct(query.shape, F32),
            jax.ShapeDtypeStruct(prompt_kv.shape, BF16),
            jax.ShapeDtypeStruct(own_kv.shape, F32),
        ],
        scratch_shapes=[
            pltpu.VMEM((parts, 2, HEAD_SIZE, block), F32),
            pltpu.VMEM((HEAD_SIZE, columns), F32),
        ],
        compiler_params=pltpu.CompilerParams(vmem_limit_bytes=56 * MIB),
        cost_estimate=pl.CostEstimate(
            flops=10 * tokens * parts * block * query.shape[0] * HEAD_SIZE,
            bytes_accessed=32 * MIB,
            transcendentals=query.shape[0] * tokens * parts * block,
        ),
        name="attn_backward",
    )(where, query, prompt_kv, own_kv, grad_out, lse, delta)


ORDER = ((0, 0), (0, 1), (3, 0), (2, 0), (3, 1), (2, 1), (1, 0), (1, 1))


def experts_kernel(
    x_hbm,
    top_hbm,
    gates_ref,
    in_ref,
    out_ref,
    all_x,
    dx_own,
    dx_core,
    dx_far,
    y_all,
    dgu_all,
    gh_all,
    dg_all,
    x_buf,
    top_buf,
    y_buf,
    dx_buf,
    dgu_buf,
    gh_buf,
    relay,
    y_acc,
    dx_acc,
    gates_all,
    gates_now,
    dg_now,
    dg_mine,
    in_sem,
    out_sem,
    copy_sem,
    send_sem,
    recv_sem,
    small_send,
    small_recv,
):
    tile = x_buf.shape[1]
    count = in_ref.shape[1] // (2 * F)
    step = pl.program_id(0)
    steps = len(ORDER)
    slot = lax.rem(step, 2)
    me = lax.axis_index("rep")
    home = [me, me + 1 - 2 * lax.rem(me, 2), lax.rem(me + 2, 4), 3 - me]

    def remote(source, target, send, receive, relation):
        return pltpu.make_async_remote_copy(
            src_ref=source,
            dst_ref=target,
            send_sem=send,
            recv_sem=receive,
            device_id={"rep": home[relation]},
            device_id_type=pl.DeviceIdType.MESH,
        )

    def half(ref, half_index, *lead):
        return ref.at[(*lead, pl.ds(half_index * tile, tile))]

    def to_core(h):
        return remote(half(x_hbm, h), half(all_x, h, me), send_sem.at[0, h], recv_sem.at[0, h], 1)

    def to_far(h):
        return remote(half(x_hbm, h), half(all_x, h, me), send_sem.at[1, h], recv_sem.at[1, h], 2)

    def forward(h):
        part = half(all_x, h, home[2])
        return remote(part, part, send_sem.at[2, h], recv_sem.at[2, h], 1)

    def give(kind, h, buffer):
        if kind == 3:
            return remote(buffer, relay.at[h], send_sem.at[3, h], recv_sem.at[3, h], 1)
        if kind == 2:
            return remote(buffer, half(dx_far, h), send_sem.at[4, h], recv_sem.at[4, h], 2)
        return remote(buffer, half(dx_core, h), send_sem.at[5, h], recv_sem.at[5, h], 1)

    def small_gates(k):
        return remote(gates_ref.at[home[k]], gates_all.at[me], small_send.at[0, k], small_recv.at[0, k], k)

    def small_back(k):
        return remote(dg_mine.at[home[k]], dg_all.at[me], small_send.at[1, k], small_recv.at[1, k], k)

    def load_x(i):
        kind, h = ORDER[i]
        source = half(x_hbm, h) if kind == 0 else half(all_x, h, home[kind])
        return pltpu.make_async_copy(source, x_buf.at[i % 2], in_sem.at[i % 2, 0])

    def load_top(i):
        kind, h = ORDER[i]
        return pltpu.make_async_copy(half(top_hbm, h, home[kind]), top_buf.at[i % 2], in_sem.at[i % 2, 1])

    def stores(i):
        kind, h = ORDER[i]
        out = []
        for n, (buffer, target) in enumerate(((y_buf, y_all), (dgu_buf, dgu_all), (gh_buf, gh_all))):
            out.append(
                pltpu.make_async_copy(buffer.at[i % 2], half(target, h, home[kind]), out_sem.at[i % 2, n])
            )
        return out

    def store_dx(i):
        kind, h = ORDER[i]
        if kind == 0:
            return pltpu.make_async_copy(dx_buf.at[i % 2], half(dx_own, h), out_sem.at[i % 2, 3])
        return give(kind, h, dx_buf.at[i % 2])

    def finish(i):
        for copy in stores(i):
            copy.wait()
        if ORDER[i][0] == 0:
            store_dx(i).wait()
        else:
            store_dx(i).wait_send()

    own_copy = pltpu.make_async_copy(x_hbm, all_x.at[me], copy_sem)
    for i in range(steps):
        kind, h = ORDER[i]

        @pl.when(step == i)
        def _(i=i, kind=kind, h=h):
            if i == 0:
                barrier = pltpu.get_barrier_semaphore()
                for k in (1, 2, 3):
                    pl.semaphore_signal(
                        barrier, inc=1, device_id={"rep": home[k]}, device_id_type=pl.DeviceIdType.MESH
                    )
                pl.semaphore_wait(barrier, 3)
                for n in (0, 1):
                    to_far(n).start()
                for n in (0, 1):
                    to_core(n).start()
                for k in (1, 2, 3):
                    small_gates(k).start()
                own_copy.start()
                load_top(0).start()
                load_x(0).start()
                gates_all[me] = gates_ref[me]
            if i == 2:
                for k in (1, 2, 3):
                    small_gates(k).wait_recv()
                to_far(0).wait_recv()
                forward(0).start()
                forward(0).wait_recv()
                load_x(2).start()
            if i == 3:
                to_far(1).wait_recv()
                forward(1).start()
            if i == 4:
                forward(1).wait_recv()
                load_x(4).start()
            if i == 5:
                to_core(0).wait_recv()
                to_core(1).wait_recv()
            load_x(i).wait()
            load_top(i).wait()
            if i + 1 < steps:
                load_top(i + 1).start()
                if i + 1 not in (2, 4):
                    load_x(i + 1).start()
            if i >= 2:
                finish(i - 2)
            gates_now[...] = jnp.transpose(gates_all[home[kind]][:, h * tile : (h + 1) * tile])

    x = x_buf[slot]
    top = top_buf[slot]
    columns = []
    for e in range(count):
        w_in = in_ref[:, e * 2 * F : (e + 1) * 2 * F]
        w_out = out_ref[:, e * F : (e + 1) * F]
        gate_up = dot(x, w_in, (1, 0))
        g = gate_up[:, :F]
        u = gate_up[:, F:]
        sig = jax.nn.sigmoid(g)
        act = g * sig
        hidden = (act * u).astype(BF16).astype(F32)
        raw = dot(top, w_out, (1, 0))
        columns.append(jnp.sum(hidden * raw, axis=1, keepdims=True))
        gate = gates_now[:, e : e + 1]
        gated = (hidden * gate).astype(BF16)
        gh_buf[slot, :, e * F : (e + 1) * F] = gated
        grad_hidden = raw * gate
        dg = (grad_hidden * u * sig * (1.0 + g * (1.0 - sig))).astype(BF16)
        du = (grad_hidden * act).astype(BF16)
        dgu = jnp.concatenate([dg, du], axis=1)
        dgu_buf[slot, :, e * 2 * F : (e + 1) * 2 * F] = dgu
        y = dot(gated, w_out, (1, 1))
        dx = dot(dgu, w_in, (1, 1))
        if e == 0:
            y_acc[...] = y
            dx_acc[...] = dx
        elif e < count - 1:
            y_acc[...] += y
            dx_acc[...] += dx
        else:
            y_buf[slot] = (y_acc[...] + y).astype(BF16)
            dx_acc[...] += dx
    columns.append(jnp.zeros((tile, 8 - count), F32))
    dg_now[...] = jnp.transpose(jnp.concatenate(columns, axis=1))

    for i in range(steps):
        kind, h = ORDER[i]

        @pl.when(step == i)
        def _(i=i, kind=kind, h=h):
            dg_mine[home[kind], :, h * tile : (h + 1) * tile] = dg_now[...]
            if kind == 2:
                give(3, h, dx_buf.at[0]).wait_recv()
                dx_buf[i % 2] = (dx_acc[...] + relay[h].astype(F32)).astype(BF16)
            else:
                dx_buf[i % 2] = dx_acc[...].astype(BF16)
            store_dx(i).start()
            for copy in stores(i):
                copy.start()
            if i == steps - 1:
                own_back = pltpu.make_async_copy(dg_mine.at[me], dg_all.at[me], small_send.at[1, 0])
                own_back.start()
                for k in (1, 2, 3):
                    small_back(k).start()
                finish(i - 1)
                finish(i)
                own_copy.wait()
                own_back.wait()
                for n in (0, 1):
                    to_far(n).wait_send()
                    to_core(n).wait_send()
                    forward(n).wait_send()
                    give(2, n, dx_buf.at[0]).wait_recv()
                    give(1, n, dx_buf.at[0]).wait_recv()
                for k in (1, 2, 3):
                    small_gates(k).wait_send()
                    small_back(k).wait()


def experts(x, all_top, gates, w_in, w_out):
    rows, width = x.shape
    reps = all_top.shape[0]
    count = w_in.shape[1] // (2 * F)
    tile = rows // 2
    anywhere = pl.BlockSpec(memory_space=pl.ANY)
    fixed = lambda n: pl.BlockSpec((width, n), lambda i: (0, 0), pipeline_mode=pl.Buffered(1))
    small = pl.BlockSpec((reps, 8, rows), lambda i: (0, 0, 0))
    dma = pltpu.SemaphoreType.DMA
    return pl.pallas_call(
        experts_kernel,
        grid=(len(ORDER),),
        in_specs=[anywhere, anywhere, small, fixed(count * 2 * F), fixed(count * F)],
        out_specs=[anywhere] * 8,
        out_shape=[
            jax.ShapeDtypeStruct((reps, rows, width), BF16),
            jax.ShapeDtypeStruct((rows, width), BF16),
            jax.ShapeDtypeStruct((rows, width), BF16),
            jax.ShapeDtypeStruct((rows, width), BF16),
            jax.ShapeDtypeStruct((reps, rows, width), BF16),
            jax.ShapeDtypeStruct((reps, rows, count * 2 * F), BF16),
            jax.ShapeDtypeStruct((reps, rows, count * F), BF16),
            jax.ShapeDtypeStruct((reps, 8, rows), F32),
        ],
        scratch_shapes=[
            pltpu.VMEM((2, tile, width), BF16),
            pltpu.VMEM((2, tile, width), BF16),
            pltpu.VMEM((2, tile, width), BF16),
            pltpu.VMEM((2, tile, width), BF16),
            pltpu.VMEM((2, tile, count * 2 * F), BF16),
            pltpu.VMEM((2, tile, count * F), BF16),
            pltpu.VMEM((2, tile, width), BF16),
            pltpu.VMEM((tile, width), F32),
            pltpu.VMEM((tile, width), F32),
            pltpu.VMEM((reps, 8, rows), F32),
            pltpu.VMEM((tile, 8), F32),
            pltpu.VMEM((8, tile), F32),
            pltpu.VMEM((reps, 8, rows), F32),
            dma((2, 2)),
            dma((2, 4)),
            dma,
            dma((6, 2)),
            dma((6, 2)),
            dma((2, 4)),
            dma((2, 4)),
        ],
        compiler_params=pltpu.CompilerParams(
            vmem_limit_bytes=58 * MIB, collective_id=1, has_side_effects=True
        ),
        cost_estimate=pl.CostEstimate(
            flops=12 * reps * rows * width * count * F,
            bytes_accessed=80 * MIB,
            transcendentals=reps * rows * count * F,
        ),
        name="experts",
    )(x, all_top, gates, w_in, w_out)


def flatten_kernel(starts, lead_ref, *refs):
    parts, flat_ref, square_ref = refs[: len(starts)], refs[len(starts)], refs[len(starts) + 1]
    scratch, sems = refs[len(starts) + 2 : -1], refs[-1]
    step = pl.program_id(0)
    steps = pl.num_programs(0)
    slot = lax.rem(step, 2)
    flat = flat_ref.reshape(flat_ref.shape[1] // LANES, LANES)
    lead_places = ((0, 0, 1), (1, starts[2] - 17 , 1), (2, starts[2] - 16, 16))

    def copies(index, where):
        out = []
        for n, (start, buffer) in enumerate(zip(starts, scratch)):
            size = buffer.shape[1]
            out.append(pltpu.make_async_copy(buffer.at[where], flat.at[pl.ds(start + index * size, size)], sems.at[where, n]))
        return out

    @pl.when(step == 0)
    def _():
        square_ref[...] = jnp.sum(lead_ref[...] * lead_ref[...], keepdims=True).reshape(1, 1) + jnp.zeros_like(square_ref)
        for n, (source, target, size) in enumerate(lead_places):
            copy = pltpu.make_async_copy(lead_ref.at[pl.ds(source, size)], flat.at[pl.ds(target, size)], sems.at[2, n])
            copy.start()
            copy.wait()

    @pl.when(step >= 2)
    def _():
        for copy in copies(step - 2, slot):
            copy.wait()

    total = jnp.zeros((8, LANES), F32)
    for part, buffer in zip(parts, scratch):
        rows = part.shape[-2]
        wide = buffer.shape[1] // rows
        reps = part.shape[0] if len(part.shape) == 3 else 1
        each = wide // reps
        for r in range(reps):
            for c in range(each):
                lanes = slice(c * LANES, (c + 1) * LANES)
                value = (part[r, :, lanes] if len(part.shape) == 3 else part[:, lanes]).astype(F32)
                buffer[slot, pl.ds(r * each + c, rows, stride=wide), :] = value
                square = value * value
                for k in range(0, rows, 8):
                    total += square[k : k + 8]
    square_ref[...] += jnp.sum(total, keepdims=True).reshape(1, 1)
    for copy in copies(step, slot):
        copy.start()

    @pl.when(step == steps - 1)
    def _():
        if True:
            for copy in copies(step - 1, 1 - slot):
                copy.wait()
        for copy in copies(step, slot):
            copy.wait()

def flatten(size, lead, *parts, tile=16):
    rows = parts[0].shape[-2]
    widths = [p.shape[-1] * (p.shape[0] if p.ndim == 3 else 1) // LANES for p in parts]
    starts, at = [], 1
    for n, w in enumerate(widths):
        if n == 2: at += 1 + 16
        starts.append(at); at += rows * w
    specs = [pl.BlockSpec((p.shape[0], tile, p.shape[2]), lambda i: (0, i, 0)) if p.ndim == 3 else pl.BlockSpec((tile, p.shape[1]), lambda i: (i, 0)) for p in parts]
    return pl.pallas_call(
        functools.partial(flatten_kernel, starts),
        grid=(rows // tile,),
        in_specs=[pl.BlockSpec(lead.shape, lambda i: (0, 0))] + specs,
        out_specs=[pl.BlockSpec(memory_space=pl.ANY), pl.BlockSpec((1, 1), lambda i: (0, 0))],
        out_shape=[jax.ShapeDtypeStruct((1, size), F32), jax.ShapeDtypeStruct((1, 1), F32)],
        scratch_shapes=[pltpu.VMEM((2, tile * w, LANES), F32) for w in widths] + [pltpu.SemaphoreType.DMA((3, 4))],
        compiler_params=pltpu.CompilerParams(vmem_limit_bytes=48 * MIB),
        name="flatten",
    )(lead, *parts)

def optimizer_math(grad, first, second, weight, scale):
    clipped = grad * scale
    new_first = BETA_ONE * first + (1.0 - BETA_ONE) * clipped
    new_second = BETA_TWO * second + (1.0 - BETA_TWO) * clipped * clipped
    root = jnp.sqrt(new_second * (1.0 / (1.0 - BETA_TWO**STEP))) + ADAM_EPS
    step = -INNER_RATE * (new_first * (1.0 / (1.0 - BETA_ONE**STEP)) / root + DECAY_RATE * weight)
    return new_first, new_second, step

CHUNK=1024
def stream(body, ins, outs, rows):
    whole = rows // CHUNK
    pipe = pltpu.emit_pipeline(body, grid=(whole,), in_specs=[pl.BlockSpec((CHUNK, LANES), lambda i: (i, 0))] * len(ins), out_specs=[pl.BlockSpec((CHUNK, LANES), lambda i: (i, 0))] * len(outs))
    pipe(*ins, *outs)

def adam_kernel(scale_ref, g, f, s, w, nf, ns, st, tg, tf, ts, tw, tnf, tns, tst, sems):
    rows = g.shape[-1] // LANES
    def view(r):
        return r.reshape(rows, LANES)
    scale = scale_ref[0]
    def body(gr, fr, sr, wr, nfr, nsr, str_):
        a, b, c = optimizer_math(gr[...], fr[...], sr[...], wr[...], scale)
        nfr[...] = a; nsr[...] = b; str_[...] = c.astype(BF16)
    ins = [view(r) for r in (g, f, s, w)]
    outs = [view(nf), view(ns), st]
    stream(body, ins, outs, rows)
    done = rows // CHUNK * CHUNK
    rest = rows - done
    for n, (r, t) in enumerate(zip(ins, (tg, tf, ts, tw))):
        pltpu.make_async_copy(r.at[pl.ds(done, rest)], t.at[pl.ds(0, rest)], sems.at[n]).start()
    for n, (r, t) in enumerate(zip(ins, (tg, tf, ts, tw))):
        pltpu.make_async_copy(r.at[pl.ds(done, rest)], t.at[pl.ds(0, rest)], sems.at[n]).wait()
    body(tg, tf, ts, tw, tnf, tns, tst)
    tail = st.shape[0] - done
    cs = [pltpu.make_async_copy(tnf.at[pl.ds(0, rest)], outs[0].at[pl.ds(done, rest)], sems.at[0]),
          pltpu.make_async_copy(tns.at[pl.ds(0, rest)], outs[1].at[pl.ds(done, rest)], sems.at[1]),
          pltpu.make_async_copy(tst.at[pl.ds(0, tail)], outs[2].at[pl.ds(done, tail)], sems.at[2])]
    for c in cs: c.start()
    for c in cs: c.wait()

def adam(scale, g, f, s, w):
    n = g.shape[-1]
    rows = n // LANES
    pad = -(-rows // 16) * 16
    tail = pad - rows // CHUNK * CHUNK
    anys = pl.BlockSpec(memory_space=pl.ANY)
    return pl.pallas_call(adam_kernel, in_specs=[pl.BlockSpec(memory_space=pltpu.SMEM)] + [anys] * 4, out_specs=[anys] * 3,
      out_shape=[jax.ShapeDtypeStruct(f.shape, F32), jax.ShapeDtypeStruct(s.shape, F32), jax.ShapeDtypeStruct((pad, LANES), BF16)],
      scratch_shapes=[pltpu.VMEM((tail, LANES), F32)] * 6 + [pltpu.VMEM((tail, LANES), BF16), pltpu.SemaphoreType.DMA((4,))],
      compiler_params=pltpu.CompilerParams(vmem_limit_bytes=48 * MIB), name="adam")(scale, g, f, s, w)

def outer_kernel(reps, st, mom, nm, up, ts, tm, tnm, tup, sems):
    rows = mom.shape[-1] // LANES
    def body(sr, mr, nmr, upr):
        pseudo = sr[...].astype(F32) * (-1.0 / reps)
        new = OUTER_MOMENTUM * mr[...] + pseudo
        nmr[...] = new
        upr[...] = -OUTER_RATE * (pseudo + OUTER_MOMENTUM * new)
    view = lambda r: r.reshape(rows, LANES)
    m, a, b = view(mom), view(nm), view(up)
    stream(body, [st, m], [a, b], rows)
    done = rows // CHUNK * CHUNK
    rest = rows - done
    tail = st.shape[0] - done
    cs = [pltpu.make_async_copy(st.at[pl.ds(done, tail)], ts.at[pl.ds(0, tail)], sems.at[0]),
          pltpu.make_async_copy(m.at[pl.ds(done, rest)], tm.at[pl.ds(0, rest)], sems.at[1])]
    for c in cs: c.start()
    for c in cs: c.wait()
    body(ts, tm, tnm, tup)
    cs = [pltpu.make_async_copy(tnm.at[pl.ds(0, rest)], a.at[pl.ds(done, rest)], sems.at[0]),
          pltpu.make_async_copy(tup.at[pl.ds(0, rest)], b.at[pl.ds(done, rest)], sems.at[1])]
    for c in cs: c.start()
    for c in cs: c.wait()

def outer(reps, st, mom):
    rows = mom.shape[-1] // LANES
    tail = st.shape[0] - rows // CHUNK * CHUNK
    anys = pl.BlockSpec(memory_space=pl.ANY)
    return pl.pallas_call(functools.partial(outer_kernel, reps), in_specs=[anys] * 2, out_specs=[anys] * 2,
      out_shape=[jax.ShapeDtypeStruct(mom.shape, F32)] * 2,
      scratch_shapes=[pltpu.VMEM((tail, LANES), BF16)] + [pltpu.VMEM((tail, LANES), F32)] * 3 + [pltpu.SemaphoreType.DMA((2,))],
      compiler_params=pltpu.CompilerParams(vmem_limit_bytes=48 * MIB), name="outer")(st, mom)


def rms_scale(rows):
    return lax.rsqrt(jnp.mean(rows * rows, axis=-1, keepdims=True) + EPSILON)


def rms_backward(rows, scale, gain, grad_out):
    grad_gain = jnp.sum(grad_out * rows * scale, axis=0)
    inner = jnp.sum(grad_out * gain * rows, axis=-1, keepdims=True)
    grad_in = scale * gain * grad_out - rows * scale * scale * scale * inner / rows.shape[-1]
    return grad_in, grad_gain


def rotate(rows, cosine, sine):
    half = HEAD_SIZE // 2
    front, back = rows[:, :half], rows[:, half:]
    return jnp.concatenate([front * cosine - back * sine, back * cosine + front * sine], axis=1)


def per_device(
    tokens,
    cotangent,
    routes,
    branch,
    attn_gain,
    query_key_value_weight,
    w_attn_out,
    ffn_gain,
    w_router,
    w_in,
    w_out,
    adam_first,
    adam_second,
    outer_mom,
):
    shards = lax.axis_size("shard")
    reps = lax.axis_size("rep")
    count = tokens.shape[2]
    width = tokens.shape[3]
    prompt = count - CONTINUATION_LEN
    local = EXPERTS // reps
    groups = None
    if shards > GROUP_SIZE:
        groups = [list(range(i, i + GROUP_SIZE)) for i in range(0, shards, GROUP_SIZE)]
    shard_pos = lax.axis_index("shard") % GROUP_SIZE
    rep_pos = lax.axis_index("rep")
    branch_len = branch.reshape(())
    x_in = tokens.reshape(count, width).astype(F32)
    top_low = cotangent.reshape(count, width)
    grad_top = top_low.astype(F32)
    route_ids = routes.reshape(count, TOP)
    gather = functools.partial(lax.all_gather, axis_name="shard", axis=0, tiled=True)

    flat_path = width // shards == LANES and outer_mom.shape[-1] % LANES == 0

    gains = gather(jnp.stack([attn_gain, ffn_gain], axis=1)).astype(F32)
    attn_gain_full, ffn_gain_full = gains[:, 0], gains[:, 1]
    qkv_full = gather(query_key_value_weight)

    attn_scale = rms_scale(x_in)
    normed_attn = (x_in * attn_scale * attn_gain_full).astype(BF16)
    positions = jnp.concatenate(
        [
            shard_pos * prompt + jnp.arange(prompt, dtype=jnp.int32),
            branch_len + jnp.arange(CONTINUATION_LEN, dtype=jnp.int32),
        ]
    )
    half = HEAD_SIZE // 2
    inverse_freq = ROPE_BASE ** (-(jnp.arange(half, dtype=F32) * 2.0) / HEAD_SIZE)
    angles = inverse_freq[:, None] * positions.astype(F32)[None, :]
    cosine, sine = jnp.cos(angles)[None], jnp.sin(angles)[None]

    def project(start, size, spin):
        rows = dot(qkv_full[:, start : start + size], normed_attn, (0, 1))
        rows = rows.reshape(size // HEAD_SIZE, HEAD_SIZE, count)
        return (rotate(rows, cosine, sine) if spin else rows).astype(BF16)

    key_value = jnp.stack(
        [project(Q_WIDTH, KV_WIDTH, True), project(Q_WIDTH + KV_WIDTH, KV_WIDTH, False)]
    )
    pieces = 2
    per_piece = KEY_VALUE_HEADS // pieces
    kv_piece = [slice(i * per_piece, (i + 1) * per_piece) for i in range(pieces)]
    q_piece = [slice(p.start * PER_KEY, p.stop * PER_KEY) for p in kv_piece]
    prompt_kv = [
        lax.all_gather(key_value[:, p, :, :prompt], "shard", axis=0, tiled=False, axis_index_groups=groups)
        for p in kv_piece
    ]
    own_kv = [key_value[:, p, :, prompt:] for p in kv_piece]
    query_all = project(0, Q_WIDTH, True)
    query = [query_all[p] for p in q_piece]
    attn_out_full = gather(w_attn_out)
    router_full = gather(w_router)
    w_in_mine = gather(lax.dynamic_slice_in_dim(w_in, rep_pos * local * 2 * F, local * 2 * F, 1))
    w_out_mine = gather(lax.dynamic_slice_in_dim(w_out, rep_pos * local * F, local * F, 1))
    all_top = lax.all_gather(top_low, "rep", axis=0, tiled=False)
    where = jnp.stack([shard_pos.astype(jnp.int32), branch_len])
    attn, lse = zip(*[attn_forward(where, *part) for part in zip(query, prompt_kv, own_kv)])
    attn = jnp.concatenate(attn, axis=0)
    attn_low = attn.astype(BF16).reshape(Q_WIDTH, count)
    x_mid = x_in + dot(attn_low, attn_out_full, (0, 1))

    ffn_scale = rms_scale(x_mid)
    normed_ffn = (x_mid * ffn_scale * ffn_gain_full).astype(BF16)
    logits = dot(normed_ffn, router_full, (1, 0))
    chosen = jnp.any(route_ids[:, :, None] == jnp.arange(EXPERTS, dtype=jnp.int32), axis=1)
    gates = jax.nn.softmax(jnp.where(chosen, logits, NEGATIVE), axis=-1)
    gates = jnp.where(chosen, gates, 0.0)

    gates_out = jnp.pad(gates.T.reshape(reps, local, count), ((0, 0), (0, 8 - local), (0, 0)))
    all_normed, dx_own, dx_core, dx_far, y_part, dgu, gated, dgate_part = experts(
        normed_ffn, all_top, gates_out, w_in_mine, w_out_mine
    )
    grad_from_experts = dx_own.astype(F32) + dx_core.astype(F32) + dx_far.astype(F32)
    grad_gates = dgate_part[:, :local].reshape(EXPERTS, count).T
    y_sum = lax.psum_scatter(y_part, "rep", scatter_dimension=0, tiled=False).astype(F32)
    block_out = (x_mid + y_sum).astype(BF16)

    def expert_term(left, right):
        term = dot(left.reshape(reps * count, width), right.reshape(reps * count, -1), (0, 0)).astype(BF16)
        rows = lax.psum_scatter(term, "shard", scatter_dimension=0, tiled=True)
        return lax.all_gather(rows, "rep", axis=0, tiled=False)

    expert_in = expert_term(all_normed, dgu)
    expert_out = expert_term(all_top, gated)

    grad_logits = (gates * (grad_gates - jnp.sum(gates * grad_gates, axis=-1, keepdims=True))).astype(BF16)
    grad_router_w = dot(normed_ffn, grad_logits, (0, 0))
    grad_normed_ffn = grad_from_experts + dot(grad_logits, router_full, (1, 1))
    grad_mid_norm, grad_ffn_gain = rms_backward(x_mid, ffn_scale, ffn_gain_full, grad_normed_ffn)
    grad_mid = grad_top + grad_mid_norm
    grad_branch = grad_mid.astype(BF16)
    grad_attn_w = dot(grad_branch, attn_low, (0, 1))
    grad_attn = dot(attn_out_full, grad_branch, (0, 1)).astype(BF16).reshape(QUERY_HEADS, HEAD_SIZE, count)
    early = jnp.concatenate([grad_attn_w, grad_ffn_gain[:, None], grad_router_w], axis=1).astype(BF16)
    early = jnp.pad(early, ((0, 0), (0, -early.shape[1] % LANES)))
    early = lax.psum_scatter(early, "shard", scatter_dimension=0, tiled=True)

    delta = jnp.sum(grad_attn.astype(F32) * attn, axis=1).reshape(KEY_VALUE_HEADS, PER_KEY, count)
    grad_query, grad_kv = [], []
    for n in range(pieces):
        dq, dkv, own = attn_backward(
            where, query[n], prompt_kv[n], own_kv[n], grad_attn[q_piece[n]], lse[n], delta[kv_piece[n]]
        )
        dkv = lax.psum_scatter(dkv, "shard", scatter_dimension=0, tiled=False, axis_index_groups=groups)
        grad_query.append(dq)
        grad_kv.append(jnp.concatenate([dkv.astype(F32), own], axis=-1))
    grad_query = jnp.concatenate(grad_query, axis=0)
    grad_kv = jnp.concatenate(grad_kv, axis=1)
    grad_projected = jnp.concatenate(
        [rotate(grad_query, cosine, -sine), rotate(grad_kv[0], cosine, -sine), grad_kv[1]], axis=0
    ).astype(BF16).reshape(Q_WIDTH + 2 * KV_WIDTH, count)
    grad_qkv_w = dot(normed_attn, grad_projected, (0, 1))
    grad_normed_attn = dot(grad_projected, qkv_full, (0, 1))
    grad_x_norm, grad_attn_gain = rms_backward(x_in, attn_scale, attn_gain_full, grad_normed_attn)
    grad_input = grad_mid + grad_x_norm

    late = jnp.concatenate([grad_qkv_w, grad_attn_gain[:, None]], axis=1).astype(BF16)
    late = jnp.pad(late, ((0, 0), (0, -late.shape[1] % LANES)))
    late = lax.psum_scatter(late, "shard", scatter_dimension=0, tiled=True)
    both = lax.psum(jnp.concatenate([early, late], axis=1), "rep")
    early, late = both[:, : early.shape[1]], both[:, early.shape[1] :]
    qkv_rows, attn_gain_rows = late[:, : Q_WIDTH + 2 * KV_WIDTH], late[:, Q_WIDTH + 2 * KV_WIDTH]
    attn_rows, ffn_gain_rows = early[:, :Q_WIDTH], early[:, Q_WIDTH]
    router_rows = early[:, Q_WIDTH + 1 : Q_WIDTH + 1 + EXPERTS]
    if flat_path:
        size = outer_mom.shape[-1]

        def lead(first, second, rest):
            return jnp.concatenate([first[None], second[None], rest.reshape(-1, LANES)], axis=0).astype(F32)

        weight_flat, _ = flatten(
            size, lead(attn_gain, ffn_gain, w_router), query_key_value_weight, w_attn_out, w_in, w_out
        )
        total_grad, square = flatten(
            size, lead(attn_gain_rows, ffn_gain_rows, router_rows), qkv_rows, attn_rows, expert_in, expert_out
        )
        norm_square = lax.psum(square.reshape(()), "shard")
    else:
        weight_flat = jnp.concatenate(
            [
                portion.astype(F32).reshape(-1)
                for portion in (attn_gain, query_key_value_weight, w_attn_out, ffn_gain, w_router, w_in, w_out)
            ]
        )
        total_grad = jnp.concatenate(
            [
                portion.astype(F32).reshape(-1)
                for portion in (
                    attn_gain_rows,
                    qkv_rows,
                    attn_rows,
                    ffn_gain_rows,
                    router_rows,
                    expert_in.transpose(1, 0, 2),
                    expert_out.transpose(1, 0, 2),
                )
            ]
        )
        norm_square = lax.psum(jnp.sum(total_grad * total_grad), "shard")
    grad_norm = jnp.sqrt(norm_square)
    clip_scale = CLIP_NORM / jnp.maximum(grad_norm, CLIP_NORM)
    if flat_path:
        new_first, new_second, step = adam(
            clip_scale.reshape(1), total_grad, adam_first, adam_second, weight_flat
        )
        new_mom, weight_update = outer(reps, lax.psum(step, "rep"), outer_mom)
    else:
        new_first, new_second, step = optimizer_math(
            total_grad, adam_first.reshape(-1), adam_second.reshape(-1), weight_flat, clip_scale
        )
        pseudo = -(lax.psum(step.astype(BF16), "rep").astype(F32) / reps)
        new_mom = OUTER_MOMENTUM * outer_mom.reshape(-1) + pseudo
        weight_update = -OUTER_RATE * (pseudo + OUTER_MOMENTUM * new_mom)
    return (
        block_out.reshape(tokens.shape),
        grad_input.reshape(tokens.shape),
        total_grad.reshape(outer_mom.shape),
        grad_norm,
        new_first.reshape(adam_first.shape),
        new_second.reshape(adam_second.shape),
        new_mom.reshape(outer_mom.shape),
        weight_update.reshape(outer_mom.shape),
    )


def solution(mesh):
    by_token = P("rep", "shard", None, None)
    by_state = P("rep", "shard", None)
    by_row = P("shard", None)
    placed = (
        by_token,
        by_token,
        by_token,
        P("rep", "shard"),
        P("shard"),
        by_row,
        by_row,
        P("shard"),
        by_row,
        by_row,
        by_row,
        by_state,
        by_state,
        by_row,
    )
    return jax.shard_map(
        per_device,
        mesh=mesh,
        in_specs=placed,
        out_specs=(by_token, by_token, by_row, P(), by_state, by_state, by_row, by_row),
        check_vma=False,
    )
```

time: 5070 us -> 1860 us (0.37); the launches traced: 4980 us -> 1850 us
  local copies, waits for them, and re-layouts: 1010 us -> 54.6 us
  waiting for transfers between devices: 1770 us -> 1090 us
  other arithmetic: 711 us -> 36.5 us
  Pallas kernels: 0 us -> 463 us
  matrix products: 570 us -> 116 us
  blocking collectives: 511 us -> 70.7 us
  starting transfers between devices: 384 us -> 0.73 us
    unnamed x11 -> x19, waiting for transfers between devices: 1530 us -> 28.9 us
    reduce_scatter x3 -> x6, waiting for transfers between devices: 0.02 us -> 491 us  [the longest x1 151 us: expert_term(): rows = lax.psum_scatter(term, 'shard', scatter_dimension=0, tiled=True)]
    pallas_call x0 -> x9, Pallas kernels: none -> 463 us  [the longest x1 169 us: experts(): pl.pallas_call(experts_kernel, grid=(len(ORDER),), in_specs=[anywhere, an...]
    dot_general x63 -> x13, matrix products: 570 us -> 116 us  [dot(): lax.dot_general(left, right, ((dims[:1], dims[1:]), ((), ())), preferred_...]
    all_gather x3 -> x2, blocking collectives: 471 us -> 48.7 us  [the longest x1 26.4 us: per_device(): router_full = gather(w_router)]
    reshape x9 -> x4, local copies, waits for them, and re-layouts: 409 us -> 0.24 us  [the longest x2 0.19 us: lead(): rest.reshape(-1, LANES)]
    ppermute x6 -> x0, starting transfers between devices: 383 us -> none  [partner(): lax.ppermute(x, axis, [(i, i ^ 1 << bit) for i in range(lax.axis_size(axi...]
    all_gather x4 -> x9, waiting for transfers between devices: 44.1 us -> 413 us  [the longest x1 128 us: per_device(): gather(lax.dynamic_slice_in_dim(w_in, rep_pos * local * 2 * F, local * 2...]
  transfers between devices with their start and end apart: 16 -> 18, of which waited for: 7 -> 18; matrix products, arithmetic and copies ran while one was open for 28% -> 9% of each run, Pallas kernels for 0% -> 8%
where the time goes in v1:
time: 1860 us; the launch traced here: 1850 us
  waiting for transfers between devices  1090 us (59%)
  Pallas kernels  463 us (25%)
  matrix products  116 us (6%)
  blocking collectives  70.7 us (4%)
  local copies, waits for them, and re-layouts  54.6 us (3%)
  other arithmetic  36.5 us (2%)
    pallas_call x1, Pallas kernels, experts(): pl.pallas_call(experts_kernel, grid=(len(ORDER),), in_specs=[anywhere, an...  169 us
    reduce_scatter x1, waiting for transfers between devices, expert_term(): rows = lax.psum_scatter(term, 'shard', scatter_dimension=0, tiled=True)  151 us
    all_gather x1, waiting for transfers between devices, per_device(): gather(lax.dynamic_slice_in_dim(w_in, rep_pos * local * 2 * F, local * 2...  128 us
    psum x1, waiting for transfers between devices, per_device(): new_mom, weight_update = outer(reps, lax.psum(step, 'rep'), outer_mom)  121 us
    pallas_call x2, Pallas kernels, attn_backward(): pl.pallas_call(attn_backward_kernel, grid=(query.shape[0] // PER_KEY,), i...  117 us
    dot_general x13, matrix products, dot(): lax.dot_general(left, right, ((dims[:1], dims[1:]), ((), ())), preferred_...  116 us
    reduce_scatter x2, waiting for transfers between devices, per_device(): lax.psum_scatter(dkv, 'shard', scatter_dimension=0, tiled=False, axis_ind...  112 us
    reduce_scatter x1, waiting for transfers between devices, per_device(): late = lax.psum_scatter(late, 'shard', scatter_dimension=0, tiled=True)  94.9 us
  transfers between devices with their start and end apart: 18, of which 18 were waited for; matrix products, arithmetic and copies ran while one was open for 9% of the time, Pallas kernels for 8%

profile of v1, /device:TPU:0, one launch (start us, length us, event | category | flops | bytes accessed | tf_op | source)
XLA Modules:
  0.0 1847.7 jit_solution(11839771269523379672)
XLA Ops:
  9.3 22.3 %all_gather.45 = bf16[1024,2]{0,1:T(2,128)(2,1)S(1)} all-gather(bf16[128,2]{0,1:T(2,128)(2,1)S(1)} %pad_maximum_fusion.3), channel_id=1, replica_groups=mesh['shard'=8,'rep'=4] {'shard'}, dimensions={0}, use_global_device_ids=true | all-gather | bytes 4608 | tf_op jit(solution)/shard_map/all_gather | solution.py:774
  31.6 2.1 fusion.17
  34.9 51.4 %all-gather.15.cloned.1.call-done = bf16[1024,2048]{1,0:T(8,128)(2,1)} async-done(((bf16[128,2048]{1,0:T(8,128)(2,1)}), bf16[1024,2048]{1,0:T(8,128)(2,1)}) %all-gather.15.cloned.1.call-update) | async-done | bytes 4194320 | tf_op jit(solution)/shard_map/all_gather | solution.py:776
  86.3 3.4 fusion.35
  90.0 2.6 convolution_convert_fusion.3
  92.9 1.3 fusion.57
  97.2 2.3 constant_dynamic-slice_fusion.1
  99.6 26.4 %all_gather.53 = bf16[1024,16]{0,1:T(8,128)(2,1)S(1)} all-gather(bf16[128,16]{0,1:T(8,128)(2,1)S(1)} %copy-done.25), channel_id=1, replica_groups=mesh['shard'=8,'rep'=4] {'shard'}, dimensions={0}, use_global_device_ids=true | all-gather | bytes 36864 | tf_op jit(solution)/shard_map/all_gather | solution.py:811
  126.2 5.2 fusion.29
  133.3 33.3 %all-gather.23.cloned.1.call-done = bf16[16,4,64,512]{3,2,1,0:T(8,128)(2,1)} async-done(((bf16[2,4,64,512]{3,2,1,0:T(8,128)(2,1)}), bf16[16,4,64,512]{3,2,1,0:T(8,128)(2,1)}) %all-gather.23.cloned.1.call-update) | async-done | bytes 4194320 | tf_op jit(solution)/shard_map/all_gather | solution.py:804
  168.9 38.0 %attn_forward.2 = (f32[8,64,1024]{2,1,0:T(8,128)S(1)}, f32[4,2,1024]{2,1,0:T(2,128)S(1)}) custom-call(s32[2]{0:T(128)S(1)} %pad_add_fusion.where_ref, bf16[8,64,1024]{2,1,0:T(8,128)(2,1)S(1)} %copy-done.3, bf16[8,2,4,64,512]{4,3,2,1,0:T(8,128)(2,1)} %bitcast.186, bf16[2,4,64,512]{3,2,1,0:T(8,128)(2,1)S(1)} %copy-done.6), custom_call_target="tpu_custom_call" | custom-call | flops 8589934592 | bytes 16777216 | tf_op jit(solution)/shard_map/attn_forward/pallas_call | solution.py:133
  207.5 1.6 constant_dynamic-update-slice_fusion.1
  209.1 32.4 %all-gather.25.cloned.1.call-done = bf16[16,4,64,512]{3,2,1,0:T(8,128)(2,1)} async-done(((bf16[2,4,64,512]{3,2,1,0:T(8,128)(2,1)}), bf16[16,4,64,512]{3,2,1,0:T(8,128)(2,1)}) %all-gather.25.cloned.1.call-update) | async-done | bytes 4194320 | tf_op jit(solution)/shard_map/all_gather | solution.py:804
  242.5 37.9 %attn_forward.3 = (f32[8,64,1024]{2,1,0:T(8,128)S(1)}, f32[4,2,1024]{2,1,0:T(2,128)S(1)}) custom-call(s32[2]{0:T(128)S(1)} %pad_add_fusion.where_ref, bf16[8,64,1024]{2,1,0:T(8,128)(2,1)S(1)} %get-tuple-element.82.q_ref, bf16[8,2,4,64,512]{4,3,2,1,0:T(8,128)(2,1)} %bitcast.184, bf16[2,4,64,512]{3,2,1,0:T(8,128)(2,1)S(1)} %copy-done.5), custom_call_target="tpu_custom_call" | custom-call | flops 8589934592 | bytes 16777216 | tf_op jit(solution)/shard_map/attn_forward/pallas_call | solution.py:133
  281.1 2.0 copy-done.14
  283.1 1.6 convert_element_type.161
  284.7 6.3 all-gather.17.cloned.1.call-done
  291.0 5.4 multiply_reduce_fusion.2
  299.9 65.0 %all-gather.21.cloned.1.call-done.out_ref = bf16[1024,2048]{1,0:T(8,128)(2,1)} async-done(((bf16[128,2048]{1,0:T(8,128)(2,1)}), bf16[1024,2048]{1,0:T(8,128)(2,1)}) %all-gather.21.cloned.1.call-update) | async-done | bytes 4194320 | tf_op jit(solution)/shard_map/all_gather | solution.py:813
  364.9 58.0 %all-gather.27.cloned.1.call-done = bf16[4,1,1024,1024]{3,2,1,0:T(8,128)(2,1)} async-done(((bf16[1,1,1024,1024]{3,2,1,0:T(8,128)(2,1)}), bf16[4,1,1024,1024]{3,2,1,0:T(8,128)(2,1)}) %all-gather.27.cloned.1.call-update) | async-done | bytes 8388624 | tf_op jit(solution)/shard_map/all_gather | solution.py:814
  422.9 127.7 %all-gather.19.cloned.1.call-done.in_ref = bf16[1024,4096]{1,0:T(8,128)(2,1)} async-done(((bf16[128,4096]{1,0:T(8,128)(2,1)}), bf16[1024,4096]{1,0:T(8,128)(2,1)}) %all-gather.19.cloned.1.call-update) | async-done | bytes 8388624 | tf_op jit(solution)/shard_map/all_gather | solution.py:812
  550.6 168.8 %experts.1 = (bf16[4,1024,1024]{2,1,0:T(8,128)(2,1)}, bf16[1024,1024]{1,0:T(8,128)(2,1)}, bf16[1024,1024]{1,0:T(8,128)(2,1)}, bf16[1024,1024]{1,0:T(8,128)(2,1)}...) custom-call(bf16[1024,1024]{1,0:T(8,128)(2,1)} %copy-done.11, ...), custom_call_target="tpu_custom_call" | custom-call | flops 103079215104 | bytes 83886080 | tf_op jit(solution)/shard_map/experts/pallas_call | solution.py:515
  720.5 7.2 multiply_reduce_fusion
  727.7 61.4 %reduce-scatter.10.cloned.1.call-done = bf16[1,1024,1024]{2,1,0:T(8,128)(2,1)} async-done(((bf16[4,1024,1024]{2,1,0:T(8,128)(2,1)}), bf16[1,1024,1024]{2,1,0:T(8,128)(2,1)}) %reduce-scatter.10.cloned.1.call-update) | async-done | bytes 2097168 | tf_op jit(solution)/shard_map/reduce_scatter | solution.py:834
  789.1 6.6 convert_add_fusion
  796.4 2.7 fusion.23
  799.2 1.5 fusion.56
  801.3 58.4 %attn_backward.2 = (f32[8,64,1024]{2,1,0:T(8,128)}, bf16[8,2,4,64,512]{4,3,2,1,0:T(8,128)(2,1)}, f32[2,4,64,512]{3,2,1,0:T(8,128)}) custom-call(s32[2]{0:T(128)} %copy-done.7, bf16[8,64,1024]{2,1,0:T(8,128)(2,1)} %get-tuple-element.83.q_ref, bf16[8,2,4,64,512]{4,3,2,1,0:T(8,128)(2,1)} %bitcast.187, bf16[2,4,64,512]{3,2,1,0:T(8,128)(2,1)} %get-tuple-element.80.own_ref, ...), custom_call_target="tpu_custom_call" | custom-call | flops 21474836480 | bytes 33554432 | tf_op jit(solution)/shard_map/attn_backward/pallas_call | solution.py:249
  860.4 58.6 %attn_backward.3 = (f32[8,64,1024]{2,1,0:T(8,128)}, bf16[8,2,4,64,512]{4,3,2,1,0:T(8,128)(2,1)}, f32[2,4,64,512]{3,2,1,0:T(8,128)}) custom-call(s32[2]{0:T(128)} %copy-done.7, bf16[8,64,1024]{2,1,0:T(8,128)(2,1)} %copy-done.2, bf16[8,2,4,64,512]{4,3,2,1,0:T(8,128)(2,1)} %bitcast.185, bf16[2,4,64,512]{3,2,1,0:T(8,128)(2,1)} %get-tuple-element.78.own_ref, ...), custom_call_target="tpu_custom_call" | custom-call | flops 21474836480 | bytes 33554432 | tf_op jit(solution)/shard_map/attn_backward/pallas_call | solution.py:249
  919.1 23.9 %fusion.25 = bf16[1024,2048]{0,1:T(8,128)(2,1)} fusion(bf16[4,1024,2048]{2,1,0:T(8,128)(2,1)} %get-tuple-element.51, bf16[4,1,1024,1024]{3,2,1,0:T(8,128)(2,1)} %all-gather.27.cloned.1.call-done), kind=kOutput, calls=%fused_computation.41 | convolution fusion | flops 17181966336 | bytes 29360128 | tf_op jit(solution)/shard_map/dot_general | solution.py:43
  942.9 6.5 copy.74
  949.5 2.0 convolution_convert_fusion.4
  951.9 6.7 convolution_convert_fusion.1
  958.6 5.0 concatenate.80
  963.6 3.3 pad.13
  966.8 3.2 constant_dynamic-update-slice_fusion.3
  970.1 3.2 constant_dynamic-update-slice_fusion.2
  973.3 3.9 multiply_subtract_fusion
  977.2 12.3 reduce-scatter.12.cloned.1.call-done
  989.5 2.1 bitcast_convert_fusion.3
  991.7 100.2 %reduce-scatter.14.cloned.1.call-done = bf16[1,2,4,64,512]{4,3,2,1,0:T(8,128)(2,1)} async-done(((bf16[8,2,4,64,512]{4,3,2,1,0:T(8,128)(2,1)}), bf16[1,2,4,64,512]{4,3,2,1,0:T(8,128)(2,1)}) %reduce-scatter.14.cloned.1.call-update) | async-done | bytes 524304 | tf_op jit(solution)/shard_map/reduce_scatter | solution.py:863
  1093.0 2.2 maximum_maximum_fusion
  1099.3 7.1 fusion.20
  1106.6 5.3 convolution_convert_fusion
  1111.9 2.3 fusion.9
  1114.3 43.5 %bitcast_convert_fusion = bf16[1024,4096]{1,0:T(8,128)(2,1)} fusion(bf16[4,1024,1024]{2,1,0:T(8,128)(2,1)} %get-tuple-element.49, bf16[4,1024,4096]{2,1,0:T(8,128)(2,1)} %get-tuple-element.50), kind=kOutput, calls=%fused_computation | convolution fusion | flops 34363932672 | bytes 50331648 | tf_op jit(solution)/shard_map/dot_general | solution.py:43
  1157.9 26.3 %reduce-scatter.22.cloned.1.call-done = bf16[128,2048]{1,0:T(8,128)(2,1)} async-done(((bf16[1024,2048]{1,0:T(8,128)(2,1)}), bf16[128,2048]{1,0:T(8,128)(2,1)}) %reduce-scatter.22.cloned.1.call-update) | async-done | bytes 524304
  1184.2 2.0 copy.75
  1186.3 70.8 %reduce-scatter.16.cloned.1.call-done = bf16[128,1152]{1,0:T(8,128)(2,1)} async-done(((bf16[1024,1152]{1,0:T(8,128)(2,1)}), bf16[128,1152]{1,0:T(8,128)(2,1)}) %reduce-scatter.16.cloned.1.call-update) | async-done | bytes 294928 | tf_op jit(solution)/shard_map/reduce_scatter | solution.py:855
  1257.1 94.9 %reduce-scatter.18.cloned.1.call-done = bf16[128,2176]{1,0:T(8,128)(2,1)} async-done(((bf16[1024,2176]{1,0:T(8,128)(2,1)}), bf16[128,2176]{1,0:T(8,128)(2,1)}) %reduce-scatter.18.cloned.1.call-update) | async-done | bytes 557072 | tf_op jit(solution)/shard_map/reduce_scatter | solution.py:878
  1352.0 2.1 pad_maximum_fusion.2
  1354.1 151.1 %reduce-scatter.20.cloned.1.call-done = bf16[128,4096]{1,0:T(8,128)(2,1)} async-done(((bf16[1024,4096]{1,0:T(8,128)(2,1)}), bf16[128,4096]{1,0:T(8,128)(2,1)}) %reduce-scatter.20.cloned.1.call-update) | async-done | bytes 1048592 | tf_op jit(solution)/shard_map/reduce_scatter | solution.py:839
  1505.6 16.9 flatten.3
  1522.5 6.6 all-gather.31.cloned.1.call-done
  1529.1 2.9 copy.68
  1532.0 34.9 %all-reduce.6.cloned.1.call-done = bf16[128,3328]{1,0:T(8,128)(2,1)} async-done(((bf16[128,3328]{1,0:T(8,128)(2,1)}), bf16[128,3328]{1,0:T(8,128)(2,1)}) %all-reduce.6.cloned.1.call-update) | async-done | bytes 851984 | tf_op jit(solution)/shard_map/psum | solution.py:879
  1570.8 32.3 %all-gather.29.cloned.1.call-done = bf16[512,4096]{1,0:T(8,128)(2,1)} async-done(((bf16[128,4096]{1,0:T(8,128)(2,1)}), bf16[512,4096]{1,0:T(8,128)(2,1)}) %all-gather.29.cloned.1.call-update) | async-done | bytes 4194320 | tf_op jit(solution)/shard_map/all_gather | solution.py:840
  1603.1 17.0 flatten.2
  1620.2 22.0 %psum.22 = f32[]{:T(128)} all-reduce(f32[]{:T(128)} %bitcast.45), channel_id=1, replica_groups=mesh['shard'=8,'rep'=4] {'shard'}, use_global_device_ids=true, to_apply=%region_19.20 | all-reduce | flops 1 | bytes 8 | tf_op jit(solution)/shard_map/psum | solution.py:896
  1642.9 39.0 %adam.1 = (f32[1,1,3541248]{2,1,0:T(1,128)}, f32[1,1,3541248]{2,1,0:T(1,128)}, bf16[27680,128]{1,0:T(8,128)(2,1)}) custom-call(f32[1]{0:T(128)} %bitcast.46.scale_ref, f32[1,3541248]{1,0:T(1,128)} %get-tuple-element.28.g, f32[1,1,3541248]{2,1,0:T(1,128)} %f.1, f32[1,1,3541248]{2,1,0:T(1,128)} %s.1, f32[1,3541248]{1,0:T(1,128)} %get-tuple-element.54.w), custom_call_target="tpu_custom_call" | custom-call | tf_op jit(solution)/shard_map/adam/pallas_call | solution.py:683
  1681.9 1.6 copy-done.18
  1683.5 6.2 fusion.16
  1689.7 121.4 %all-reduce.8.cloned.1.call-done.st = bf16[27680,128]{1,0:T(8,128)(2,1)} async-done(((bf16[27680,128]{1,0:T(8,128)(2,1)}), bf16[27680,128]{1,0:T(8,128)(2,1)}) %all-reduce.8.cloned.1.call-update) | async-done | bytes 7086096 | tf_op jit(solution)/shard_map/psum | solution.py:925
  1811.2 28.3 %outer.1 = (f32[1,3541248]{1,0:T(1,128)}, f32[1,3541248]{1,0:T(1,128)}) custom-call(bf16[27680,128]{1,0:T(8,128)(2,1)} %all-reduce.8.cloned.1.call-done.st, f32[1,3541248]{1,0:T(1,128)} %mom.1), custom_call_target="tpu_custom_call" | custom-call | tf_op jit(solution)/shard_map/outer/pallas_call | solution.py:715
  (150 shorter events, 29.4 us)
Async XLA Ops:
  7.2 79.1 %all-gather.15.cloned.1.call-start = ((), (), s32[]{:S(2)}) async-start(), calls=%async_computation.7 | async-start | bytes 4718592 | tf_op jit(solution)/shard_map/all_gather | solution.py:776
  7.9 158.7 %all-gather.23.cloned.1.call-start = ((), (), s32[]{:S(2)}) async-start(), calls=%async_computation.19 | async-start | bytes 4718592 | tf_op jit(solution)/shard_map/all_gather | solution.py:804
  33.7 92.5 %copy-start.27 = (f32[1024]{0:T(1024)}, f32[1024]{0:T(1024)S(1)}, u32[]{:S(2)}) copy-start(f32[1024]{0:T(1024)S(1)} %add_rsqrt_fusion.1) | copy-start | bytes 12292
  33.7 92.4 %copy-start.29 = (f32[1024,1]{0,1:T(1,128)}, f32[1024,1]{0,1:T(1,128)S(1)}, u32[]{:S(2)}) copy-start(f32[1024,1]{0,1:T(1,128)S(1)} %get-tuple-element.90) | copy-start | bytes 12292
  34.9 96.5 %copy-start.20 = (f32[32,1024]{1,0:T(8,128)}, f32[32,1024]{1,0:T(8,128)S(1)}, u32[]{:S(2)}) copy-start(f32[32,1024]{1,0:T(8,128)S(1)} %get-tuple-element.88) | copy-start | bytes 393220
  86.3 3.8 copy-start.16
  92.7 3.0 copy-start
  94.3 5.3 copy-start.25
  94.3 31.8 %copy-start.23 = (s32[1,1,1024,8]{2,3,1,0:T(8,128)S(1)}, s32[1,1,1024,8]{2,3,1,0:T(8,128)}, u32[]{:S(2)}) copy-start(s32[1,1,1024,8]{2,3,1,0:T(8,128)} %param.16) | copy-start | bytes 98308
  94.3 147.1 %all-gather.25.cloned.1.call-start = ((), (), s32[]{:S(2)}) async-start(), calls=%async_computation.20 | async-start | bytes 4718592 | tf_op jit(solution)/shard_map/all_gather | solution.py:804
  95.1 195.9 %all-gather.17.cloned.1.call-start = ((), (), s32[]{:S(2)}) async-start(), calls=%async_computation.8 | async-start | bytes 2359296 | tf_op jit(solution)/shard_map/all_gather | solution.py:810
  95.6 269.3 %all-gather.21.cloned.1.call-start = ((), (), s32[]{:S(2)}) async-start(), calls=%async_computation.10 | async-start | bytes 4718592 | tf_op jit(solution)/shard_map/all_gather | solution.py:813
  96.6 326.3 %all-gather.27.cloned.1.call-start = ((), (), s32[]{:S(2)}) async-start(), calls=%async_computation.21 | async-start | bytes 10485760 | tf_op jit(solution)/shard_map/all_gather | solution.py:814
  97.2 453.4 %all-gather.19.cloned.1.call-start = ((), (), s32[]{:S(2)}) async-start(), calls=%async_computation.9 | async-start | bytes 9437184 | tf_op jit(solution)/shard_map/all_gather | solution.py:812
  99.5 689.6 %reduce-scatter.10.cloned.1.call-start = ((), (), s32[]{:S(2)}) async-start(), calls=%async_computation.11 | async-start | bytes 10485760 | tf_op jit(solution)/shard_map/reduce_scatter | solution.py:834
  126.1 115.4 %copy-start.7 = (s32[2]{0:T(128)}, s32[2]{0:T(128)S(1)}, u32[]{:S(2)}) copy-start(s32[2]{0:T(128)S(1)} %pad_add_fusion.where_ref) | copy-start | bytes 28
  133.3 108.2 %copy-start.2 = (bf16[8,64,1024]{2,1,0:T(8,128)(2,1)}, bf16[8,64,1024]{2,1,0:T(8,128)(2,1)S(1)}, u32[]{:S(2)}) copy-start(bf16[8,64,1024]{2,1,0:T(8,128)(2,1)S(1)} %get-tuple-element.82.q_ref) | copy-start | bytes 3145732
  166.6 1.2 copy-start.3
  167.8 1.0 copy-start.6
  206.9 0.6 copy-start.9
  241.5 1.0 copy-start.5
  242.5 38.0 %copy-start.13 = (f32[16,64,1024]{2,1,0:T(8,128)S(1)}, f32[16,64,1024]{2,1,0:T(8,128)}, u32[]{:S(2)}) copy-start(f32[16,64,1024]{2,1,0:T(8,128)} %constant_dynamic-update-slice_fusion.1) | copy-start | bytes 12582916
  280.5 0.6 copy-start.8
  281.1 2.0 copy-start.14
  296.4 2.0 copy-start.10
  296.9 2.2 copy-start.11
  719.4 0.9 copy-start.24
  719.5 270.0 %reduce-scatter.12.cloned.1.call-start = ((), (), s32[]{:S(2)}) async-start(), calls=%async_computation.12 | async-start | bytes 4718592 | tf_op jit(solution)/shard_map/reduce_scatter | solution.py:863
  789.1 6.7 copy-start.15
  789.1 7.3 copy-start.34
  795.8 3.4 copy-start.12
  859.7 232.1 %reduce-scatter.14.cloned.1.call-start = ((), (), s32[]{:S(2)}) async-start(), calls=%async_computation.13 | async-start | bytes 4718592 | tf_op jit(solution)/shard_map/reduce_scatter | solution.py:863
  919.0 265.1 %reduce-scatter.22.cloned.1.call-start = ((), (), s32[]{:S(2)}) async-start(), calls=%async_computation.24 | async-start | bytes 4718592
  949.4 307.6 %reduce-scatter.16.cloned.1.call-start = ((), (), s32[]{:S(2)}) async-start(), calls=%async_computation.14 | async-start | bytes 2654208 | tf_op jit(solution)/shard_map/reduce_scatter | solution.py:855
  970.0 3.3 copy-start.21
  970.0 3.3 copy-start.22
  970.0 382.0 %reduce-scatter.18.cloned.1.call-start = ((), (), s32[]{:S(2)}) async-start(), calls=%async_computation.15 | async-start | bytes 5013504 | tf_op jit(solution)/shard_map/reduce_scatter | solution.py:878
  1095.2 1.2 copy-start.19
  1096.5 1.6 copy-start.17
  1096.5 1.6 copy-start.28
  1096.5 1.6 copy-start.30
  1096.5 2.8 copy-start.33
  1114.2 391.0 %reduce-scatter.20.cloned.1.call-start = ((), (), s32[]{:S(2)}) async-start(), calls=%async_computation.17 | async-start | bytes 9437184 | tf_op jit(solution)/shard_map/reduce_scatter | solution.py:839
  1157.8 347.5 %copy-start.26 = (bf16[128,16]{0,1:T(8,128)(2,1)S(1)}, bf16[128,16]{0,1:T(8,128)(2,1)}, u32[]{:S(2)}) copy-start(bf16[128,16]{0,1:T(8,128)(2,1)} %param.22) | copy-start | bytes 12292
  1157.8 347.7 %copy-start.31 = (bf16[128]{0:T(256)(128)(2,1)S(1)}, bf16[128]{0:T(256)(128)(2,1)}, u32[]{:S(2)}) copy-start(bf16[128]{0:T(256)(128)(2,1)} %param.21) | copy-start | bytes 772
  1157.8 347.7 %copy-start.32 = (bf16[128]{0:T(256)(128)(2,1)S(1)}, bf16[128]{0:T(256)(128)(2,1)}, u32[]{:S(2)}) copy-start(bf16[128]{0:T(256)(128)(2,1)} %param.18) | copy-start | bytes 772
  1157.8 347.7 %copy-start.1 = (bf16[128,2048]{1,0:T(8,128)(2,1)S(1)}, bf16[128,2048]{1,0:T(8,128)(2,1)}, u32[]{:S(2)}) copy-start(bf16[128,2048]{1,0:T(8,128)(2,1)} %refs_0_.1) | copy-start | bytes 1572868
  1157.8 347.7 %copy-start.4 = (bf16[128,1024]{1,0:T(8,128)(2,1)S(1)}, bf16[128,1024]{1,0:T(8,128)(2,1)}, u32[]{:S(2)}) copy-start(bf16[128,1024]{1,0:T(8,128)(2,1)} %refs_1_.1) | copy-start | bytes 786436
  1157.8 371.3 %all-gather.31.cloned.1.call-start = ((), (), s32[]{:S(2)}) async-start(), calls=%async_computation.23 | async-start | bytes 2621440 | tf_op jit(solution)/shard_map/all_gather | solution.py:840
  1186.2 380.7 %all-reduce.6.cloned.1.call-start = ((), (), s32[]{:S(2)}) async-start(), calls=%async_computation.16 | async-start | bytes 1703936 | tf_op jit(solution)/shard_map/psum | solution.py:879
  1354.1 249.0 %all-gather.29.cloned.1.call-start = ((), (), s32[]{:S(2)}) async-start(), calls=%async_computation.22 | async-start | bytes 5242880 | tf_op jit(solution)/shard_map/all_gather | solution.py:840
  1505.2 305.9 %all-reduce.8.cloned.1.call-start = ((), (), s32[]{:S(2)}) async-start(), calls=%async_computation.18 | async-start | bytes 14172160 | tf_op jit(solution)/shard_map/psum | solution.py:925
  1681.9 1.6 copy-start.18
Sparse Core Ops, SparseCore 0:
  10.1 76.0 all-gather.14
  94.4 72.1 all-gather.22
  169.3 72.0 all-gather.24
  243.4 47.5 all-gather.16
  293.0 71.9 all-gather.20
  366.3 56.5 all-gather.26
  425.6 124.9 all-gather.18
  719.6 69.4 reduce-scatter.9
  859.8 129.6 reduce-scatter.11
  993.6 98.2 reduce-scatter.13
  1096.5 87.6 reduce-scatter.21
  1188.1 68.9 reduce-scatter.15
  1261.3 90.6 reduce-scatter.17
  1356.5 148.6 reduce-scatter.19
  1507.2 21.8 all-gather.30
  1531.9 34.9 all-reduce.5
  1568.4 34.6 all-gather.28
  1682.0 129.0 all-reduce.7

commit v2 on v1

--- a/solution.py
+++ b/solution.py
@@ -57,6 +57,11 @@
     high = scaled.astype(BF16)
     low = (scaled - high.astype(F32)).astype(BF16)
     return rows, high, low
+
+
+def block_of(ref, index, block):
+    span = pl.ds(pl.multiple_of(index * block, block), block)
+    return ref[0, 0, :, span], ref[1, 0, :, span]
 
 
 def causal(width, columns):
@@ -102,14 +107,14 @@
 
     def full(query):
         def body(index, carry):
-            advance(query, kv_ref[index, 0, 0], kv_ref[index, 1, 0], None)
+            advance(query, *block_of(kv_ref, index, block), None)
             return carry
 
         return body
 
     query = begin(0)
     lax.fori_loop(0, shard_pos, full(query), 0)
-    advance(query, kv_ref[shard_pos, 0, 0], kv_ref[shard_pos, 1, 0], causal(block, columns))
+    advance(query, *block_of(kv_ref, shard_pos, block), causal(block, columns))
     finish(0)
 
     query = begin(block)
@@ -119,7 +124,7 @@
     @pl.when(branch % block != 0)
     def _():
         key_pos = lax.broadcasted_iota(jnp.int32, (block, columns), 0)
-        advance(query, kv_ref[whole, 0, 0], kv_ref[whole, 1, 0], key_pos < branch % block)
+        advance(query, *block_of(kv_ref, whole, block), key_pos < branch % block)
 
     advance(query, own_ref[0, 0], own_ref[1, 0], causal(block, columns))
     finish(block)
@@ -129,14 +134,14 @@
     tokens = query.shape[-1]
     block = own_kv.shape[-1]
     columns = PER_KEY * block
-    parts = prompt_kv.shape[0]
+    keys = prompt_kv.shape[-1]
     return pl.pallas_call(
         attn_forward_kernel,
         grid=(query.shape[0] // PER_KEY,),
         in_specs=[
             pl.BlockSpec(memory_space=pltpu.SMEM),
             pl.BlockSpec((PER_KEY, HEAD_SIZE, tokens), lambda h: (h, 0, 0)),
-            pl.BlockSpec((parts, 2, 1, HEAD_SIZE, block), lambda h: (0, 0, h, 0, 0)),
+            pl.BlockSpec((2, 1, HEAD_SIZE, keys), lambda h: (0, h, 0, 0)),
             pl.BlockSpec((2, 1, HEAD_SIZE, block), lambda h: (0, h, 0, 0)),
         ],
         out_specs=[
@@ -154,9 +159,9 @@
         ],
         compiler_params=pltpu.CompilerParams(vmem_limit_bytes=48 * MIB),
         cost_estimate=pl.CostEstimate(
-            flops=4 * tokens * parts * block * query.shape[0] * HEAD_SIZE,
+            flops=4 * tokens * keys * query.shape[0] * HEAD_SIZE,
             bytes_accessed=16 * MIB,
-            transcendentals=query.shape[0] * tokens * parts * block,
+            transcendentals=query.shape[0] * tokens * keys,
         ),
         name="attn_forward",
     )(where, query, prompt_kv, own_kv)
@@ -199,9 +204,10 @@
         return dot(scaled, grad_scores, (1, 1)), dot(grad, probs.astype(BF16), (1, 1))
 
     def add(index, state, mask):
-        dk, dv = terms(state, kv_ref[index, 0, 0], kv_ref[index, 1, 0], mask)
-        dkv_acc[index, 0] += dk
-        dkv_acc[index, 1] += dv
+        dk, dv = terms(state, *block_of(kv_ref, index, block), mask)
+        span = pl.ds(pl.multiple_of(index * block, block), block)
+        dkv_acc[0, :, span] += dk
+        dkv_acc[1, :, span] += dv
 
     def finish(start):
         total = dq_acc[...] * HEAD_SIZE**-0.5
@@ -234,51 +240,355 @@
     down_ref[0, 0] = dk
     down_ref[1, 0] = dv
     finish(block)
-    dkv_ref[:, :, 0] = dkv_acc[...].astype(BF16)
+    dkv_ref[:, 0] = dkv_acc[...].astype(BF16)
 
 
 def attn_backward(where, query, prompt_kv, own_kv, grad_out, lse, delta):
     tokens = query.shape[-1]
     block = own_kv.shape[-1]
     columns = PER_KEY * block
-    parts = prompt_kv.shape[0]
+    keys = prompt_kv.shape[-1]
     by_head = pl.BlockSpec((PER_KEY, HEAD_SIZE, tokens), lambda h: (h, 0, 0))
-    by_parts = pl.BlockSpec((parts, 2, 1, HEAD_SIZE, block), lambda h: (0, 0, h, 0, 0))
+    by_keys = pl.BlockSpec((2, 1, HEAD_SIZE, keys), lambda h: (0, h, 0, 0))
     by_own = pl.BlockSpec((2, 1, HEAD_SIZE, block), lambda h: (0, h, 0, 0))
     by_row = pl.BlockSpec((1, PER_KEY, tokens), lambda h: (h, 0, 0))
     return pl.pallas_call(
         attn_backward_kernel,
         grid=(query.shape[0] // PER_KEY,),
-        in_specs=[pl.BlockSpec(memory_space=pltpu.SMEM), by_head, by_parts, by_own, by_head, by_row, by_row],
-        out_specs=[by_head, by_parts, by_own],
+        in_specs=[pl.BlockSpec(memory_space=pltpu.SMEM), by_head, by_keys, by_own, by_head, by_row, by_row],
+        out_specs=[by_head, by_keys, by_own],
         out_shape=[
             jax.ShapeDtypeStruct(query.shape, F32),
             jax.ShapeDtypeStruct(prompt_kv.shape, BF16),
             jax.ShapeDtypeStruct(own_kv.shape, F32),
         ],
         scratch_shapes=[
-            pltpu.VMEM((parts, 2, HEAD_SIZE, block), F32),
+            pltpu.VMEM((2, HEAD_SIZE, keys), F32),
             pltpu.VMEM((HEAD_SIZE, columns), F32),
         ],
         compiler_params=pltpu.CompilerParams(vmem_limit_bytes=56 * MIB),
         cost_estimate=pl.CostEstimate(
-            flops=10 * tokens * parts * block * query.shape[0] * HEAD_SIZE,
+            flops=10 * tokens * keys * query.shape[0] * HEAD_SIZE,
             bytes_accessed=32 * MIB,
-            transcendentals=query.shape[0] * tokens * parts * block,
+            transcendentals=query.shape[0] * tokens * keys,
         ),
         name="attn_backward",
     )(where, query, prompt_kv, own_kv, grad_out, lse, delta)
 
 
+MESH = pl.DeviceIdType.MESH
+LINE = 4
+TOKEN_PARTS = 4
+
+
+def start_kernel(
+    x_ref,
+    w_ref,
+    top_ref,
+    tok_all,
+    w_all,
+    top_all,
+    own_sem,
+    line_recv,
+    right_send,
+    left_send,
+    y_send,
+    y_recv,
+    x_send,
+    x_recv,
+    core_send,
+    core_recv,
+    top_send,
+    top_recv,
+):
+    part = tok_all.shape[1] // TOKEN_PARTS
+    quarter = w_all.shape[2]
+    half = top_ref.shape[0] // 2
+    me = lax.axis_index("shard")
+    place, column = me // 2, lax.rem(me, 2)
+    rep = lax.axis_index("rep")
+    far, core = lax.rem(rep + 2, 4), rep + 1 - 2 * lax.rem(rep, 2)
+    to_right, to_left, to_y = {"shard": me + 2}, {"shard": me - 2}, {"shard": me + 1 - 2 * column}
+    to_far, to_core = {"rep": far}, {"rep": core}
+    weights, mirrored = 0, TOKEN_PARTS + 1
+    last = TOKEN_PARTS
+    streams = TOKEN_PARTS + 2
+
+    def piece(i, origin, side):
+        if i == weights:
+            return w_all.at[2 * origin + side, rep]
+        k = (i if i != mirrored else last) - 1
+        return tok_all.at[2 * origin + side, pl.ds(k * part, part)]
+
+    def side_of(i):
+        return 1 - column if i == mirrored else column
+
+    def own(i):
+        if i == weights:
+            return w_ref.at[pl.ds(pl.multiple_of(rep * quarter, quarter), quarter)]
+        if i == mirrored:
+            return piece(i, place, 1 - column)
+        return x_ref.at[pl.ds((i - 1) * part, part)]
+
+    def remote(source, target, send, receive, device):
+        return pltpu.make_async_remote_copy(
+            src_ref=source, dst_ref=target, send_sem=send, recv_sem=receive, device_id=device, device_id_type=MESH
+        )
+
+    def source(i, origin, at_home):
+        return own(i) if at_home else piece(i, origin, side_of(i))
+
+    def right(i, origin, at_home=False):
+        return remote(
+            source(i, origin, at_home),
+            piece(i, origin, side_of(i)),
+            right_send.at[i, origin],
+            line_recv.at[i, origin],
+            to_right,
+        )
+
+    def left(i, origin, at_home=False):
+        return remote(
+            source(i, origin, at_home),
+            piece(i, origin, side_of(i)),
+            left_send.at[i, origin],
+            line_recv.at[i, origin],
+            to_left,
+        )
+
+    def abreast(i, origin, at_home=False):
+        return remote(
+            source(i, origin, at_home), piece(i, origin, column), y_send.at[i, origin], y_recv.at[i, origin], to_y
+        )
+
+    def over_x(origin, side, at_home=False):
+        target = piece(weights, origin, side)
+        source_ref = own(weights) if at_home else target
+        return remote(source_ref, target, x_send.at[origin, side], x_recv.at[origin, side], to_far)
+
+    def over_core(group, origin, side, at_home=False):
+        target = w_all.at[2 * origin + side, rep if group == 0 else far]
+        source_ref = own(weights) if at_home else target
+        return remote(
+            source_ref, target, core_send.at[group, origin, side], core_recv.at[group, origin, side], to_core
+        )
+
+    def top_far(h):
+        return remote(
+            top_ref.at[pl.ds(h * half, half)],
+            top_all.at[2, pl.ds(h * half, half)],
+            top_send.at[0, h],
+            top_recv.at[0, h],
+            to_far,
+        )
+
+    def top_core(h):
+        return remote(
+            top_ref.at[pl.ds(h * half, half)],
+            top_all.at[1, pl.ds(h * half, half)],
+            top_send.at[1, h],
+            top_recv.at[1, h],
+            to_core,
+        )
+
+    def top_diagonal(h):
+        return remote(
+            top_all.at[2, pl.ds(h * half, half)],
+            top_all.at[3, pl.ds(h * half, half)],
+            top_send.at[2, h],
+            top_recv.at[2, h],
+            to_core,
+        )
+
+    has_right, has_left = place < LINE - 1, place > 0
+    barrier = pltpu.get_barrier_semaphore()
+
+    def greet(device):
+        pl.semaphore_signal(barrier, inc=1, device_id=device, device_id_type=MESH)
+
+    for device in (to_y, to_far, to_core):
+        greet(device)
+
+    @pl.when(has_right)
+    def _():
+        greet(to_right)
+
+    @pl.when(has_left)
+    def _():
+        greet(to_left)
+
+    pl.semaphore_wait(barrier, 3 + has_right.astype(jnp.int32) + has_left.astype(jnp.int32))
+
+    def along(i, origin, at_home=False):
+        @pl.when(has_right)
+        def _():
+            right(i, origin, at_home).start()
+
+        @pl.when(has_left)
+        def _():
+            left(i, origin, at_home).start()
+
+    order = [weights, last] + list(range(1, last))
+    for i in order:
+        along(i, place, True)
+        abreast(i, place, True).start()
+        if i == weights:
+            over_x(place, column, True).start()
+            over_core(0, place, column, True).start()
+            for h in (0, 1):
+                top_far(h).start()
+    for h in (0, 1):
+        top_core(h).start()
+    own_copies = [
+        pltpu.make_async_copy(own(i), piece(i, place, column), own_sem.at[i]) for i in range(streams - 1)
+    ]
+    own_copies.append(pltpu.make_async_copy(top_ref, top_all.at[0], own_sem.at[streams - 1]))
+    for copy in own_copies:
+        copy.start()
+    abreast(last, place).wait_recv()
+    along(mirrored, place, True)
+
+    def weights_across(origin):
+        abreast(weights, origin).wait_recv()
+        over_x(origin, 1 - column).start()
+        over_core(0, origin, 1 - column).start()
+
+    weights_across(place)
+    for d in range(1, LINE):
+        before, after = place - d, place + d
+        from_left, from_right = before >= 0, after < LINE
+        for i in [weights, last, mirrored] + list(range(1, last)):
+
+            @pl.when(from_left)
+            def _(i=i):
+                right(i, before).wait_recv()
+
+                @pl.when(has_right)
+                def _():
+                    right(i, before).start()
+
+                if i != last and i != mirrored:
+                    abreast(i, before).start()
+                if i == weights:
+                    over_x(before, column).start()
+                    over_core(0, before, column).start()
+
+            @pl.when(from_right)
+            def _(i=i):
+                left(i, after).wait_recv()
+
+                @pl.when(has_left)
+                def _():
+                    left(i, after).start()
+
+                if i != last and i != mirrored:
+                    abreast(i, after).start()
+                if i == weights:
+                    over_x(after, column).start()
+                    over_core(0, after, column).start()
+
+        @pl.when(from_left)
+        def _():
+            weights_across(before)
+
+        @pl.when(from_right)
+        def _():
+            weights_across(after)
+
+        if d >= 2:
+            h = d - 2
+            top_far(h).wait_recv()
+            top_diagonal(h).start()
+
+    for origin in range(LINE):
+        for side in (0, 1):
+            remote(
+                w_all.at[2 * origin + side, far],
+                w_all.at[2 * origin + side, far],
+                x_send.at[origin, side],
+                x_recv.at[origin, side],
+                to_far,
+            ).wait_recv()
+            over_core(1, origin, side).start()
+
+    for origin in range(LINE):
+        for i in range(1, last):
+            abreast(i, origin).wait_recv()
+        for side in (0, 1):
+            for group in (0, 1):
+                over_core(group, origin, side).wait_recv()
+    for h in (0, 1):
+        top_core(h).wait_recv()
+        top_diagonal(h).wait_recv()
+        for copy in (top_far(h), top_core(h), top_diagonal(h)):
+            copy.wait_send()
+    for copy in own_copies:
+        copy.wait()
+    for origin in range(LINE):
+        for i in range(streams):
+
+            @pl.when(has_right & (origin <= place))
+            def _(i=i, origin=origin):
+                right(i, origin).wait_send()
+
+            @pl.when(has_left & (origin >= place))
+            def _(i=i, origin=origin):
+                left(i, origin).wait_send()
+
+            if i != last and i != mirrored:
+                abreast(i, origin).wait_send()
+        for side in (0, 1):
+            over_x(origin, side).wait_send()
+            for group in (0, 1):
+                over_core(group, origin, side).wait_send()
+    abreast(last, place).wait_send()
+
+
+def start_gather(x, small, top):
+    rows, width = x.shape
+    prompt = rows - CONTINUATION_LEN
+    own_rows, columns = small.shape
+    dma = pltpu.SemaphoreType.DMA
+    streams = TOKEN_PARTS + 2
+    anywhere = pl.BlockSpec(memory_space=pl.ANY)
+    return pl.pallas_call(
+        start_kernel,
+        in_specs=[anywhere] * 3,
+        out_specs=[anywhere] * 3,
+        out_shape=[
+            jax.ShapeDtypeStruct((2 * LINE, prompt, width), BF16),
+            jax.ShapeDtypeStruct((2 * LINE, 4, own_rows // 4, columns), BF16),
+            jax.ShapeDtypeStruct((4, rows, width), BF16),
+        ],
+        scratch_shapes=[
+            dma((streams,)),
+            dma((streams, LINE)),
+            dma((streams, LINE)),
+            dma((streams, LINE)),
+            dma((streams, LINE)),
+            dma((streams, LINE)),
+            dma((LINE, 2)),
+            dma((LINE, 2)),
+            dma((2, LINE, 2)),
+            dma((2, LINE, 2)),
+            dma((3, 2)),
+            dma((3, 2)),
+        ],
+        compiler_params=pltpu.CompilerParams(collective_id=2, has_side_effects=True),
+        cost_estimate=pl.CostEstimate(flops=0, bytes_accessed=64 * MIB, transcendentals=0),
+        name="start_gather",
+    )(x, small, top)
+
+
 ORDER = ((0, 0), (0, 1), (3, 0), (2, 0), (3, 1), (2, 1), (1, 0), (1, 1))
+Y_PLACE = (0, 2, 1, 3)
 
 
 def experts_kernel(
     x_hbm,
     top_hbm,
     gates_ref,
-    in_ref,
-    out_ref,
+    w_ref,
     all_x,
     dx_own,
     dx_core,
@@ -309,7 +619,7 @@
     small_recv,
 ):
     tile = x_buf.shape[1]
-    count = in_ref.shape[1] // (2 * F)
+    count = w_ref.shape[1] // (3 * F)
     step = pl.program_id(0)
     steps = len(ORDER)
     slot = lax.rem(step, 2)
@@ -323,7 +633,7 @@
             send_sem=send,
             recv_sem=receive,
             device_id={"rep": home[relation]},
-            device_id_type=pl.DeviceIdType.MESH,
+            device_id_type=MESH,
         )
 
     def half(ref, half_index, *lead):
@@ -359,15 +669,14 @@
 
     def load_top(i):
         kind, h = ORDER[i]
-        return pltpu.make_async_copy(half(top_hbm, h, home[kind]), top_buf.at[i % 2], in_sem.at[i % 2, 1])
+        return pltpu.make_async_copy(half(top_hbm, h, kind), top_buf.at[i % 2], in_sem.at[i % 2, 1])
 
     def stores(i):
         kind, h = ORDER[i]
         out = []
-        for n, (buffer, target) in enumerate(((y_buf, y_all), (dgu_buf, dgu_all), (gh_buf, gh_all))):
-            out.append(
-                pltpu.make_async_copy(buffer.at[i % 2], half(target, h, home[kind]), out_sem.at[i % 2, n])
-            )
+        places = (y_buf, y_all, Y_PLACE[kind]), (dgu_buf, dgu_all, home[kind]), (gh_buf, gh_all, kind)
+        for n, (buffer, target, place) in enumerate(places):
+            out.append(pltpu.make_async_copy(buffer.at[i % 2], half(target, h, place), out_sem.at[i % 2, n]))
         return out
 
     def store_dx(i):
@@ -394,7 +703,7 @@
                 barrier = pltpu.get_barrier_semaphore()
                 for k in (1, 2, 3):
                     pl.semaphore_signal(
-                        barrier, inc=1, device_id={"rep": home[k]}, device_id_type=pl.DeviceIdType.MESH
+                        barrier, inc=1, device_id={"rep": home[k]}, device_id_type=MESH
                     )
                 pl.semaphore_wait(barrier, 3)
                 for n in (0, 1):
@@ -437,8 +746,8 @@
     top = top_buf[slot]
     columns = []
     for e in range(count):
-        w_in = in_ref[:, e * 2 * F : (e + 1) * 2 * F]
-        w_out = out_ref[:, e * F : (e + 1) * F]
+        w_in = w_ref[:, e * 2 * F : (e + 1) * 2 * F]
+        w_out = w_ref[:, (count * 2 + e) * F : (count * 2 + e + 1) * F]
         gate_up = dot(x, w_in, (1, 0))
         g = gate_up[:, :F]
         u = gate_up[:, F:]
@@ -503,19 +812,19 @@
                     small_back(k).wait()
 
 
-def experts(x, all_top, gates, w_in, w_out):
+def experts(x, all_top, gates, weights):
     rows, width = x.shape
     reps = all_top.shape[0]
-    count = w_in.shape[1] // (2 * F)
+    count = weights.shape[1] // (3 * F)
     tile = rows // 2
     anywhere = pl.BlockSpec(memory_space=pl.ANY)
-    fixed = lambda n: pl.BlockSpec((width, n), lambda i: (0, 0), pipeline_mode=pl.Buffered(1))
+    fixed = pl.BlockSpec(weights.shape, lambda i: (0, 0), pipeline_mode=pl.Buffered(1))
     small = pl.BlockSpec((reps, 8, rows), lambda i: (0, 0, 0))
     dma = pltpu.SemaphoreType.DMA
     return pl.pallas_call(
         experts_kernel,
         grid=(len(ORDER),),
-        in_specs=[anywhere, anywhere, small, fixed(count * 2 * F), fixed(count * F)],
+        in_specs=[anywhere, anywhere, small, fixed],
         out_specs=[anywhere] * 8,
         out_shape=[
             jax.ShapeDtypeStruct((reps, rows, width), BF16),
@@ -558,7 +867,7 @@
             transcendentals=reps * rows * count * F,
         ),
         name="experts",
-    )(x, all_top, gates, w_in, w_out)
+    )(x, all_top, gates, weights)
 
 
 def flatten_kernel(starts, lead_ref, *refs):
@@ -610,20 +919,24 @@
 
     @pl.when(step == steps - 1)
     def _():
-        if True:
-            for copy in copies(step - 1, 1 - slot):
-                copy.wait()
+        for copy in copies(step - 1, 1 - slot):
+            copy.wait()
         for copy in copies(step, slot):
             copy.wait()
 
-def flatten(size, lead, *parts, tile=16):
-    rows = parts[0].shape[-2]
-    widths = [p.shape[-1] * (p.shape[0] if p.ndim == 3 else 1) // LANES for p in parts]
+def flatten(size, lead, parts, tile=16):
+    rows = parts[0][0].shape[-2]
+    widths = [columns * (p.shape[0] if p.ndim == 3 else 1) // LANES for p, columns, _ in parts]
     starts, at = [], 1
     for n, w in enumerate(widths):
         if n == 2: at += 1 + 16
         starts.append(at); at += rows * w
-    specs = [pl.BlockSpec((p.shape[0], tile, p.shape[2]), lambda i: (0, i, 0)) if p.ndim == 3 else pl.BlockSpec((tile, p.shape[1]), lambda i: (i, 0)) for p in parts]
+    specs = []
+    for p, columns, place in parts:
+        if p.ndim == 3:
+            specs.append(pl.BlockSpec((p.shape[0], tile, columns), lambda i, place=place: (0, i, place)))
+        else:
+            specs.append(pl.BlockSpec((tile, columns), lambda i, place=place: (i, place)))
     return pl.pallas_call(
         functools.partial(flatten_kernel, starts),
         grid=(rows // tile,),
@@ -633,89 +946,302 @@
         scratch_shapes=[pltpu.VMEM((2, tile * w, LANES), F32) for w in widths] + [pltpu.SemaphoreType.DMA((3, 4))],
         compiler_params=pltpu.CompilerParams(vmem_limit_bytes=48 * MIB),
         name="flatten",
-    )(lead, *parts)
-
-def optimizer_math(grad, first, second, weight, scale):
+    )(lead, *[p for p, _, _ in parts])
+
+HALF_ROWS = 1056
+
+
+def moments(grad, first, second, scale):
     clipped = grad * scale
     new_first = BETA_ONE * first + (1.0 - BETA_ONE) * clipped
     new_second = BETA_TWO * second + (1.0 - BETA_TWO) * clipped * clipped
+    return new_first, new_second
+
+
+def inner_step(new_first, new_second, weight):
     root = jnp.sqrt(new_second * (1.0 / (1.0 - BETA_TWO**STEP))) + ADAM_EPS
-    step = -INNER_RATE * (new_first * (1.0 / (1.0 - BETA_ONE**STEP)) / root + DECAY_RATE * weight)
-    return new_first, new_second, step
-
-CHUNK=1024
-def stream(body, ins, outs, rows):
-    whole = rows // CHUNK
-    pipe = pltpu.emit_pipeline(body, grid=(whole,), in_specs=[pl.BlockSpec((CHUNK, LANES), lambda i: (i, 0))] * len(ins), out_specs=[pl.BlockSpec((CHUNK, LANES), lambda i: (i, 0))] * len(outs))
-    pipe(*ins, *outs)
-
-def adam_kernel(scale_ref, g, f, s, w, nf, ns, st, tg, tf, ts, tw, tnf, tns, tst, sems):
+    return -INNER_RATE * (new_first * (1.0 / (1.0 - BETA_ONE**STEP)) / root + DECAY_RATE * weight)
+
+
+def flat_chunks(rows):
+    chunks, at, half_at = [], 0, 0
+    while at < rows:
+        size = min(2 * HALF_ROWS, rows - at)
+        half = -(-size // 32) * 16
+        chunks.append((at, size, half_at, half))
+        at, half_at = at + size, half_at + half
+    return chunks
+
+
+def step_kernel(
+    square_ref,
+    g_ref,
+    f_ref,
+    s_ref,
+    w_ref,
+    norm_ref,
+    total,
+    g_buf,
+    f_buf,
+    s_buf,
+    w_buf,
+    step_buf,
+    near_buf,
+    far_buf,
+    sum_buf,
+    square_mine,
+    square_all,
+    in_sem,
+    near_send,
+    near_recv,
+    far_send,
+    far_recv,
+    back_send,
+    back_recv,
+    own_sem,
+    square_send,
+    square_recv,
+):
+    rows = g_ref.shape[-1] // LANES
+    chunks = flat_chunks(rows)
+    count = len(chunks)
+    shards = lax.axis_size("shard")
+    shard, rep = lax.axis_index("shard"), lax.axis_index("rep")
+    side = lax.rem(rep, 2)
+    to_core, to_far = {"rep": rep + 1 - 2 * side}, {"rep": lax.rem(rep + 2, 4)}
+
+    def other(k):
+        return {"shard": lax.rem(shard + k, shards)}
+
+    barrier = pltpu.get_barrier_semaphore()
+    greeted = [to_core, to_far] + [other(k) for k in range(1, shards)]
+    for device in greeted:
+        pl.semaphore_signal(barrier, inc=1, device_id=device, device_id_type=MESH)
+
+    def loads(i):
+        at, size, _, _ = chunks[i]
+        pairs = (g_ref, g_buf), (f_ref.at[0], f_buf), (s_ref.at[0], s_buf), (w_ref, w_buf)
+        return [
+            pltpu.make_async_copy(
+                ref.at[:, pl.ds(at * LANES, size * LANES)],
+                buf.at[i % 2, :, pl.ds(0, size * LANES)],
+                in_sem.at[i % 2, n],
+            )
+            for n, (ref, buf) in enumerate(pairs)
+        ]
+
+    def remote(source, target, send, receive, device):
+        return pltpu.make_async_remote_copy(
+            src_ref=source, dst_ref=target, send_sem=send, recv_sem=receive, device_id=device, device_id_type=MESH
+        )
+
+    def near(i):
+        _, _, at, half = chunks[i]
+        span = pl.ds(at, half)
+        return remote(step_buf.at[1 - side, span], near_buf.at[span], near_send.at[i], near_recv.at[i], to_core)
+
+    def far(i):
+        _, _, at, half = chunks[i]
+        span = pl.ds(at, half)
+        return remote(step_buf.at[side, span], far_buf.at[span], far_send.at[i], far_recv.at[i], to_far)
+
+    def back(i):
+        _, _, at, half = chunks[i]
+        span = pl.ds(at, half)
+        return remote(sum_buf.at[span], total.at[side, span], back_send.at[i], back_recv.at[i], to_core)
+
+    def keep(i):
+        _, _, at, half = chunks[i]
+        span = pl.ds(at, half)
+        return pltpu.make_async_copy(sum_buf.at[span], total.at[side, span], own_sem.at[i])
+
+    for copy in loads(0):
+        copy.start()
+    pl.semaphore_wait(barrier, len(greeted))
+
+    def square_copy(k):
+        return remote(square_mine, square_all.at[shard], square_send.at[k], square_recv.at[shard], other(k))
+
+    square_mine[...] = jnp.broadcast_to(square_ref[...], square_mine.shape)
+    square_all[shard] = square_mine[...]
+    for k in range(1, shards):
+        square_copy(k).start()
+    for k in range(1, shards):
+        source = lax.rem(shard + k, shards)
+        remote(
+            square_mine, square_all.at[source], square_send.at[k], square_recv.at[source], other(k)
+        ).wait_recv()
+    norm = jnp.sqrt(jnp.sum(square_all[...], axis=0))
+    norm_ref[...] = norm[:1, :1]
+    scale = (CLIP_NORM / jnp.maximum(norm, CLIP_NORM))[:1]
+
+    def blocks(size):
+        return 48 if size % 48 == 0 else 16
+
+    def compute(i):
+        _, _, at, half = chunks[i]
+        block = blocks(half)
+        for h in (0, 1):
+
+            def body(j, carry):
+                here = pl.multiple_of(j * block, 16)
+                span = pl.ds(pl.multiple_of((h * half + here) * LANES, LANES), block * LANES)
+                grad, first, second, weight = (
+                    buf[i % 2, :, span].reshape(block, LANES) for buf in (g_buf, f_buf, s_buf, w_buf)
+                )
+                new_first, new_second = moments(grad, first, second, scale)
+                step = inner_step(new_first, new_second, weight)
+                step_buf[h, pl.ds(at + here, block)] = step.astype(BF16)
+                return carry
+
+            lax.fori_loop(0, half // block, body, 0)
+
+    def add(i, left, right, target):
+        _, _, at, half = chunks[i]
+        block = blocks(half)
+
+        def body(j, carry):
+            span = pl.ds(pl.multiple_of(at + j * block, 16), block)
+            target[span] = (left[span].astype(F32) + right[span].astype(F32)).astype(BF16)
+            return carry
+
+        lax.fori_loop(0, half // block, body, 0)
+
+    for i in range(count + 2):
+        if i < count:
+            for copy in loads(i):
+                copy.wait()
+            if i + 1 < count:
+                for copy in loads(i + 1):
+                    copy.start()
+            compute(i)
+            near(i).start()
+        if 1 <= i <= count:
+            near(i - 1).wait_recv()
+            add(i - 1, step_buf.at[side], near_buf, step_buf.at[side])
+            far(i - 1).start()
+        if i >= 2:
+            far(i - 2).wait_recv()
+            add(i - 2, step_buf.at[side], far_buf, sum_buf)
+            back(i - 2).start()
+            keep(i - 2).start()
+    for k in range(1, shards):
+        square_copy(k).wait_send()
+    for i in range(count):
+        near(i).wait_send()
+        far(i).wait_send()
+        back(i).wait_send()
+        keep(i).wait()
+        _, _, at, half = chunks[i]
+        span = pl.ds(at, half)
+        remote(
+            sum_buf.at[span], total.at[1 - side, span], back_send.at[i], back_recv.at[i], to_core
+        ).wait_recv()
+
+
+def summed_step(square, grad, first, second, weight):
+    rows = grad.shape[-1] // LANES
+    chunks = flat_chunks(rows)
+    count = len(chunks)
+    halves = sum(chunk[3] for chunk in chunks)
+    size = chunks[0][3] * 2
+    shards = lax.axis_size("shard")
+    dma = pltpu.SemaphoreType.DMA
+    anywhere = pl.BlockSpec(memory_space=pl.ANY)
+    return pl.pallas_call(
+        step_kernel,
+        in_specs=[pl.BlockSpec(memory_space=pltpu.VMEM)] + [anywhere] * 4,
+        out_specs=[pl.BlockSpec(memory_space=pltpu.VMEM), anywhere],
+        out_shape=[jax.ShapeDtypeStruct((1, 1), F32), jax.ShapeDtypeStruct((2, halves, LANES), BF16)],
+        scratch_shapes=[pltpu.VMEM((2, 1, size * LANES), F32)] * 4
+        + [
+            pltpu.VMEM((2, halves, LANES), BF16),
+            pltpu.VMEM((halves, LANES), BF16),
+            pltpu.VMEM((halves, LANES), BF16),
+            pltpu.VMEM((halves, LANES), BF16),
+            pltpu.VMEM((8, LANES), F32),
+            pltpu.VMEM((shards, 8, LANES), F32),
+            dma((2, 4)),
+        ]
+        + [dma((count,))] * 7
+        + [dma((shards,))] * 2,
+        compiler_params=pltpu.CompilerParams(
+            vmem_limit_bytes=48 * MIB, collective_id=3, has_side_effects=True
+        ),
+        cost_estimate=pl.CostEstimate(flops=0, bytes_accessed=64 * MIB, transcendentals=0),
+        name="summed_step",
+    )(square, grad, first, second, weight)
+
+
+def update_kernel(
+    reps, norm_ref, g, f, s, total, mom, nf, ns, nm, up, tg, tf, ts, tm, tt, tnf, tns, tnm, tup, sems
+):
     rows = g.shape[-1] // LANES
-    def view(r):
-        return r.reshape(rows, LANES)
-    scale = scale_ref[0]
-    def body(gr, fr, sr, wr, nfr, nsr, str_):
-        a, b, c = optimizer_math(gr[...], fr[...], sr[...], wr[...], scale)
-        nfr[...] = a; nsr[...] = b; str_[...] = c.astype(BF16)
-    ins = [view(r) for r in (g, f, s, w)]
-    outs = [view(nf), view(ns), st]
-    stream(body, ins, outs, rows)
-    done = rows // CHUNK * CHUNK
-    rest = rows - done
-    for n, (r, t) in enumerate(zip(ins, (tg, tf, ts, tw))):
-        pltpu.make_async_copy(r.at[pl.ds(done, rest)], t.at[pl.ds(0, rest)], sems.at[n]).start()
-    for n, (r, t) in enumerate(zip(ins, (tg, tf, ts, tw))):
-        pltpu.make_async_copy(r.at[pl.ds(done, rest)], t.at[pl.ds(0, rest)], sems.at[n]).wait()
-    body(tg, tf, ts, tw, tnf, tns, tst)
-    tail = st.shape[0] - done
-    cs = [pltpu.make_async_copy(tnf.at[pl.ds(0, rest)], outs[0].at[pl.ds(done, rest)], sems.at[0]),
-          pltpu.make_async_copy(tns.at[pl.ds(0, rest)], outs[1].at[pl.ds(done, rest)], sems.at[1]),
-          pltpu.make_async_copy(tst.at[pl.ds(0, tail)], outs[2].at[pl.ds(done, tail)], sems.at[2])]
-    for c in cs: c.start()
-    for c in cs: c.wait()
-
-def adam(scale, g, f, s, w):
-    n = g.shape[-1]
-    rows = n // LANES
-    pad = -(-rows // 16) * 16
-    tail = pad - rows // CHUNK * CHUNK
-    anys = pl.BlockSpec(memory_space=pl.ANY)
-    return pl.pallas_call(adam_kernel, in_specs=[pl.BlockSpec(memory_space=pltpu.SMEM)] + [anys] * 4, out_specs=[anys] * 3,
-      out_shape=[jax.ShapeDtypeStruct(f.shape, F32), jax.ShapeDtypeStruct(s.shape, F32), jax.ShapeDtypeStruct((pad, LANES), BF16)],
-      scratch_shapes=[pltpu.VMEM((tail, LANES), F32)] * 6 + [pltpu.VMEM((tail, LANES), BF16), pltpu.SemaphoreType.DMA((4,))],
-      compiler_params=pltpu.CompilerParams(vmem_limit_bytes=48 * MIB), name="adam")(scale, g, f, s, w)
-
-def outer_kernel(reps, st, mom, nm, up, ts, tm, tnm, tup, sems):
-    rows = mom.shape[-1] // LANES
-    def body(sr, mr, nmr, upr):
-        pseudo = sr[...].astype(F32) * (-1.0 / reps)
-        new = OUTER_MOMENTUM * mr[...] + pseudo
-        nmr[...] = new
-        upr[...] = -OUTER_RATE * (pseudo + OUTER_MOMENTUM * new)
-    view = lambda r: r.reshape(rows, LANES)
-    m, a, b = view(mom), view(nm), view(up)
-    stream(body, [st, m], [a, b], rows)
-    done = rows // CHUNK * CHUNK
-    rest = rows - done
-    tail = st.shape[0] - done
-    cs = [pltpu.make_async_copy(st.at[pl.ds(done, tail)], ts.at[pl.ds(0, tail)], sems.at[0]),
-          pltpu.make_async_copy(m.at[pl.ds(done, rest)], tm.at[pl.ds(0, rest)], sems.at[1])]
-    for c in cs: c.start()
-    for c in cs: c.wait()
-    body(ts, tm, tnm, tup)
-    cs = [pltpu.make_async_copy(tnm.at[pl.ds(0, rest)], a.at[pl.ds(done, rest)], sems.at[0]),
-          pltpu.make_async_copy(tup.at[pl.ds(0, rest)], b.at[pl.ds(done, rest)], sems.at[1])]
-    for c in cs: c.start()
-    for c in cs: c.wait()
-
-def outer(reps, st, mom):
-    rows = mom.shape[-1] // LANES
-    tail = st.shape[0] - rows // CHUNK * CHUNK
-    anys = pl.BlockSpec(memory_space=pl.ANY)
-    return pl.pallas_call(functools.partial(outer_kernel, reps), in_specs=[anys] * 2, out_specs=[anys] * 2,
-      out_shape=[jax.ShapeDtypeStruct(mom.shape, F32)] * 2,
-      scratch_shapes=[pltpu.VMEM((tail, LANES), BF16)] + [pltpu.VMEM((tail, LANES), F32)] * 3 + [pltpu.SemaphoreType.DMA((2,))],
-      compiler_params=pltpu.CompilerParams(vmem_limit_bytes=48 * MIB), name="outer")(st, mom)
+    chunks = flat_chunks(rows)
+    whole = [c for c in chunks if c[1] == 2 * HALF_ROWS]
+    scale = CLIP_NORM / jnp.maximum(norm_ref[...], CLIP_NORM)
+
+    def body(g_ref, f_ref, s_ref, t_ref, m_ref, nf_ref, ns_ref, nm_ref, up_ref):
+        half = t_ref.shape[1]
+        size = g_ref.shape[0]
+        nf_ref[...], ns_ref[...] = moments(g_ref[...], f_ref[...], s_ref[...], scale)
+        for h in (0, 1):
+            span = slice(h * half, min((h + 1) * half, size))
+            pseudo = t_ref[h, : span.stop - span.start].astype(F32) * (-1.0 / reps)
+            new = OUTER_MOMENTUM * m_ref[span] + pseudo
+            nm_ref[span] = new
+            up_ref[span] = -OUTER_RATE * (pseudo + OUTER_MOMENTUM * new)
+
+    def view(ref):
+        return ref.reshape(rows, LANES)
+
+    ins, outs = [view(g), view(f), view(s), total, view(mom)], [view(r) for r in (nf, ns, nm, up)]
+    wide = pl.BlockSpec((2 * HALF_ROWS, LANES), lambda i: (i, 0))
+    halves = pl.BlockSpec((2, HALF_ROWS, LANES), lambda i: (0, i, 0))
+    if whole:
+        pltpu.emit_pipeline(
+            body, grid=(len(whole),), in_specs=[wide, wide, wide, halves, wide], out_specs=[wide] * 4
+        )(*ins, *outs)
+    for at, size, half_at, half in chunks[len(whole) :]:
+
+        def part(n, ref):
+            return ref.at[:, pl.ds(half_at, half)] if n == 3 else ref.at[pl.ds(at, size)]
+
+        copies = [
+            pltpu.make_async_copy(part(n, ref), buf, sems.at[n]) for n, (ref, buf) in enumerate(zip(ins, (tg, tf, ts, tt, tm)))
+        ]
+        for copy in copies:
+            copy.start()
+        for copy in copies:
+            copy.wait()
+        body(tg, tf, ts, tt, tm, tnf, tns, tnm, tup)
+        copies = [
+            pltpu.make_async_copy(buf, ref.at[pl.ds(at, size)], sems.at[n])
+            for n, (buf, ref) in enumerate(zip((tnf, tns, tnm, tup), outs))
+        ]
+        for copy in copies:
+            copy.start()
+        for copy in copies:
+            copy.wait()
+
+
+def update(reps, norm, grad, first, second, total, mom):
+    _, size, _, half = flat_chunks(grad.shape[-1] // LANES)[-1]
+    anywhere = pl.BlockSpec(memory_space=pl.ANY)
+    tail = pltpu.VMEM((size, LANES), F32)
+    return pl.pallas_call(
+        functools.partial(update_kernel, reps),
+        in_specs=[pl.BlockSpec(memory_space=pltpu.VMEM)] + [anywhere] * 5,
+        out_specs=[anywhere] * 4,
+        out_shape=[jax.ShapeDtypeStruct(ref.shape, F32) for ref in (first, second, mom, mom)],
+        scratch_shapes=[tail] * 4
+        + [pltpu.VMEM((2, half, LANES), BF16)]
+        + [tail] * 4
+        + [pltpu.SemaphoreType.DMA((5,))],
+        compiler_params=pltpu.CompilerParams(vmem_limit_bytes=48 * MIB),
+        cost_estimate=pl.CostEstimate(flops=0, bytes_accessed=120 * MIB, transcendentals=0),
+        name="update",
+    )(norm, grad, first, second, total, mom)
 
 
 def rms_scale(rows):
@@ -768,53 +1294,76 @@
     grad_top = top_low.astype(F32)
     route_ids = routes.reshape(count, TOP)
     gather = functools.partial(lax.all_gather, axis_name="shard", axis=0, tiled=True)
-
-    flat_path = width // shards == LANES and outer_mom.shape[-1] % LANES == 0
-
-    gains = gather(jnp.stack([attn_gain, ffn_gain], axis=1)).astype(F32)
+    rows = width // shards
+    qkv_columns = Q_WIDTH + 2 * KV_WIDTH
+    fast = shards == 2 * LINE and reps == 4 and rows == LANES
+    flat_path = fast and outer_mom.shape[-1] % LANES == 0
+
+    small = jnp.concatenate(
+        [query_key_value_weight, w_attn_out, w_router, attn_gain[:, None], ffn_gain[:, None]], axis=1
+    )
+    small = jnp.pad(small, ((0, 0), (0, -small.shape[1] % LANES)))
+    tokens_low = tokens.reshape(count, width)
+    if fast:
+        prompt_low, small_full, all_top = start_gather(tokens_low, small, top_low)
+        small_full = small_full.reshape(width, small.shape[1])
+    else:
+        prompt_low = lax.all_gather(tokens_low[:prompt], "shard", axis=0, tiled=False, axis_index_groups=groups)
+        small_full = gather(small)
+        by_rep = lax.all_gather(top_low, "rep", axis=0, tiled=False)
+        core_pos = rep_pos + 1 - 2 * (rep_pos % 2)
+        all_top = jnp.stack([top_low] + [by_rep[i] for i in (core_pos, (rep_pos + 2) % 4, 3 - rep_pos)])
+    prompt_low = prompt_low.reshape(GROUP_SIZE * prompt, width)
+    qkv_full = small_full[:, :qkv_columns]
+    attn_out_full = small_full[:, qkv_columns : qkv_columns + Q_WIDTH]
+    router_full = small_full[:, qkv_columns + Q_WIDTH : qkv_columns + Q_WIDTH + EXPERTS]
+    gains = small_full[:, qkv_columns + Q_WIDTH + EXPERTS :].astype(F32)
     attn_gain_full, ffn_gain_full = gains[:, 0], gains[:, 1]
-    qkv_full = gather(query_key_value_weight)
-
-    attn_scale = rms_scale(x_in)
-    normed_attn = (x_in * attn_scale * attn_gain_full).astype(BF16)
-    positions = jnp.concatenate(
+    w_both = jnp.concatenate(
         [
-            shard_pos * prompt + jnp.arange(prompt, dtype=jnp.int32),
-            branch_len + jnp.arange(CONTINUATION_LEN, dtype=jnp.int32),
-        ]
+            lax.dynamic_slice_in_dim(w_in, rep_pos * local * 2 * F, local * 2 * F, 1),
+            lax.dynamic_slice_in_dim(w_out, rep_pos * local * F, local * F, 1),
+        ],
+        axis=1,
     )
-    half = HEAD_SIZE // 2
-    inverse_freq = ROPE_BASE ** (-(jnp.arange(half, dtype=F32) * 2.0) / HEAD_SIZE)
-    angles = inverse_freq[:, None] * positions.astype(F32)[None, :]
-    cosine, sine = jnp.cos(angles)[None], jnp.sin(angles)[None]
-
-    def project(start, size, spin):
-        rows = dot(qkv_full[:, start : start + size], normed_attn, (0, 1))
-        rows = rows.reshape(size // HEAD_SIZE, HEAD_SIZE, count)
-        return (rotate(rows, cosine, sine) if spin else rows).astype(BF16)
-
-    key_value = jnp.stack(
-        [project(Q_WIDTH, KV_WIDTH, True), project(Q_WIDTH + KV_WIDTH, KV_WIDTH, False)]
+    w_both, prompt_low = lax.optimization_barrier((w_both, prompt_low))
+    w_both = gather(w_both)
+
+    def normed(values):
+        scale = rms_scale(values)
+        return (values * scale * attn_gain_full).astype(BF16), scale
+
+    def angles_of(positions):
+        half = HEAD_SIZE // 2
+        inverse_freq = ROPE_BASE ** (-(jnp.arange(half, dtype=F32) * 2.0) / HEAD_SIZE)
+        angles = inverse_freq[:, None] * positions.astype(F32)[None, :]
+        return jnp.cos(angles)[None], jnp.sin(angles)[None]
+
+    def project(source, start, size, turn):
+        rows = dot(qkv_full[:, start : start + size], source, (0, 1))
+        rows = rows.reshape(size // HEAD_SIZE, HEAD_SIZE, source.shape[0])
+        return (rotate(rows, *turn) if turn is not None else rows).astype(BF16)
+
+    def keys_values(source, turn):
+        return jnp.stack([project(source, Q_WIDTH, KV_WIDTH, turn), project(source, Q_WIDTH + KV_WIDTH, KV_WIDTH, None)])
+
+    normed_attn, attn_scale = normed(x_in)
+    normed_prompt, _ = normed(prompt_low.astype(F32))
+    prompt_turn = angles_of(jnp.arange(GROUP_SIZE * prompt, dtype=jnp.int32))
+    own_turn = angles_of(
+        jnp.concatenate(
+            [
+                shard_pos * prompt + jnp.arange(prompt, dtype=jnp.int32),
+                branch_len + jnp.arange(CONTINUATION_LEN, dtype=jnp.int32),
+            ]
+        )
     )
-    pieces = 2
-    per_piece = KEY_VALUE_HEADS // pieces
-    kv_piece = [slice(i * per_piece, (i + 1) * per_piece) for i in range(pieces)]
-    q_piece = [slice(p.start * PER_KEY, p.stop * PER_KEY) for p in kv_piece]
-    prompt_kv = [
-        lax.all_gather(key_value[:, p, :, :prompt], "shard", axis=0, tiled=False, axis_index_groups=groups)
-        for p in kv_piece
-    ]
-    own_kv = [key_value[:, p, :, prompt:] for p in kv_piece]
-    query_all = project(0, Q_WIDTH, True)
-    query = [query_all[p] for p in q_piece]
-    attn_out_full = gather(w_attn_out)
-    router_full = gather(w_router)
-    w_in_mine = gather(lax.dynamic_slice_in_dim(w_in, rep_pos * local * 2 * F, local * 2 * F, 1))
-    w_out_mine = gather(lax.dynamic_slice_in_dim(w_out, rep_pos * local * F, local * F, 1))
-    all_top = lax.all_gather(top_low, "rep", axis=0, tiled=False)
+    continued_turn = tuple(part[..., prompt:] for part in own_turn)
+    prompt_kv = keys_values(normed_prompt, prompt_turn)
+    own_kv = keys_values(normed_attn[prompt:], continued_turn)
+    query = project(normed_attn, 0, Q_WIDTH, own_turn)
     where = jnp.stack([shard_pos.astype(jnp.int32), branch_len])
-    attn, lse = zip(*[attn_forward(where, *part) for part in zip(query, prompt_kv, own_kv)])
-    attn = jnp.concatenate(attn, axis=0)
+    attn, lse = attn_forward(where, query, prompt_kv, own_kv)
     attn_low = attn.astype(BF16).reshape(Q_WIDTH, count)
     x_mid = x_in + dot(attn_low, attn_out_full, (0, 1))
 
@@ -827,20 +1376,23 @@
 
     gates_out = jnp.pad(gates.T.reshape(reps, local, count), ((0, 0), (0, 8 - local), (0, 0)))
     all_normed, dx_own, dx_core, dx_far, y_part, dgu, gated, dgate_part = experts(
-        normed_ffn, all_top, gates_out, w_in_mine, w_out_mine
+        normed_ffn, all_top, gates_out, w_both
     )
     grad_from_experts = dx_own.astype(F32) + dx_core.astype(F32) + dx_far.astype(F32)
     grad_gates = dgate_part[:, :local].reshape(EXPERTS, count).T
-    y_sum = lax.psum_scatter(y_part, "rep", scatter_dimension=0, tiled=False).astype(F32)
+    to_core = [(i, i + 1 - 2 * (i % 2)) for i in range(reps)]
+    to_far = [(i, (i + 2) % reps) for i in range(reps)]
+    y_near = y_part[:2].astype(F32) + lax.ppermute(y_part[2:], "rep", to_core).astype(F32)
+    y_sum = y_near[0] + lax.ppermute(y_near[1].astype(BF16), "rep", to_far).astype(F32)
     block_out = (x_mid + y_sum).astype(BF16)
 
+    def rep_sum(values):
+        for pairs in (to_core, to_far):
+            values = (values.astype(F32) + lax.ppermute(values, "rep", pairs).astype(F32)).astype(BF16)
+        return values
+
     def expert_term(left, right):
-        term = dot(left.reshape(reps * count, width), right.reshape(reps * count, -1), (0, 0)).astype(BF16)
-        rows = lax.psum_scatter(term, "shard", scatter_dimension=0, tiled=True)
-        return lax.all_gather(rows, "rep", axis=0, tiled=False)
-
-    expert_in = expert_term(all_normed, dgu)
-    expert_out = expert_term(all_top, gated)
+        return dot(left.reshape(reps * count, width), right.reshape(reps * count, -1), (0, 0)).astype(BF16)
 
     grad_logits = (gates * (grad_gates - jnp.sum(gates * grad_gates, axis=-1, keepdims=True))).astype(BF16)
     grad_router_w = dot(normed_ffn, grad_logits, (0, 0))
@@ -850,50 +1402,100 @@
     grad_branch = grad_mid.astype(BF16)
     grad_attn_w = dot(grad_branch, attn_low, (0, 1))
     grad_attn = dot(attn_out_full, grad_branch, (0, 1)).astype(BF16).reshape(QUERY_HEADS, HEAD_SIZE, count)
-    early = jnp.concatenate([grad_attn_w, grad_ffn_gain[:, None], grad_router_w], axis=1).astype(BF16)
+    early = jnp.concatenate(
+        [
+            expert_term(all_normed, dgu),
+            expert_term(all_top, gated),
+            grad_attn_w.astype(BF16),
+            grad_router_w.astype(BF16),
+            grad_ffn_gain[:, None].astype(BF16),
+        ],
+        axis=1,
+    )
     early = jnp.pad(early, ((0, 0), (0, -early.shape[1] % LANES)))
+    grad_attn, early = lax.optimization_barrier((grad_attn, early))
     early = lax.psum_scatter(early, "shard", scatter_dimension=0, tiled=True)
+    expert_columns = local * 3 * F
+    expert_rows = lax.all_gather(early[:, :expert_columns], "rep", axis=0, tiled=False)
+    early = rep_sum(early[:, expert_columns:])
+    attn_rows, router_rows = early[:, :Q_WIDTH], early[:, Q_WIDTH : Q_WIDTH + EXPERTS]
+    ffn_gain_rows = early[:, Q_WIDTH + EXPERTS]
 
     delta = jnp.sum(grad_attn.astype(F32) * attn, axis=1).reshape(KEY_VALUE_HEADS, PER_KEY, count)
-    grad_query, grad_kv = [], []
-    for n in range(pieces):
-        dq, dkv, own = attn_backward(
-            where, query[n], prompt_kv[n], own_kv[n], grad_attn[q_piece[n]], lse[n], delta[kv_piece[n]]
-        )
-        dkv = lax.psum_scatter(dkv, "shard", scatter_dimension=0, tiled=False, axis_index_groups=groups)
-        grad_query.append(dq)
-        grad_kv.append(jnp.concatenate([dkv.astype(F32), own], axis=-1))
-    grad_query = jnp.concatenate(grad_query, axis=0)
-    grad_kv = jnp.concatenate(grad_kv, axis=1)
+    grad_query, grad_prompt_kv, grad_own_kv = attn_backward(
+        where, query, prompt_kv, own_kv, grad_attn, lse, delta
+    )
+
+    def turn_back(values, turn):
+        spun = rotate(values, turn[0], -turn[1])
+        return spun.astype(BF16).reshape(-1, values.shape[-1])
+
+    grad_query = turn_back(grad_query, own_turn)
+    grad_prompt_kv = jnp.concatenate(
+        [
+            turn_back(grad_prompt_kv[0].astype(F32), prompt_turn),
+            grad_prompt_kv[1].reshape(KV_WIDTH, GROUP_SIZE * prompt),
+        ],
+        axis=0,
+    )
+    grad_own_kv = jnp.concatenate(
+        [turn_back(grad_own_kv[0], continued_turn), grad_own_kv[1].astype(BF16).reshape(KV_WIDTH, -1)], axis=0
+    )
+    late = jnp.concatenate(
+        [
+            dot(normed_attn, grad_query, (0, 1)).astype(BF16),
+            (dot(normed_prompt, grad_prompt_kv, (0, 1)) + dot(normed_attn[prompt:], grad_own_kv, (0, 1))).astype(BF16),
+        ],
+        axis=1,
+    )
+    late = lax.psum_scatter(late, "shard", scatter_dimension=0, tiled=True)
+    late, grad_prompt_kv = lax.optimization_barrier((late, grad_prompt_kv))
+    qkv_rows = rep_sum(late)
+    attn_gain_rows = jnp.sum(
+        qkv_rows.astype(F32) * query_key_value_weight.astype(F32), axis=1
+    ) / attn_gain.astype(F32)
+
+    grad_prompt_kv = lax.psum_scatter(
+        grad_prompt_kv, "shard", scatter_dimension=1, tiled=True, axis_index_groups=groups
+    )
     grad_projected = jnp.concatenate(
-        [rotate(grad_query, cosine, -sine), rotate(grad_kv[0], cosine, -sine), grad_kv[1]], axis=0
-    ).astype(BF16).reshape(Q_WIDTH + 2 * KV_WIDTH, count)
-    grad_qkv_w = dot(normed_attn, grad_projected, (0, 1))
+        [grad_query, jnp.concatenate([grad_prompt_kv, grad_own_kv], axis=1)], axis=0
+    )
     grad_normed_attn = dot(grad_projected, qkv_full, (0, 1))
-    grad_x_norm, grad_attn_gain = rms_backward(x_in, attn_scale, attn_gain_full, grad_normed_attn)
+    grad_x_norm, _ = rms_backward(x_in, attn_scale, attn_gain_full, grad_normed_attn)
     grad_input = grad_mid + grad_x_norm
 
-    late = jnp.concatenate([grad_qkv_w, grad_attn_gain[:, None]], axis=1).astype(BF16)
-    late = jnp.pad(late, ((0, 0), (0, -late.shape[1] % LANES)))
-    late = lax.psum_scatter(late, "shard", scatter_dimension=0, tiled=True)
-    both = lax.psum(jnp.concatenate([early, late], axis=1), "rep")
-    early, late = both[:, : early.shape[1]], both[:, early.shape[1] :]
-    qkv_rows, attn_gain_rows = late[:, : Q_WIDTH + 2 * KV_WIDTH], late[:, Q_WIDTH + 2 * KV_WIDTH]
-    attn_rows, ffn_gain_rows = early[:, :Q_WIDTH], early[:, Q_WIDTH]
-    router_rows = early[:, Q_WIDTH + 1 : Q_WIDTH + 1 + EXPERTS]
+    in_columns = local * 2 * F
     if flat_path:
         size = outer_mom.shape[-1]
 
         def lead(first, second, rest):
-            return jnp.concatenate([first[None], second[None], rest.reshape(-1, LANES)], axis=0).astype(F32)
+            parts = [first[None].astype(F32), second[None].astype(F32), rest.reshape(-1, LANES).astype(F32)]
+            return jnp.concatenate(parts, axis=0)
+
+        def whole(values):
+            return values, values.shape[-1], 0
 
         weight_flat, _ = flatten(
-            size, lead(attn_gain, ffn_gain, w_router), query_key_value_weight, w_attn_out, w_in, w_out
+            size,
+            lead(attn_gain, ffn_gain, w_router),
+            [whole(query_key_value_weight), whole(w_attn_out), whole(w_in), whole(w_out)],
         )
         total_grad, square = flatten(
-            size, lead(attn_gain_rows, ffn_gain_rows, router_rows), qkv_rows, attn_rows, expert_in, expert_out
-        )
-        norm_square = lax.psum(square.reshape(()), "shard")
+            size,
+            lead(attn_gain_rows, ffn_gain_rows, router_rows),
+            [
+                whole(qkv_rows),
+                whole(attn_rows),
+                (expert_rows, in_columns, 0),
+                (expert_rows, expert_columns - in_columns, in_columns // (expert_columns - in_columns)),
+            ],
+        )
+        grad_norm, step_sum = summed_step(square, total_grad, adam_first, adam_second, weight_flat)
+        new_first, new_second, new_mom, weight_update = update(
+            reps, grad_norm, total_grad, adam_first, adam_second, step_sum, outer_mom
+        )
+        grad_norm = grad_norm.reshape(())
     else:
         weight_flat = jnp.concatenate(
             [
@@ -910,23 +1512,19 @@
                     attn_rows,
                     ffn_gain_rows,
                     router_rows,
-                    expert_in.transpose(1, 0, 2),
-                    expert_out.transpose(1, 0, 2),
+                    expert_rows[:, :, :in_columns].transpose(1, 0, 2),
+                    expert_rows[:, :, in_columns:].transpose(1, 0, 2),
                 )
             ]
         )
-        norm_square = lax.psum(jnp.sum(total_grad * total_grad), "shard")
-    grad_norm = jnp.sqrt(norm_square)
-    clip_scale = CLIP_NORM / jnp.maximum(grad_norm, CLIP_NORM)
-    if flat_path:
-        new_first, new_second, step = adam(
-            clip_scale.reshape(1), total_grad, adam_first, adam_second, weight_flat
-        )
-        new_mom, weight_update = outer(reps, lax.psum(step, "rep"), outer_mom)
-    else:
-        new_first, new_second, step = optimizer_math(
-            total_grad, adam_first.reshape(-1), adam_second.reshape(-1), weight_flat, clip_scale
-        )
+        grad_norm = jnp.sqrt(lax.psum(jnp.sum(total_grad * total_grad), "shard"))
+        new_first, new_second = moments(
+            total_grad,
+            adam_first.reshape(-1),
+            adam_second.reshape(-1),
+            CLIP_NORM / jnp.maximum(grad_norm, CLIP_NORM),
+        )
+        step = inner_step(new_first, new_second, weight_flat)
         pseudo = -(lax.psum(step.astype(BF16), "rep").astype(F32) / reps)
         new_mom = OUTER_MOMENTUM * outer_mom.reshape(-1) + pseudo
         weight_update = -OUTER_RATE * (pseudo + OUTER_MOMENTUM * new_mom)

time: 1860 us -> 1630 us (0.88)
  waiting for transfers between devices: 1090 us -> 781 us
  Pallas kernels: 463 us -> 545 us
  blocking collectives: 70.7 us -> 0 us
  matrix products: 116 us -> 145 us
  other arithmetic: 36.5 us -> 58.3 us
    all_gather x9 -> x2, waiting for transfers between devices: 413 us -> 111 us  [the longest x1 82.8 us: per_device(): w_both = gather(w_both)]
    reduce_scatter x4 -> x1, waiting for transfers between devices: 325 us -> 126 us  [per_device(): lax.psum_scatter(grad_prompt_kv, 'shard', scatter_dimension=1, tiled=True...]
    pallas_call x2 -> x3, Pallas kernels: 67.3 us -> 246 us  [the longest x1 112 us: start_gather(): pl.pallas_call(start_kernel, in_specs=[anywhere] * 3, out_specs=[anywhere...]
    reduce_scatter x1, waiting for transfers between devices: 70.8 us -> 244 us  [per_device(): early = lax.psum_scatter(early, 'shard', scatter_dimension=0, tiled=True)]
    reduce_scatter x1, waiting for transfers between devices: 94.9 us -> 265 us  [per_device(): late = lax.psum_scatter(late, 'shard', scatter_dimension=0, tiled=True)]
    psum x2 -> x0, waiting for transfers between devices: 156 us -> none  [the longest x1 121 us: per_device(): new_mom, weight_update = outer(reps, lax.psum(step, 'rep'), outer_mom)]
    pallas_call x2 -> x1, Pallas kernels: 117 us -> 53.1 us  [attn_backward(): pl.pallas_call(attn_backward_kernel, grid=(query.shape[0] // PER_KEY,), i...]
    all_gather x2 -> x0, blocking collectives: 48.7 us -> none  [the longest x1 26.4 us: per_device(): router_full = gather(w_router)]
  transfers between devices with their start and end apart: 18 -> 11, of which waited for: 18 -> 8; matrix products, arithmetic and copies ran while one was open for 9% -> 10% of each run, Pallas kernels for 8% -> 3%
where the time goes in v2:
time: 1630 us; the launch traced here: 1620 us
  waiting for transfers between devices  781 us (48%)
  Pallas kernels  545 us (33%)
  matrix products  145 us (9%)
  local copies, waits for them, and re-layouts  68.7 us (4%)
  other arithmetic  58.3 us (4%)
  between operations  17.4 us (1%)
    reduce_scatter x1, waiting for transfers between devices, per_device(): late = lax.psum_scatter(late, 'shard', scatter_dimension=0, tiled=True)  265 us
    reduce_scatter x1, waiting for transfers between devices, per_device(): early = lax.psum_scatter(early, 'shard', scatter_dimension=0, tiled=True)  244 us
    pallas_call x1, Pallas kernels, experts(): pl.pallas_call(experts_kernel, grid=(len(ORDER),), in_specs=[anywhere, an...  178 us
    dot_general x17, matrix products, dot(): lax.dot_general(left, right, ((dims[:1], dims[1:]), ((), ())), preferred_...  145 us
    reduce_scatter x1, waiting for transfers between devices, per_device(): lax.psum_scatter(grad_prompt_kv, 'shard', scatter_dimension=1, tiled=True...  126 us
    pallas_call x1, Pallas kernels, start_gather(): pl.pallas_call(start_kernel, in_specs=[anywhere] * 3, out_specs=[anywhere...  112 us
    pallas_call x1, Pallas kernels, summed_step(): pl.pallas_call(step_kernel, in_specs=[pl.BlockSpec(memory_space=pltpu.VME...  90.5 us
    all_gather x1, waiting for transfers between devices, per_device(): w_both = gather(w_both)  82.8 us
  transfers between devices with their start and end apart: 11, of which 8 were waited for; matrix products, arithmetic and copies ran while one was open for 10% of the time, Pallas kernels for 3%

profile of v2, /device:TPU:0, one launch (start us, length us, event | category | flops | bytes accessed | tf_op | source)
XLA Modules:
  0.0 1620.3 jit_solution(6027047894859535523)
XLA Ops:
  9.6 1.2 concatenate.82
  11.8 1.3 constant_dynamic-slice_fusion.1
  14.2 1.3 pad_maximum_fusion.5
  15.4 111.9 %start_gather.1 = (bf16[8,512,1024]{2,1,0:T(8,128)(2,1)}, bf16[8,4,32,3200]{3,2,1,0:T(8,128)(2,1)}, bf16[4,1024,1024]{2,1,0:T(8,128)(2,1)}) custom-call(bf16[1024,1024]{1,0:T(8,128)(2,1)} %bitcast.129, bf16[128,3200]{1,0:T(8,128)(2,1)} %pad.12.w_ref, bf16[1024,1024]{1,0:T(8,128)(2,1)} %bitcast.136), custom_call_target="tpu_custom_call" | custom-call | bytes 67108864 | tf_op jit(solution)/shard_map/start_gather/pallas_call | solution.py:554
  129.3 3.2 slice_bitcast_fusion.1
  132.6 3.9 copy.76
  138.7 2.5 fusion.38
  141.4 2.1 convolution_convert_fusion.3
  143.7 1.2 fusion.58
  144.9 2.5 fusion.22
  148.4 1.7 fusion
  150.1 2.7 fusion.48
  152.8 9.3 fusion.40
  162.1 4.7 fusion.17
  166.9 7.0 convolution_convert_fusion
  173.9 3.7 pad_maximum_fusion.kv_ref
  177.6 34.2 %attn_forward.1 = (f32[16,64,1024]{2,1,0:T(8,128)}, f32[8,2,1024]{2,1,0:T(2,128)S(1)}) custom-call(s32[2]{0:T(128)S(1)} %pad_add_fusion.where_ref, bf16[16,64,1024]{2,1,0:T(8,128)(2,1)S(1)} %pad_maximum_fusion.4.q_ref, bf16[2,8,64,4096]{3,2,1,0:T(8,128)(2,1)} %pad_maximum_fusion.kv_ref, bf16[2,8,64,512]{3,2,1,0:T(8,128)(2,1)S(1)} %pad_maximum_fusion.6.own_ref), custom_call_target="tpu_custom_call" | custom-call | flops 17179869184 | bytes 16777216 | tf_op jit(solution)/shard_map/attn_forward/pallas_call | solution.py:138
  211.8 2.6 convert_element_type.310
  214.5 4.8 multiply_reduce_fusion.3
  219.8 1.8 fusion.59
  222.4 82.8 %all-gather.4.cloned.1.call-done.w_ref = bf16[1024,6144]{1,0:T(8,128)(2,1)} async-done(((bf16[128,6144]{1,0:T(8,128)(2,1)}), bf16[1024,6144]{1,0:T(8,128)(2,1)}) %all-gather.4.cloned.1.call-update) | async-done | bytes 12582928 | tf_op jit(solution)/shard_map/all_gather | solution.py:1330
  305.3 178.3 %experts.1 = (bf16[4,1024,1024]{2,1,0:T(8,128)(2,1)}, bf16[1024,1024]{1,0:T(8,128)(2,1)}, bf16[1024,1024]{1,0:T(8,128)(2,1)}, bf16[1024,1024]{1,0:T(8,128)(2,1)}...) custom-call(bf16[1024,1024]{1,0:T(8,128)(2,1)} %copy-done.15, ...), custom_call_target="tpu_custom_call" | custom-call | flops 103079215104 | bytes 83886080 | tf_op jit(solution)/shard_map/experts/pallas_call | solution.py:824
  484.6 2.8 slice.140
  489.3 5.1 multiply_reduce_fusion.1
  494.4 43.3 %bitcast_convert_fusion = bf16[1024,4096]{1,0:T(8,128)(2,1)} fusion(bf16[4,1024,1024]{2,1,0:T(8,128)(2,1)} %get-tuple-element.50, bf16[4,1024,4096]{2,1,0:T(8,128)(2,1)} %get-tuple-element.51), kind=kOutput, calls=%fused_computation.5 | convolution fusion | flops 34363932672 | bytes 50331648 | tf_op jit(solution)/shard_map/dot_general | solution.py:43
  537.7 2.0 convert_add_fusion
  539.7 3.4 copy-done.13
  543.1 1.6 fusion.20
  546.6 24.0 %bitcast_convert_fusion.1 = bf16[1024,2048]{1,0:T(8,128)(2,1)} fusion(bf16[4,1024,1024]{2,1,0:T(8,128)(2,1)} %get-tuple-element.43.top_hbm, bf16[4,1024,2048]{2,1,0:T(8,128)(2,1)} %get-tuple-element.52), kind=kOutput, calls=%fused_computation.8 | convolution fusion | flops 17181966336 | bytes 29360128 | tf_op jit(solution)/shard_map/dot_general | solution.py:43
  570.6 22.1 %collective-permute-done.1 = bf16[1024,1024]{1,0:T(8,128)(2,1)S(1)} collective-permute-done((bf16[1024,1024]{1,0:T(8,128)(2,1)}, bf16[1024,1024]{1,0:T(8,128)(2,1)S(1)}, u32[]{:S(2)}, u32[]{:S(2)}) %collective-permute-start.1) | collective-permute-done | bytes 2097184 | tf_op jit(solution)/shard_map/ppermute | solution.py:1386
  592.7 3.3 subtract_add_fusion
  596.1 2.4 convolution_convert_fusion.1
  598.5 5.3 convolution_convert_fusion.2
  603.8 21.5 %concatenate.92 = bf16[1024,7185]{1,0:T(8,128)(2,1)} concatenate(bf16[1024,4096]{1,0:T(8,128)(2,1)} %bitcast_convert_fusion, bf16[1024,2048]{1,0:T(8,128)(2,1)} %bitcast_convert_fusion.1, bf16[1024,1024]{1,0:T(8,128)(2,1)S(1)} %convolution_convert_fusion.1, bf16[1024,16]{1,0:T(8,128)(2,1)S(1)} %copy.82, bf16[1024,1]{1,0:T(8,128)(2,1)S(1)} %convert_element_type.369), dimensions={1} | concatenate | bytes 29429760 | tf_op jit(solution)/shard_map/concatenate | solution.py:1405
  625.3 11.1 pad.14
  636.4 3.0 multiply_reduce_fusion
  640.0 53.1 %attn_backward.1 = (f32[16,64,1024]{2,1,0:T(8,128)}, bf16[2,8,64,4096]{3,2,1,0:T(8,128)(2,1)}, f32[2,8,64,512]{3,2,1,0:T(8,128)}) custom-call(s32[2]{0:T(128)} %copy-done.5, bf16[16,64,1024]{2,1,0:T(8,128)(2,1)} %copy-done.2, bf16[2,8,64,4096]{3,2,1,0:T(8,128)(2,1)} %pad_maximum_fusion.kv_ref, bf16[2,8,64,512]{3,2,1,0:T(8,128)(2,1)} %copy-done.3, ...), custom_call_target="tpu_custom_call" | custom-call | flops 42949672960 | bytes 33554432 | tf_op jit(solution)/shard_map/attn_backward/pallas_call | solution.py:255
  693.1 1.3 slice_bitcast_fusion.2
  694.4 1.3 slice.277
  695.8 6.0 bitcast_convert_fusion.2
  703.7 4.0 fusion.26
  707.7 1.3 subtract_convert_fusion
  709.1 2.5 pad_maximum_fusion.2
  711.6 17.6 %fusion.63 = f32[1024,1024]{1,0:T(8,128)} fusion(bf16[512,4096]{1,0:T(8,128)(2,1)} %bitcast.132, bf16[512,4096]{1,0:T(8,128)(2,1)} %bitcast.134, bf16[4096,1024]{1,0:T(8,128)(2,1)} %bitcast.137, f32[1024]{0:T(1024)S(1)} %bitcast.179, f32[4096]{0:T(1024)S(1)} %copy-done.51), kind=kOutput, calls=%fused_computation.151 | convolution fusion | flops 8623489024 | bytes 20992000 | tf_op jit(solution)/shard_map/dot_general | solution.py:43
  730.3 3.6 add_convert_fusion
  733.9 2.5 pad_maximum_fusion.3
  737.2 8.0 pad_maximum_fusion.1
  745.2 265.5 %reduce-scatter.4.cloned.1.call-done = bf16[128,2048]{1,0:T(8,128)(2,1)} async-done(((bf16[1024,2048]{1,0:T(8,128)(2,1)}), bf16[128,2048]{1,0:T(8,128)(2,1)}) %reduce-scatter.4.cloned.1.call-update) | async-done | bytes 524304 | tf_op jit(solution)/shard_map/reduce_scatter | solution.py:1451
  1010.8 243.9 %reduce-scatter.8.cloned.1.call-done = bf16[128,7296]{1,0:T(8,128)(2,1)} async-done(((bf16[1024,7296]{1,0:T(8,128)(2,1)}), bf16[128,7296]{1,0:T(8,128)(2,1)}) %reduce-scatter.8.cloned.1.call-update) | async-done | bytes 1867792 | tf_op jit(solution)/shard_map/reduce_scatter | solution.py:1417
  1254.7 2.7 slice.189
  1257.5 1.9 collective-permute-done.2
  1259.4 1.2 add_convert_fusion.5
  1260.6 1.5 collective-permute-start.3
  1262.4 16.9 %flatten.3 = (f32[1,3541248]{1,0:T(1,128)}, f32[1,1]{1,0:T(1,128)}) custom-call(f32[18,128]{1,0:T(8,128)S(1)} %pad_maximum_fusion.9.lead_ref, bf16[128,2048]{1,0:T(8,128)(2,1)S(1)} %copy-done, bf16[128,1024]{1,0:T(8,128)(2,1)S(1)} %copy-done.4, bf16[128,16384]{1,0:T(8,128)(2,1)} %refs_2_.1, bf16[128,8192]{1,0:T(8,128)(2,1)S(1)} %copy-done.1), custom_call_target="tpu_custom_call" | custom-call | tf_op jit(solution)/shard_map/flatten/pallas_call | solution.py:940
  1279.3 1.3 multiply_reduce_fusion.4
  1281.8 125.5 %reduce-scatter.6.cloned.1.call-done = bf16[1024,512]{1,0:T(8,128)(2,1)} async-done(((bf16[1024,4096]{1,0:T(8,128)(2,1)}), bf16[1024,512]{1,0:T(8,128)(2,1)}) %reduce-scatter.6.cloned.1.call-update) | async-done | bytes 1048592 | tf_op jit(solution)/shard_map/reduce_scatter | solution.py:1458
  1407.3 8.9 fusion.4
  1417.2 1.6 collective-permute-start.5
  1418.8 3.0 add_bitcast_fusion
  1421.8 11.1 collective-permute-done.5
  1433.3 27.8 %all-gather.6.cloned.1.call-done = bf16[512,6144]{1,0:T(8,128)(2,1)} async-done(((bf16[128,6144]{1,0:T(8,128)(2,1)}), bf16[512,6144]{1,0:T(8,128)(2,1)}) %all-gather.6.cloned.1.call-update) | async-done | bytes 6291472 | tf_op jit(solution)/shard_map/all_gather | solution.py:1419
  1461.1 17.0 %flatten.2 = (f32[1,3541248]{1,0:T(1,128)}, f32[1,1]{1,0:T(1,128)}) custom-call(f32[18,128]{1,0:T(8,128)S(1)} %pad_maximum_fusion.8.lead_ref, bf16[128,2048]{1,0:T(8,128)(2,1)S(1)} %get-tuple-element.73.refs_0_, bf16[128,1024]{1,0:T(8,128)(2,1)S(1)} %slice.188.refs_1_, bf16[4,128,6144]{2,1,0:T(8,128)(2,1)} %bitcast.130, bf16[4,128,6144]{2,1,0:T(8,128)(2,1)} %bitcast.131), custom_call_target="tpu_custom_call" | custom-call | tf_op jit(solution)/shard_map/flatten/pallas_call | solution.py:940
  1478.1 90.5 %summed_step.1 = (f32[1,1]{1,0:T(1,128)}, bf16[2,13840,128]{2,1,0:T(8,128)(2,1)}) custom-call(f32[1,1]{1,0:T(1,128)} %get-tuple-element.62.square_ref, f32[1,3541248]{1,0:T(1,128)} %get-tuple-element.122.g_ref.g, f32[1,1,3541248]{2,1,0:T(1,128)} %f.1, f32[1,1,3541248]{2,1,0:T(1,128)} %s.1, f32[1,3541248]{1,0:T(1,128)} %get-tuple-element.63.w_ref), custom_call_target="tpu_custom_call" | custom-call | bytes 67108864 | tf_op jit(solution)/shard_map/summed_step/pallas_call | solution.py:1151
  1568.6 43.2 %update.1 = (f32[1,1,3541248]{2,1,0:T(1,128)}, f32[1,1,3541248]{2,1,0:T(1,128)}, f32[1,3541248]{1,0:T(1,128)}, f32[1,3541248]{1,0:T(1,128)}) custom-call(f32[1,1]{1,0:T(1,128)} %get-tuple-element.64.norm_ref, f32[1,3541248]{1,0:T(1,128)} %get-tuple-element.122.g_ref.g, f32[1,1,3541248]{2,1,0:T(1,128)} %f.1, f32[1,1,3541248]{2,1,0:T(1,128)} %s.1, ...), custom_call_target="tpu_custom_call" | custom-call | bytes 125829120 | tf_op jit(solution)/shard_map/update/pallas_call | solution.py:1232
  (190 shorter events, 22.5 us)
Async XLA Ops:
  7.2 298.1 %all-gather.4.cloned.1.call-start = ((), (), s32[]{:S(2)}) async-start(), calls=%async_computation.3 | async-start | bytes 14155776 | tf_op jit(solution)/shard_map/all_gather | solution.py:1330
  127.4 883.3 %reduce-scatter.4.cloned.1.call-start = ((), (), s32[]{:S(2)}) async-start(), calls=%async_computation.4 | async-start | bytes 4718592 | tf_op jit(solution)/shard_map/reduce_scatter | solution.py:1451
  129.3 7.3 copy-start.10
  136.6 41.0 %copy-start.5 = (s32[2]{0:T(128)}, s32[2]{0:T(128)S(1)}, u32[]{:S(2)}) copy-start(s32[2]{0:T(128)S(1)} %pad_add_fusion.where_ref) | copy-start | bytes 28
  137.1 7.7 copy-start.46
  137.1 29.7 %copy-start.44 = (f32[1024,1]{0,1:T(1,128)}, f32[1024,1]{0,1:T(1,128)S(1)}, u32[]{:S(2)}) copy-start(f32[1024,1]{0,1:T(1,128)S(1)} %get-tuple-element.91) | copy-start | bytes 12292
  138.1 3.1 copy-start.39
  138.7 4.8 copy-start.24
  141.2 3.6 copy-start.32
  143.6 34.0 %copy-start.3 = (bf16[2,8,64,512]{3,2,1,0:T(8,128)(2,1)}, bf16[2,8,64,512]{3,2,1,0:T(8,128)(2,1)S(1)}, u32[]{:S(2)}) copy-start(bf16[2,8,64,512]{3,2,1,0:T(8,128)(2,1)S(1)} %pad_maximum_fusion.6.own_ref) | copy-start | bytes 3145732
  144.8 2.5 copy-start.37
  144.9 3.5 slice-start
  144.9 3.5 slice-start.1
  148.4 29.2 %copy-start.2 = (bf16[16,64,1024]{2,1,0:T(8,128)(2,1)}, bf16[16,64,1024]{2,1,0:T(8,128)(2,1)S(1)}, u32[]{:S(2)}) copy-start(bf16[16,64,1024]{2,1,0:T(8,128)(2,1)S(1)} %pad_maximum_fusion.4.q_ref) | copy-start | bytes 6291460
  150.1 16.8 %copy-start.50 = (f32[4096]{0:T(1024)}, f32[4096]{0:T(1024)S(1)}, u32[]{:S(2)}) copy-start(f32[4096]{0:T(1024)S(1)} %add_rsqrt_fusion) | copy-start | bytes 49156
  152.8 9.3 copy-start.21
  211.8 7.5 copy-start.6
  211.8 2.6 copy-start.48
  214.4 4.9 copy-start.26
  219.8 85.5 %copy-start.15 = (bf16[1024,1024]{1,0:T(8,128)(2,1)}, bf16[1024,1024]{1,0:T(8,128)(2,1)S(1)}, u32[]{:S(2)}) copy-start(bf16[1024,1024]{1,0:T(8,128)(2,1)S(1)} %multiply_convert_fusion.x_hbm) | copy-start | bytes 6291460
  484.6 3.5 copy-start.8
  484.6 4.1 copy-start.33
  484.6 4.7 copy-start.34
  487.4 50.3 %collective-permute-start = (bf16[2,1024,1024]{2,1,0:T(8,128)(2,1)S(1)}, bf16[2,1024,1024]{2,1,0:T(8,128)(2,1)S(1)}, u32[]{:S(2)}, u32[]{:S(2)}) collective-permute-start(bf16[2,1024,1024]{2,1,0:T(8,128)(2,1)S(1)} %slice.140), channel_id=1, source_target_pairs={{0,1},{1,0},{2,3},{3,2},{4,5},{5,4},{6,7},{7,6},{8,9},{9,8},{10,11... | collective-permute-start | bytes 12582920 | tf_op jit(solution)/shard_map/ppermute | solution.py:1385
  489.3 48.4 %slice-start.2 = ((s8[8388608]{0:T(1024)(128)(4,1)}), s8[4194304]{0:T(1024)(128)(4,1)S(1)}, s32[]{:S(2)}) async-start(s8[8388608]{0:T(1024)(128)(4,1)} %bitcast.143), calls=%async_computation.10 | async-start | bytes 8388608
  494.4 43.3 %slice-start.3 = ((s8[8388608]{0:T(1024)(128)(4,1)}), s8[4194304]{0:T(1024)(128)(4,1)S(1)}, s32[]{:S(2)}) async-start(s8[8388608]{0:T(1024)(128)(4,1)} %bitcast.143), calls=%async_computation.11 | async-start | bytes 8388608
  539.7 3.4 copy-start.13
  543.1 2.7 copy-start.16
  544.8 47.9 %collective-permute-start.1 = (bf16[1024,1024]{1,0:T(8,128)(2,1)}, bf16[1024,1024]{1,0:T(8,128)(2,1)S(1)}, u32[]{:S(2)}, u32[]{:S(2)}) collective-permute-start(bf16[1024,1024]{1,0:T(8,128)(2,1)} %fusion.20), channel_id=1, source_target_pairs={{0,2},{1,3},{2,0},{3,1},{4,6},{5,7},{6,4},{7,5},{8,10},{9,11},{10,... | collective-permute-start | bytes 6291464 | tf_op jit(solution)/shard_map/ppermute | solution.py:1386
  546.6 46.1 %copy-start.9 = (f32[1024,1024]{1,0:T(8,128)S(1)}, f32[1024,1024]{1,0:T(8,128)}, u32[]{:S(2)}) copy-start(f32[1024,1024]{1,0:T(8,128)} %copy-done.7) | copy-start | bytes 12582916
  546.6 46.1 %copy-start.14 = (f32[2,1024,1024]{2,1,0:T(8,128)S(1)}, f32[2,1024,1024]{2,1,0:T(8,128)}, u32[]{:S(2)}) copy-start(f32[2,1024,1024]{2,1,0:T(8,128)} %copy-done.13) | copy-start | bytes 25165828
  546.6 46.1 %copy-start.19 = (f32[1024,1024]{1,0:T(8,128)S(1)}, f32[1024,1024]{1,0:T(8,128)}, u32[]{:S(2)}) copy-start(f32[1024,1024]{1,0:T(8,128)} %get-tuple-element.105) | copy-start | bytes 12582916
  546.6 46.1 %copy-start.20 = (bf16[1,1,1024,1024]{3,2,1,0:T(8,128)(2,1)S(1)}, bf16[1,1,1024,1024]{3,2,1,0:T(8,128)(2,1)}, u32[]{:S(2)}) copy-start(bf16[1,1,1024,1024]{3,2,1,0:T(8,128)(2,1)} %param.15) | copy-start | bytes 6291460
  592.7 3.4 copy-start.27
  596.0 2.4 copy-start.17
  625.3 11.1 copy-start.28
  695.7 33.7 %copy-start.29 = (bf16[1,8,64,512]{3,2,1,0:T(8,128)(2,1)}, bf16[1,8,64,512]{3,2,1,0:T(8,128)(2,1)S(1)}, u32[]{:S(2)}) copy-start(bf16[1,8,64,512]{3,2,1,0:T(8,128)(2,1)S(1)} %slice.277) | copy-start | bytes 1572868
  695.8 6.4 copy-start.23
  695.8 6.3 copy-start.38
  695.8 6.3 copy-start.42
  703.1 4.7 copy-start.31
  703.7 4.0 copy-start.22
  703.7 4.0 copy-start.36
  709.1 2.5 copy-start.51
  711.6 17.6 %copy-start.40 = (f32[32,512]{1,0:T(8,128)S(1)}, f32[32,512]{1,0:T(8,128)}, u32[]{:S(2)}) copy-start(f32[32,512]{1,0:T(8,128)} %copy-done.39) | copy-start | bytes 196612
  711.6 17.6 %copy-start.43 = (f32[32,512]{1,0:T(8,128)S(1)}, f32[32,512]{1,0:T(8,128)}, u32[]{:S(2)}) copy-start(f32[32,512]{1,0:T(8,128)} %get-tuple-element.92) | copy-start | bytes 196612
  711.6 18.7 %copy-start.25 = (bf16[512,1024]{1,0:T(8,128)(2,1)S(1)}, bf16[512,1024]{1,0:T(8,128)(2,1)}, u32[]{:S(2)}) copy-start(bf16[512,1024]{1,0:T(8,128)(2,1)} %copy-done.24) | copy-start | bytes 3145732
  730.3 3.7 copy-start.35
  736.4 518.3 %reduce-scatter.8.cloned.1.call-start = ((), (), s32[]{:S(2)}) async-start(), calls=%async_computation.6 | async-start | bytes 16809984 | tf_op jit(solution)/shard_map/reduce_scatter | solution.py:1417
  737.1 670.1 %reduce-scatter.6.cloned.1.call-start = ((), (), s32[]{:S(2)}) async-start(), calls=%async_computation.5 | async-start | bytes 9437184 | tf_op jit(solution)/shard_map/reduce_scatter | solution.py:1458
  1010.6 246.8 %copy-start.41 = (bf16[128,2048]{1,0:T(8,128)(2,1)S(1)}, bf16[128,2048]{1,0:T(8,128)(2,1)}, u32[]{:S(2)}) copy-start(bf16[128,2048]{1,0:T(8,128)(2,1)} %reduce-scatter.4.cloned.1.call-done) | copy-start | bytes 1572868
  1010.7 251.5 %copy-start.49 = (bf16[128,16]{0,1:T(8,128)(2,1)S(1)}, bf16[128,16]{0,1:T(8,128)(2,1)}, u32[]{:S(2)}) copy-start(bf16[128,16]{0,1:T(8,128)(2,1)} %param.22) | copy-start | bytes 12292
  1010.7 251.7 %copy-start.52 = (bf16[128]{0:T(256)(128)(2,1)S(1)}, bf16[128]{0:T(256)(128)(2,1)}, u32[]{:S(2)}) copy-start(bf16[128]{0:T(256)(128)(2,1)} %param.21) | copy-start | bytes 772
  1010.7 251.6 %copy-start.53 = (bf16[128]{0:T(256)(128)(2,1)S(1)}, bf16[128]{0:T(256)(128)(2,1)}, u32[]{:S(2)}) copy-start(bf16[128]{0:T(256)(128)(2,1)} %param.18) | copy-start | bytes 772
  1010.7 251.7 %copy-start = (bf16[128,2048]{1,0:T(8,128)(2,1)S(1)}, bf16[128,2048]{1,0:T(8,128)(2,1)}, u32[]{:S(2)}) copy-start(bf16[128,2048]{1,0:T(8,128)(2,1)} %refs_0_.1) | copy-start | bytes 1572868
  1010.7 251.7 %copy-start.1 = (bf16[128,8192]{1,0:T(8,128)(2,1)S(1)}, bf16[128,8192]{1,0:T(8,128)(2,1)}, u32[]{:S(2)}) copy-start(bf16[128,8192]{1,0:T(8,128)(2,1)} %refs_3_.1) | copy-start | bytes 6291460
  1010.7 251.7 %copy-start.4 = (bf16[128,1024]{1,0:T(8,128)(2,1)S(1)}, bf16[128,1024]{1,0:T(8,128)(2,1)}, u32[]{:S(2)}) copy-start(bf16[128,1024]{1,0:T(8,128)(2,1)} %refs_1_.1) | copy-start | bytes 786436
  1010.7 450.3 %all-gather.6.cloned.1.call-start = ((), (), s32[]{:S(2)}) async-start(), calls=%async_computation.7 | async-start | bytes 7864320 | tf_op jit(solution)/shard_map/all_gather | solution.py:1419
  1257.4 2.0 collective-permute-start.2
  1260.6 18.7 %collective-permute-start.3 = (bf16[128,2048]{1,0:T(8,128)(2,1)S(1)}, bf16[128,2048]{1,0:T(8,128)(2,1)}, u32[]{:S(2)}, u32[]{:S(2)}) collective-permute-start(bf16[128,2048]{1,0:T(8,128)(2,1)S(1)} %add_convert_fusion.5), channel_id=1, source_target_pairs={{0,2},{1,3},{2,0},{3,1},{4,6},{5,7},{6,4},{7,5},{8,10},{9,11},{10,... | collective-permute-start | bytes 1572872 | tf_op jit(solution)/shard_map/ppermute | solution.py:1391
  1281.7 137.1 %copy-start.12 = (bf16[1,1,1024,1024]{3,2,1,0:T(8,128)(2,1)S(1)}, bf16[1,1,1024,1024]{3,2,1,0:T(8,128)(2,1)}, u32[]{:S(2)}) copy-start(bf16[1,1,1024,1024]{3,2,1,0:T(8,128)(2,1)} %param.14) | copy-start | bytes 6291460
  1281.7 134.5 %collective-permute-start.4 = (bf16[128,1152]{1,0:T(8,128)(2,1)S(1)}, bf16[128,1152]{1,0:T(8,128)(2,1)S(1)}, u32[]{:S(2)}, u32[]{:S(2)}) collective-permute-start(bf16[128,1152]{1,0:T(8,128)(2,1)S(1)} %slice.185), channel_id=1, source_target_pairs={{0,1},{1,0},{2,3},{3,2},{4,5},{5,4},{6,7},{7,6},{8,9},{9,8},{10,11... | collective-permute-start | bytes 884744 | tf_op jit(solution)/shard_map/ppermute | solution.py:1391
  1407.3 11.5 copy-start.18
  1417.2 15.7 collective-permute-start.5
  (5 other events, 7.9 us)
Sparse Core Ops, SparseCore 0:
  127.5 177.7 all-gather.3
  736.5 274.0 reduce-scatter.3
  1014.7 239.9 reduce-scatter.7
  1258.8 148.4 reduce-scatter.5
  1409.4 51.6 all-gather.5

commit v3 on v2

--- a/solution.py
+++ b/solution.py
@@ -580,7 +580,7 @@
     )(x, small, top)
 
 
-ORDER = ((0, 0), (0, 1), (3, 0), (2, 0), (3, 1), (2, 1), (1, 0), (1, 1))
+ORDER = ((0, 0), (0, 1), (1, 0), (3, 0), (2, 0), (3, 1), (2, 1), (1, 1))
 Y_PLACE = (0, 2, 1, 3)
 
 
@@ -706,8 +706,7 @@
                         barrier, inc=1, device_id={"rep": home[k]}, device_id_type=MESH
                     )
                 pl.semaphore_wait(barrier, 3)
-                for n in (0, 1):
-                    to_far(n).start()
+                to_far(0).start()
                 for n in (0, 1):
                     to_core(n).start()
                 for k in (1, 2, 3):
@@ -716,27 +715,25 @@
                 load_top(0).start()
                 load_x(0).start()
                 gates_all[me] = gates_ref[me]
+            if i == 1:
+                to_far(1).start()
+                for n in (0, 1):
+                    to_core(n).wait_recv()
             if i == 2:
                 for k in (1, 2, 3):
                     small_gates(k).wait_recv()
                 to_far(0).wait_recv()
                 forward(0).start()
-                forward(0).wait_recv()
-                load_x(2).start()
             if i == 3:
                 to_far(1).wait_recv()
                 forward(1).start()
             if i == 4:
                 forward(1).wait_recv()
-                load_x(4).start()
-            if i == 5:
-                to_core(0).wait_recv()
-                to_core(1).wait_recv()
             load_x(i).wait()
             load_top(i).wait()
             if i + 1 < steps:
                 load_top(i + 1).start()
-                if i + 1 not in (2, 4):
+                if i + 1 != 3:
                     load_x(i + 1).start()
             if i >= 2:
                 finish(i - 2)
@@ -792,6 +789,9 @@
             store_dx(i).start()
             for copy in stores(i):
                 copy.start()
+            if i == 2:
+                forward(0).wait_recv()
+                load_x(3).start()
             if i == steps - 1:
                 own_back = pltpu.make_async_copy(dg_mine.at[me], dg_all.at[me], small_send.at[1, 0])
                 own_back.start()
@@ -870,6 +870,408 @@
     )(x, all_top, gates, weights)
 
 
+def send_to(source, target, send, receive, device):
+    return pltpu.make_async_remote_copy(
+        src_ref=source, dst_ref=target, send_sem=send, recv_sem=receive, device_id=device, device_id_type=MESH
+    )
+
+
+def line_reduce(parts, y_buf, right_buf, left_buf, y_sems, right_sems, left_sems):
+    me = lax.axis_index("shard")
+    place, side = me // 2, lax.rem(me, 2)
+    to_y, to_right, to_left = {"shard": me + 1 - 2 * side}, {"shard": me + 2}, {"shard": me - 2}
+
+    def across(c):
+        return send_to(parts.at[c, 1 - side], y_buf.at[c], y_sems.at[0, c], y_sems.at[1, c], to_y)
+
+    def add_across(c):
+        across(c).wait_recv()
+        for p in range(LINE):
+            parts[c, side, p] = (parts[c, side, p].astype(F32) + y_buf[c, p].astype(F32)).astype(BF16)
+
+    def hop(c, p, buf, sems, device, first):
+        source = parts.at[c, side, p] if first else buf.at[c, p]
+        return send_to(source, buf.at[c, p], sems.at[0, c, p], sems.at[1, c, p], device)
+
+    def run(c, p, buf, sems, device, is_first, passes):
+        @pl.when(passes & is_first)
+        def _():
+            hop(c, p, buf, sems, device, True).start()
+
+        @pl.when(passes & jnp.logical_not(is_first))
+        def _():
+            hop(c, p, buf, sems, device, False).wait_recv()
+            buf[c, p] = (parts[c, side, p].astype(F32) + buf[c, p].astype(F32)).astype(BF16)
+            hop(c, p, buf, sems, device, False).start()
+
+    def step_right(c):
+        for p in range(1, LINE):
+            run(c, p, right_buf, right_sems, to_right, place == 0, place < p)
+
+    def step_left(c):
+        for p in range(LINE - 1):
+            run(c, p, left_buf, left_sems, to_left, place == LINE - 1, place > p)
+
+    def collect(c, total):
+        total[...] = parts[c, side, place].astype(F32)
+
+        @pl.when(place > 0)
+        def _():
+            hop(c, place, right_buf, right_sems, to_right, False).wait_recv()
+            total[...] += right_buf[c, place].astype(F32)
+
+        @pl.when(place < LINE - 1)
+        def _():
+            hop(c, place, left_buf, left_sems, to_left, False).wait_recv()
+            total[...] += left_buf[c, place].astype(F32)
+
+    def drain(c):
+        across(c).wait_send()
+        for p in range(1, LINE):
+
+            @pl.when(place < p)
+            def _(p=p):
+                hop(c, p, right_buf, right_sems, to_right, False).wait_send()
+
+        for p in range(LINE - 1):
+
+            @pl.when(place > p)
+            def _(p=p):
+                hop(c, p, left_buf, left_sems, to_left, False).wait_send()
+
+    def greet(extra):
+        barrier = pltpu.get_barrier_semaphore()
+        for device in [to_y] + extra:
+            pl.semaphore_signal(barrier, inc=1, device_id=device, device_id_type=MESH)
+        has_right, has_left = place < LINE - 1, place > 0
+
+        @pl.when(has_right)
+        def _():
+            pl.semaphore_signal(barrier, inc=1, device_id=to_right, device_id_type=MESH)
+
+        @pl.when(has_left)
+        def _():
+            pl.semaphore_signal(barrier, inc=1, device_id=to_left, device_id_type=MESH)
+
+        count = 1 + len(extra) + has_right.astype(jnp.int32) + has_left.astype(jnp.int32)
+        pl.semaphore_wait(barrier, count)
+
+    return place, across, add_across, step_right, step_left, collect, drain, greet
+
+
+def between(step, low, high, body):
+    @pl.when((step >= low) & (step < high))
+    def _():
+        body()
+
+
+def expert_grads_kernel(
+    xt_ref,
+    tt_ref,
+    dgu_ref,
+    gh_ref,
+    out_ref,
+    left_op,
+    right_op,
+    parts,
+    y_buf,
+    right_buf,
+    left_buf,
+    total,
+    mine,
+    load_sem,
+    lhs_sem,
+    y_sems,
+    right_sems,
+    left_sems,
+    own_sem,
+    far_sems,
+    near_sems,
+    pass_sems,
+):
+    n = parts.shape[0]
+    columns = right_op.shape[2]
+    first = dgu_ref.shape[1] // columns
+    rows = parts.shape[3]
+    rep = lax.axis_index("rep")
+    far = lax.rem(rep + 2, 4)
+    to_core, to_far = {"rep": rep + 1 - 2 * lax.rem(rep, 2)}, {"rep": far}
+    place, across, add_across, step_right, step_left, collect, drain, greet = line_reduce(
+        parts, y_buf, right_buf, left_buf, y_sems, right_sems, left_sems
+    )
+
+    def load(c, act):
+        slot = lax.rem(c, 2)
+
+        @pl.when(c < first)
+        def _():
+            here = pl.ds(pl.multiple_of(c * columns, columns), columns)
+            act(pltpu.make_async_copy(dgu_ref.at[:, here], right_op.at[slot], load_sem.at[slot]))
+
+        @pl.when(c >= first)
+        def _():
+            here = pl.ds(pl.multiple_of((c - first) * columns, columns), columns)
+            act(pltpu.make_async_copy(gh_ref.at[:, here], right_op.at[slot], load_sem.at[slot]))
+
+    def start(copy):
+        copy.start()
+
+    def wait(copy):
+        copy.wait()
+
+    def place_of(owner, c):
+        return out_ref.at[owner, :, pl.ds(pl.multiple_of(c * columns, columns), columns)]
+
+    def over_x(c):
+        return send_to(mine.at[c], place_of(rep, c), far_sems.at[0, c], far_sems.at[1, c], to_far)
+
+    def over_core(c):
+        return send_to(mine.at[c], place_of(rep, c), near_sems.at[0, c], near_sems.at[1, c], to_core)
+
+    def keep(c):
+        return pltpu.make_async_copy(mine.at[c], place_of(rep, c), own_sem.at[c])
+
+    def pass_on(c):
+        return send_to(place_of(far, c), place_of(far, c), pass_sems.at[0, c], pass_sems.at[1, c], to_core)
+
+    lhs = pltpu.make_async_copy(xt_ref, left_op, lhs_sem)
+    lhs.start()
+    load(0, start)
+    greet([to_core, to_far])
+    lhs.wait()
+
+    def produce(c):
+        @pl.when(c == first)
+        def _():
+            swap = pltpu.make_async_copy(tt_ref, left_op, lhs_sem)
+            swap.start()
+            swap.wait()
+
+        load(c, wait)
+
+        @pl.when(c + 1 < n)
+        def _():
+            load(c + 1, start)
+
+        result = dot(left_op[...], right_op[lax.rem(c, 2)], (1, 0)).astype(BF16)
+        for t in range(2 * LINE):
+            parts[c, t % 2, t // 2] = result[t * rows : (t + 1) * rows]
+        across(c).start()
+
+    def finish(c):
+        collect(c, total)
+        mine[c] = total[...].astype(BF16)
+        over_x(c).start()
+        over_core(c).start()
+        keep(c).start()
+
+    def forward(c):
+        over_x(c).wait_recv()
+        pass_on(c).start()
+
+    def step(i, carry):
+        between(i, 0, n, lambda: produce(i))
+        between(i, 1, n + 1, lambda: add_across(i - 1))
+        to_right_chunk, to_left_chunk = i - 1 - place, i - LINE + place
+        between(to_right_chunk, 0, n, lambda: step_right(to_right_chunk))
+        between(to_left_chunk, 0, n, lambda: step_left(to_left_chunk))
+        between(i, 5, n + 5, lambda: finish(i - 5))
+        between(i, 7, n + 7, lambda: forward(i - 7))
+        return carry
+
+    lax.fori_loop(0, n + 7, step, 0)
+
+    def end(c, carry):
+        drain(c)
+        over_x(c).wait_send()
+        over_core(c).wait()
+        keep(c).wait()
+        pass_on(c).wait()
+        return carry
+
+    lax.fori_loop(0, n, end, 0)
+
+
+def expert_grads(x_t, top_t, dgu, gated, columns=256):
+    width, tokens = x_t.shape
+    wide = dgu.shape[1] + gated.shape[1]
+    n = wide // columns
+    rows = width // (2 * LINE)
+    dma = pltpu.SemaphoreType.DMA
+    anywhere = pl.BlockSpec(memory_space=pl.ANY)
+    return pl.pallas_call(
+        expert_grads_kernel,
+        in_specs=[anywhere] * 4,
+        out_specs=anywhere,
+        out_shape=jax.ShapeDtypeStruct((4, rows, wide), BF16),
+        scratch_shapes=[
+            pltpu.VMEM((width, tokens), BF16),
+            pltpu.VMEM((2, tokens, columns), BF16),
+            pltpu.VMEM((n, 2, LINE, rows, columns), BF16),
+            pltpu.VMEM((n, LINE, rows, columns), BF16),
+            pltpu.VMEM((n, LINE, rows, columns), BF16),
+            pltpu.VMEM((n, LINE, rows, columns), BF16),
+            pltpu.VMEM((rows, columns), F32),
+            pltpu.VMEM((n, rows, columns), BF16),
+            dma((2,)),
+            dma,
+            dma((2, n)),
+            dma((2, n, LINE)),
+            dma((2, n, LINE)),
+            dma((n,)),
+            dma((2, n)),
+            dma((2, n)),
+            dma((2, n)),
+        ],
+        compiler_params=pltpu.CompilerParams(vmem_limit_bytes=60 * MIB, collective_id=4, has_side_effects=True),
+        cost_estimate=pl.CostEstimate(
+            flops=2 * width * tokens * wide, bytes_accessed=80 * MIB, transcendentals=0
+        ),
+        name="expert_grads",
+    )(x_t, top_t, dgu, gated)
+
+
+def late_reduce_kernel(
+    in_ref,
+    out_ref,
+    own_buf,
+    core_buf,
+    parts,
+    y_buf,
+    right_buf,
+    left_buf,
+    total,
+    mine,
+    far_buf,
+    whole,
+    load_sem,
+    core_sems,
+    y_sems,
+    right_sems,
+    left_sems,
+    own_sem,
+    far_sems,
+    near_sems,
+):
+    n = parts.shape[0]
+    rows, columns = parts.shape[3:]
+    rep = lax.axis_index("rep")
+    half = lax.rem(rep, 2)
+    to_core, to_far = {"rep": rep + 1 - 2 * half}, {"rep": lax.rem(rep + 2, 4)}
+    place, across, add_across, step_right, step_left, collect, drain, greet = line_reduce(
+        parts, y_buf, right_buf, left_buf, y_sems, right_sems, left_sems
+    )
+
+    def span(which, c):
+        return pl.ds(pl.multiple_of((which * n + c) * columns, columns), columns)
+
+    def load(c):
+        return pltpu.make_async_copy(in_ref.at[:, span(half, c)], own_buf.at[c], load_sem.at[c])
+
+    def from_core(c):
+        return send_to(
+            in_ref.at[:, span(1 - half, c)], core_buf.at[c], core_sems.at[0, c], core_sems.at[1, c], to_core
+        )
+
+    def over_x(c):
+        return send_to(mine.at[c], far_buf.at[c], far_sems.at[0, c], far_sems.at[1, c], to_far)
+
+    def over_core(c):
+        return send_to(
+            whole.at[c], out_ref.at[:, span(half, c)], near_sems.at[0, c], near_sems.at[1, c], to_core
+        )
+
+    def keep(c):
+        return pltpu.make_async_copy(whole.at[c], out_ref.at[:, span(half, c)], own_sem.at[c])
+
+    for c in range(n):
+        load(c).start()
+    greet([to_core, to_far])
+    for c in range(n):
+        from_core(c).start()
+
+    def produce(c):
+        load(c).wait()
+        from_core(c).wait_recv()
+        for t in range(2 * LINE):
+            here = pl.ds(t * rows, rows)
+            parts[c, t % 2, t // 2] = (own_buf[c, here].astype(F32) + core_buf[c, here].astype(F32)).astype(BF16)
+        across(c).start()
+
+    def finish(c):
+        collect(c, total)
+        mine[c] = total[...].astype(BF16)
+        over_x(c).start()
+
+    def complete(c):
+        over_x(c).wait_recv()
+        whole[c] = (mine[c].astype(F32) + far_buf[c].astype(F32)).astype(BF16)
+        over_core(c).start()
+        keep(c).start()
+
+    def step(i, carry):
+        between(i, 0, n, lambda: produce(i))
+        between(i, 1, n + 1, lambda: add_across(i - 1))
+        to_right_chunk, to_left_chunk = i - 1 - place, i - LINE + place
+        between(to_right_chunk, 0, n, lambda: step_right(to_right_chunk))
+        between(to_left_chunk, 0, n, lambda: step_left(to_left_chunk))
+        between(i, LINE, n + LINE, lambda: finish(i - LINE))
+        between(i, LINE + 1, n + LINE + 1, lambda: complete(i - LINE - 1))
+        return carry
+
+    lax.fori_loop(0, n + LINE + 1, step, 0)
+
+    def end(c, carry):
+        drain(c)
+        from_core(c).wait_send()
+        over_x(c).wait_send()
+        over_core(c).wait_send()
+        keep(c).wait()
+        send_to(
+            whole.at[c], out_ref.at[:, span(1 - half, c)], near_sems.at[0, c], near_sems.at[1, c], to_core
+        ).wait_recv()
+        return carry
+
+    lax.fori_loop(0, n, end, 0)
+
+
+def late_reduce(values, columns=256):
+    width, wide = values.shape
+    n = wide // 2 // columns
+    rows = width // (2 * LINE)
+    dma = pltpu.SemaphoreType.DMA
+    anywhere = pl.BlockSpec(memory_space=pl.ANY)
+    return pl.pallas_call(
+        late_reduce_kernel,
+        in_specs=[anywhere],
+        out_specs=anywhere,
+        out_shape=jax.ShapeDtypeStruct((rows, wide), BF16),
+        scratch_shapes=[
+            pltpu.VMEM((n, width, columns), BF16),
+            pltpu.VMEM((n, width, columns), BF16),
+            pltpu.VMEM((n, 2, LINE, rows, columns), BF16),
+            pltpu.VMEM((n, LINE, rows, columns), BF16),
+            pltpu.VMEM((n, LINE, rows, columns), BF16),
+            pltpu.VMEM((n, LINE, rows, columns), BF16),
+            pltpu.VMEM((rows, columns), F32),
+            pltpu.VMEM((n, rows, columns), BF16),
+            pltpu.VMEM((n, rows, columns), BF16),
+            pltpu.VMEM((n, rows, columns), BF16),
+            dma((n,)),
+            dma((2, n)),
+            dma((2, n)),
+            dma((2, n, LINE)),
+            dma((2, n, LINE)),
+            dma((n,)),
+            dma((2, n)),
+            dma((2, n)),
+        ],
+        compiler_params=pltpu.CompilerParams(vmem_limit_bytes=48 * MIB, collective_id=5, has_side_effects=True),
+        cost_estimate=pl.CostEstimate(flops=0, bytes_accessed=16 * MIB, transcendentals=0),
+        name="late_reduce",
+    )(values)
+
+
 def flatten_kernel(starts, lead_ref, *refs):
     parts, flat_ref, square_ref = refs[: len(starts)], refs[len(starts)], refs[len(starts) + 1]
     scratch, sems = refs[len(starts) + 2 : -1], refs[-1]
@@ -1402,22 +1804,24 @@
     grad_branch = grad_mid.astype(BF16)
     grad_attn_w = dot(grad_branch, attn_low, (0, 1))
     grad_attn = dot(attn_out_full, grad_branch, (0, 1)).astype(BF16).reshape(QUERY_HEADS, HEAD_SIZE, count)
+    expert_columns = local * 3 * F
+    if fast:
+        expert_rows = expert_grads(
+            all_normed.reshape(reps * count, width).T,
+            all_top.reshape(reps * count, width).T,
+            dgu.reshape(reps * count, -1),
+            gated.reshape(reps * count, -1),
+        )
+    else:
+        terms = jnp.concatenate([expert_term(all_normed, dgu), expert_term(all_top, gated)], axis=1)
+        terms = lax.psum_scatter(terms, "shard", scatter_dimension=0, tiled=True)
+        expert_rows = lax.all_gather(terms, "rep", axis=0, tiled=False)
     early = jnp.concatenate(
-        [
-            expert_term(all_normed, dgu),
-            expert_term(all_top, gated),
-            grad_attn_w.astype(BF16),
-            grad_router_w.astype(BF16),
-            grad_ffn_gain[:, None].astype(BF16),
-        ],
-        axis=1,
+        [grad_attn_w.astype(BF16), grad_router_w.astype(BF16), grad_ffn_gain[:, None].astype(BF16)], axis=1
     )
     early = jnp.pad(early, ((0, 0), (0, -early.shape[1] % LANES)))
-    grad_attn, early = lax.optimization_barrier((grad_attn, early))
-    early = lax.psum_scatter(early, "shard", scatter_dimension=0, tiled=True)
-    expert_columns = local * 3 * F
-    expert_rows = lax.all_gather(early[:, :expert_columns], "rep", axis=0, tiled=False)
-    early = rep_sum(early[:, expert_columns:])
+    grad_attn, early, expert_rows = lax.optimization_barrier((grad_attn, early, expert_rows))
+    early = rep_sum(lax.psum_scatter(early, "shard", scatter_dimension=0, tiled=True))
     attn_rows, router_rows = early[:, :Q_WIDTH], early[:, Q_WIDTH : Q_WIDTH + EXPERTS]
     ffn_gain_rows = early[:, Q_WIDTH + EXPERTS]
 
@@ -1448,9 +1852,11 @@
         ],
         axis=1,
     )
-    late = lax.psum_scatter(late, "shard", scatter_dimension=0, tiled=True)
-    late, grad_prompt_kv = lax.optimization_barrier((late, grad_prompt_kv))
-    qkv_rows = rep_sum(late)
+    if fast:
+        qkv_rows = late_reduce(late)
+    else:
+        qkv_rows = rep_sum(lax.psum_scatter(late, "shard", scatter_dimension=0, tiled=True))
+    qkv_rows, grad_prompt_kv = lax.optimization_barrier((qkv_rows, grad_prompt_kv))
     attn_gain_rows = jnp.sum(
         qkv_rows.astype(F32) * query_key_value_weight.astype(F32), axis=1
     ) / attn_gain.astype(F32)

time: 1630 us -> 1250 us (0.77)
  waiting for transfers between devices: 781 us -> 39.5 us
  Pallas kernels: 545 us -> 978 us
  matrix products: 145 us -> 76.6 us
    reduce_scatter x2 -> x1, waiting for transfers between devices: 509 us -> 0.01 us  [per_device(): lax.psum_scatter(early, 'shard', scatter_dimension=0, tiled=True)]
    pallas_call x0 -> x2, Pallas kernels: none -> 327 us  [the longest x1 192 us: expert_grads(): pl.pallas_call(expert_grads_kernel, in_specs=[anywhere] * 4, out_specs=an...]
    reduce_scatter x1, waiting for transfers between devices: 126 us -> 0.02 us  [per_device(): lax.psum_scatter(grad_prompt_kv, 'shard', scatter_dimension=1, tiled=True...]
    pallas_call x1, Pallas kernels: 53.1 us -> 127 us  [attn_backward(): pl.pallas_call(attn_backward_kernel, grid=(query.shape[0] // PER_KEY,), i...]
    dot_general x17 -> x15, matrix products: 145 us -> 76.6 us  [dot(): lax.dot_general(left, right, ((dims[:1], dims[1:]), ((), ())), preferred_...]
    all_gather x1, waiting for transfers between devices: 82.8 us -> 32.1 us  [per_device(): w_both = gather(w_both)]
    pallas_call x1, Pallas kernels: 34.2 us -> 83.7 us  [attn_forward(): pl.pallas_call(attn_forward_kernel, grid=(query.shape[0] // PER_KEY,), in...]
    all_gather x1 -> x0, waiting for transfers between devices: 27.8 us -> none  [per_device(): lax.all_gather(early[:, :expert_columns], 'rep', axis=0, tiled=False)]
  transfers between devices with their start and end apart: 11 -> 7, of which waited for: 8 -> 2; matrix products, arithmetic and copies ran while one was open for 10% -> 11% of each run, Pallas kernels for 3% -> 47%
where the time goes in v3:
time: 1250 us; the launch traced here: 1240 us
  Pallas kernels  978 us (78%)
  matrix products  76.6 us (6%)
  local copies, waits for them, and re-layouts  65.6 us (5%)
  other arithmetic  59.4 us (5%)
  waiting for transfers between devices  39.5 us (3%)
  between operations  17.7 us (1%)
    pallas_call x1, Pallas kernels, expert_grads(): pl.pallas_call(expert_grads_kernel, in_specs=[anywhere] * 4, out_specs=an...  192 us
    pallas_call x1, Pallas kernels, experts(): pl.pallas_call(experts_kernel, grid=(len(ORDER),), in_specs=[anywhere, an...  159 us
    pallas_call x1, Pallas kernels, late_reduce(): pl.pallas_call(late_reduce_kernel, in_specs=[anywhere], out_specs=anywher...  136 us
    pallas_call x1, Pallas kernels, attn_backward(): pl.pallas_call(attn_backward_kernel, grid=(query.shape[0] // PER_KEY,), i...  127 us
    pallas_call x1, Pallas kernels, start_gather(): pl.pallas_call(start_kernel, in_specs=[anywhere] * 3, out_specs=[anywhere...  112 us
    pallas_call x1, Pallas kernels, summed_step(): pl.pallas_call(step_kernel, in_specs=[pl.BlockSpec(memory_space=pltpu.VME...  91.7 us
    pallas_call x1, Pallas kernels, attn_forward(): pl.pallas_call(attn_forward_kernel, grid=(query.shape[0] // PER_KEY,), in...  83.7 us
    dot_general x15, matrix products, dot(): lax.dot_general(left, right, ((dims[:1], dims[1:]), ((), ())), preferred_...  76.6 us
  transfers between devices with their start and end apart: 7, of which 2 were waited for; matrix products, arithmetic and copies ran while one was open for 11% of the time, Pallas kernels for 47%

profile of v3, /device:TPU:0, one launch (start us, length us, event | category | flops | bytes accessed | tf_op | source)
XLA Modules:
  0.0 1241.4 jit_solution(5158458309638957443)
XLA Ops:
  7.2 0.8 copy.73
  8.0 0.8 copy.74
  9.6 1.2 concatenate.82
  10.8 1.0 pad.12.w_ref
  11.8 1.3 constant_dynamic-slice_fusion.1
  13.1 1.1 constant_dynamic-slice_fusion
  14.2 1.3 pad_maximum_fusion.5
  15.4 111.9 %start_gather.1 = (bf16[8,512,1024]{2,1,0:T(8,128)(2,1)}, bf16[8,4,32,3200]{3,2,1,0:T(8,128)(2,1)}, bf16[4,1024,1024]{2,1,0:T(8,128)(2,1)}) custom-call(bf16[1024,1024]{1,0:T(8,128)(2,1)} %bitcast.126, bf16[128,3200]{1,0:T(8,128)(2,1)} %pad.12.w_ref, bf16[1024,1024]{1,0:T(8,128)(2,1)} %bitcast.131), custom_call_target="tpu_custom_call" | custom-call | bytes 67108864 | tf_op jit(solution)/shard_map/start_gather/pallas_call | solution.py:554
  128.1 1.1 slice.153
  129.3 3.2 slice_bitcast_fusion.1
  132.6 3.9 copy.76
  137.2 0.9 negate_bitcast_fusion
  138.7 2.5 fusion.38
  141.4 2.1 convolution_convert_fusion.3
  143.7 1.2 fusion.58
  144.9 2.5 fusion.22
  148.4 1.7 fusion
  150.1 2.7 fusion.48
  152.9 9.2 fusion.40
  162.1 4.7 fusion.17
  166.9 7.0 convolution_convert_fusion
  173.9 3.7 pad_maximum_fusion.kv_ref
  177.6 83.7 %attn_forward.1 = (f32[16,64,1024]{2,1,0:T(8,128)}, f32[8,2,1024]{2,1,0:T(2,128)S(1)}) custom-call(s32[2]{0:T(128)S(1)} %pad_add_fusion.where_ref, bf16[16,64,1024]{2,1,0:T(8,128)(2,1)S(1)} %pad_maximum_fusion.4.q_ref, bf16[2,8,64,4096]{3,2,1,0:T(8,128)(2,1)} %pad_maximum_fusion.kv_ref, bf16[2,8,64,512]{3,2,1,0:T(8,128)(2,1)S(1)} %pad_maximum_fusion.6.own_ref), custom_call_target="tpu_custom_call" | custom-call | flops 17179869184 | bytes 16777216 | tf_op jit(solution)/shard_map/attn_forward/pallas_call | solution.py:138
  261.4 2.5 convert_element_type.286
  264.0 4.8 multiply_reduce_fusion.3
  269.3 1.9 fusion.59
  273.2 32.1 %all-gather.2.cloned.1.call-done.w_ref = bf16[1024,6144]{1,0:T(8,128)(2,1)} async-done(((bf16[128,6144]{1,0:T(8,128)(2,1)}), bf16[1024,6144]{1,0:T(8,128)(2,1)}) %all-gather.2.cloned.1.call-update) | async-done | bytes 12582928 | tf_op jit(solution)/shard_map/all_gather | solution.py:1732
  305.3 158.5 %experts.1 = (bf16[4,1024,1024]{2,1,0:T(8,128)(2,1)}, bf16[1024,1024]{1,0:T(8,128)(2,1)}, bf16[1024,1024]{1,0:T(8,128)(2,1)}, bf16[1024,1024]{1,0:T(8,128)(2,1)}...) custom-call(bf16[1024,1024]{1,0:T(8,128)(2,1)} %copy-done.14, ...), custom_call_target="tpu_custom_call" | custom-call | flops 103079215104 | bytes 83886080 | tf_op jit(solution)/shard_map/experts/pallas_call | solution.py:824
  463.8 4.6 slice.134
  468.6 11.9 copy.97
  480.5 11.9 copy.96
  492.4 5.5 convert_add_fusion
  497.9 3.4 copy-done.12
  501.3 1.7 fusion.20
  503.0 1.6 collective-permute-start.1
  504.6 191.8 %expert_grads.1.refs_2_.refs_3_ = bf16[4,128,6144]{2,1,0:T(8,128)(2,1)} custom-call(bf16[1024,4096]{1,0:T(8,128)(2,1)} %bitcast.141, bf16[1024,4096]{1,0:T(8,128)(2,1)} %bitcast.140, bf16[4096,4096]{1,0:T(8,128)(2,1)} %bitcast.183, bf16[4096,2048]{1,0:T(8,128)(2,1)} %bitcast.184), custom_call_target="tpu_custom_call" | custom-call | flops 51539607552 | bytes 83886080 | tf_op jit(solution)/shard_map/expert_grads/pallas_call | solution.py:1102
  697.3 5.4 multiply_reduce_fusion.1
  702.9 2.1 copy-done.13
  705.7 4.5 subtract_add_fusion
  710.1 3.7 convolution_convert_fusion.1
  713.9 5.3 convolution_convert_fusion.2
  719.2 4.2 concatenate.92
  723.4 1.6 pad.14
  725.0 3.7 multiply_reduce_fusion
  729.3 126.9 %attn_backward.1 = (f32[16,64,1024]{2,1,0:T(8,128)}, bf16[2,8,64,4096]{3,2,1,0:T(8,128)(2,1)}, f32[2,8,64,512]{3,2,1,0:T(8,128)}) custom-call(s32[2]{0:T(128)} %copy-done.5, bf16[16,64,1024]{2,1,0:T(8,128)(2,1)} %copy-done.2, bf16[2,8,64,4096]{3,2,1,0:T(8,128)(2,1)} %pad_maximum_fusion.kv_ref, bf16[2,8,64,512]{3,2,1,0:T(8,128)(2,1)} %copy-done.3, ...), custom_call_target="tpu_custom_call" | custom-call | flops 42949672960 | bytes 33554432 | tf_op jit(solution)/shard_map/attn_backward/pallas_call | solution.py:255
  856.2 1.3 slice_bitcast_fusion.2
  857.5 1.3 slice.266
  858.9 5.7 bitcast_convert_fusion
  864.7 1.3 subtract_convert_fusion
  867.8 1.6 maximum_convert_fusion
  869.4 2.5 pad_maximum_fusion.2
  871.9 17.4 %fusion.63 = f32[1024,1024]{1,0:T(8,128)} fusion(bf16[512,4096]{1,0:T(8,128)(2,1)} %bitcast.127, bf16[512,4096]{1,0:T(8,128)(2,1)} %bitcast.129, bf16[4096,1024]{1,0:T(8,128)(2,1)} %bitcast.132, f32[1024]{0:T(1024)S(1)} %bitcast.175, f32[4096]{0:T(1024)S(1)} %copy-done.60), kind=kOutput, calls=%fused_computation.147 | convolution fusion | flops 8623489024 | bytes 20992000 | tf_op jit(solution)/shard_map/dot_general | solution.py:43
  889.4 3.6 add_convert_fusion
  893.1 2.6 fusion.26
  896.2 135.5 %late_reduce.1.refs_0_ = bf16[128,2048]{1,0:T(8,128)(2,1)S(1)} custom-call(bf16[1024,2048]{1,0:T(8,128)(2,1)S(1)} %pad_maximum_fusion.3.in_ref), custom_call_target="tpu_custom_call" | custom-call | bytes 16777216 | tf_op jit(solution)/shard_map/late_reduce/pallas_call | solution.py:1244
  1031.7 7.9 pad_maximum_fusion.1
  1041.4 16.9 %flatten.3 = (f32[1,3541248]{1,0:T(1,128)}, f32[1,1]{1,0:T(1,128)}) custom-call(f32[18,128]{1,0:T(8,128)S(1)} %pad_maximum_fusion.9.lead_ref, bf16[128,2048]{1,0:T(8,128)(2,1)S(1)} %copy-done, bf16[128,1024]{1,0:T(8,128)(2,1)S(1)} %copy-done.4, bf16[128,16384]{1,0:T(8,128)(2,1)} %refs_2_.1, bf16[128,8192]{1,0:T(8,128)(2,1)S(1)} %copy-done.1), custom_call_target="tpu_custom_call" | custom-call | tf_op jit(solution)/shard_map/flatten/pallas_call | solution.py:1342
  1058.4 3.1 collective-permute-start.3
  1061.7 7.3 collective-permute-done.3
  1069.4 17.1 %flatten.2 = (f32[1,3541248]{1,0:T(1,128)}, f32[1,1]{1,0:T(1,128)}) custom-call(f32[18,128]{1,0:T(8,128)S(1)} %pad_maximum_fusion.8.lead_ref, bf16[128,2048]{1,0:T(8,128)(2,1)S(1)} %late_reduce.1.refs_0_, bf16[128,1024]{1,0:T(8,128)(2,1)S(1)} %slice.179.refs_1_, bf16[4,128,6144]{2,1,0:T(8,128)(2,1)} %expert_grads.1.refs_2_.refs_3_, ...), custom_call_target="tpu_custom_call" | custom-call | tf_op jit(solution)/shard_map/flatten/pallas_call | solution.py:1342
  1086.5 91.7 %summed_step.1 = (f32[1,1]{1,0:T(1,128)}, bf16[2,13840,128]{2,1,0:T(8,128)(2,1)}) custom-call(f32[1,1]{1,0:T(1,128)} %get-tuple-element.64.square_ref, f32[1,3541248]{1,0:T(1,128)} %get-tuple-element.122.g_ref.g, f32[1,1,3541248]{2,1,0:T(1,128)} %f.1, f32[1,1,3541248]{2,1,0:T(1,128)} %s.1, f32[1,3541248]{1,0:T(1,128)} %get-tuple-element.65.w_ref), custom_call_target="tpu_custom_call" | custom-call | bytes 67108864 | tf_op jit(solution)/shard_map/summed_step/pallas_call | solution.py:1553
  1178.2 43.5 %update.1 = (f32[1,1,3541248]{2,1,0:T(1,128)}, f32[1,1,3541248]{2,1,0:T(1,128)}, f32[1,3541248]{1,0:T(1,128)}, f32[1,3541248]{1,0:T(1,128)}) custom-call(f32[1,1]{1,0:T(1,128)} %get-tuple-element.66.norm_ref, f32[1,3541248]{1,0:T(1,128)} %get-tuple-element.122.g_ref.g, f32[1,1,3541248]{2,1,0:T(1,128)} %f.1, f32[1,1,3541248]{2,1,0:T(1,128)} %s.1, ...), custom_call_target="tpu_custom_call" | custom-call | bytes 125829120 | tf_op jit(solution)/shard_map/update/pallas_call | solution.py:1634
  1221.8 8.0 fusion.4
  1229.7 3.0 add_bitcast_fusion
  (192 shorter events, 13.1 us)
Async XLA Ops:
  7.2 298.1 %all-gather.2.cloned.1.call-start = ((), (), s32[]{:S(2)}) async-start(), calls=%async_computation.2 | async-start | bytes 14155776 | tf_op jit(solution)/shard_map/all_gather | solution.py:1732
  127.4 913.1 %reduce-scatter.5.cloned.1.call-start = ((), (), s32[]{:S(2)}) async-start(), calls=%async_computation.4 | async-start | bytes 2654208 | tf_op jit(solution)/shard_map/reduce_scatter | solution.py:1824
  129.3 7.3 copy-start.9
  136.6 41.0 %copy-start.5 = (s32[2]{0:T(128)}, s32[2]{0:T(128)S(1)}, u32[]{:S(2)}) copy-start(s32[2]{0:T(128)S(1)} %pad_add_fusion.where_ref) | copy-start | bytes 28
  137.1 7.8 copy-start.54
  137.1 29.7 %copy-start.52 = (f32[1024,1]{0,1:T(1,128)}, f32[1024,1]{0,1:T(1,128)S(1)}, u32[]{:S(2)}) copy-start(f32[1024,1]{0,1:T(1,128)S(1)} %get-tuple-element.91) | copy-start | bytes 12292
  137.1 131.8 %copy-start.50 = (f32[1024,1]{0,1:T(1,128)}, f32[1024,1]{0,1:T(1,128)S(1)}, u32[]{:S(2)}) copy-start(f32[1024,1]{0,1:T(1,128)S(1)} %get-tuple-element.90) | copy-start | bytes 12292
  138.1 3.2 copy-start.39
  138.7 4.8 copy-start.22
  141.2 3.6 copy-start.31
  143.7 34.0 %copy-start.3 = (bf16[2,8,64,512]{3,2,1,0:T(8,128)(2,1)}, bf16[2,8,64,512]{3,2,1,0:T(8,128)(2,1)S(1)}, u32[]{:S(2)}) copy-start(bf16[2,8,64,512]{3,2,1,0:T(8,128)(2,1)S(1)} %pad_maximum_fusion.6.own_ref) | copy-start | bytes 3145732
  144.9 2.5 copy-start.35
  144.9 3.5 slice-start
  144.9 3.5 slice-start.1
  148.4 29.2 %copy-start.2 = (bf16[16,64,1024]{2,1,0:T(8,128)(2,1)}, bf16[16,64,1024]{2,1,0:T(8,128)(2,1)S(1)}, u32[]{:S(2)}) copy-start(bf16[16,64,1024]{2,1,0:T(8,128)(2,1)S(1)} %pad_maximum_fusion.4.q_ref) | copy-start | bytes 6291460
  150.1 16.7 %copy-start.59 = (f32[4096]{0:T(1024)}, f32[4096]{0:T(1024)S(1)}, u32[]{:S(2)}) copy-start(f32[4096]{0:T(1024)S(1)} %add_rsqrt_fusion) | copy-start | bytes 49156
  152.9 9.3 copy-start.19
  261.4 7.5 copy-start.6
  261.4 2.6 copy-start.56
  263.9 5.0 copy-start.24
  264.0 7.3 copy-start.37
  268.9 2.3 copy-start.7
  268.9 2.3 copy-start.48
  269.3 35.9 %copy-start.14 = (bf16[1024,1024]{1,0:T(8,128)(2,1)}, bf16[1024,1024]{1,0:T(8,128)(2,1)S(1)}, u32[]{:S(2)}) copy-start(bf16[1024,1024]{1,0:T(8,128)(2,1)S(1)} %multiply_convert_fusion.x_hbm) | copy-start | bytes 6291460
  468.5 24.0 %collective-permute-start = (bf16[2,1024,1024]{2,1,0:T(8,128)(2,1)}, bf16[2,1024,1024]{2,1,0:T(8,128)(2,1)}, u32[]{:S(2)}, u32[]{:S(2)}) collective-permute-start(bf16[2,1024,1024]{2,1,0:T(8,128)(2,1)} %slice.134), channel_id=1, source_target_pairs={{0,1},{1,0},{2,3},{3,2},{4,5},{5,4},{6,7},{7,6},{8,9},{9,8},{10,11... | collective-permute-start | bytes 12582920 | tf_op jit(solution)/shard_map/ppermute | solution.py:1787
  497.9 3.4 copy-start.12
  503.0 199.9 %collective-permute-start.1 = (bf16[1024,1024]{1,0:T(8,128)(2,1)}, bf16[1024,1024]{1,0:T(8,128)(2,1)}, u32[]{:S(2)}, u32[]{:S(2)}) collective-permute-start(bf16[1024,1024]{1,0:T(8,128)(2,1)} %fusion.20), channel_id=1, source_target_pairs={{0,2},{1,3},{2,0},{3,1},{4,6},{5,7},{6,4},{7,5},{8,10},{9,11},{10,... | collective-permute-start | bytes 6291464 | tf_op jit(solution)/shard_map/ppermute | solution.py:1788
  504.6 191.9 %copy-start.57 = (f32[4,8,1024]{2,1,0:T(8,128)S(1)}, f32[4,8,1024]{2,1,0:T(8,128)}, u32[]{:S(2)}) copy-start(f32[4,8,1024]{2,1,0:T(8,128)} %get-tuple-element.50) | copy-start | bytes 393220
  504.6 191.9 %copy-start.34 = (f32[1024,16]{0,1:T(8,128)S(1)}, f32[1024,16]{0,1:T(8,128)}, u32[]{:S(2)}) copy-start(f32[1024,16]{0,1:T(8,128)} %copy-done.33) | copy-start | bytes 196612
  504.6 191.9 %copy-start.38 = (pred[1024,16]{0,1:T(8,128)(4,1)S(1)}, pred[1024,16]{0,1:T(8,128)(4,1)}, u32[]{:S(2)}) copy-start(pred[1024,16]{0,1:T(8,128)(4,1)} %copy-done.37) | copy-start | bytes 49156
  504.6 192.0 %copy-start.45 = (f32[1024]{0:T(1024)S(1)}, f32[1024]{0:T(1024)}, u32[]{:S(2)}) copy-start(f32[1024]{0:T(1024)} %copy-done.44) | copy-start | bytes 12292
  504.6 192.0 %copy-start.47 = (f32[1024]{0:T(1024)S(1)}, f32[1024]{0:T(1024)}, u32[]{:S(2)}) copy-start(f32[1024]{0:T(1024)} %copy-done.46) | copy-start | bytes 12292
  504.6 192.0 %copy-start.15 = (bf16[1024,1024]{1,0:T(8,128)(2,1)S(1)}, bf16[1024,1024]{1,0:T(8,128)(2,1)}, u32[]{:S(2)}) copy-start(bf16[1024,1024]{1,0:T(8,128)(2,1)} %copy-done.14) | copy-start | bytes 6291460
  504.6 192.6 %copy-start.49 = (f32[1024]{0:T(1024)S(1)}, f32[1024]{0:T(1024)}, u32[]{:S(2)}) copy-start(f32[1024]{0:T(1024)} %copy-done.48) | copy-start | bytes 12292
  504.6 192.6 %copy-start.51 = (f32[1024,1]{0,1:T(1,128)S(1)}, f32[1024,1]{0,1:T(1,128)}, u32[]{:S(2)}) copy-start(f32[1024,1]{0,1:T(1,128)} %copy-done.50) | copy-start | bytes 12292
  697.3 5.7 copy-start.8
  697.3 7.8 copy-start.13
  697.3 8.4 copy-start.18
  705.7 4.5 copy-start.25
  710.1 3.7 copy-start.16
  858.8 30.5 %copy-start.26 = (bf16[1,8,64,512]{3,2,1,0:T(8,128)(2,1)}, bf16[1,8,64,512]{3,2,1,0:T(8,128)(2,1)S(1)}, u32[]{:S(2)}) copy-start(bf16[1,8,64,512]{3,2,1,0:T(8,128)(2,1)S(1)} %slice.266) | copy-start | bytes 1572868
  858.9 362.8 %reduce-scatter.3.cloned.1.call-start = ((), (), s32[]{:S(2)}) async-start(), calls=%async_computation.3 | async-start | bytes 9437184 | tf_op jit(solution)/shard_map/reduce_scatter | solution.py:1864
  858.9 5.7 copy-start.20
  858.9 5.7 copy-start.32
  864.7 2.2 copy-start.21
  864.7 2.2 copy-start.36
  864.7 2.2 copy-start.41
  866.0 1.6 copy-start.40
  867.8 21.6 %copy-start.28 = (bf16[8,64,512]{2,1,0:T(8,128)(2,1)}, bf16[8,64,512]{2,1,0:T(8,128)(2,1)S(1)}, u32[]{:S(2)}) copy-start(bf16[8,64,512]{2,1,0:T(8,128)(2,1)S(1)} %pad_maximum_fusion.7) | copy-start | bytes 1572868
  869.4 2.5 copy-start.53
  869.4 2.5 copy-start.60
  871.9 17.4 %copy-start.23 = (bf16[512,1024]{1,0:T(8,128)(2,1)S(1)}, bf16[512,1024]{1,0:T(8,128)(2,1)}, u32[]{:S(2)}) copy-start(bf16[512,1024]{1,0:T(8,128)(2,1)} %copy-done.22) | copy-start | bytes 3145732
  889.4 3.7 copy-start.10
  889.4 3.7 copy-start.30
  889.4 3.7 copy-start.55
  1039.6 1.8 copy-start.1
  1039.6 1.8 copy-start.4
  1040.5 17.8 %copy-start.42 = (bf16[128,1152]{1,0:T(8,128)(2,1)S(1)}, bf16[128,1152]{1,0:T(8,128)(2,1)}, u32[]{:S(2)}) copy-start(bf16[128,1152]{1,0:T(8,128)(2,1)} %reduce-scatter.5.cloned.1.call-done) | copy-start | bytes 884740
  1040.5 17.8 %collective-permute-start.2 = (bf16[128,1152]{1,0:T(8,128)(2,1)}, bf16[128,1152]{1,0:T(8,128)(2,1)S(1)}, u32[]{:S(2)}, u32[]{:S(2)}) collective-permute-start(bf16[128,1152]{1,0:T(8,128)(2,1)} %reduce-scatter.5.cloned.1.call-done), channel_id=1, source_target_pairs={{0,1},{1,0},{2,3},{3,2},{4,5},{5,4},{6,7},{7,6},{8,9},{9,8},{10,11... | collective-permute-start | bytes 884744 | tf_op jit(solution)/shard_map/ppermute | solution.py:1793
  1058.4 10.6 collective-permute-start.3
  1178.1 43.6 %copy-start.11 = (bf16[1,1,1024,1024]{3,2,1,0:T(8,128)(2,1)S(1)}, bf16[1,1,1024,1024]{3,2,1,0:T(8,128)(2,1)}, u32[]{:S(2)}) copy-start(bf16[1,1,1024,1024]{3,2,1,0:T(8,128)(2,1)} %param.14) | copy-start | bytes 6291460
  1178.2 43.6 %copy-start.27 = (bf16[1,8,64,512]{3,2,1,0:T(8,128)(2,1)S(1)}, bf16[1,8,64,512]{3,2,1,0:T(8,128)(2,1)}, u32[]{:S(2)}) copy-start(bf16[1,8,64,512]{3,2,1,0:T(8,128)(2,1)} %copy-done.26) | copy-start | bytes 1572868
  1178.2 43.6 %copy-start.29 = (bf16[8,64,512]{2,1,0:T(8,128)(2,1)S(1)}, bf16[8,64,512]{2,1,0:T(8,128)(2,1)}, u32[]{:S(2)}) copy-start(bf16[8,64,512]{2,1,0:T(8,128)(2,1)} %copy-done.28) | copy-start | bytes 1572868
  1221.8 8.0 copy-start.17
  (8 other events, 7.5 us)
Sparse Core Ops, SparseCore 0:
  127.5 177.7 all-gather.1
  859.0 166.3 reduce-scatter.4
  1039.8 148.8 reduce-scatter.2

commit v4 on v3

--- a/solution.py
+++ b/solution.py
@@ -70,64 +70,97 @@
     return key_pos <= query_pos
 
 
-def attn_forward_kernel(where_ref, q_ref, kv_ref, own_ref, o_ref, lse_ref, peak_ref, sum_ref, acc_ref):
+SAFE_BOUND = 48.0
+
+
+def attn_forward_kernel(where_ref, q_ref, kv_ref, own_ref, o_ref, lse_ref, peak_ref, acc_ref):
     block = own_ref.shape[-1]
     columns = PER_KEY * block
     shard_pos = where_ref[0]
     branch = where_ref[1]
-
-    def advance(query, key, value, mask):
-        scores = dot(jnp.concatenate([key, key], axis=0), query, (0, 0))
-        if mask is not None:
-            scores = jnp.where(mask, scores, NEGATIVE)
-        old = peak_ref[...]
-        new = jnp.maximum(old, jnp.max(scores, axis=0, keepdims=True))
-        probs = jnp.exp2(scores - new).astype(BF16)
-        shrink = jnp.exp2(old - new)
-        ones = jnp.ones((16, block), BF16)
-        part = dot(jnp.concatenate([value, ones], axis=0), probs, (1, 0))
-        peak_ref[...] = new
-        sum_ref[...] = sum_ref[...] * shrink + part[HEAD_SIZE : HEAD_SIZE + 1]
-        acc_ref[...] = acc_ref[...] * shrink + part[:HEAD_SIZE]
-
-    def begin(start):
-        _, high, low = augment_query(q_ref, start, block)
-        peak_ref[...] = jnp.full_like(peak_ref, NEGATIVE)
-        sum_ref[...] = jnp.zeros_like(sum_ref)
-        acc_ref[...] = jnp.zeros_like(acc_ref)
-        return jnp.concatenate([high, low], axis=0)
-
-    def finish(start):
-        total = sum_ref[...]
-        result = acc_ref[...] / total
-        lse = peak_ref[...] + jnp.log2(total)
+    ones = jnp.ones((16, block), BF16)
+    pad = jnp.zeros((16 - 3, columns), BF16)
+    whole = branch // block
+
+    def longest(key):
+        squares = key.astype(F32)
+        return jnp.max(jnp.sum(squares * squares, axis=0, keepdims=True), axis=1, keepdims=True)
+
+    longest_key = jnp.sqrt(jnp.maximum(longest(kv_ref[0, 0]), longest(own_ref[0, 0])))
+
+    def emit(start, result, lse):
         for g in range(PER_KEY):
             o_ref[g, :, start : start + block] = result[:, g * block : (g + 1) * block]
             lse_ref[0, g : g + 1, start : start + block] = lse[:, g * block : (g + 1) * block]
 
-    def full(query):
+    def sweep(advance, start):
         def body(index, carry):
-            advance(query, *block_of(kv_ref, index, block), None)
+            advance(*block_of(kv_ref, index, block), None)
             return carry
 
-        return body
-
-    query = begin(0)
-    lax.fori_loop(0, shard_pos, full(query), 0)
-    advance(query, *block_of(kv_ref, shard_pos, block), causal(block, columns))
-    finish(0)
-
-    query = begin(block)
-    whole = branch // block
-    lax.fori_loop(0, whole, full(query), 0)
-
-    @pl.when(branch % block != 0)
-    def _():
-        key_pos = lax.broadcasted_iota(jnp.int32, (block, columns), 0)
-        advance(query, *block_of(kv_ref, whole, block), key_pos < branch % block)
-
-    advance(query, own_ref[0, 0], own_ref[1, 0], causal(block, columns))
-    finish(block)
+        if start == 0:
+            lax.fori_loop(0, shard_pos, body, 0)
+            advance(*block_of(kv_ref, shard_pos, block), causal(block, columns))
+        else:
+            lax.fori_loop(0, whole, body, 0)
+
+            @pl.when(branch % block != 0)
+            def _():
+                key_pos = lax.broadcasted_iota(jnp.int32, (block, columns), 0)
+                advance(*block_of(kv_ref, whole, block), key_pos < branch % block)
+
+            advance(own_ref[0, 0], own_ref[1, 0], causal(block, columns))
+
+    def bounded(start, high, low, bound):
+        query = jnp.concatenate([high, low, *split_three(-bound), pad], axis=0)
+
+        def advance(key, value, mask):
+            scores = dot(jnp.concatenate([key, key, ones], axis=0), query, (0, 0))
+            if mask is not None:
+                scores = jnp.where(mask, scores, NEGATIVE)
+            probs = jnp.exp2(scores).astype(BF16)
+            acc_ref[...] += dot(jnp.concatenate([value, ones], axis=0), probs, (1, 0))
+
+        acc_ref[...] = jnp.zeros_like(acc_ref)
+        sweep(advance, start)
+        total = acc_ref[HEAD_SIZE : HEAD_SIZE + 1]
+        emit(start, acc_ref[:HEAD_SIZE] / total, bound + jnp.log2(total))
+
+    def running(start, high, low):
+        query = jnp.concatenate([high, low], axis=0)
+
+        def advance(key, value, mask):
+            scores = dot(jnp.concatenate([key, key], axis=0), query, (0, 0))
+            if mask is not None:
+                scores = jnp.where(mask, scores, NEGATIVE)
+            old = peak_ref[...]
+            new = jnp.maximum(old, jnp.max(scores, axis=0, keepdims=True))
+            probs = jnp.exp2(scores - new).astype(BF16)
+            shrink = jnp.exp2(old - new)
+            part = dot(jnp.concatenate([value, ones], axis=0), probs, (1, 0))
+            peak_ref[...] = new
+            acc_ref[...] = acc_ref[...] * shrink + part
+
+        peak_ref[...] = jnp.full_like(peak_ref, NEGATIVE)
+        acc_ref[...] = jnp.zeros_like(acc_ref)
+        sweep(advance, start)
+        total = acc_ref[HEAD_SIZE : HEAD_SIZE + 1]
+        emit(start, acc_ref[:HEAD_SIZE] / total, peak_ref[...] + jnp.log2(total))
+
+    for start in (0, block):
+        rows, high, low = augment_query(q_ref, start, block)
+        wide = rows.astype(F32)
+        length = jnp.sqrt(jnp.sum(wide * wide, axis=0, keepdims=True))
+        bound = length * longest_key * (1.02 * HEAD_SIZE**-0.5 * LOG2E)
+        safe = jnp.max(bound) < SAFE_BOUND
+
+        @pl.when(safe)
+        def _(start=start, high=high, low=low, bound=bound):
+            bounded(start, high, low, bound)
+
+        @pl.when(jnp.logical_not(safe))
+        def _(start=start, high=high, low=low):
+            running(start, high, low)
 
 
 def attn_forward(where, query, prompt_kv, own_kv):
@@ -154,8 +187,7 @@
         ],
         scratch_shapes=[
             pltpu.VMEM((1, columns), F32),
-            pltpu.VMEM((1, columns), F32),
-            pltpu.VMEM((HEAD_SIZE, columns), F32),
+            pltpu.VMEM((HEAD_SIZE + 16, columns), F32),
         ],
         compiler_params=pltpu.CompilerParams(vmem_limit_bytes=48 * MIB),
         cost_estimate=pl.CostEstimate(
@@ -198,10 +230,11 @@
         if mask is not None:
             scores = jnp.where(mask, scores, NEGATIVE)
         probs = jnp.exp2(scores)
+        dv = dot(grad, probs.astype(BF16), (1, 1))
         grad_probs = dot(jnp.concatenate([value, ones], axis=0), grad_plus, (0, 0))
         grad_scores = (probs * grad_probs).astype(BF16)
         dq_acc[...] += dot(key, grad_scores, (1, 0))
-        return dot(scaled, grad_scores, (1, 1)), dot(grad, probs.astype(BF16), (1, 1))
+        return dot(scaled, grad_scores, (1, 1)), dv
 
     def add(index, state, mask):
         dk, dv = terms(state, *block_of(kv_ref, index, block), mask)
@@ -214,22 +247,27 @@
         for g in range(PER_KEY):
             dq_ref[g, :, start : start + block] = total[:, g * block : (g + 1) * block]
 
-    def full(state):
+    def run(state, count):
         def body(index, carry):
-            add(index, state, None)
+            add(2 * index, state, None)
+            add(2 * index + 1, state, None)
             return carry
 
-        return body
+        lax.fori_loop(0, count // 2, body, 0)
+
+        @pl.when(count % 2 == 1)
+        def _():
+            add(count - 1, state, None)
 
     dkv_acc[...] = jnp.zeros_like(dkv_acc)
     state = begin(0)
-    lax.fori_loop(0, shard_pos, full(state), 0)
+    run(state, shard_pos)
     add(shard_pos, state, causal(block, columns))
     finish(0)
 
     state = begin(block)
     whole = branch // block
-    lax.fori_loop(0, whole, full(state), 0)
+    run(state, whole)
 
     @pl.when(branch % block != 0)
     def _():
@@ -581,7 +619,6 @@
 
 
 ORDER = ((0, 0), (0, 1), (1, 0), (3, 0), (2, 0), (3, 1), (2, 1), (1, 1))
-Y_PLACE = (0, 2, 1, 3)
 
 
 def experts_kernel(
@@ -593,7 +630,10 @@
     dx_own,
     dx_core,
     dx_far,
-    y_all,
+    y_keep,
+    y_give,
+    xt_all,
+    tt_all,
     dgu_all,
     gh_all,
     dg_all,
@@ -601,6 +641,8 @@
     top_buf,
     y_buf,
     dx_buf,
+    xt_buf,
+    tt_buf,
     dgu_buf,
     gh_buf,
     relay,
@@ -674,15 +716,27 @@
     def stores(i):
         kind, h = ORDER[i]
         out = []
-        places = (y_buf, y_all, Y_PLACE[kind]), (dgu_buf, dgu_all, home[kind]), (gh_buf, gh_all, kind)
-        for n, (buffer, target, place) in enumerate(places):
-            out.append(pltpu.make_async_copy(buffer.at[i % 2], half(target, h, place), out_sem.at[i % 2, n]))
+        rows = 2 * tile
+
+        def turned(ref, place):
+            here = pl.multiple_of(place * rows + h * tile, LANES)
+            return ref.at[:, pl.ds(here, tile)]
+
+        targets = (
+            (y_buf, half((y_keep, y_give, y_keep, y_give)[kind], h, (0, 0, 1, 1)[kind])),
+            (dgu_buf, half(dgu_all, h, home[kind])),
+            (gh_buf, half(gh_all, h, kind)),
+            (xt_buf, turned(xt_all, home[kind])),
+            (tt_buf, turned(tt_all, kind)),
+        )
+        for n, (buffer, target) in enumerate(targets):
+            out.append(pltpu.make_async_copy(buffer.at[i % 2], target, out_sem.at[i % 2, n]))
         return out
 
     def store_dx(i):
         kind, h = ORDER[i]
         if kind == 0:
-            return pltpu.make_async_copy(dx_buf.at[i % 2], half(dx_own, h), out_sem.at[i % 2, 3])
+            return pltpu.make_async_copy(dx_buf.at[i % 2], half(dx_own, h), out_sem.at[i % 2, 5])
         return give(kind, h, dx_buf.at[i % 2])
 
     def finish(i):
@@ -741,6 +795,8 @@
 
     x = x_buf[slot]
     top = top_buf[slot]
+    xt_buf[slot] = x.T
+    tt_buf[slot] = top.T
     columns = []
     for e in range(count):
         w_in = w_ref[:, e * 2 * F : (e + 1) * 2 * F]
@@ -825,13 +881,16 @@
         experts_kernel,
         grid=(len(ORDER),),
         in_specs=[anywhere, anywhere, small, fixed],
-        out_specs=[anywhere] * 8,
+        out_specs=[anywhere] * 11,
         out_shape=[
             jax.ShapeDtypeStruct((reps, rows, width), BF16),
             jax.ShapeDtypeStruct((rows, width), BF16),
             jax.ShapeDtypeStruct((rows, width), BF16),
             jax.ShapeDtypeStruct((rows, width), BF16),
-            jax.ShapeDtypeStruct((reps, rows, width), BF16),
+            jax.ShapeDtypeStruct((2, rows, width), BF16),
+            jax.ShapeDtypeStruct((2, rows, width), BF16),
+            jax.ShapeDtypeStruct((width, reps * rows), BF16),
+            jax.ShapeDtypeStruct((width, reps * rows), BF16),
             jax.ShapeDtypeStruct((reps, rows, count * 2 * F), BF16),
             jax.ShapeDtypeStruct((reps, rows, count * F), BF16),
             jax.ShapeDtypeStruct((reps, 8, rows), F32),
@@ -841,6 +900,8 @@
             pltpu.VMEM((2, tile, width), BF16),
             pltpu.VMEM((2, tile, width), BF16),
             pltpu.VMEM((2, tile, width), BF16),
+            pltpu.VMEM((2, width, tile), BF16),
+            pltpu.VMEM((2, width, tile), BF16),
             pltpu.VMEM((2, tile, count * 2 * F), BF16),
             pltpu.VMEM((2, tile, count * F), BF16),
             pltpu.VMEM((2, tile, width), BF16),
@@ -851,7 +912,7 @@
             pltpu.VMEM((8, tile), F32),
             pltpu.VMEM((reps, 8, rows), F32),
             dma((2, 2)),
-            dma((2, 4)),
+            dma((2, 6)),
             dma,
             dma((6, 2)),
             dma((6, 2)),
@@ -1777,14 +1838,14 @@
     gates = jnp.where(chosen, gates, 0.0)
 
     gates_out = jnp.pad(gates.T.reshape(reps, local, count), ((0, 0), (0, 8 - local), (0, 0)))
-    all_normed, dx_own, dx_core, dx_far, y_part, dgu, gated, dgate_part = experts(
+    _, dx_own, dx_core, dx_far, y_keep, y_give, normed_t, top_t, dgu, gated, dgate_part = experts(
         normed_ffn, all_top, gates_out, w_both
     )
     grad_from_experts = dx_own.astype(F32) + dx_core.astype(F32) + dx_far.astype(F32)
     grad_gates = dgate_part[:, :local].reshape(EXPERTS, count).T
     to_core = [(i, i + 1 - 2 * (i % 2)) for i in range(reps)]
     to_far = [(i, (i + 2) % reps) for i in range(reps)]
-    y_near = y_part[:2].astype(F32) + lax.ppermute(y_part[2:], "rep", to_core).astype(F32)
+    y_near = y_keep.astype(F32) + lax.ppermute(y_give, "rep", to_core).astype(F32)
     y_sum = y_near[0] + lax.ppermute(y_near[1].astype(BF16), "rep", to_far).astype(F32)
     block_out = (x_mid + y_sum).astype(BF16)
 
@@ -1794,7 +1855,7 @@
         return values
 
     def expert_term(left, right):
-        return dot(left.reshape(reps * count, width), right.reshape(reps * count, -1), (0, 0)).astype(BF16)
+        return dot(left, right.reshape(reps * count, -1), (1, 0)).astype(BF16)
 
     grad_logits = (gates * (grad_gates - jnp.sum(gates * grad_gates, axis=-1, keepdims=True))).astype(BF16)
     grad_router_w = dot(normed_ffn, grad_logits, (0, 0))
@@ -1807,13 +1868,13 @@
     expert_columns = local * 3 * F
     if fast:
         expert_rows = expert_grads(
-            all_normed.reshape(reps * count, width).T,
-            all_top.reshape(reps * count, width).T,
+            normed_t,
+            top_t,
             dgu.reshape(reps * count, -1),
             gated.reshape(reps * count, -1),
         )
     else:
-        terms = jnp.concatenate([expert_term(all_normed, dgu), expert_term(all_top, gated)], axis=1)
+        terms = jnp.concatenate([expert_term(normed_t, dgu), expert_term(top_t, gated)], axis=1)
         terms = lax.psum_scatter(terms, "shard", scatter_dimension=0, tiled=True)
         expert_rows = lax.all_gather(terms, "rep", axis=0, tiled=False)
     early = jnp.concatenate(
@@ -1821,37 +1882,34 @@
     )
     early = jnp.pad(early, ((0, 0), (0, -early.shape[1] % LANES)))
     grad_attn, early, expert_rows = lax.optimization_barrier((grad_attn, early, expert_rows))
-    early = rep_sum(lax.psum_scatter(early, "shard", scatter_dimension=0, tiled=True))
-    attn_rows, router_rows = early[:, :Q_WIDTH], early[:, Q_WIDTH : Q_WIDTH + EXPERTS]
-    ffn_gain_rows = early[:, Q_WIDTH + EXPERTS]
+    early = lax.psum_scatter(early, "shard", scatter_dimension=0, tiled=True)
 
     delta = jnp.sum(grad_attn.astype(F32) * attn, axis=1).reshape(KEY_VALUE_HEADS, PER_KEY, count)
     grad_query, grad_prompt_kv, grad_own_kv = attn_backward(
         where, query, prompt_kv, own_kv, grad_attn, lse, delta
     )
 
+    early, grad_query, grad_prompt_kv, grad_own_kv = lax.optimization_barrier(
+        (early, grad_query, grad_prompt_kv, grad_own_kv)
+    )
+    early = rep_sum(early)
+    attn_rows, router_rows = early[:, :Q_WIDTH], early[:, Q_WIDTH : Q_WIDTH + EXPERTS]
+    ffn_gain_rows = early[:, Q_WIDTH + EXPERTS]
+
     def turn_back(values, turn):
         spun = rotate(values, turn[0], -turn[1])
         return spun.astype(BF16).reshape(-1, values.shape[-1])
 
     grad_query = turn_back(grad_query, own_turn)
-    grad_prompt_kv = jnp.concatenate(
-        [
-            turn_back(grad_prompt_kv[0].astype(F32), prompt_turn),
-            grad_prompt_kv[1].reshape(KV_WIDTH, GROUP_SIZE * prompt),
-        ],
-        axis=0,
+    grad_prompt_kv = (
+        turn_back(grad_prompt_kv[0].astype(F32), prompt_turn),
+        grad_prompt_kv[1].reshape(KV_WIDTH, GROUP_SIZE * prompt),
     )
-    grad_own_kv = jnp.concatenate(
-        [turn_back(grad_own_kv[0], continued_turn), grad_own_kv[1].astype(BF16).reshape(KV_WIDTH, -1)], axis=0
-    )
-    late = jnp.concatenate(
-        [
-            dot(normed_attn, grad_query, (0, 1)).astype(BF16),
-            (dot(normed_prompt, grad_prompt_kv, (0, 1)) + dot(normed_attn[prompt:], grad_own_kv, (0, 1))).astype(BF16),
-        ],
-        axis=1,
-    )
+    grad_own_kv = (turn_back(grad_own_kv[0], continued_turn), grad_own_kv[1].astype(BF16).reshape(KV_WIDTH, -1))
+    late = [dot(normed_attn, grad_query, (0, 1)).astype(BF16)]
+    for shared, own in zip(grad_prompt_kv, grad_own_kv):
+        late.append((dot(normed_prompt, shared, (0, 1)) + dot(normed_attn[prompt:], own, (0, 1))).astype(BF16))
+    late = jnp.concatenate(late, axis=1)
     if fast:
         qkv_rows = late_reduce(late)
     else:
@@ -1861,12 +1919,11 @@
         qkv_rows.astype(F32) * query_key_value_weight.astype(F32), axis=1
     ) / attn_gain.astype(F32)
 
-    grad_prompt_kv = lax.psum_scatter(
-        grad_prompt_kv, "shard", scatter_dimension=1, tiled=True, axis_index_groups=groups
-    )
-    grad_projected = jnp.concatenate(
-        [grad_query, jnp.concatenate([grad_prompt_kv, grad_own_kv], axis=1)], axis=0
-    )
+    grad_projected = [grad_query]
+    for shared, own in zip(grad_prompt_kv, grad_own_kv):
+        shared = lax.psum_scatter(shared, "shard", scatter_dimension=1, tiled=True, axis_index_groups=groups)
+        grad_projected.append(jnp.concatenate([shared, own], axis=1))
+    grad_projected = jnp.concatenate(grad_projected, axis=0)
     grad_normed_attn = dot(grad_projected, qkv_full, (0, 1))
     grad_x_norm, _ = rms_backward(x_in, attn_scale, attn_gain_full, grad_normed_attn)
     grad_input = grad_mid + grad_x_norm

time: 1250 us -> 1160 us (0.928)
  Pallas kernels: 978 us -> 867 us
  waiting for transfers between devices: 39.5 us -> 98.2 us
  local copies, waits for them, and re-layouts: 65.6 us -> 35.8 us
    pallas_call x1, Pallas kernels: 127 us -> 62.4 us  [attn_backward(): pl.pallas_call(attn_backward_kernel, grid=(query.shape[0] // PER_KEY,), i...]
    all_gather x1, waiting for transfers between devices: 32.1 us -> 81.8 us  [per_device(): w_both = gather(w_both)]
    pallas_call x1, Pallas kernels: 83.7 us -> 34.1 us  [attn_forward(): pl.pallas_call(attn_forward_kernel, grid=(query.shape[0] // PER_KEY,), in...]
    pallas_call x1, Pallas kernels: 136 us -> 174 us  [late_reduce(): pl.pallas_call(late_reduce_kernel, in_specs=[anywhere], out_specs=anywher...]
    pallas_call x1, Pallas kernels: 192 us -> 166 us  [expert_grads(): pl.pallas_call(expert_grads_kernel, in_specs=[anywhere] * 4, out_specs=an...]
    reshape x2 -> x0, local copies, waits for them, and re-layouts: 23.8 us -> none  [the longest x1 11.9 us: per_device(): all_normed.reshape(reps * count, width)]
    dot_general x15 -> x17, matrix products: 76.6 us -> 79.6 us  [dot(): lax.dot_general(left, right, ((dims[:1], dims[1:]), ((), ())), preferred_...]
  transfers between devices with their start and end apart: 7 -> 8, of which waited for: 2 -> 4; matrix products, arithmetic and copies ran while one was open for 11% -> 6% of each run, Pallas kernels for 47% -> 38%
where the time goes in v4:
time: 1160 us; the launch traced here: 1150 us
  Pallas kernels  867 us (75%)
  waiting for transfers between devices  98.2 us (8%)
  matrix products  79.6 us (7%)
  other arithmetic  48.7 us (4%)
  local copies, waits for them, and re-layouts  35.8 us (3%)
  between operations  17.6 us (2%)
    pallas_call x1, Pallas kernels, late_reduce(): pl.pallas_call(late_reduce_kernel, in_specs=[anywhere], out_specs=anywher...  174 us
    pallas_call x1, Pallas kernels, expert_grads(): pl.pallas_call(expert_grads_kernel, in_specs=[anywhere] * 4, out_specs=an...  166 us
    pallas_call x1, Pallas kernels, experts(): pl.pallas_call(experts_kernel, grid=(len(ORDER),), in_specs=[anywhere, an...  149 us
    pallas_call x1, Pallas kernels, start_gather(): pl.pallas_call(start_kernel, in_specs=[anywhere] * 3, out_specs=[anywhere...  112 us
    pallas_call x1, Pallas kernels, summed_step(): pl.pallas_call(step_kernel, in_specs=[pl.BlockSpec(memory_space=pltpu.VME...  91.7 us
    all_gather x1, waiting for transfers between devices, per_device(): w_both = gather(w_both)  81.8 us
    dot_general x17, matrix products, dot(): lax.dot_general(left, right, ((dims[:1], dims[1:]), ((), ())), preferred_...  79.6 us
    pallas_call x1, Pallas kernels, attn_backward(): pl.pallas_call(attn_backward_kernel, grid=(query.shape[0] // PER_KEY,), i...  62.4 us
  transfers between devices with their start and end apart: 8, of which 4 were waited for; matrix products, arithmetic and copies ran while one was open for 6% of the time, Pallas kernels for 38%

profile of v4, /device:TPU:0, one launch (start us, length us, event | category | flops | bytes accessed | tf_op | source)
XLA Modules:
  0.0 1152.1 jit_solution(16620037374495955402)
XLA Ops:
  7.2 0.8 copy.73
  8.0 0.8 copy.74
  8.8 0.8 copy.75
  9.6 1.2 concatenate.79
  10.8 1.0 pad.12.w_ref
  11.8 1.3 constant_dynamic-slice_fusion.1
  13.1 1.1 constant_dynamic-slice_fusion
  14.2 1.3 pad_maximum_fusion.4
  15.4 111.9 %start_gather.1 = (bf16[8,512,1024]{2,1,0:T(8,128)(2,1)}, bf16[8,4,32,3200]{3,2,1,0:T(8,128)(2,1)}, bf16[4,1024,1024]{2,1,0:T(8,128)(2,1)}) custom-call(bf16[1024,1024]{1,0:T(8,128)(2,1)} %bitcast.127, bf16[128,3200]{1,0:T(8,128)(2,1)} %pad.12.w_ref, bf16[1024,1024]{1,0:T(8,128)(2,1)} %bitcast.132), custom_call_target="tpu_custom_call" | custom-call | bytes 67108864 | tf_op jit(solution)/shard_map/start_gather/pallas_call | solution.py:592
  128.1 1.1 slice.146
  129.3 3.2 slice_bitcast_fusion.1
  132.6 3.9 copy.76
  137.2 0.9 negate_bitcast_fusion
  138.7 2.5 fusion.37
  141.5 2.1 convolution_convert_fusion.3
  143.7 1.2 fusion.57
  144.9 2.5 fusion.24
  148.4 1.7 fusion
  150.2 2.7 fusion.47
  152.9 9.2 fusion.39
  162.1 4.7 fusion.19
  166.9 7.0 convolution_convert_fusion
  173.9 3.7 pad_maximum_fusion.kv_ref
  177.6 34.1 %attn_forward.1 = (f32[16,64,1024]{2,1,0:T(8,128)}, f32[8,2,1024]{2,1,0:T(2,128)S(1)}) custom-call(s32[2]{0:T(128)S(1)} %pad_add_fusion.where_ref, bf16[16,64,1024]{2,1,0:T(8,128)(2,1)S(1)} %pad_maximum_fusion.3.q_ref, bf16[2,8,64,4096]{3,2,1,0:T(8,128)(2,1)} %pad_maximum_fusion.kv_ref, bf16[2,8,64,512]{3,2,1,0:T(8,128)(2,1)S(1)} %pad_maximum_fusion.5.own_ref), custom_call_target="tpu_custom_call" | custom-call | flops 17179869184 | bytes 16777216 | tf_op jit(solution)/shard_map/attn_forward/pallas_call | solution.py:171
  211.7 2.6 convert_element_type.289
  214.4 4.8 multiply_reduce_fusion.3
  219.7 1.9 fusion.58
  223.6 81.8 %all-gather.2.cloned.1.call-done.w_ref = bf16[1024,6144]{1,0:T(8,128)(2,1)} async-done(((bf16[128,6144]{1,0:T(8,128)(2,1)}), bf16[1024,6144]{1,0:T(8,128)(2,1)}) %all-gather.2.cloned.1.call-update) | async-done | bytes 12582928 | tf_op jit(solution)/shard_map/all_gather | solution.py:1793
  305.3 149.2 %experts.1 = (bf16[4,1024,1024]{2,1,0:T(8,128)(2,1)}, bf16[1024,1024]{1,0:T(8,128)(2,1)}, bf16[1024,1024]{1,0:T(8,128)(2,1)}, bf16[1024,1024]{1,0:T(8,128)(2,1)}...) custom-call(bf16[1024,1024]{1,0:T(8,128)(2,1)} %copy-done.14, ...), custom_call_target="tpu_custom_call" | custom-call | flops 103079215104 | bytes 83886080 | tf_op jit(solution)/shard_map/experts/pallas_call | solution.py:880
  454.7 7.2 collective-permute-done
  462.0 4.2 convert_add_fusion
  466.1 3.4 copy-done.12
  469.5 1.6 fusion.22
  471.2 1.6 collective-permute-start.1
  472.8 165.9 %expert_grads.1.refs_2_.refs_3_ = bf16[4,128,6144]{2,1,0:T(8,128)(2,1)} custom-call(bf16[1024,4096]{1,0:T(8,128)(2,1)} %get-tuple-element.59.xt_ref, bf16[1024,4096]{1,0:T(8,128)(2,1)} %get-tuple-element.60.tt_ref, bf16[4096,4096]{1,0:T(8,128)(2,1)} %bitcast.184, bf16[4096,2048]{1,0:T(8,128)(2,1)} %bitcast.185), custom_call_target="tpu_custom_call" | custom-call | flops 51539607552 | bytes 83886080 | tf_op jit(solution)/shard_map/expert_grads/pallas_call | solution.py:1163
  639.5 5.4 multiply_reduce_fusion.1
  645.2 2.1 copy-done.13
  647.9 4.5 subtract_add_fusion
  652.4 3.7 convolution_convert_fusion.1
  656.1 5.3 convolution_convert_fusion.2
  661.5 3.8 concatenate.89
  665.2 1.6 pad.14
  667.1 3.7 multiply_reduce_fusion
  671.4 62.4 %attn_backward.1 = (f32[16,64,1024]{2,1,0:T(8,128)}, bf16[2,8,64,4096]{3,2,1,0:T(8,128)(2,1)}, f32[2,8,64,512]{3,2,1,0:T(8,128)}) custom-call(s32[2]{0:T(128)} %copy-done.5, bf16[16,64,1024]{2,1,0:T(8,128)(2,1)} %copy-done.2, bf16[2,8,64,4096]{3,2,1,0:T(8,128)(2,1)} %pad_maximum_fusion.kv_ref, bf16[2,8,64,512]{3,2,1,0:T(8,128)(2,1)} %copy-done.3, ...), custom_call_target="tpu_custom_call" | custom-call | flops 42949672960 | bytes 33554432 | tf_op jit(solution)/shard_map/attn_backward/pallas_call | solution.py:293
  733.8 1.3 reduce-scatter.4.cloned.1.call-done
  735.2 1.3 slice_bitcast_fusion.2
  736.5 1.3 slice.258
  737.8 3.1 multiply_subtract_fusion
  741.2 4.0 fusion.28
  745.7 3.2 bitcast_convert_fusion
  748.9 1.3 subtract_convert_fusion
  750.3 2.5 pad_maximum_fusion.1
  752.8 11.1 fusion.63
  763.9 10.1 fusion.61
  775.1 0.8 add_convert_fusion.2
  776.6 173.7 %late_reduce.1.refs_0_ = bf16[128,2048]{1,0:T(8,128)(2,1)S(1)} custom-call(bf16[1024,2048]{1,0:T(8,128)(2,1)S(1)} %pad_maximum_fusion.2.in_ref), custom_call_target="tpu_custom_call" | custom-call | bytes 16777216 | tf_op jit(solution)/shard_map/late_reduce/pallas_call | solution.py:1305
  952.1 16.9 %flatten.3 = (f32[1,3541248]{1,0:T(1,128)}, f32[1,1]{1,0:T(1,128)}) custom-call(f32[18,128]{1,0:T(8,128)S(1)} %pad_maximum_fusion.8.lead_ref, bf16[128,2048]{1,0:T(8,128)(2,1)S(1)} %copy-done, bf16[128,1024]{1,0:T(8,128)(2,1)S(1)} %copy-done.4, bf16[128,16384]{1,0:T(8,128)(2,1)} %refs_2_.1, bf16[128,8192]{1,0:T(8,128)(2,1)S(1)} %copy-done.1), custom_call_target="tpu_custom_call" | custom-call | tf_op jit(solution)/shard_map/flatten/pallas_call | solution.py:1403
  969.1 2.7 collective-permute-start.3
  972.0 7.3 collective-permute-done.3
  979.6 17.1 %flatten.2 = (f32[1,3541248]{1,0:T(1,128)}, f32[1,1]{1,0:T(1,128)}) custom-call(f32[18,128]{1,0:T(8,128)S(1)} %pad_maximum_fusion.7.lead_ref, bf16[128,2048]{1,0:T(8,128)(2,1)S(1)} %late_reduce.1.refs_0_, bf16[128,1024]{1,0:T(8,128)(2,1)S(1)} %slice.172.refs_1_, bf16[4,128,6144]{2,1,0:T(8,128)(2,1)} %expert_grads.1.refs_2_.refs_3_, ...), custom_call_target="tpu_custom_call" | custom-call | tf_op jit(solution)/shard_map/flatten/pallas_call | solution.py:1403
  996.7 91.7 %summed_step.1 = (f32[1,1]{1,0:T(1,128)}, bf16[2,13840,128]{2,1,0:T(8,128)(2,1)}) custom-call(f32[1,1]{1,0:T(1,128)} %get-tuple-element.78.square_ref, f32[1,3541248]{1,0:T(1,128)} %get-tuple-element.136.g_ref.g, f32[1,1,3541248]{2,1,0:T(1,128)} %f.1, f32[1,1,3541248]{2,1,0:T(1,128)} %s.1, f32[1,3541248]{1,0:T(1,128)} %get-tuple-element.79.w_ref), custom_call_target="tpu_custom_call" | custom-call | bytes 67108864 | tf_op jit(solution)/shard_map/summed_step/pallas_call | solution.py:1614
  1088.5 44.1 %update.1 = (f32[1,1,3541248]{2,1,0:T(1,128)}, f32[1,1,3541248]{2,1,0:T(1,128)}, f32[1,3541248]{1,0:T(1,128)}, f32[1,3541248]{1,0:T(1,128)}) custom-call(f32[1,1]{1,0:T(1,128)} %get-tuple-element.80.norm_ref, f32[1,3541248]{1,0:T(1,128)} %get-tuple-element.136.g_ref.g, f32[1,1,3541248]{2,1,0:T(1,128)} %f.1, f32[1,1,3541248]{2,1,0:T(1,128)} %s.1, ...), custom_call_target="tpu_custom_call" | custom-call | bytes 125829120 | tf_op jit(solution)/shard_map/update/pallas_call | solution.py:1695
  1132.6 8.0 fusion.4
  1140.6 3.0 add_bitcast_fusion
  (200 shorter events, 12.8 us)
Async XLA Ops:
  7.2 298.2 %all-gather.2.cloned.1.call-start = ((), (), s32[]{:S(2)}) async-start(), calls=%async_computation.3 | async-start | bytes 14155776 | tf_op jit(solution)/shard_map/all_gather | solution.py:1793
  127.4 607.8 %reduce-scatter.4.cloned.1.call-start = ((), (), s32[]{:S(2)}) async-start(), calls=%async_computation.4 | async-start | bytes 2654208 | tf_op jit(solution)/shard_map/reduce_scatter | solution.py:1885
  129.3 7.3 copy-start.9
  136.6 41.0 %copy-start.5 = (s32[2]{0:T(128)}, s32[2]{0:T(128)S(1)}, u32[]{:S(2)}) copy-start(s32[2]{0:T(128)S(1)} %pad_add_fusion.where_ref) | copy-start | bytes 28
  137.1 7.8 copy-start.55
  137.1 29.7 %copy-start.53 = (f32[1024,1]{0,1:T(1,128)}, f32[1024,1]{0,1:T(1,128)S(1)}, u32[]{:S(2)}) copy-start(f32[1024,1]{0,1:T(1,128)S(1)} %get-tuple-element.105) | copy-start | bytes 12292
  137.1 82.1 %copy-start.51 = (f32[1024,1]{0,1:T(1,128)}, f32[1024,1]{0,1:T(1,128)S(1)}, u32[]{:S(2)}) copy-start(f32[1024,1]{0,1:T(1,128)S(1)} %get-tuple-element.104) | copy-start | bytes 12292
  138.1 3.1 copy-start.40
  138.7 4.8 copy-start.18
  141.3 3.6 copy-start.30
  143.7 33.9 %copy-start.3 = (bf16[2,8,64,512]{3,2,1,0:T(8,128)(2,1)}, bf16[2,8,64,512]{3,2,1,0:T(8,128)(2,1)S(1)}, u32[]{:S(2)}) copy-start(bf16[2,8,64,512]{3,2,1,0:T(8,128)(2,1)S(1)} %pad_maximum_fusion.5.own_ref) | copy-start | bytes 3145732
  144.9 2.5 copy-start.36
  144.9 3.5 slice-start
  144.9 3.5 slice-start.1
  148.4 29.2 %copy-start.2 = (bf16[16,64,1024]{2,1,0:T(8,128)(2,1)}, bf16[16,64,1024]{2,1,0:T(8,128)(2,1)S(1)}, u32[]{:S(2)}) copy-start(bf16[16,64,1024]{2,1,0:T(8,128)(2,1)S(1)} %pad_maximum_fusion.3.q_ref) | copy-start | bytes 6291460
  150.2 16.7 %copy-start.60 = (f32[4096]{0:T(1024)}, f32[4096]{0:T(1024)S(1)}, u32[]{:S(2)}) copy-start(f32[4096]{0:T(1024)S(1)} %add_rsqrt_fusion) | copy-start | bytes 49156
  152.9 9.2 copy-start.21
  211.7 7.5 copy-start.6
  211.7 2.6 copy-start.57
  214.3 5.0 copy-start.23
  214.4 7.3 copy-start.38
  219.3 2.3 copy-start.7
  219.7 85.6 %copy-start.14 = (bf16[1024,1024]{1,0:T(8,128)(2,1)}, bf16[1024,1024]{1,0:T(8,128)(2,1)S(1)}, u32[]{:S(2)}) copy-start(bf16[1024,1024]{1,0:T(8,128)(2,1)S(1)} %multiply_convert_fusion.x_hbm) | copy-start | bytes 6291460
  454.5 7.4 collective-permute-start
  466.1 3.4 copy-start.12
  471.2 174.0 %collective-permute-start.1 = (bf16[1024,1024]{1,0:T(8,128)(2,1)}, bf16[1024,1024]{1,0:T(8,128)(2,1)}, u32[]{:S(2)}, u32[]{:S(2)}) collective-permute-start(bf16[1024,1024]{1,0:T(8,128)(2,1)} %fusion.22), channel_id=1, source_target_pairs={{0,2},{1,3},{2,0},{3,1},{4,6},{5,7},{6,4},{7,5},{8,10},{9,11},{10,... | collective-permute-start | bytes 6291464 | tf_op jit(solution)/shard_map/ppermute | solution.py:1849
  472.7 166.0 %copy-start.58 = (f32[4,8,1024]{2,1,0:T(8,128)S(1)}, f32[4,8,1024]{2,1,0:T(8,128)}, u32[]{:S(2)}) copy-start(f32[4,8,1024]{2,1,0:T(8,128)} %get-tuple-element.58) | copy-start | bytes 393220
  472.8 166.0 %copy-start.35 = (f32[1024,16]{0,1:T(8,128)S(1)}, f32[1024,16]{0,1:T(8,128)}, u32[]{:S(2)}) copy-start(f32[1024,16]{0,1:T(8,128)} %copy-done.34) | copy-start | bytes 196612
  472.8 166.0 %copy-start.39 = (pred[1024,16]{0,1:T(8,128)(4,1)S(1)}, pred[1024,16]{0,1:T(8,128)(4,1)}, u32[]{:S(2)}) copy-start(pred[1024,16]{0,1:T(8,128)(4,1)} %copy-done.38) | copy-start | bytes 49156
  472.8 166.0 %copy-start.46 = (f32[1024]{0:T(1024)S(1)}, f32[1024]{0:T(1024)}, u32[]{:S(2)}) copy-start(f32[1024]{0:T(1024)} %copy-done.45) | copy-start | bytes 12292
  472.8 166.1 %copy-start.48 = (f32[1024]{0:T(1024)S(1)}, f32[1024]{0:T(1024)}, u32[]{:S(2)}) copy-start(f32[1024]{0:T(1024)} %copy-done.47) | copy-start | bytes 12292
  472.8 166.1 %copy-start.15 = (bf16[1024,1024]{1,0:T(8,128)(2,1)S(1)}, bf16[1024,1024]{1,0:T(8,128)(2,1)}, u32[]{:S(2)}) copy-start(bf16[1024,1024]{1,0:T(8,128)(2,1)} %copy-done.14) | copy-start | bytes 6291460
  472.8 166.7 %copy-start.50 = (f32[1024]{0:T(1024)S(1)}, f32[1024]{0:T(1024)}, u32[]{:S(2)}) copy-start(f32[1024]{0:T(1024)} %copy-done.49) | copy-start | bytes 12292
  472.8 166.7 %copy-start.52 = (f32[1024,1]{0,1:T(1,128)S(1)}, f32[1024,1]{0,1:T(1,128)}, u32[]{:S(2)}) copy-start(f32[1024,1]{0,1:T(1,128)} %copy-done.51) | copy-start | bytes 12292
  639.5 5.7 copy-start.8
  639.5 7.8 copy-start.13
  639.5 8.4 copy-start.20
  647.9 4.5 copy-start.24
  652.4 3.7 copy-start.16
  666.8 465.7 %reduce-scatter.6.cloned.1.call-start = ((), (), s32[]{:S(2)}) async-start(), calls=%async_computation.5 | async-start | bytes 4718592 | tf_op jit(solution)/shard_map/reduce_scatter | solution.py:1924
  671.4 66.4 %copy-start.37 = (f32[32,1024]{1,0:T(8,128)S(1)}, f32[32,1024]{1,0:T(8,128)}, u32[]{:S(2)}) copy-start(f32[32,1024]{1,0:T(8,128)} %copy-done.36) | copy-start | bytes 393220
  671.4 66.4 %copy-start.42 = (f32[32,1024]{1,0:T(8,128)S(1)}, f32[32,1024]{1,0:T(8,128)}, u32[]{:S(2)}) copy-start(f32[32,1024]{1,0:T(8,128)} %get-tuple-element.112) | copy-start | bytes 393220
  737.8 37.4 %copy-start.25 = (bf16[1,8,64,512]{3,2,1,0:T(8,128)(2,1)}, bf16[1,8,64,512]{3,2,1,0:T(8,128)(2,1)S(1)}, u32[]{:S(2)}) copy-start(bf16[1,8,64,512]{3,2,1,0:T(8,128)(2,1)S(1)} %slice.258) | copy-start | bytes 1572868
  737.8 3.4 copy-start.10
  737.8 3.4 copy-start.54
  737.8 3.4 copy-start.56
  740.9 4.3 slice-start.2
  741.2 4.1 copy-start.29
  741.2 4.5 slice-start.3
  745.7 3.2 copy-start.22
  745.7 3.2 copy-start.33
  750.3 2.5 copy-start.61
  763.9 10.2 copy-start.41
  763.9 10.2 copy-start.44
  763.9 10.4 copy-start.19
  763.9 10.4 copy-start.31
  950.4 182.2 %reduce-scatter.8.cloned.1.call-start = ((), (), s32[]{:S(2)}) async-start(), calls=%async_computation.6 | async-start | bytes 4718592 | tf_op jit(solution)/shard_map/reduce_scatter | solution.py:1924
  951.1 17.8 %copy-start.43 = (bf16[128,1152]{1,0:T(8,128)(2,1)S(1)}, bf16[128,1152]{1,0:T(8,128)(2,1)}, u32[]{:S(2)}) copy-start(bf16[128,1152]{1,0:T(8,128)(2,1)} %reduce-scatter.4.cloned.1.call-done) | copy-start | bytes 884740
  951.1 17.8 %collective-permute-start.2 = (bf16[128,1152]{1,0:T(8,128)(2,1)}, bf16[128,1152]{1,0:T(8,128)(2,1)S(1)}, u32[]{:S(2)}, u32[]{:S(2)}) collective-permute-start(bf16[128,1152]{1,0:T(8,128)(2,1)} %reduce-scatter.4.cloned.1.call-done), channel_id=1, source_target_pairs={{0,1},{1,0},{2,3},{3,2},{4,5},{5,4},{6,7},{7,6},{8,9},{9,8},{10,11... | collective-permute-start | bytes 884744 | tf_op jit(solution)/shard_map/ppermute | solution.py:1854
  969.1 10.2 collective-permute-start.3
  1088.4 44.2 %copy-start.11 = (bf16[1,1,1024,1024]{3,2,1,0:T(8,128)(2,1)S(1)}, bf16[1,1,1024,1024]{3,2,1,0:T(8,128)(2,1)}, u32[]{:S(2)}) copy-start(bf16[1,1,1024,1024]{3,2,1,0:T(8,128)(2,1)} %param.14) | copy-start | bytes 6291460
  1088.4 44.2 %copy-start.26 = (bf16[1,8,64,512]{3,2,1,0:T(8,128)(2,1)S(1)}, bf16[1,8,64,512]{3,2,1,0:T(8,128)(2,1)}, u32[]{:S(2)}) copy-start(bf16[1,8,64,512]{3,2,1,0:T(8,128)(2,1)} %copy-done.25) | copy-start | bytes 1572868
  1088.4 44.2 %copy-start.28 = (bf16[8,64,512]{2,1,0:T(8,128)(2,1)S(1)}, bf16[8,64,512]{2,1,0:T(8,128)(2,1)}, u32[]{:S(2)}) copy-start(bf16[8,64,512]{2,1,0:T(8,128)(2,1)} %copy-done.27) | copy-start | bytes 1572868
  1132.6 8.0 copy-start.17
  (12 other events, 14.8 us)
Sparse Core Ops, SparseCore 0:
  127.5 177.7 all-gather.1
  667.0 68.1 reduce-scatter.3
  950.5 86.8 reduce-scatter.5
  1041.9 88.1 reduce-scatter.7

commit v5 on v4

--- a/solution.py
+++ b/solution.py
@@ -90,7 +90,7 @@
 
     def emit(start, result, lse):
         for g in range(PER_KEY):
-            o_ref[g, :, start : start + block] = result[:, g * block : (g + 1) * block]
+            o_ref[g, :, start : start + block] = result[:, g * block : (g + 1) * block].astype(BF16)
             lse_ref[0, g : g + 1, start : start + block] = lse[:, g * block : (g + 1) * block]
 
     def sweep(advance, start):
@@ -182,7 +182,7 @@
             pl.BlockSpec((1, PER_KEY, tokens), lambda h: (h, 0, 0)),
         ],
         out_shape=[
-            jax.ShapeDtypeStruct(query.shape, F32),
+            jax.ShapeDtypeStruct(query.shape, BF16),
             jax.ShapeDtypeStruct((query.shape[0] // PER_KEY, PER_KEY, tokens), F32),
         ],
         scratch_shapes=[
@@ -200,7 +200,7 @@
 
 
 def attn_backward_kernel(
-    where_ref, q_ref, kv_ref, own_ref, go_ref, lse_ref, delta_ref, dq_ref, dkv_ref, down_ref, dkv_acc, dq_acc
+    where_ref, q_ref, kv_ref, own_ref, go_ref, o_ref, lse_ref, dq_ref, dkv_ref, down_ref, dkv_acc, dq_acc
 ):
     block = own_ref.shape[-1]
     columns = PER_KEY * block
@@ -216,8 +216,11 @@
             return jnp.concatenate([ref[0, g : g + 1, start : start + block] for g in range(PER_KEY)], axis=1)
 
         lse = split_three(-lanes(lse_ref))
-        delta = split_three(-lanes(delta_ref))
-        grad = jnp.concatenate([go_ref[g, :, start : start + block] for g in range(PER_KEY)], axis=1)
+        grad, out = (
+            jnp.concatenate([ref[g, :, start : start + block] for g in range(PER_KEY)], axis=1)
+            for ref in (go_ref, o_ref)
+        )
+        delta = split_three(-jnp.sum(grad.astype(F32) * out.astype(F32), axis=0, keepdims=True))
         query = jnp.concatenate([high, low, *lse, pad], axis=0)
         grad_plus = jnp.concatenate([grad, *delta, pad], axis=0)
         dq_acc[...] = jnp.zeros_like(dq_acc)
@@ -281,7 +284,7 @@
     dkv_ref[:, 0] = dkv_acc[...].astype(BF16)
 
 
-def attn_backward(where, query, prompt_kv, own_kv, grad_out, lse, delta):
+def attn_backward(where, query, prompt_kv, own_kv, grad_out, out, lse):
     tokens = query.shape[-1]
     block = own_kv.shape[-1]
     columns = PER_KEY * block
@@ -293,7 +296,7 @@
     return pl.pallas_call(
         attn_backward_kernel,
         grid=(query.shape[0] // PER_KEY,),
-        in_specs=[pl.BlockSpec(memory_space=pltpu.SMEM), by_head, by_keys, by_own, by_head, by_row, by_row],
+        in_specs=[pl.BlockSpec(memory_space=pltpu.SMEM), by_head, by_keys, by_own, by_head, by_head, by_row],
         out_specs=[by_head, by_keys, by_own],
         out_shape=[
             jax.ShapeDtypeStruct(query.shape, F32),
@@ -311,7 +314,7 @@
             transcendentals=query.shape[0] * tokens * keys,
         ),
         name="attn_backward",
-    )(where, query, prompt_kv, own_kv, grad_out, lse, delta)
+    )(where, query, prompt_kv, own_kv, grad_out, out, lse)
 
 
 MESH = pl.DeviceIdType.MESH
@@ -1826,8 +1829,24 @@
     own_kv = keys_values(normed_attn[prompt:], continued_turn)
     query = project(normed_attn, 0, Q_WIDTH, own_turn)
     where = jnp.stack([shard_pos.astype(jnp.int32), branch_len])
+    if flat_path:
+        size = outer_mom.shape[-1]
+
+        def lead(first, second, rest):
+            parts = [first[None].astype(F32), second[None].astype(F32), rest.reshape(-1, LANES).astype(F32)]
+            return jnp.concatenate(parts, axis=0)
+
+        def whole(values):
+            return values, values.shape[-1], 0
+
+        weight_flat, _ = flatten(
+            size,
+            lead(attn_gain, ffn_gain, w_router),
+            [whole(query_key_value_weight), whole(w_attn_out), whole(w_in), whole(w_out)],
+        )
+        weight_flat, query = lax.optimization_barrier((weight_flat, query))
     attn, lse = attn_forward(where, query, prompt_kv, own_kv)
-    attn_low = attn.astype(BF16).reshape(Q_WIDTH, count)
+    attn_low = attn.reshape(Q_WIDTH, count)
     x_mid = x_in + dot(attn_low, attn_out_full, (0, 1))
 
     ffn_scale = rms_scale(x_mid)
@@ -1845,10 +1864,6 @@
     grad_gates = dgate_part[:, :local].reshape(EXPERTS, count).T
     to_core = [(i, i + 1 - 2 * (i % 2)) for i in range(reps)]
     to_far = [(i, (i + 2) % reps) for i in range(reps)]
-    y_near = y_keep.astype(F32) + lax.ppermute(y_give, "rep", to_core).astype(F32)
-    y_sum = y_near[0] + lax.ppermute(y_near[1].astype(BF16), "rep", to_far).astype(F32)
-    block_out = (x_mid + y_sum).astype(BF16)
-
     def rep_sum(values):
         for pairs in (to_core, to_far):
             values = (values.astype(F32) + lax.ppermute(values, "rep", pairs).astype(F32)).astype(BF16)
@@ -1877,24 +1892,26 @@
         terms = jnp.concatenate([expert_term(normed_t, dgu), expert_term(top_t, gated)], axis=1)
         terms = lax.psum_scatter(terms, "shard", scatter_dimension=0, tiled=True)
         expert_rows = lax.all_gather(terms, "rep", axis=0, tiled=False)
+    y_keep, y_give, expert_rows = lax.optimization_barrier((y_keep, y_give, expert_rows))
+    y_near = y_keep.astype(F32) + lax.ppermute(y_give, "rep", to_core).astype(F32)
+    y_sum = y_near[0] + lax.ppermute(y_near[1].astype(BF16), "rep", to_far).astype(F32)
+    block_out = (x_mid + y_sum).astype(BF16)
+
+    blank = jnp.zeros((width, -(Q_WIDTH + EXPERTS + 1) % LANES), BF16)
     early = jnp.concatenate(
-        [grad_attn_w.astype(BF16), grad_router_w.astype(BF16), grad_ffn_gain[:, None].astype(BF16)], axis=1
+        [grad_attn_w.astype(BF16), grad_router_w.astype(BF16), grad_ffn_gain[:, None].astype(BF16), blank], axis=1
     )
-    early = jnp.pad(early, ((0, 0), (0, -early.shape[1] % LANES)))
     grad_attn, early, expert_rows = lax.optimization_barrier((grad_attn, early, expert_rows))
     early = lax.psum_scatter(early, "shard", scatter_dimension=0, tiled=True)
 
-    delta = jnp.sum(grad_attn.astype(F32) * attn, axis=1).reshape(KEY_VALUE_HEADS, PER_KEY, count)
     grad_query, grad_prompt_kv, grad_own_kv = attn_backward(
-        where, query, prompt_kv, own_kv, grad_attn, lse, delta
+        where, query, prompt_kv, own_kv, grad_attn, attn, lse
     )
 
     early, grad_query, grad_prompt_kv, grad_own_kv = lax.optimization_barrier(
         (early, grad_query, grad_prompt_kv, grad_own_kv)
     )
     early = rep_sum(early)
-    attn_rows, router_rows = early[:, :Q_WIDTH], early[:, Q_WIDTH : Q_WIDTH + EXPERTS]
-    ffn_gain_rows = early[:, Q_WIDTH + EXPERTS]
 
     def turn_back(values, turn):
         spun = rotate(values, turn[0], -turn[1])
@@ -1910,6 +1927,9 @@
     for shared, own in zip(grad_prompt_kv, grad_own_kv):
         late.append((dot(normed_prompt, shared, (0, 1)) + dot(normed_attn[prompt:], own, (0, 1))).astype(BF16))
     late = jnp.concatenate(late, axis=1)
+    late, early = lax.optimization_barrier((late, early))
+    attn_rows, router_rows = early[:, :Q_WIDTH], early[:, Q_WIDTH : Q_WIDTH + EXPERTS]
+    ffn_gain_rows = early[:, Q_WIDTH + EXPERTS]
     if fast:
         qkv_rows = late_reduce(late)
     else:
@@ -1930,20 +1950,6 @@
 
     in_columns = local * 2 * F
     if flat_path:
-        size = outer_mom.shape[-1]
-
-        def lead(first, second, rest):
-            parts = [first[None].astype(F32), second[None].astype(F32), rest.reshape(-1, LANES).astype(F32)]
-            return jnp.concatenate(parts, axis=0)
-
-        def whole(values):
-            return values, values.shape[-1], 0
-
-        weight_flat, _ = flatten(
-            size,
-            lead(attn_gain, ffn_gain, w_router),
-            [whole(query_key_value_weight), whole(w_attn_out), whole(w_in), whole(w_out)],
-        )
         total_grad, square = flatten(
             size,
             lead(attn_gain_rows, ffn_gain_rows, router_rows),

time: 1160 us -> 1200 us (1.034)
  waiting for transfers between devices: 98.2 us -> 125 us
  Pallas kernels: 867 us -> 885 us
    ppermute x1, waiting for transfers between devices: 0.01 us -> 41.2 us  [per_device(): lax.ppermute(y_near[1].astype(BF16), 'rep', to_far).astype(F32)]
    all_gather x1, waiting for transfers between devices: 81.8 us -> 45.1 us  [per_device(): w_both = gather(w_both)]
    pallas_call x1, Pallas kernels: 62.4 us -> 85.8 us  [attn_backward(): pl.pallas_call(attn_backward_kernel, grid=(query.shape[0] // PER_KEY,), i...]
    reduce_scatter x2, waiting for transfers between devices: 0.04 us -> 22.7 us  [per_device(): lax.psum_scatter(shared, 'shard', scatter_dimension=1, tiled=True, axis_i...]
    pallas_call x1, Pallas kernels: 174 us -> 152 us  [late_reduce(): pl.pallas_call(late_reduce_kernel, in_specs=[anywhere], out_specs=anywher...]
  transfers between devices with their start and end apart: 8 -> 8, of which waited for: 4 -> 5; matrix products, arithmetic and copies ran while one was open for 6% -> 10% of each run, Pallas kernels for 38% -> 25%
where the time goes in v5:
time: 1200 us
  Pallas kernels  885 us (74%)
  waiting for transfers between devices  125 us (10%)
  matrix products  84.8 us (7%)
  other arithmetic  52.4 us (4%)
  local copies, waits for them, and re-layouts  33.2 us (3%)
  between operations  17.7 us (1%)
    pallas_call x1, Pallas kernels, expert_grads(): pl.pallas_call(expert_grads_kernel, in_specs=[anywhere] * 4, out_specs=an...  173 us
    pallas_call x1, Pallas kernels, late_reduce(): pl.pallas_call(late_reduce_kernel, in_specs=[anywhere], out_specs=anywher...  152 us
    pallas_call x1, Pallas kernels, experts(): pl.pallas_call(experts_kernel, grid=(len(ORDER),), in_specs=[anywhere, an...  149 us
    pallas_call x1, Pallas kernels, start_gather(): pl.pallas_call(start_kernel, in_specs=[anywhere] * 3, out_specs=[anywhere...  112 us
    pallas_call x1, Pallas kernels, summed_step(): pl.pallas_call(step_kernel, in_specs=[pl.BlockSpec(memory_space=pltpu.VME...  90.1 us
    pallas_call x1, Pallas kernels, attn_backward(): pl.pallas_call(attn_backward_kernel, grid=(query.shape[0] // PER_KEY,), i...  85.8 us
    dot_general x17, matrix products, dot(): lax.dot_general(left, right, ((dims[:1], dims[1:]), ((), ())), preferred_...  84.8 us
    all_gather x1, waiting for transfers between devices, per_device(): w_both = gather(w_both)  45.1 us
  transfers between devices with their start and end apart: 8, of which 5 were waited for; matrix products, arithmetic and copies ran while one was open for 10% of the time, Pallas kernels for 25%

profile of v5, /device:TPU:0, one launch (start us, length us, event | category | flops | bytes accessed | tf_op | source)
XLA Modules:
  0.0 1198.8 jit_solution(17344169305025822936)
XLA Ops:
  7.2 0.9 copy.74
  8.2 0.8 copy.75
  9.0 0.8 copy.76
  9.7 1.2 concatenate.80
  11.0 1.0 pad.8.w_ref
  11.9 2.3 constant_dynamic-slice_fusion.1
  14.3 2.5 pad_maximum_fusion.4
  16.8 111.9 %start_gather.1 = (bf16[8,512,1024]{2,1,0:T(8,128)(2,1)}, bf16[8,4,32,3200]{3,2,1,0:T(8,128)(2,1)}, bf16[4,1024,1024]{2,1,0:T(8,128)(2,1)}) custom-call(bf16[1024,1024]{1,0:T(8,128)(2,1)} %bitcast.129, bf16[128,3200]{1,0:T(8,128)(2,1)} %pad.8.w_ref, bf16[1024,1024]{1,0:T(8,128)(2,1)} %bitcast.134), custom_call_target="tpu_custom_call" | custom-call | bytes 67108864 | tf_op jit(solution)/shard_map/start_gather/pallas_call | solution.py:595
  129.6 1.1 slice.146
  130.8 3.2 slice_bitcast_fusion.1
  134.0 3.9 copy.77
  138.1 17.0 %flatten.2 = (f32[1,3541248]{1,0:T(1,128)}, f32[1,1]{1,0:T(1,128)}) custom-call(f32[18,128]{1,0:T(8,128)S(1)} %pad_maximum_fusion.7.lead_ref, bf16[128,2048]{1,0:T(8,128)(2,1)S(1)} %copy-done, bf16[128,1024]{1,0:T(8,128)(2,1)S(1)} %copy-done.4, bf16[128,16384]{1,0:T(8,128)(2,1)} %refs_2_.1, bf16[128,8192]{1,0:T(8,128)(2,1)S(1)} %copy-done.1), custom_call_target="tpu_custom_call" | custom-call | tf_op jit(solution)/shard_map/flatten/pallas_call | solution.py:1406
  155.1 2.1 fusion.3
  157.3 1.2 fusion.57
  158.5 4.7 fusion.24
  164.5 1.1 negate_bitcast_fusion
  166.1 2.4 fusion.37
  168.7 2.0 convolution_convert_fusion.3
  170.8 5.5 fusion
  176.3 2.9 fusion.47
  179.3 12.6 %fusion.39 = f32[512,4096]{1,0:T(8,128)} fusion(bf16[1024,3200]{1,0:T(8,128)(2,1)} %bitcast.155, bf16[4096,1024]{1,0:T(8,128)(2,1)} %bitcast.136, f32[1024]{0:T(1024)S(1)} %bitcast.169, f32[4096]{0:T(1024)S(1)} %add_rsqrt_fusion), kind=kOutput, calls=%fused_computation.82 | convolution fusion | flops 4311744512 | bytes 17846272 | tf_op jit(solution)/shard_map/dot_general | solution.py:43
  191.8 4.7 fusion.19
  196.6 8.1 convolution_convert_fusion
  204.6 3.7 pad_maximum_fusion.kv_ref
  208.3 43.9 %attn_forward.1 = (bf16[16,64,1024]{2,1,0:T(8,128)(2,1)S(1)}, f32[8,2,1024]{2,1,0:T(2,128)S(1)}) custom-call(s32[2]{0:T(128)S(1)} %pad_add_fusion.where_ref, bf16[16,64,1024]{2,1,0:T(8,128)(2,1)S(1)} %pad_maximum_fusion.3.q_ref, bf16[2,8,64,4096]{3,2,1,0:T(8,128)(2,1)} %pad_maximum_fusion.kv_ref, bf16[2,8,64,512]{3,2,1,0:T(8,128)(2,1)S(1)} %pad_maximum_fusion.5.own_ref), custom_call_target="tpu_custom_call" | custom-call | flops 17179869184 | bytes 16777216 | tf_op jit(solution)/shard_map/attn_forward/pallas_call | solution.py:171
  252.3 5.0 multiply_reduce_fusion.2
  257.8 1.8 fusion.58
  261.6 45.1 %all-gather.2.cloned.1.call-done.w_ref = bf16[1024,6144]{1,0:T(8,128)(2,1)} async-done(((bf16[128,6144]{1,0:T(8,128)(2,1)}), bf16[1024,6144]{1,0:T(8,128)(2,1)}) %all-gather.2.cloned.1.call-update) | async-done | bytes 12582928 | tf_op jit(solution)/shard_map/all_gather | solution.py:1796
  306.7 149.1 %experts.1 = (bf16[4,1024,1024]{2,1,0:T(8,128)(2,1)}, bf16[1024,1024]{1,0:T(8,128)(2,1)}, bf16[1024,1024]{1,0:T(8,128)(2,1)}, bf16[1024,1024]{1,0:T(8,128)(2,1)}...) custom-call(bf16[1024,1024]{1,0:T(8,128)(2,1)} %copy-done.15, ...), custom_call_target="tpu_custom_call" | custom-call | flops 103079215104 | bytes 83886080 | tf_op jit(solution)/shard_map/experts/pallas_call | solution.py:883
  455.8 173.3 %expert_grads.1.refs_2_.refs_3_ = bf16[4,128,6144]{2,1,0:T(8,128)(2,1)} custom-call(bf16[1024,4096]{1,0:T(8,128)(2,1)} %get-tuple-element.64.xt_ref, bf16[1024,4096]{1,0:T(8,128)(2,1)} %get-tuple-element.65.tt_ref, bf16[4096,4096]{1,0:T(8,128)(2,1)} %bitcast.180, bf16[4096,2048]{1,0:T(8,128)(2,1)} %bitcast.181), custom_call_target="tpu_custom_call" | custom-call | flops 51539607552 | bytes 83886080 | tf_op jit(solution)/shard_map/expert_grads/pallas_call | solution.py:1166
  629.5 7.0 collective-permute-done
  636.5 4.2 convert_add_fusion
  640.7 3.4 copy-done.13
  644.1 1.6 fusion.22
  647.2 5.4 multiply_reduce_fusion
  652.8 41.2 %collective-permute-done.1 = bf16[1024,1024]{1,0:T(8,128)(2,1)} collective-permute-done((bf16[1024,1024]{1,0:T(8,128)(2,1)}, bf16[1024,1024]{1,0:T(8,128)(2,1)}, u32[]{:S(2)}, u32[]{:S(2)}) %collective-permute-start.1) | collective-permute-done | bytes 2097184 | tf_op jit(solution)/shard_map/ppermute | solution.py:1897
  694.0 4.5 subtract_add_fusion
  698.5 2.4 convolution_convert_fusion.1
  700.9 5.4 convolution_convert_fusion.2
  706.3 3.5 concatenate.90
  709.9 85.8 %attn_backward.1 = (f32[16,64,1024]{2,1,0:T(8,128)}, bf16[2,8,64,4096]{3,2,1,0:T(8,128)(2,1)}, f32[2,8,64,512]{3,2,1,0:T(8,128)}) custom-call(s32[2]{0:T(128)} %copy-done.7, bf16[16,64,1024]{2,1,0:T(8,128)(2,1)} %copy-done.2, bf16[2,8,64,4096]{3,2,1,0:T(8,128)(2,1)} %pad_maximum_fusion.kv_ref, bf16[2,8,64,512]{3,2,1,0:T(8,128)(2,1)} %copy-done.3, ...), custom_call_target="tpu_custom_call" | custom-call | flops 42949672960 | bytes 33554432 | tf_op jit(solution)/shard_map/attn_backward/pallas_call | solution.py:296
  795.7 2.3 slice_bitcast_fusion.2
  798.0 1.3 slice.255
  799.4 3.1 multiply_subtract_fusion
  802.7 1.4 copy-done.29
  804.1 4.0 fusion.28
  808.1 2.9 bitcast_convert_fusion
  811.0 1.3 subtract_convert_fusion
  812.4 2.5 pad_maximum_fusion.1
  814.9 11.1 fusion.63
  826.1 10.1 fusion.61
  837.3 0.8 add_convert_fusion.2
  838.1 1.1 add_convert_fusion.6
  839.7 8.9 collective-permute-done.3
  848.6 0.8 add_convert_fusion.5
  849.4 152.3 %late_reduce.1.refs_0_ = bf16[128,2048]{1,0:T(8,128)(2,1)S(1)} custom-call(bf16[1024,2048]{1,0:T(8,128)(2,1)S(1)} %pad_maximum_fusion.2.in_ref), custom_call_target="tpu_custom_call" | custom-call | bytes 16777216 | tf_op jit(solution)/shard_map/late_reduce/pallas_call | solution.py:1308
  1002.3 1.0 slice.144.refs_1_
  1004.2 0.9 convert_reduce_fusion
  1005.4 17.1 %flatten.3 = (f32[1,3541248]{1,0:T(1,128)}, f32[1,1]{1,0:T(1,128)}) custom-call(f32[18,128]{1,0:T(8,128)S(1)} %pad_maximum_fusion.8.lead_ref, bf16[128,2048]{1,0:T(8,128)(2,1)S(1)} %late_reduce.1.refs_0_, bf16[128,1024]{1,0:T(8,128)(2,1)S(1)} %slice.144.refs_1_, bf16[4,128,6144]{2,1,0:T(8,128)(2,1)} %expert_grads.1.refs_2_.refs_3_, ...), custom_call_target="tpu_custom_call" | custom-call | tf_op jit(solution)/shard_map/flatten/pallas_call | solution.py:1406
  1022.4 90.1 %summed_step.1 = (f32[1,1]{1,0:T(1,128)}, bf16[2,13840,128]{2,1,0:T(8,128)(2,1)}) custom-call(f32[1,1]{1,0:T(1,128)} %get-tuple-element.92.square_ref, f32[1,3541248]{1,0:T(1,128)} %get-tuple-element.150.g_ref.g, f32[1,1,3541248]{2,1,0:T(1,128)} %f.1, f32[1,1,3541248]{2,1,0:T(1,128)} %s.1, f32[1,3541248]{1,0:T(1,128)} %get-tuple-element.93.w_ref), custom_call_target="tpu_custom_call" | custom-call | bytes 67108864 | tf_op jit(solution)/shard_map/summed_step/pallas_call | solution.py:1617
  1112.6 44.0 %update.1 = (f32[1,1,3541248]{2,1,0:T(1,128)}, f32[1,1,3541248]{2,1,0:T(1,128)}, f32[1,3541248]{1,0:T(1,128)}, f32[1,3541248]{1,0:T(1,128)}) custom-call(f32[1,1]{1,0:T(1,128)} %get-tuple-element.94.norm_ref, f32[1,3541248]{1,0:T(1,128)} %get-tuple-element.150.g_ref.g, f32[1,1,3541248]{2,1,0:T(1,128)} %f.1, f32[1,1,3541248]{2,1,0:T(1,128)} %s.1, ...), custom_call_target="tpu_custom_call" | custom-call | bytes 125829120 | tf_op jit(solution)/shard_map/update/pallas_call | solution.py:1698
  1156.6 22.6 %reduce-scatter.8.cloned.1.call-done = bf16[512,512]{1,0:T(8,128)(2,1)} async-done(((bf16[512,4096]{1,0:T(8,128)(2,1)}), bf16[512,512]{1,0:T(8,128)(2,1)}) %reduce-scatter.8.cloned.1.call-update) | async-done | bytes 524304 | tf_op jit(solution)/shard_map/reduce_scatter | solution.py:1944
  1179.2 8.0 fusion.4
  1187.2 3.0 add_bitcast_fusion
  (192 shorter events, 10.7 us)
Async XLA Ops:
  7.2 7.1 copy-start.1
  7.2 299.5 %all-gather.2.cloned.1.call-start = ((), (), s32[]{:S(2)}) async-start(), calls=%async_computation.3 | async-start | bytes 14155776 | tf_op jit(solution)/shard_map/all_gather | solution.py:1796
  14.3 114.5 %copy-start.58 = (bf16[128,16]{0,1:T(8,128)(2,1)S(1)}, bf16[128,16]{0,1:T(8,128)(2,1)}, u32[]{:S(2)}) copy-start(bf16[128,16]{0,1:T(8,128)(2,1)} %param.22) | copy-start | bytes 12292
  128.7 667.0 %reduce-scatter.4.cloned.1.call-start = ((), (), s32[]{:S(2)}) async-start(), calls=%async_computation.4 | async-start | bytes 2654208 | tf_op jit(solution)/shard_map/reduce_scatter | solution.py:1905
  130.8 7.2 copy-start.61
  130.8 7.2 copy-start.62
  130.8 7.2 copy-start
  130.8 7.2 copy-start.4
  157.2 8.3 copy-start.54
  157.3 39.3 %copy-start.52 = (f32[1024,1]{0,1:T(1,128)}, f32[1024,1]{0,1:T(1,128)S(1)}, u32[]{:S(2)}) copy-start(f32[1024,1]{0,1:T(1,128)S(1)} %get-tuple-element.119) | copy-start | bytes 12292
  157.3 100.1 %copy-start.50 = (f32[1024,1]{0,1:T(1,128)}, f32[1024,1]{0,1:T(1,128)S(1)}, u32[]{:S(2)}) copy-start(f32[1024,1]{0,1:T(1,128)S(1)} %get-tuple-element.118) | copy-start | bytes 12292
  158.5 4.7 copy-start.35
  163.2 2.3 copy-start.11
  164.2 44.2 %copy-start.2 = (bf16[16,64,1024]{2,1,0:T(8,128)(2,1)}, bf16[16,64,1024]{2,1,0:T(8,128)(2,1)S(1)}, u32[]{:S(2)}) copy-start(bf16[16,64,1024]{2,1,0:T(8,128)(2,1)S(1)} %pad_maximum_fusion.3.q_ref) | copy-start | bytes 6291460
  164.3 44.1 %copy-start.7 = (s32[2]{0:T(128)}, s32[2]{0:T(128)S(1)}, u32[]{:S(2)}) copy-start(s32[2]{0:T(128)S(1)} %pad_add_fusion.where_ref) | copy-start | bytes 28
  164.4 95.3 %copy-start.37 = (pred[1024,16]{0,1:T(8,128)(4,1)}, pred[1024,16]{0,1:T(8,128)(4,1)S(1)}, u32[]{:S(2)}) copy-start(pred[1024,16]{0,1:T(8,128)(4,1)S(1)} %fusion.41) | copy-start | bytes 49156
  165.5 3.0 copy-start.39
  166.1 4.6 copy-start.19
  170.8 37.5 %copy-start.3 = (bf16[2,8,64,512]{3,2,1,0:T(8,128)(2,1)}, bf16[2,8,64,512]{3,2,1,0:T(8,128)(2,1)S(1)}, u32[]{:S(2)}) copy-start(bf16[2,8,64,512]{3,2,1,0:T(8,128)(2,1)S(1)} %pad_maximum_fusion.5.own_ref) | copy-start | bytes 3145732
  176.3 20.2 %copy-start.59 = (f32[4096]{0:T(1024)}, f32[4096]{0:T(1024)S(1)}, u32[]{:S(2)}) copy-start(f32[4096]{0:T(1024)S(1)} %add_rsqrt_fusion) | copy-start | bytes 49156
  179.2 12.6 %copy-start.22 = (f32[32,4096]{1,0:T(8,128)}, f32[32,4096]{1,0:T(8,128)S(1)}, u32[]{:S(2)}) copy-start(f32[32,4096]{1,0:T(8,128)S(1)} %get-tuple-element.125) | copy-start | bytes 1572868
  252.3 5.0 copy-start.5
  252.3 5.0 copy-start.8
  257.3 2.3 copy-start.9
  257.3 2.3 copy-start.48
  257.8 48.9 %copy-start.15 = (bf16[1024,1024]{1,0:T(8,128)(2,1)}, bf16[1024,1024]{1,0:T(8,128)(2,1)S(1)}, u32[]{:S(2)}) copy-start(bf16[1024,1024]{1,0:T(8,128)(2,1)S(1)} %multiply_convert_fusion.x_hbm) | copy-start | bytes 6291460
  629.1 7.4 collective-permute-start
  640.7 3.4 copy-start.13
  644.1 1.8 copy-start.45
  644.1 1.8 copy-start.47
  644.1 2.5 copy-start.16
  644.1 3.0 copy-start.49
  644.1 3.0 copy-start.51
  645.8 48.2 %collective-permute-start.1 = (bf16[1024,1024]{1,0:T(8,128)(2,1)}, bf16[1024,1024]{1,0:T(8,128)(2,1)}, u32[]{:S(2)}, u32[]{:S(2)}) collective-permute-start(bf16[1024,1024]{1,0:T(8,128)(2,1)} %fusion.22), channel_id=1, source_target_pairs={{0,2},{1,3},{2,0},{3,1},{4,6},{5,7},{6,4},{7,5},{8,10},{9,11},{10,... | collective-permute-start | bytes 6291464 | tf_op jit(solution)/shard_map/ppermute | solution.py:1897
  647.2 46.8 %copy-start.10 = (f32[1024,1024]{1,0:T(8,128)S(1)}, f32[1024,1024]{1,0:T(8,128)}, u32[]{:S(2)}) copy-start(f32[1024,1024]{1,0:T(8,128)} %copy-done.9) | copy-start | bytes 12582916
  647.2 46.8 %copy-start.14 = (f32[2,1024,1024]{2,1,0:T(8,128)S(1)}, f32[2,1024,1024]{2,1,0:T(8,128)}, u32[]{:S(2)}) copy-start(f32[2,1024,1024]{2,1,0:T(8,128)} %copy-done.13) | copy-start | bytes 25165828
  647.2 46.8 %copy-start.21 = (bf16[1,1,1024,1024]{3,2,1,0:T(8,128)(2,1)S(1)}, bf16[1,1,1024,1024]{3,2,1,0:T(8,128)(2,1)}, u32[]{:S(2)}) copy-start(bf16[1,1,1024,1024]{3,2,1,0:T(8,128)(2,1)} %param.15) | copy-start | bytes 6291460
  694.0 4.5 copy-start.6
  698.5 2.4 copy-start.17
  709.8 446.8 %reduce-scatter.6.cloned.1.call-start = ((), (), s32[]{:S(2)}) async-start(), calls=%async_computation.5 | async-start | bytes 4718592 | tf_op jit(solution)/shard_map/reduce_scatter | solution.py:1944
  709.8 89.5 %copy-start.36 = (f32[32,1024]{1,0:T(8,128)S(1)}, f32[32,1024]{1,0:T(8,128)}, u32[]{:S(2)}) copy-start(f32[32,1024]{1,0:T(8,128)} %copy-done.35) | copy-start | bytes 393220
  709.9 89.5 %copy-start.41 = (f32[32,1024]{1,0:T(8,128)S(1)}, f32[32,1024]{1,0:T(8,128)}, u32[]{:S(2)}) copy-start(f32[32,1024]{1,0:T(8,128)} %get-tuple-element.126) | copy-start | bytes 393220
  799.3 38.0 %copy-start.25 = (bf16[1,8,64,512]{3,2,1,0:T(8,128)(2,1)}, bf16[1,8,64,512]{3,2,1,0:T(8,128)(2,1)S(1)}, u32[]{:S(2)}) copy-start(bf16[1,8,64,512]{3,2,1,0:T(8,128)(2,1)S(1)} %slice.255) | copy-start | bytes 1572868
  799.3 38.8 %collective-permute-start.2 = (bf16[128,1152]{1,0:T(8,128)(2,1)}, bf16[128,1152]{1,0:T(8,128)(2,1)}, u32[]{:S(2)}, u32[]{:S(2)}) collective-permute-start(bf16[128,1152]{1,0:T(8,128)(2,1)} %reduce-scatter.4.cloned.1.call-done), channel_id=1, source_target_pairs={{0,1},{1,0},{2,3},{3,2},{4,5},{5,4},{6,7},{7,6},{8,9},{9,8},{10,11... | collective-permute-start | bytes 884744 | tf_op jit(solution)/shard_map/ppermute | solution.py:1869
  799.4 4.7 copy-start.12
  799.4 4.7 copy-start.53
  799.4 4.7 copy-start.55
  802.5 5.6 slice-start
  804.1 4.0 slice-start.1
  808.1 2.9 copy-start.23
  808.1 2.9 copy-start.32
  812.4 2.5 copy-start.60
  826.0 10.2 copy-start.24
  826.0 10.2 copy-start.40
  826.0 10.2 copy-start.43
  826.0 10.4 copy-start.20
  826.1 10.4 copy-start.30
  836.5 2.7 copy-start.31
  839.2 9.4 collective-permute-start.3
  1001.7 3.6 copy-start.63
  1001.8 177.4 %reduce-scatter.8.cloned.1.call-start = ((), (), s32[]{:S(2)}) async-start(), calls=%async_computation.6 | async-start | bytes 4718592 | tf_op jit(solution)/shard_map/reduce_scatter | solution.py:1944
  1112.5 66.7 %copy-start.26 = (bf16[1,8,64,512]{3,2,1,0:T(8,128)(2,1)S(1)}, bf16[1,8,64,512]{3,2,1,0:T(8,128)(2,1)}, u32[]{:S(2)}) copy-start(bf16[1,8,64,512]{3,2,1,0:T(8,128)(2,1)} %copy-done.25) | copy-start | bytes 1572868
  1112.5 66.7 %copy-start.28 = (bf16[8,64,512]{2,1,0:T(8,128)(2,1)S(1)}, bf16[8,64,512]{2,1,0:T(8,128)(2,1)}, u32[]{:S(2)}) copy-start(bf16[8,64,512]{2,1,0:T(8,128)(2,1)} %copy-done.27) | copy-start | bytes 1572868
  1179.2 8.0 copy-start.18
  (10 other events, 11.9 us)
Sparse Core Ops, SparseCore 0:
  128.8 177.7 all-gather.1
  709.9 67.8 reduce-scatter.3
  1001.9 85.1 reduce-scatter.5
  1091.0 88.1 reduce-scatter.7

commit v6 on v5

--- a/solution.py
+++ b/solution.py
@@ -59,9 +59,9 @@
     return rows, high, low
 
 
-def block_of(ref, index, block):
+def block_of(refs, index, block):
     span = pl.ds(pl.multiple_of(index * block, block), block)
-    return ref[0, 0, :, span], ref[1, 0, :, span]
+    return tuple(ref[0, :, span] for ref in refs)
 
 
 def causal(width, columns):
@@ -73,7 +73,7 @@
 SAFE_BOUND = 48.0
 
 
-def attn_forward_kernel(where_ref, q_ref, kv_ref, own_ref, o_ref, lse_ref, peak_ref, acc_ref):
+def attn_forward_kernel(where_ref, q_ref, k_ref, v_ref, own_ref, o_ref, lse_ref, peak_ref, acc_ref):
     block = own_ref.shape[-1]
     columns = PER_KEY * block
     shard_pos = where_ref[0]
@@ -81,12 +81,13 @@
     ones = jnp.ones((16, block), BF16)
     pad = jnp.zeros((16 - 3, columns), BF16)
     whole = branch // block
+    kv_ref = (k_ref, v_ref)
 
     def longest(key):
         squares = key.astype(F32)
         return jnp.max(jnp.sum(squares * squares, axis=0, keepdims=True), axis=1, keepdims=True)
 
-    longest_key = jnp.sqrt(jnp.maximum(longest(kv_ref[0, 0]), longest(own_ref[0, 0])))
+    longest_key = jnp.sqrt(jnp.maximum(longest(k_ref[0]), longest(own_ref[0, 0])))
 
     def emit(start, result, lse):
         for g in range(PER_KEY):
@@ -167,14 +168,15 @@
     tokens = query.shape[-1]
     block = own_kv.shape[-1]
     columns = PER_KEY * block
-    keys = prompt_kv.shape[-1]
+    keys = prompt_kv[0].shape[-1]
     return pl.pallas_call(
         attn_forward_kernel,
         grid=(query.shape[0] // PER_KEY,),
         in_specs=[
             pl.BlockSpec(memory_space=pltpu.SMEM),
             pl.BlockSpec((PER_KEY, HEAD_SIZE, tokens), lambda h: (h, 0, 0)),
-            pl.BlockSpec((2, 1, HEAD_SIZE, keys), lambda h: (0, h, 0, 0)),
+            pl.BlockSpec((1, HEAD_SIZE, keys), lambda h: (h, 0, 0)),
+            pl.BlockSpec((1, HEAD_SIZE, keys), lambda h: (h, 0, 0)),
             pl.BlockSpec((2, 1, HEAD_SIZE, block), lambda h: (0, h, 0, 0)),
         ],
         out_specs=[
@@ -196,11 +198,11 @@
             transcendentals=query.shape[0] * tokens * keys,
         ),
         name="attn_forward",
-    )(where, query, prompt_kv, own_kv)
+    )(where, query, *prompt_kv, own_kv)
 
 
 def attn_backward_kernel(
-    where_ref, q_ref, kv_ref, own_ref, go_ref, o_ref, lse_ref, dq_ref, dkv_ref, down_ref, dkv_acc, dq_acc
+    where_ref, q_ref, k_ref, v_ref, own_ref, go_ref, o_ref, lse_ref, turn_ref, own_turn_ref, dq_ref, dkv_ref, down_ref, dkv_acc, dq_acc
 ):
     block = own_ref.shape[-1]
     columns = PER_KEY * block
@@ -208,6 +210,13 @@
     branch = where_ref[1]
     ones = jnp.ones((16, block), BF16)
     pad = jnp.zeros((16 - 3, columns), BF16)
+    kv_ref = (k_ref, v_ref)
+
+    def turn_back(values, ref, span):
+        half = HEAD_SIZE // 2
+        cosine, sine = ref[0, :, span], ref[1, :, span]
+        front, back = values[:half], values[half:]
+        return jnp.concatenate([front * cosine + back * sine, back * cosine - front * sine], axis=0).astype(BF16)
 
     def begin(start):
         rows, high, low = augment_query(q_ref, start, block)
@@ -248,7 +257,8 @@
     def finish(start):
         total = dq_acc[...] * HEAD_SIZE**-0.5
         for g in range(PER_KEY):
-            dq_ref[g, :, start : start + block] = total[:, g * block : (g + 1) * block]
+            span = slice(start, start + block)
+            dq_ref[g, :, span] = turn_back(total[:, g * block : (g + 1) * block], own_turn_ref, span)
 
     def run(state, count):
         def body(index, carry):
@@ -278,30 +288,33 @@
         add(whole, state, key_pos < branch % block)
 
     dk, dv = terms(state, own_ref[0, 0], own_ref[1, 0], causal(block, columns))
-    down_ref[0, 0] = dk
-    down_ref[1, 0] = dv
+    down_ref[0, 0] = turn_back(dk, own_turn_ref, slice(block, 2 * block))
+    down_ref[1, 0] = dv.astype(BF16)
     finish(block)
-    dkv_ref[:, 0] = dkv_acc[...].astype(BF16)
-
-
-def attn_backward(where, query, prompt_kv, own_kv, grad_out, out, lse):
+    dkv_ref[0, 0] = turn_back(dkv_acc[0], turn_ref, slice(None))
+    dkv_ref[1, 0] = dkv_acc[1].astype(BF16)
+
+
+def attn_backward(where, query, prompt_kv, own_kv, grad_out, out, lse, turn, own_turn):
     tokens = query.shape[-1]
     block = own_kv.shape[-1]
     columns = PER_KEY * block
-    keys = prompt_kv.shape[-1]
+    keys = prompt_kv[0].shape[-1]
     by_head = pl.BlockSpec((PER_KEY, HEAD_SIZE, tokens), lambda h: (h, 0, 0))
     by_keys = pl.BlockSpec((2, 1, HEAD_SIZE, keys), lambda h: (0, h, 0, 0))
+    by_key = pl.BlockSpec((1, HEAD_SIZE, keys), lambda h: (h, 0, 0))
     by_own = pl.BlockSpec((2, 1, HEAD_SIZE, block), lambda h: (0, h, 0, 0))
     by_row = pl.BlockSpec((1, PER_KEY, tokens), lambda h: (h, 0, 0))
     return pl.pallas_call(
         attn_backward_kernel,
         grid=(query.shape[0] // PER_KEY,),
-        in_specs=[pl.BlockSpec(memory_space=pltpu.SMEM), by_head, by_keys, by_own, by_head, by_head, by_row],
+        in_specs=[pl.BlockSpec(memory_space=pltpu.SMEM), by_head, by_key, by_key, by_own, by_head, by_head, by_row]
+        + [pl.BlockSpec(part.shape, lambda h: (0, 0, 0)) for part in (turn, own_turn)],
         out_specs=[by_head, by_keys, by_own],
         out_shape=[
-            jax.ShapeDtypeStruct(query.shape, F32),
-            jax.ShapeDtypeStruct(prompt_kv.shape, BF16),
-            jax.ShapeDtypeStruct(own_kv.shape, F32),
+            jax.ShapeDtypeStruct(query.shape, BF16),
+            jax.ShapeDtypeStruct((2, *prompt_kv[0].shape), BF16),
+            jax.ShapeDtypeStruct(own_kv.shape, BF16),
         ],
         scratch_shapes=[
             pltpu.VMEM((2, HEAD_SIZE, keys), F32),
@@ -314,7 +327,7 @@
             transcendentals=query.shape[0] * tokens * keys,
         ),
         name="attn_backward",
-    )(where, query, prompt_kv, own_kv, grad_out, out, lse)
+    )(where, query, *prompt_kv, own_kv, grad_out, out, lse, turn, own_turn)
 
 
 MESH = pl.DeviceIdType.MESH
@@ -1197,7 +1210,13 @@
 
 def late_reduce_kernel(
     in_ref,
+    early_ref,
     out_ref,
+    early_out,
+    early_core,
+    early_mid,
+    early_far,
+    early_sems,
     own_buf,
     core_buf,
     parts,
@@ -1251,8 +1270,14 @@
     for c in range(n):
         load(c).start()
     greet([to_core, to_far])
+    early_near = send_to(early_ref, early_core, early_sems.at[0, 0], early_sems.at[1, 0], to_core)
+    early_over = send_to(early_mid, early_far, early_sems.at[0, 1], early_sems.at[1, 1], to_far)
+    early_near.start()
     for c in range(n):
         from_core(c).start()
+    early_near.wait_recv()
+    early_mid[...] = (early_ref[...].astype(F32) + early_core[...].astype(F32)).astype(BF16)
+    early_over.start()
 
     def produce(c):
         load(c).wait()
@@ -1284,6 +1309,10 @@
         return carry
 
     lax.fori_loop(0, n + LINE + 1, step, 0)
+    early_over.wait_recv()
+    early_out[...] = (early_mid[...].astype(F32) + early_far[...].astype(F32)).astype(BF16)
+    early_near.wait_send()
+    early_over.wait_send()
 
     def end(c, carry):
         drain(c)
@@ -1299,7 +1328,7 @@
     lax.fori_loop(0, n, end, 0)
 
 
-def late_reduce(values, columns=256):
+def late_reduce(values, early, columns=256):
     width, wide = values.shape
     n = wide // 2 // columns
     rows = width // (2 * LINE)
@@ -1307,10 +1336,14 @@
     anywhere = pl.BlockSpec(memory_space=pl.ANY)
     return pl.pallas_call(
         late_reduce_kernel,
-        in_specs=[anywhere],
-        out_specs=anywhere,
-        out_shape=jax.ShapeDtypeStruct((rows, wide), BF16),
+        in_specs=[anywhere, pl.BlockSpec(memory_space=pltpu.VMEM)],
+        out_specs=[anywhere, pl.BlockSpec(memory_space=pltpu.VMEM)],
+        out_shape=[jax.ShapeDtypeStruct((rows, wide), BF16), jax.ShapeDtypeStruct(early.shape, BF16)],
         scratch_shapes=[
+            pltpu.VMEM(early.shape, BF16),
+            pltpu.VMEM(early.shape, BF16),
+            pltpu.VMEM(early.shape, BF16),
+            dma((2, 2)),
             pltpu.VMEM((n, width, columns), BF16),
             pltpu.VMEM((n, width, columns), BF16),
             pltpu.VMEM((n, 2, LINE, rows, columns), BF16),
@@ -1331,9 +1364,9 @@
             dma((2, n)),
         ],
         compiler_params=pltpu.CompilerParams(vmem_limit_bytes=48 * MIB, collective_id=5, has_side_effects=True),
-        cost_estimate=pl.CostEstimate(flops=0, bytes_accessed=16 * MIB, transcendentals=0),
+        cost_estimate=pl.CostEstimate(flops=0, bytes_accessed=4 * MIB, transcendentals=0),
         name="late_reduce",
-    )(values)
+    )(values, early)
 
 
 def flatten_kernel(starts, lead_ref, *refs):
@@ -1634,7 +1667,7 @@
         compiler_params=pltpu.CompilerParams(
             vmem_limit_bytes=48 * MIB, collective_id=3, has_side_effects=True
         ),
-        cost_estimate=pl.CostEstimate(flops=0, bytes_accessed=64 * MIB, transcendentals=0),
+        cost_estimate=pl.CostEstimate(flops=0, bytes_accessed=4 * MIB, transcendentals=0),
         name="summed_step",
     )(square, grad, first, second, weight)
 
@@ -1811,7 +1844,7 @@
         return (rotate(rows, *turn) if turn is not None else rows).astype(BF16)
 
     def keys_values(source, turn):
-        return jnp.stack([project(source, Q_WIDTH, KV_WIDTH, turn), project(source, Q_WIDTH + KV_WIDTH, KV_WIDTH, None)])
+        return project(source, Q_WIDTH, KV_WIDTH, turn), project(source, Q_WIDTH + KV_WIDTH, KV_WIDTH, None)
 
     normed_attn, attn_scale = normed(x_in)
     normed_prompt, _ = normed(prompt_low.astype(F32))
@@ -1826,7 +1859,7 @@
     )
     continued_turn = tuple(part[..., prompt:] for part in own_turn)
     prompt_kv = keys_values(normed_prompt, prompt_turn)
-    own_kv = keys_values(normed_attn[prompt:], continued_turn)
+    own_kv = jnp.stack(keys_values(normed_attn[prompt:], continued_turn))
     query = project(normed_attn, 0, Q_WIDTH, own_turn)
     where = jnp.stack([shard_pos.astype(jnp.int32), branch_len])
     if flat_path:
@@ -1864,6 +1897,10 @@
     grad_gates = dgate_part[:, :local].reshape(EXPERTS, count).T
     to_core = [(i, i + 1 - 2 * (i % 2)) for i in range(reps)]
     to_far = [(i, (i + 2) % reps) for i in range(reps)]
+    y_near = y_keep.astype(F32) + lax.ppermute(y_give, "rep", to_core).astype(F32)
+    y_sum = y_near[0] + lax.ppermute(y_near[1].astype(BF16), "rep", to_far).astype(F32)
+    block_out = (x_mid + y_sum).astype(BF16)
+
     def rep_sum(values):
         for pairs in (to_core, to_far):
             values = (values.astype(F32) + lax.ppermute(values, "rep", pairs).astype(F32)).astype(BF16)
@@ -1892,11 +1929,6 @@
         terms = jnp.concatenate([expert_term(normed_t, dgu), expert_term(top_t, gated)], axis=1)
         terms = lax.psum_scatter(terms, "shard", scatter_dimension=0, tiled=True)
         expert_rows = lax.all_gather(terms, "rep", axis=0, tiled=False)
-    y_keep, y_give, expert_rows = lax.optimization_barrier((y_keep, y_give, expert_rows))
-    y_near = y_keep.astype(F32) + lax.ppermute(y_give, "rep", to_core).astype(F32)
-    y_sum = y_near[0] + lax.ppermute(y_near[1].astype(BF16), "rep", to_far).astype(F32)
-    block_out = (x_mid + y_sum).astype(BF16)
-
     blank = jnp.zeros((width, -(Q_WIDTH + EXPERTS + 1) % LANES), BF16)
     early = jnp.concatenate(
         [grad_attn_w.astype(BF16), grad_router_w.astype(BF16), grad_ffn_gain[:, None].astype(BF16), blank], axis=1
@@ -1905,48 +1937,27 @@
     early = lax.psum_scatter(early, "shard", scatter_dimension=0, tiled=True)
 
     grad_query, grad_prompt_kv, grad_own_kv = attn_backward(
-        where, query, prompt_kv, own_kv, grad_attn, attn, lse
+        where, query, prompt_kv, own_kv, grad_attn, attn, lse, jnp.concatenate(prompt_turn), jnp.concatenate(own_turn)
     )
 
     early, grad_query, grad_prompt_kv, grad_own_kv = lax.optimization_barrier(
         (early, grad_query, grad_prompt_kv, grad_own_kv)
     )
-    early = rep_sum(early)
-
-    def turn_back(values, turn):
-        spun = rotate(values, turn[0], -turn[1])
-        return spun.astype(BF16).reshape(-1, values.shape[-1])
-
-    grad_query = turn_back(grad_query, own_turn)
-    grad_prompt_kv = (
-        turn_back(grad_prompt_kv[0].astype(F32), prompt_turn),
-        grad_prompt_kv[1].reshape(KV_WIDTH, GROUP_SIZE * prompt),
-    )
-    grad_own_kv = (turn_back(grad_own_kv[0], continued_turn), grad_own_kv[1].astype(BF16).reshape(KV_WIDTH, -1))
-    late = [dot(normed_attn, grad_query, (0, 1)).astype(BF16)]
-    for shared, own in zip(grad_prompt_kv, grad_own_kv):
-        late.append((dot(normed_prompt, shared, (0, 1)) + dot(normed_attn[prompt:], own, (0, 1))).astype(BF16))
-    late = jnp.concatenate(late, axis=1)
-    late, early = lax.optimization_barrier((late, early))
+    grad_query = grad_query.reshape(Q_WIDTH, count)
+    grad_prompt_kv = grad_prompt_kv.reshape(2 * KV_WIDTH, GROUP_SIZE * prompt)
+    grad_own_kv = grad_own_kv.reshape(2 * KV_WIDTH, CONTINUATION_LEN)
+    late_kv = dot(normed_prompt, grad_prompt_kv, (0, 1)) + dot(normed_attn[prompt:], grad_own_kv, (0, 1))
+    late = jnp.concatenate([dot(normed_attn, grad_query, (0, 1)).astype(BF16), late_kv.astype(BF16)], axis=1)
+    if fast:
+        qkv_rows, early = late_reduce(late, early)
+    else:
+        qkv_rows = rep_sum(lax.psum_scatter(late, "shard", scatter_dimension=0, tiled=True))
+        early = rep_sum(early)
     attn_rows, router_rows = early[:, :Q_WIDTH], early[:, Q_WIDTH : Q_WIDTH + EXPERTS]
     ffn_gain_rows = early[:, Q_WIDTH + EXPERTS]
-    if fast:
-        qkv_rows = late_reduce(late)
-    else:
-        qkv_rows = rep_sum(lax.psum_scatter(late, "shard", scatter_dimension=0, tiled=True))
-    qkv_rows, grad_prompt_kv = lax.optimization_barrier((qkv_rows, grad_prompt_kv))
     attn_gain_rows = jnp.sum(
         qkv_rows.astype(F32) * query_key_value_weight.astype(F32), axis=1
     ) / attn_gain.astype(F32)
-
-    grad_projected = [grad_query]
-    for shared, own in zip(grad_prompt_kv, grad_own_kv):
-        shared = lax.psum_scatter(shared, "shard", scatter_dimension=1, tiled=True, axis_index_groups=groups)
-        grad_projected.append(jnp.concatenate([shared, own], axis=1))
-    grad_projected = jnp.concatenate(grad_projected, axis=0)
-    grad_normed_attn = dot(grad_projected, qkv_full, (0, 1))
-    grad_x_norm, _ = rms_backward(x_in, attn_scale, attn_gain_full, grad_normed_attn)
-    grad_input = grad_mid + grad_x_norm
 
     in_columns = local * 2 * F
     if flat_path:
@@ -1960,11 +1971,6 @@
                 (expert_rows, expert_columns - in_columns, in_columns // (expert_columns - in_columns)),
             ],
         )
-        grad_norm, step_sum = summed_step(square, total_grad, adam_first, adam_second, weight_flat)
-        new_first, new_second, new_mom, weight_update = update(
-            reps, grad_norm, total_grad, adam_first, adam_second, step_sum, outer_mom
-        )
-        grad_norm = grad_norm.reshape(())
     else:
         weight_flat = jnp.concatenate(
             [
@@ -1986,6 +1992,25 @@
                 )
             ]
         )
+
+    def scatter(shared):
+        return lax.psum_scatter(shared, "shard", scatter_dimension=1, tiled=True, axis_index_groups=groups)
+
+    reduced_kv = scatter(grad_prompt_kv)
+    if flat_path:
+        grad_norm, step_sum = summed_step(square, total_grad, adam_first, adam_second, weight_flat)
+        step_sum, reduced_kv = lax.optimization_barrier((step_sum, reduced_kv))
+    grad_projected = jnp.concatenate([grad_query, jnp.concatenate([reduced_kv, grad_own_kv], axis=1)], axis=0)
+    grad_normed_attn = dot(grad_projected, qkv_full, (0, 1))
+    grad_x_norm, _ = rms_backward(x_in, attn_scale, attn_gain_full, grad_normed_attn)
+    grad_input = grad_mid + grad_x_norm
+
+    if flat_path:
+        new_first, new_second, new_mom, weight_update = update(
+            reps, grad_norm, total_grad, adam_first, adam_second, step_sum, outer_mom
+        )
+        grad_norm = grad_norm.reshape(())
+    else:
         grad_norm = jnp.sqrt(lax.psum(jnp.sum(total_grad * total_grad), "shard"))
         new_first, new_second = moments(
             total_grad,

time: 1200 us -> 1140 us (0.950); the launches traced: 1200 us -> 1130 us
  waiting for transfers between devices: 125 us -> 71.3 us
  other arithmetic: 52.4 us -> 36.7 us
    ppermute x1, waiting for transfers between devices: 41.2 us -> 0.01 us  [per_device(): lax.ppermute(y_near[1].astype(BF16), 'rep', to_far).astype(F32)]
    pallas_call x1, Pallas kernels: 152 us -> 190 us  [late_reduce(): pl.pallas_call(late_reduce_kernel, in_specs=[anywhere, pl.BlockSpec(memor...]
    reduce_scatter x2 -> x1, waiting for transfers between devices: 22.7 us -> 0.02 us  [scatter(): lax.psum_scatter(shared, 'shard', scatter_dimension=1, tiled=True, axis_i...]
    pallas_call x1, Pallas kernels: 85.8 us -> 66.5 us  [attn_backward(): pl.pallas_call(attn_backward_kernel, grid=(query.shape[0] // PER_KEY,), i...]
    all_gather x1, waiting for transfers between devices: 45.1 us -> 64 us  [per_device(): w_both = gather(w_both)]
    dot_general x17 -> x15, matrix products: 84.8 us -> 74.6 us  [dot(): lax.dot_general(left, right, ((dims[:1], dims[1:]), ((), ())), preferred_...]
  transfers between devices with their start and end apart: 8 -> 5, of which waited for: 5 -> 2; matrix products, arithmetic and copies ran while one was open for 10% -> 8% of each run, Pallas kernels for 25% -> 52%
where the time goes in v6:
time: 1140 us; the launch traced here: 1130 us
  Pallas kernels  891 us (78%)
  matrix products  74.6 us (7%)
  waiting for transfers between devices  71.3 us (6%)
  other arithmetic  36.7 us (3%)
  local copies, waits for them, and re-layouts  32.8 us (3%)
  between operations  17.7 us (2%)
    pallas_call x1, Pallas kernels, late_reduce(): pl.pallas_call(late_reduce_kernel, in_specs=[anywhere, pl.BlockSpec(memor...  190 us
    pallas_call x1, Pallas kernels, expert_grads(): pl.pallas_call(expert_grads_kernel, in_specs=[anywhere] * 4, out_specs=an...  165 us
    pallas_call x1, Pallas kernels, experts(): pl.pallas_call(experts_kernel, grid=(len(ORDER),), in_specs=[anywhere, an...  149 us
    pallas_call x1, Pallas kernels, start_gather(): pl.pallas_call(start_kernel, in_specs=[anywhere] * 3, out_specs=[anywhere...  112 us
    pallas_call x1, Pallas kernels, summed_step(): pl.pallas_call(step_kernel, in_specs=[pl.BlockSpec(memory_space=pltpu.VME...  96.9 us
    dot_general x15, matrix products, dot(): lax.dot_general(left, right, ((dims[:1], dims[1:]), ((), ())), preferred_...  74.6 us
    pallas_call x1, Pallas kernels, attn_backward(): pl.pallas_call(attn_backward_kernel, grid=(query.shape[0] // PER_KEY,), i...  66.5 us
    all_gather x1, waiting for transfers between devices, per_device(): w_both = gather(w_both)  64 us
  transfers between devices with their start and end apart: 5, of which 2 were waited for; matrix products, arithmetic and copies ran while one was open for 8% of the time, Pallas kernels for 52%

profile of v6, /device:TPU:0, one launch (start us, length us, event | category | flops | bytes accessed | tf_op | source)
XLA Modules:
  0.0 1126.2 jit_solution(8158968897152476819)
XLA Ops:
  7.2 0.9 copy.68
  8.2 0.8 copy.69
  9.0 0.8 copy.70
  9.7 1.2 concatenate.61
  11.0 1.0 pad.8.w_ref
  11.9 2.3 constant_dynamic-slice_fusion.1
  14.3 2.5 pad_maximum_fusion.3
  16.8 111.9 %start_gather.1 = (bf16[8,512,1024]{2,1,0:T(8,128)(2,1)}, bf16[8,4,32,3200]{3,2,1,0:T(8,128)(2,1)}, bf16[4,1024,1024]{2,1,0:T(8,128)(2,1)}) custom-call(bf16[1024,1024]{1,0:T(8,128)(2,1)} %bitcast.113, bf16[128,3200]{1,0:T(8,128)(2,1)} %pad.8.w_ref, bf16[1024,1024]{1,0:T(8,128)(2,1)} %bitcast.114), custom_call_target="tpu_custom_call" | custom-call | bytes 67108864 | tf_op jit(solution)/shard_map/start_gather/pallas_call | solution.py:608
  129.6 1.1 slice.104
  130.9 3.2 slice_bitcast_fusion.1
  134.0 3.9 copy.71
  138.1 17.0 %flatten.2 = (f32[1,3541248]{1,0:T(1,128)}, f32[1,1]{1,0:T(1,128)}) custom-call(f32[18,128]{1,0:T(8,128)S(1)} %pad_maximum_fusion.7.lead_ref, bf16[128,2048]{1,0:T(8,128)(2,1)S(1)} %copy-done, bf16[128,1024]{1,0:T(8,128)(2,1)S(1)} %copy-done.4, bf16[128,16384]{1,0:T(8,128)(2,1)} %refs_2_.1, bf16[128,8192]{1,0:T(8,128)(2,1)S(1)} %copy-done.1), custom_call_target="tpu_custom_call" | custom-call | tf_op jit(solution)/shard_map/flatten/pallas_call | solution.py:1439
  155.2 2.1 fusion.3
  157.3 0.5 multiply_cosine_fusion.3
  157.8 4.7 fusion.18
  162.6 0.7 subtract_convert_fusion.1
  163.7 0.5 multiply_cosine_fusion.2
  164.3 0.6 copy-done.27
  165.6 2.7 fusion.31
  168.5 2.0 convolution_convert_fusion.3
  170.6 1.7 fusion
  172.4 1.9 multiply_cosine_fusion.1
  174.3 9.2 fusion.33
  183.5 4.7 subtract_convert_fusion
  188.2 2.5 pad_maximum_fusion.k_ref
  190.8 8.3 convolution_convert_fusion
  199.1 33.7 %attn_forward.1 = (bf16[16,64,1024]{2,1,0:T(8,128)(2,1)S(1)}, f32[8,2,1024]{2,1,0:T(2,128)S(1)}) custom-call(s32[2]{0:T(128)S(1)} %pad_add_fusion.where_ref, bf16[16,64,1024]{2,1,0:T(8,128)(2,1)S(1)} %pad_maximum_fusion.2.q_ref, bf16[8,64,4096]{2,1,0:T(8,128)(2,1)} %pad_maximum_fusion.k_ref, bf16[8,64,4096]{2,1,0:T(8,128)(2,1)} %bitcast.157, ...), custom_call_target="tpu_custom_call" | custom-call | flops 17179869184 | bytes 16777216 | tf_op jit(solution)/shard_map/attn_forward/pallas_call | solution.py:172
  232.8 4.9 multiply_reduce_fusion.2
  237.8 0.6 copy-done.38
  238.8 1.8 fusion.49
  240.7 0.6 copy-done.24
  241.3 0.6 copy-done.36
  242.0 0.7 pad.9.gates_ref
  242.6 64.0 %all-gather.2.cloned.1.call-done.w_ref = bf16[1024,6144]{1,0:T(8,128)(2,1)} async-done(((bf16[128,6144]{1,0:T(8,128)(2,1)}), bf16[1024,6144]{1,0:T(8,128)(2,1)}) %all-gather.2.cloned.1.call-update) | async-done | bytes 12582928 | tf_op jit(solution)/shard_map/all_gather | solution.py:1829
  306.6 149.1 %experts.1 = (bf16[4,1024,1024]{2,1,0:T(8,128)(2,1)}, bf16[1024,1024]{1,0:T(8,128)(2,1)}, bf16[1024,1024]{1,0:T(8,128)(2,1)}, bf16[1024,1024]{1,0:T(8,128)(2,1)}...) custom-call(bf16[1024,1024]{1,0:T(8,128)(2,1)} %copy-done.17, ...), custom_call_target="tpu_custom_call" | custom-call | flops 103079215104 | bytes 83886080 | tf_op jit(solution)/shard_map/experts/pallas_call | solution.py:896
  456.0 7.2 collective-permute-done
  463.2 4.2 convert_add_fusion
  467.4 3.4 copy-done.15
  470.8 1.6 fusion.16
  472.4 1.6 collective-permute-start.1
  474.1 165.5 %expert_grads.1.refs_2_.refs_3_ = bf16[4,128,6144]{2,1,0:T(8,128)(2,1)} custom-call(bf16[1024,4096]{1,0:T(8,128)(2,1)} %get-tuple-element.64.xt_ref, bf16[1024,4096]{1,0:T(8,128)(2,1)} %get-tuple-element.65.tt_ref, bf16[4096,4096]{1,0:T(8,128)(2,1)} %bitcast.155, bf16[4096,2048]{1,0:T(8,128)(2,1)} %bitcast.156), custom_call_target="tpu_custom_call" | custom-call | flops 51539607552 | bytes 83886080 | tf_op jit(solution)/shard_map/expert_grads/pallas_call | solution.py:1179
  640.4 5.4 multiply_reduce_fusion
  646.0 2.2 copy-done.16
  648.2 0.6 copy-done.21
  648.8 4.5 subtract_add_fusion
  653.3 2.4 convolution_convert_fusion.1
  655.7 5.3 convolution_convert_fusion.2
  661.1 3.5 concatenate.69
  664.8 2.5 multiply_cosine_fusion
  667.3 1.6 pad_maximum_fusion.6.own_turn_ref
  668.9 1.1 pad_maximum_fusion.5.turn_ref
  670.0 66.5 %attn_backward.1 = (bf16[16,64,1024]{2,1,0:T(8,128)(2,1)}, bf16[2,8,64,4096]{3,2,1,0:T(8,128)(2,1)}, bf16[2,8,64,512]{3,2,1,0:T(8,128)(2,1)}) custom-call(s32[2]{0:T(128)} %copy-done.8, bf16[16,64,1024]{2,1,0:T(8,128)(2,1)} %copy-done.2, bf16[8,64,4096]{2,1,0:T(8,128)(2,1)} %pad_maximum_fusion.k_ref, bf16[8,64,4096]{2,1,0:T(8,128)(2,1)} %bitcast.158, ...), custom_call_target="tpu_custom_call" | custom-call | flops 42949672960 | bytes 33554432 | tf_op jit(solution)/shard_map/attn_backward/pallas_call | solution.py:308
  736.6 0.6 copy-done.43
  737.3 15.3 %fusion.52 = f32[1024,1024]{1,0:T(8,128)S(1)} fusion(bf16[1024,4096]{1,0:T(8,128)(2,1)} %bitcast.122, bf16[4096,1024]{1,0:T(8,128)(2,1)} %bitcast.115, f32[1024]{0:T(1024)S(1)} %bitcast.147, f32[4096]{0:T(1024)S(1)} %copy-done.50), kind=kOutput, calls=%fused_computation.124 | convolution fusion | flops 8606711808 | bytes 20992000 | tf_op jit(solution)/shard_map/dot_general | solution.py:43
  752.7 1.3 add_convert_fusion
  754.3 0.6 copy-done.55
  754.9 2.6 fusion.22
  758.0 0.5 copy-done.5
  758.5 189.5 %late_reduce.1 = (bf16[128,2048]{1,0:T(8,128)(2,1)S(1)}, bf16[128,1152]{1,0:T(8,128)(2,1)S(1)}) custom-call(bf16[1024,2048]{1,0:T(8,128)(2,1)S(1)} %pad_maximum_fusion.1.in_ref, bf16[128,1152]{1,0:T(8,128)(2,1)S(1)} %copy-done.5), custom_call_target="tpu_custom_call" | custom-call | bytes 4194304 | tf_op jit(solution)/shard_map/late_reduce/pallas_call | solution.py:1337
  948.6 17.1 %flatten.3 = (f32[1,3541248]{1,0:T(1,128)}, f32[1,1]{1,0:T(1,128)}) custom-call(f32[18,128]{1,0:T(8,128)S(1)} %pad_maximum_fusion.8.lead_ref, bf16[128,2048]{1,0:T(8,128)(2,1)S(1)} %get-tuple-element.78.refs_0_, bf16[128,1024]{1,0:T(8,128)(2,1)S(1)} %slice.101.refs_1_, bf16[4,128,6144]{2,1,0:T(8,128)(2,1)} %expert_grads.1.refs_2_.refs_3_, ...), custom_call_target="tpu_custom_call" | custom-call | tf_op jit(solution)/shard_map/flatten/pallas_call | solution.py:1439
  965.7 96.9 %summed_step.1 = (f32[1,1]{1,0:T(1,128)}, bf16[2,13840,128]{2,1,0:T(8,128)(2,1)}) custom-call(f32[1,1]{1,0:T(1,128)} %get-tuple-element.81.square_ref, f32[1,3541248]{1,0:T(1,128)} %get-tuple-element.133.g_ref.g, f32[1,1,3541248]{2,1,0:T(1,128)} %f.1, f32[1,1,3541248]{2,1,0:T(1,128)} %s.1, f32[1,3541248]{1,0:T(1,128)} %get-tuple-element.83.w_ref), custom_call_target="tpu_custom_call" | custom-call | bytes 4194304 | tf_op jit(solution)/shard_map/summed_step/pallas_call | solution.py:1650
  1062.6 8.2 fusion.4
  1070.8 43.7 %update.1 = (f32[1,1,3541248]{2,1,0:T(1,128)}, f32[1,1,3541248]{2,1,0:T(1,128)}, f32[1,3541248]{1,0:T(1,128)}, f32[1,3541248]{1,0:T(1,128)}) custom-call(f32[1,1]{1,0:T(1,128)} %get-tuple-element.86.norm_ref, f32[1,3541248]{1,0:T(1,128)} %get-tuple-element.133.g_ref.g, f32[1,1,3541248]{2,1,0:T(1,128)} %f.1, f32[1,1,3541248]{2,1,0:T(1,128)} %s.1, ...), custom_call_target="tpu_custom_call" | custom-call | bytes 125829120 | tf_op jit(solution)/shard_map/update/pallas_call | solution.py:1731
  1114.5 3.0 add_bitcast_fusion
  (160 shorter events, 5.2 us)
Async XLA Ops:
  7.2 7.1 copy-start.1
  7.2 299.5 %all-gather.2.cloned.1.call-start = ((), (), s32[]{:S(2)}) async-start(), calls=%async_computation.2 | async-start | bytes 14155776 | tf_op jit(solution)/shard_map/all_gather | solution.py:1829
  14.3 114.5 %copy-start.48 = (bf16[128,16]{0,1:T(8,128)(2,1)S(1)}, bf16[128,16]{0,1:T(8,128)(2,1)}, u32[]{:S(2)}) copy-start(bf16[128,16]{0,1:T(8,128)(2,1)} %param.22) | copy-start | bytes 12292
  128.7 607.8 %reduce-scatter.3.cloned.1.call-start = ((), (), s32[]{:S(2)}) async-start(), calls=%async_computation.3 | async-start | bytes 2654208 | tf_op jit(solution)/shard_map/reduce_scatter | solution.py:1937
  130.8 7.2 copy-start.52
  130.8 7.2 copy-start.53
  130.8 7.2 copy-start
  130.8 7.2 copy-start.4
  155.1 17.2 %copy-start.51 = (f32[32]{0:T(128)}, f32[32]{0:T(128)S(1)}, u32[]{:S(2)}) copy-start(f32[32]{0:T(128)S(1)} %multiply_power_fusion) | copy-start | bytes 388
  157.3 7.7 copy-start.44
  157.3 33.5 %copy-start.42 = (f32[1024,1]{0,1:T(1,128)}, f32[1024,1]{0,1:T(1,128)S(1)}, u32[]{:S(2)}) copy-start(f32[1024,1]{0,1:T(1,128)S(1)} %get-tuple-element.103) | copy-start | bytes 12292
  157.3 80.5 %copy-start.40 = (f32[1024,1]{0,1:T(1,128)}, f32[1024,1]{0,1:T(1,128)S(1)}, u32[]{:S(2)}) copy-start(f32[1024,1]{0,1:T(1,128)S(1)} %get-tuple-element.102) | copy-start | bytes 12292
  162.5 1.1 copy-start.46
  162.5 2.4 copy-start.12
  163.5 35.6 %copy-start.2 = (bf16[16,64,1024]{2,1,0:T(8,128)(2,1)}, bf16[16,64,1024]{2,1,0:T(8,128)(2,1)S(1)}, u32[]{:S(2)}) copy-start(bf16[16,64,1024]{2,1,0:T(8,128)(2,1)S(1)} %pad_maximum_fusion.2.q_ref) | copy-start | bytes 6291460
  163.6 35.5 %copy-start.8 = (s32[2]{0:T(128)}, s32[2]{0:T(128)S(1)}, u32[]{:S(2)}) copy-start(s32[2]{0:T(128)S(1)} %pad_add_fusion.where_ref) | copy-start | bytes 28
  163.6 8.8 copy-start.32
  163.7 77.1 %copy-start.30 = (pred[1024,16]{0,1:T(8,128)(4,1)}, pred[1024,16]{0,1:T(8,128)(4,1)S(1)}, u32[]{:S(2)}) copy-start(pred[1024,16]{0,1:T(8,128)(4,1)S(1)} %fusion.35) | copy-start | bytes 49156
  164.2 0.7 copy-start.27
  164.2 0.7 copy-start.29
  165.0 5.6 slice-start
  165.6 4.9 copy-start.22
  165.6 5.0 slice-start.1
  170.6 28.5 %copy-start.3 = (bf16[2,8,64,512]{3,2,1,0:T(8,128)(2,1)}, bf16[2,8,64,512]{3,2,1,0:T(8,128)(2,1)S(1)}, u32[]{:S(2)}) copy-start(bf16[2,8,64,512]{3,2,1,0:T(8,128)(2,1)S(1)} %pad_maximum_fusion.4.own_ref) | copy-start | bytes 3145732
  172.4 18.4 %copy-start.49 = (f32[4096]{0:T(1024)}, f32[4096]{0:T(1024)S(1)}, u32[]{:S(2)}) copy-start(f32[4096]{0:T(1024)S(1)} %add_rsqrt_fusion) | copy-start | bytes 49156
  232.8 4.9 copy-start.6
  232.8 4.9 copy-start.9
  237.8 2.9 copy-start.10
  237.8 0.6 copy-start.38
  238.8 67.8 %copy-start.17 = (bf16[1024,1024]{1,0:T(8,128)(2,1)}, bf16[1024,1024]{1,0:T(8,128)(2,1)S(1)}, u32[]{:S(2)}) copy-start(bf16[1024,1024]{1,0:T(8,128)(2,1)S(1)} %multiply_convert_fusion.x_hbm) | copy-start | bytes 6291460
  240.7 0.6 copy-start.24
  240.7 0.6 copy-start.34
  241.3 0.6 copy-start.36
  455.8 7.4 collective-permute-start
  467.4 3.4 copy-start.15
  472.4 173.6 %collective-permute-start.1 = (bf16[1024,1024]{1,0:T(8,128)(2,1)}, bf16[1024,1024]{1,0:T(8,128)(2,1)}, u32[]{:S(2)}, u32[]{:S(2)}) collective-permute-start(bf16[1024,1024]{1,0:T(8,128)(2,1)} %fusion.16), channel_id=1, source_target_pairs={{0,2},{1,3},{2,0},{3,1},{4,6},{5,7},{6,4},{7,5},{8,10},{9,11},{10,... | collective-permute-start | bytes 6291464 | tf_op jit(solution)/shard_map/ppermute | solution.py:1901
  474.1 165.5 %copy-start.47 = (f32[4,8,1024]{2,1,0:T(8,128)S(1)}, f32[4,8,1024]{2,1,0:T(8,128)}, u32[]{:S(2)}) copy-start(f32[4,8,1024]{2,1,0:T(8,128)} %get-tuple-element.63) | copy-start | bytes 393220
  474.1 165.6 %copy-start.25 = (f32[1024,16]{0,1:T(8,128)S(1)}, f32[1024,16]{0,1:T(8,128)}, u32[]{:S(2)}) copy-start(f32[1024,16]{0,1:T(8,128)} %copy-done.24) | copy-start | bytes 196612
  474.1 165.6 %copy-start.31 = (pred[1024,16]{0,1:T(8,128)(4,1)S(1)}, pred[1024,16]{0,1:T(8,128)(4,1)}, u32[]{:S(2)}) copy-start(pred[1024,16]{0,1:T(8,128)(4,1)} %copy-done.30) | copy-start | bytes 49156
  474.1 165.6 %copy-start.35 = (f32[1024]{0:T(1024)S(1)}, f32[1024]{0:T(1024)}, u32[]{:S(2)}) copy-start(f32[1024]{0:T(1024)} %copy-done.34) | copy-start | bytes 12292
  474.1 165.6 %copy-start.37 = (f32[1024]{0:T(1024)S(1)}, f32[1024]{0:T(1024)}, u32[]{:S(2)}) copy-start(f32[1024]{0:T(1024)} %copy-done.36) | copy-start | bytes 12292
  474.1 165.7 %copy-start.18 = (bf16[1024,1024]{1,0:T(8,128)(2,1)S(1)}, bf16[1024,1024]{1,0:T(8,128)(2,1)}, u32[]{:S(2)}) copy-start(bf16[1024,1024]{1,0:T(8,128)(2,1)} %copy-done.17) | copy-start | bytes 6291460
  474.1 166.3 %copy-start.39 = (f32[1024]{0:T(1024)S(1)}, f32[1024]{0:T(1024)}, u32[]{:S(2)}) copy-start(f32[1024]{0:T(1024)} %copy-done.38) | copy-start | bytes 12292
  474.1 166.3 %copy-start.41 = (f32[1024,1]{0,1:T(1,128)S(1)}, f32[1024,1]{0,1:T(1,128)}, u32[]{:S(2)}) copy-start(f32[1024,1]{0,1:T(1,128)} %copy-done.40) | copy-start | bytes 12292
  640.4 5.6 copy-start.11
  640.4 7.8 copy-start.16
  640.4 8.4 copy-start.21
  648.8 4.5 copy-start.7
  653.3 2.4 copy-start.19
  661.0 3.8 copy-start.33
  661.0 6.2 copy-start.28
  664.6 398.0 %reduce-scatter.5.cloned.1.call-start = ((), (), s32[]{:S(2)}) async-start(), calls=%async_computation.4 | async-start | bytes 9437184 | tf_op jit(solution)/shard_map/reduce_scatter | solution.py:1997
  736.5 0.7 copy-start.43
  736.6 0.7 copy-start.50
  737.3 15.4 %copy-start.23 = (bf16[512,1024]{1,0:T(8,128)(2,1)S(1)}, bf16[512,1024]{1,0:T(8,128)(2,1)}, u32[]{:S(2)}) copy-start(bf16[512,1024]{1,0:T(8,128)(2,1)} %copy-done.22) | copy-start | bytes 3145732
  737.3 15.4 %copy-start.26 = (bf16[2,8,64,512]{3,2,1,0:T(8,128)(2,1)S(1)}, bf16[2,8,64,512]{3,2,1,0:T(8,128)(2,1)}, u32[]{:S(2)}) copy-start(bf16[2,8,64,512]{3,2,1,0:T(8,128)(2,1)} %get-tuple-element.76) | copy-start | bytes 3145732
  752.7 1.6 copy-start.13
  752.7 1.6 copy-start.45
  752.7 2.2 copy-start.55
  757.5 1.0 copy-start.5
  758.5 190.1 %copy-start.54 = (bf16[128]{0:T(256)(128)(2,1)S(1)}, bf16[128]{0:T(256)(128)(2,1)}, u32[]{:S(2)}) copy-start(bf16[128]{0:T(256)(128)(2,1)} %param.18) | copy-start | bytes 772
  965.6 96.9 %copy-start.14 = (bf16[1,1,1024,1024]{3,2,1,0:T(8,128)(2,1)S(1)}, bf16[1,1,1024,1024]{3,2,1,0:T(8,128)(2,1)}, u32[]{:S(2)}) copy-start(bf16[1,1,1024,1024]{3,2,1,0:T(8,128)(2,1)} %param.14) | copy-start | bytes 6291460
  1070.8 43.7 %copy-start.20 = (f32[1024,1024]{1,0:T(8,128)S(1)}, f32[1024,1024]{1,0:T(8,128)}, u32[]{:S(2)}) copy-start(f32[1024,1024]{1,0:T(8,128)} %copy-done.19) | copy-start | bytes 12582916
Sparse Core Ops, SparseCore 0:
  128.9 177.7 all-gather.1
  664.7 68.3 reduce-scatter.2
  737.3 297.9 reduce-scatter.4

commit v7 on v6

--- a/solution.py
+++ b/solution.py
@@ -1897,9 +1897,7 @@
     grad_gates = dgate_part[:, :local].reshape(EXPERTS, count).T
     to_core = [(i, i + 1 - 2 * (i % 2)) for i in range(reps)]
     to_far = [(i, (i + 2) % reps) for i in range(reps)]
-    y_near = y_keep.astype(F32) + lax.ppermute(y_give, "rep", to_core).astype(F32)
-    y_sum = y_near[0] + lax.ppermute(y_near[1].astype(BF16), "rep", to_far).astype(F32)
-    block_out = (x_mid + y_sum).astype(BF16)
+    y_core = lax.ppermute(y_give, "rep", to_core)
 
     def rep_sum(values):
         for pairs in (to_core, to_far):
@@ -1929,6 +1927,10 @@
         terms = jnp.concatenate([expert_term(normed_t, dgu), expert_term(top_t, gated)], axis=1)
         terms = lax.psum_scatter(terms, "shard", scatter_dimension=0, tiled=True)
         expert_rows = lax.all_gather(terms, "rep", axis=0, tiled=False)
+    y_core, expert_rows = lax.optimization_barrier((y_core, expert_rows))
+    y_near = y_keep.astype(F32) + y_core.astype(F32)
+    y_far = lax.ppermute(y_near[1].astype(BF16), "rep", to_far)
+
     blank = jnp.zeros((width, -(Q_WIDTH + EXPERTS + 1) % LANES), BF16)
     early = jnp.concatenate(
         [grad_attn_w.astype(BF16), grad_router_w.astype(BF16), grad_ffn_gain[:, None].astype(BF16), blank], axis=1
@@ -1940,9 +1942,10 @@
         where, query, prompt_kv, own_kv, grad_attn, attn, lse, jnp.concatenate(prompt_turn), jnp.concatenate(own_turn)
     )
 
-    early, grad_query, grad_prompt_kv, grad_own_kv = lax.optimization_barrier(
-        (early, grad_query, grad_prompt_kv, grad_own_kv)
+    early, y_far, grad_query, grad_prompt_kv, grad_own_kv = lax.optimization_barrier(
+        (early, y_far, grad_query, grad_prompt_kv, grad_own_kv)
     )
+    block_out = (x_mid + y_near[0] + y_far.astype(F32)).astype(BF16)
     grad_query = grad_query.reshape(Q_WIDTH, count)
     grad_prompt_kv = grad_prompt_kv.reshape(2 * KV_WIDTH, GROUP_SIZE * prompt)
     grad_own_kv = grad_own_kv.reshape(2 * KV_WIDTH, CONTINUATION_LEN)

time: 1140 us -> 1130 us (level)
  waiting for transfers between devices: 71.3 us -> 41.5 us
  Pallas kernels: 891 us -> 920 us
    pallas_call x1, Pallas kernels: 66.5 us -> 111 us  [attn_backward(): pl.pallas_call(attn_backward_kernel, grid=(query.shape[0] // PER_KEY,), i...]
    pallas_call x1, Pallas kernels: 190 us -> 148 us  [late_reduce(): pl.pallas_call(late_reduce_kernel, in_specs=[anywhere, pl.BlockSpec(memor...]
    all_gather x1, waiting for transfers between devices: 64 us -> 41.4 us  [per_device(): w_both = gather(w_both)]
    pallas_call x1, Pallas kernels: 33.7 us -> 54.8 us  [attn_forward(): pl.pallas_call(attn_forward_kernel, grid=(query.shape[0] // PER_KEY,), in...]
  transfers between devices with their start and end apart: 5 -> 5, of which waited for: 2 -> 1; matrix products, arithmetic and copies ran while one was open for 8% -> 9% of each run, Pallas kernels for 52% -> 55%
where the time goes in v7:
time: 1130 us
  Pallas kernels  920 us (81%)
  matrix products  80.7 us (7%)
  waiting for transfers between devices  41.5 us (4%)
  other arithmetic  37.8 us (3%)
  local copies, waits for them, and re-layouts  28.2 us (2%)
  between operations  17.5 us (2%)
    pallas_call x1, Pallas kernels, expert_grads(): pl.pallas_call(expert_grads_kernel, in_specs=[anywhere] * 4, out_specs=an...  167 us
    pallas_call x1, Pallas kernels, experts(): pl.pallas_call(experts_kernel, grid=(len(ORDER),), in_specs=[anywhere, an...  149 us
    pallas_call x1, Pallas kernels, late_reduce(): pl.pallas_call(late_reduce_kernel, in_specs=[anywhere, pl.BlockSpec(memor...  148 us
    pallas_call x1, Pallas kernels, start_gather(): pl.pallas_call(start_kernel, in_specs=[anywhere] * 3, out_specs=[anywhere...  112 us
    pallas_call x1, Pallas kernels, attn_backward(): pl.pallas_call(attn_backward_kernel, grid=(query.shape[0] // PER_KEY,), i...  111 us
    pallas_call x1, Pallas kernels, summed_step(): pl.pallas_call(step_kernel, in_specs=[pl.BlockSpec(memory_space=pltpu.VME...  101 us
    dot_general x15, matrix products, dot(): lax.dot_general(left, right, ((dims[:1], dims[1:]), ((), ())), preferred_...  80.7 us
    pallas_call x1, Pallas kernels, attn_forward(): pl.pallas_call(attn_forward_kernel, grid=(query.shape[0] // PER_KEY,), in...  54.8 us
  transfers between devices with their start and end apart: 5, of which 1 were waited for; matrix products, arithmetic and copies ran while one was open for 9% of the time, Pallas kernels for 55%

profile of v7, /device:TPU:0, one launch (start us, length us, event | category | flops | bytes accessed | tf_op | source)
XLA Modules:
  0.0 1126.5 jit_solution(10462871150489570876)
XLA Ops:
  7.2 0.9 copy.68
  8.2 0.8 copy.69
  9.0 0.8 copy.70
  9.7 1.2 concatenate.61
  11.0 1.0 pad.8.w_ref
  11.9 2.3 constant_dynamic-slice_fusion.1
  14.3 2.5 pad_maximum_fusion.3
  16.8 111.9 %start_gather.1 = (bf16[8,512,1024]{2,1,0:T(8,128)(2,1)}, bf16[8,4,32,3200]{3,2,1,0:T(8,128)(2,1)}, bf16[4,1024,1024]{2,1,0:T(8,128)(2,1)}) custom-call(bf16[1024,1024]{1,0:T(8,128)(2,1)} %bitcast.113, bf16[128,3200]{1,0:T(8,128)(2,1)} %pad.8.w_ref, bf16[1024,1024]{1,0:T(8,128)(2,1)} %bitcast.125), custom_call_target="tpu_custom_call" | custom-call | bytes 67108864 | tf_op jit(solution)/shard_map/start_gather/pallas_call | solution.py:608
  129.6 1.1 slice.104
  130.9 3.2 slice_bitcast_fusion.1
  134.0 3.9 copy.71
  138.1 17.0 %flatten.2 = (f32[1,3541248]{1,0:T(1,128)}, f32[1,1]{1,0:T(1,128)}) custom-call(f32[18,128]{1,0:T(8,128)S(1)} %pad_maximum_fusion.7.lead_ref, bf16[128,2048]{1,0:T(8,128)(2,1)S(1)} %copy-done, bf16[128,1024]{1,0:T(8,128)(2,1)S(1)} %copy-done.4, bf16[128,16384]{1,0:T(8,128)(2,1)} %refs_2_.1, bf16[128,8192]{1,0:T(8,128)(2,1)S(1)} %copy-done.1), custom_call_target="tpu_custom_call" | custom-call | tf_op jit(solution)/shard_map/flatten/pallas_call | solution.py:1439
  155.1 2.1 fusion.3
  157.3 0.5 multiply_cosine_fusion.3
  157.8 4.7 fusion.18
  162.5 0.7 subtract_convert_fusion.1
  163.7 0.5 multiply_cosine_fusion.2
  164.3 0.3 convert_multiply_fusion.3
  164.9 2.7 fusion.31
  167.8 2.0 convolution_convert_fusion.3
  169.9 1.7 fusion
  171.6 1.9 multiply_cosine_fusion.1
  173.5 9.2 fusion.33
  182.8 4.7 subtract_convert_fusion
  187.5 2.5 pad_maximum_fusion.k_ref
  190.0 8.3 convolution_convert_fusion
  198.3 54.8 %attn_forward.1 = (bf16[16,64,1024]{2,1,0:T(8,128)(2,1)S(1)}, f32[8,2,1024]{2,1,0:T(2,128)S(1)}) custom-call(s32[2]{0:T(128)S(1)} %pad_add_fusion.where_ref, bf16[16,64,1024]{2,1,0:T(8,128)(2,1)S(1)} %pad_maximum_fusion.2.q_ref, bf16[8,64,4096]{2,1,0:T(8,128)(2,1)} %pad_maximum_fusion.k_ref, bf16[8,64,4096]{2,1,0:T(8,128)(2,1)} %bitcast.157, ...), custom_call_target="tpu_custom_call" | custom-call | flops 17179869184 | bytes 16777216 | tf_op jit(solution)/shard_map/attn_forward/pallas_call | solution.py:172
  253.1 4.9 multiply_reduce_fusion.2
  258.1 0.4 multiply_convert_fusion.x_hbm
  258.5 1.8 fusion.49
  260.4 0.4 copy-done.16
  260.9 0.7 pad.9.gates_ref
  261.6 0.7 pad_maximum_fusion.6.own_turn_ref
  262.3 1.9 multiply_cosine_fusion
  264.2 1.0 pad_maximum_fusion.5.turn_ref
  265.2 41.4 %all-gather.2.cloned.1.call-done.w_ref = bf16[1024,6144]{1,0:T(8,128)(2,1)} async-done(((bf16[128,6144]{1,0:T(8,128)(2,1)}), bf16[1024,6144]{1,0:T(8,128)(2,1)}) %all-gather.2.cloned.1.call-update) | async-done | bytes 12582928 | tf_op jit(solution)/shard_map/all_gather | solution.py:1829
  306.6 149.1 %experts.1 = (bf16[4,1024,1024]{2,1,0:T(8,128)(2,1)}, bf16[1024,1024]{1,0:T(8,128)(2,1)}, bf16[1024,1024]{1,0:T(8,128)(2,1)}, bf16[1024,1024]{1,0:T(8,128)(2,1)}...) custom-call(bf16[1024,1024]{1,0:T(8,128)(2,1)} %copy-done.16, ...), custom_call_target="tpu_custom_call" | custom-call | flops 103079215104 | bytes 83886080 | tf_op jit(solution)/shard_map/experts/pallas_call | solution.py:896
  455.7 0.9 slice.97
  456.7 2.0 convolution_convert_fusion.4
  458.7 5.4 multiply_reduce_fusion
  464.1 0.6 copy-done.19
  464.7 1.6 subtract_add_fusion
  466.4 3.7 convolution_convert_fusion.1
  470.1 5.4 convolution_convert_fusion.2
  476.1 3.5 concatenate.69
  479.6 166.6 %expert_grads.1.refs_2_.refs_3_ = bf16[4,128,6144]{2,1,0:T(8,128)(2,1)} custom-call(bf16[1024,4096]{1,0:T(8,128)(2,1)} %get-tuple-element.63.xt_ref, bf16[1024,4096]{1,0:T(8,128)(2,1)} %get-tuple-element.64.tt_ref, bf16[4096,4096]{1,0:T(8,128)(2,1)} %bitcast.155, bf16[4096,2048]{1,0:T(8,128)(2,1)} %bitcast.156), custom_call_target="tpu_custom_call" | custom-call | flops 51539607552 | bytes 83886080 | tf_op jit(solution)/shard_map/expert_grads/pallas_call | solution.py:1179
  646.5 5.5 convert_add_fusion
  651.9 3.4 copy-done.15
  655.3 0.3 fusion.16
  655.7 111.0 %attn_backward.1 = (bf16[16,64,1024]{2,1,0:T(8,128)(2,1)}, bf16[2,8,64,4096]{3,2,1,0:T(8,128)(2,1)}, bf16[2,8,64,512]{3,2,1,0:T(8,128)(2,1)}) custom-call(s32[2]{0:T(128)} %copy-done.7, bf16[16,64,1024]{2,1,0:T(8,128)(2,1)} %copy-done.2, bf16[8,64,4096]{2,1,0:T(8,128)(2,1)} %pad_maximum_fusion.k_ref, bf16[8,64,4096]{2,1,0:T(8,128)(2,1)} %bitcast.158, ...), custom_call_target="tpu_custom_call" | custom-call | flops 42949672960 | bytes 33554432 | tf_op jit(solution)/shard_map/attn_backward/pallas_call | solution.py:308
  766.8 1.2 copy-done.22
  768.0 0.3 copy-done.35
  768.3 3.3 fusion.56
  771.7 2.7 fusion.22
  774.4 16.3 %add_convert_fusion = bf16[1024,1024]{1,0:T(8,128)(2,1)S(1)} fusion(f32[1024,1024]{1,0:T(8,128)} %fusion.56, bf16[1024,4096]{1,0:T(8,128)(2,1)} %bitcast.123, bf16[4096,1024]{1,0:T(8,128)(2,1)} %bitcast.116, f32[1024]{0:T(1024)S(1)} %bitcast.148, f32[4096]{0:T(1024)S(1)} %copy-done.30), kind=kOutput, calls=%fused_computation.28 | convolution fusion | flops 8608808960 | bytes 23089152 | tf_op jit(solution)/shard_map/dot_general | solution.py:43
  790.7 0.3 pad_maximum_fusion.1.in_ref
  791.0 0.6 copy-done.5
  791.6 148.4 %late_reduce.1 = (bf16[128,2048]{1,0:T(8,128)(2,1)S(1)}, bf16[128,1152]{1,0:T(8,128)(2,1)S(1)}) custom-call(bf16[1024,2048]{1,0:T(8,128)(2,1)S(1)} %pad_maximum_fusion.1.in_ref, bf16[128,1152]{1,0:T(8,128)(2,1)S(1)} %copy-done.5), custom_call_target="tpu_custom_call" | custom-call | bytes 4194304 | tf_op jit(solution)/shard_map/late_reduce/pallas_call | solution.py:1337
  940.6 17.2 %flatten.3 = (f32[1,3541248]{1,0:T(1,128)}, f32[1,1]{1,0:T(1,128)}) custom-call(f32[18,128]{1,0:T(8,128)S(1)} %pad_maximum_fusion.8.lead_ref, bf16[128,2048]{1,0:T(8,128)(2,1)S(1)} %get-tuple-element.84.refs_0_, bf16[128,1024]{1,0:T(8,128)(2,1)S(1)} %slice.101.refs_1_, bf16[4,128,6144]{2,1,0:T(8,128)(2,1)} %expert_grads.1.refs_2_.refs_3_, ...), custom_call_target="tpu_custom_call" | custom-call | tf_op jit(solution)/shard_map/flatten/pallas_call | solution.py:1439
  957.9 100.6 %summed_step.1 = (f32[1,1]{1,0:T(1,128)}, bf16[2,13840,128]{2,1,0:T(8,128)(2,1)}) custom-call(f32[1,1]{1,0:T(1,128)} %get-tuple-element.87.square_ref, f32[1,3541248]{1,0:T(1,128)} %get-tuple-element.137.g_ref.g, f32[1,1,3541248]{2,1,0:T(1,128)} %f.1, f32[1,1,3541248]{2,1,0:T(1,128)} %s.1, f32[1,3541248]{1,0:T(1,128)} %get-tuple-element.89.w_ref), custom_call_target="tpu_custom_call" | custom-call | bytes 4194304 | tf_op jit(solution)/shard_map/summed_step/pallas_call | solution.py:1650
  1058.6 4.3 fusion.15
  1062.9 8.2 fusion.4
  1071.1 43.7 %update.1 = (f32[1,1,3541248]{2,1,0:T(1,128)}, f32[1,1,3541248]{2,1,0:T(1,128)}, f32[1,3541248]{1,0:T(1,128)}, f32[1,3541248]{1,0:T(1,128)}) custom-call(f32[1,1]{1,0:T(1,128)} %get-tuple-element.92.norm_ref, f32[1,3541248]{1,0:T(1,128)} %get-tuple-element.137.g_ref.g, f32[1,1,3541248]{2,1,0:T(1,128)} %f.1, f32[1,1,3541248]{2,1,0:T(1,128)} %s.1, ...), custom_call_target="tpu_custom_call" | custom-call | bytes 125829120 | tf_op jit(solution)/shard_map/update/pallas_call | solution.py:1731
  1114.8 3.0 add_bitcast_fusion
  (126 shorter events, 3.2 us)
Async XLA Ops:
  7.2 7.1 copy-start.1
  7.2 299.4 %all-gather.2.cloned.1.call-start = ((), (), s32[]{:S(2)}) async-start(), calls=%async_computation.2 | async-start | bytes 14155776 | tf_op jit(solution)/shard_map/all_gather | solution.py:1829
  14.3 114.5 %copy-start.28 = (bf16[128,16]{0,1:T(8,128)(2,1)S(1)}, bf16[128,16]{0,1:T(8,128)(2,1)}, u32[]{:S(2)}) copy-start(bf16[128,16]{0,1:T(8,128)(2,1)} %param.22) | copy-start | bytes 12292
  128.7 638.0 %reduce-scatter.3.cloned.1.call-start = ((), (), s32[]{:S(2)}) async-start(), calls=%async_computation.3 | async-start | bytes 2654208 | tf_op jit(solution)/shard_map/reduce_scatter | solution.py:1939
  130.8 7.2 copy-start.31
  130.8 7.2 copy-start.32
  130.8 7.2 copy-start
  130.8 7.2 copy-start.4
  157.2 7.0 copy-start.25
  157.3 32.7 %copy-start.23 = (f32[1024,1]{0,1:T(1,128)}, f32[1024,1]{0,1:T(1,128)S(1)}, u32[]{:S(2)}) copy-start(f32[1024,1]{0,1:T(1,128)S(1)} %get-tuple-element.107) | copy-start | bytes 12292
  162.5 1.1 copy-start.27
  162.5 1.7 copy-start.12
  163.5 34.8 %copy-start.2 = (bf16[16,64,1024]{2,1,0:T(8,128)(2,1)}, bf16[16,64,1024]{2,1,0:T(8,128)(2,1)S(1)}, u32[]{:S(2)}) copy-start(bf16[16,64,1024]{2,1,0:T(8,128)(2,1)S(1)} %pad_maximum_fusion.2.q_ref) | copy-start | bytes 6291460
  163.6 34.7 %copy-start.7 = (s32[2]{0:T(128)}, s32[2]{0:T(128)S(1)}, u32[]{:S(2)}) copy-start(s32[2]{0:T(128)S(1)} %pad_add_fusion.where_ref) | copy-start | bytes 28
  164.2 5.6 slice-start.2
  164.9 4.9 copy-start.21
  164.9 5.0 slice-start.3
  169.9 28.4 %copy-start.3 = (bf16[2,8,64,512]{3,2,1,0:T(8,128)(2,1)}, bf16[2,8,64,512]{3,2,1,0:T(8,128)(2,1)S(1)}, u32[]{:S(2)}) copy-start(bf16[2,8,64,512]{3,2,1,0:T(8,128)(2,1)S(1)} %pad_maximum_fusion.4.own_ref) | copy-start | bytes 3145732
  171.6 18.4 %copy-start.29 = (f32[4096]{0:T(1024)}, f32[4096]{0:T(1024)S(1)}, u32[]{:S(2)}) copy-start(f32[4096]{0:T(1024)S(1)} %add_rsqrt_fusion) | copy-start | bytes 49156
  253.1 5.0 copy-start.8
  253.1 213.2 %copy-start.6 = (bf16[16,64,1024]{2,1,0:T(8,128)(2,1)}, bf16[16,64,1024]{2,1,0:T(8,128)(2,1)S(1)}, u32[]{:S(2)}) copy-start(bf16[16,64,1024]{2,1,0:T(8,128)(2,1)S(1)} %get-tuple-element.58.o_ref) | copy-start | bytes 6291460
  258.1 2.3 copy-start.9
  258.5 2.3 copy-start.16
  458.7 5.4 copy-start.10
  458.7 6.0 copy-start.19
  466.4 3.7 copy-start.17
  470.1 6.0 copy-start.20
  475.5 170.7 %collective-permute-start = (bf16[2,1024,1024]{2,1,0:T(8,128)(2,1)}, bf16[2,1024,1024]{2,1,0:T(8,128)(2,1)}, u32[]{:S(2)}, u32[]{:S(2)}) collective-permute-start(bf16[2,1024,1024]{2,1,0:T(8,128)(2,1)} %get-tuple-element.62), channel_id=1, source_target_pairs={{0,1},{1,0},{2,3},{3,2},{4,5},{5,4},{6,7},{7,6},{8,9},{9,8},{10,11... | collective-permute-start | bytes 12582920 | tf_op jit(solution)/shard_map/ppermute | solution.py:1900
  646.2 416.7 %reduce-scatter.5.cloned.1.call-start = ((), (), s32[]{:S(2)}) async-start(), calls=%async_computation.4 | async-start | bytes 9437184 | tf_op jit(solution)/shard_map/reduce_scatter | solution.py:2000
  651.9 3.4 copy-start.15
  655.6 111.1 %collective-permute-start.1 = (bf16[1024,1024]{1,0:T(8,128)(2,1)S(1)}, bf16[1024,1024]{1,0:T(8,128)(2,1)}, u32[]{:S(2)}, u32[]{:S(2)}) collective-permute-start(bf16[1024,1024]{1,0:T(8,128)(2,1)S(1)} %fusion.16), channel_id=1, source_target_pairs={{0,2},{1,3},{2,0},{3,1},{4,6},{5,7},{6,4},{7,5},{8,10},{9,11},{10,... | collective-permute-start | bytes 6291464 | tf_op jit(solution)/shard_map/ppermute | solution.py:1932
  766.8 1.2 copy-start.22
  766.8 1.5 copy-start.35
  768.3 3.3 copy-start.13
  768.3 3.3 copy-start.24
  768.3 3.3 copy-start.26
  768.3 3.3 copy-start.34
  771.7 2.7 copy-start.30
  790.7 1.0 copy-start.5
  791.6 149.0 %copy-start.33 = (bf16[128]{0:T(256)(128)(2,1)S(1)}, bf16[128]{0:T(256)(128)(2,1)}, u32[]{:S(2)}) copy-start(bf16[128]{0:T(256)(128)(2,1)} %param.18) | copy-start | bytes 772
  940.6 117.9 %slice-start = ((s8[8388608]{0:T(1024)(128)(4,1)}), s8[4194304]{0:T(1024)(128)(4,1)S(1)}, s32[]{:S(2)}) async-start(s8[8388608]{0:T(1024)(128)(4,1)} %bitcast.114), calls=%async_computation.5 | async-start | bytes 8388608
  957.9 100.7 %copy-start.11 = (f32[1024,1024]{1,0:T(8,128)S(1)}, f32[1024,1024]{1,0:T(8,128)}, u32[]{:S(2)}) copy-start(f32[1024,1024]{1,0:T(8,128)} %copy-done.9) | copy-start | bytes 12582916
  957.9 100.7 %slice-start.1 = ((s8[8388608]{0:T(1024)(128)(4,1)}), s8[4194304]{0:T(1024)(128)(4,1)S(1)}, s32[]{:S(2)}) async-start(s8[8388608]{0:T(1024)(128)(4,1)} %bitcast.114), calls=%async_computation.6 | async-start | bytes 8388608
  1058.6 4.3 copy-start.14
  1071.1 43.7 %copy-start.18 = (f32[1024,1024]{1,0:T(8,128)S(1)}, f32[1024,1024]{1,0:T(8,128)}, u32[]{:S(2)}) copy-start(f32[1024,1024]{1,0:T(8,128)} %copy-done.17) | copy-start | bytes 12582916
Sparse Core Ops, SparseCore 0:
  128.9 177.6 all-gather.1
  646.4 68.3 reduce-scatter.2
  766.9 257.3 reduce-scatter.4
